TPU v7x, 128 devices: a whole 4x4x4 slice. The times are simulated.
128 devices in a mesh: row: 8 (over y, z_hi), col: 16 (over z_lo, x, core).
Axes of the slice: x: 4, y: 4, z: 4 (z_hi: 2, z_lo: 2; z = z_hi * 2 + z_lo), core: 2. Of those that a mesh axis runs over, the one named last changes fastest.
Arguments:
- alignment: bfloat16 [256, 1024, 256], P(('row', 'col')), may hold values from -6 to 6
- left_weight: bfloat16 [256, 32], replicated, may hold values from -0.375 to 0.375
- right_weight: bfloat16 [256, 32], replicated, may hold values from -0.375 to 0.375
- out_weight: bfloat16 [1024, 128], replicated, may hold values from -1 to 1
- out_bias: bfloat16 [128], replicated, may hold values from -3 to 3
- pair_cotangent: bfloat16 [1024, 1024, 128], P('row', 'col'), may hold values from -6 to 6
Outputs:
- pair_update: bfloat16 [1024, 1024, 128], P('row', 'col')
- grad_alignment: bfloat16 [256, 1024, 256], P(('row', 'col'))
- grad_out_weight: float32 [1024, 128], P(('row', 'col'))
- grad_left_weight: float32 [256, 32], replicated
- grad_right_weight: float32 [256, 32], replicated
All inputs are finite; a program needn't handle non-finite values.
Results may differ from a plain program's by a relative error of at most 0.024.
Values may be sent and summed in bfloat16 or wider, within the bound.
No kernel may reach another device: no remote copies, remote signals or barrier semaphores. Data moves between devices by JAX's collectives and lax.ppermute only.
A program may use at most 192 MiB of HBM per device.

v0:
```python
import jax
import jax.numpy as jnp
from jax import lax
from jax.sharding import PartitionSpec as P


def layer_norm(values):
    centered = values - jnp.mean(values, axis=-1, keepdims=True)
    inv_sigma = lax.rsqrt(jnp.mean(centered * centered, axis=-1, keepdims=True) + 1e-05)
    return (centered * inv_sigma, inv_sigma)


def norm_backward(upstream, normed, inv_sigma):
    first = jnp.mean(upstream, axis=-1, keepdims=True)
    second = jnp.mean(upstream * normed, axis=-1, keepdims=True)
    return inv_sigma * (upstream - first - normed * second)


def reorder(panel, outer_groups, inner_groups):
    local = panel.shape[0] // (outer_groups * inner_groups)
    grouped = panel.reshape((outer_groups, inner_groups, local) + panel.shape[1:])
    return jnp.swapaxes(grouped, 0, 1).reshape(panel.shape)


def body(alignment, left_weight, right_weight, out_weight, out_bias, pair_cotangent):
    rows_count = lax.axis_size("row")
    cols_count = lax.axis_size("col")
    local_seqs = alignment.shape[0]
    total_seqs = local_seqs * rows_count * cols_count
    inverse_count = 1.0 / total_seqs
    width = left_weight.shape[1]
    model_width = alignment.shape[2]
    normed, inv_sigma = layer_norm(alignment.astype(jnp.float32))
    normed_low = normed.astype(jnp.bfloat16)
    left = jnp.einsum(
        "src,ch->srh", normed_low, left_weight, preferred_element_type=jnp.float32
    ).astype(jnp.bfloat16)
    right = jnp.einsum(
        "src,ch->srh", normed_low, right_weight, preferred_element_type=jnp.float32
    ).astype(jnp.bfloat16)
    grid_row = lax.all_gather(left, "col", axis=0, tiled=True)
    left_panel = lax.all_to_all(grid_row, "row", split_axis=1, concat_axis=0, tiled=True)
    grid_col = lax.all_gather(right, "row", axis=0, tiled=True)
    right_panel = reorder(
        lax.all_to_all(grid_col, "col", split_axis=1, concat_axis=0, tiled=True),
        cols_count,
        rows_count,
    )
    row_block = left_panel.shape[1]
    col_block = right_panel.shape[1]
    pair_width = out_weight.shape[1]
    outer_mean = (
        jnp.einsum("sic,sje->ijce", left_panel, right_panel, preferred_element_type=jnp.float32)
        * inverse_count
    )
    outer_low = outer_mean.astype(jnp.bfloat16).reshape(row_block * col_block, width * width)
    update = jnp.dot(outer_low, out_weight, preferred_element_type=jnp.float32) + out_bias.astype(
        jnp.float32
    )
    pair_update = update.astype(jnp.bfloat16).reshape(row_block, col_block, pair_width)
    cot_flat = pair_cotangent.reshape(row_block * col_block, pair_width)
    weight_term = jnp.dot(outer_low.T, cot_flat, preferred_element_type=jnp.float32)
    outer_grad = (
        jnp.dot(cot_flat, out_weight.T, preferred_element_type=jnp.float32) * inverse_count
    ).astype(jnp.bfloat16)
    outer_grad = outer_grad.reshape(row_block, col_block, width, width)
    right_cross = reorder(right_panel, rows_count, cols_count)
    piece = right_cross
    left_part = lax.psum_scatter(
        jnp.einsum("ijce,sje->sic", outer_grad, piece, preferred_element_type=jnp.float32).astype(
            jnp.bfloat16
        ),
        "col",
        scatter_dimension=0,
        tiled=True,
    )
    left_grad = lax.all_to_all(left_part, "row", split_axis=0, concat_axis=1, tiled=True)
    piece = left_panel
    right_part = lax.psum_scatter(
        jnp.einsum("ijce,sic->sje", outer_grad, piece, preferred_element_type=jnp.float32).astype(
            jnp.bfloat16
        ),
        "row",
        scatter_dimension=0,
        tiled=True,
    )
    right_grad = lax.all_to_all(right_part, "col", split_axis=0, concat_axis=1, tiled=True)
    residues = alignment.shape[1]
    flat_normed = normed_low.reshape(local_seqs * residues, model_width)
    flat_left = left_grad.reshape(local_seqs * residues, width)
    flat_right = right_grad.reshape(local_seqs * residues, width)
    left_wgrad = jnp.dot(flat_normed.T, flat_left, preferred_element_type=jnp.float32)
    right_wgrad = jnp.dot(flat_normed.T, flat_right, preferred_element_type=jnp.float32)
    grad_left_weight, grad_right_weight = lax.psum((left_wgrad, right_wgrad), ("row", "col"))
    whole_grad = lax.psum(weight_term, ("row", "col"))
    share_rows = whole_grad.shape[0] // (rows_count * cols_count)
    grad_out_weight = lax.dynamic_slice_in_dim(
        whole_grad, lax.axis_index(("row", "col")) * share_rows, share_rows, 0
    )
    upstream = jnp.dot(flat_left, left_weight.T, preferred_element_type=jnp.float32) + jnp.dot(
        flat_right, right_weight.T, preferred_element_type=jnp.float32
    )
    upstream = upstream.reshape(local_seqs, residues, model_width)
    grad_alignment = norm_backward(upstream, normed, inv_sigma).astype(jnp.bfloat16)
    return (pair_update, grad_alignment, grad_out_weight, grad_left_weight, grad_right_weight)


def solution(mesh):
    return jax.shard_map(
        body,
        mesh=mesh,
        in_specs=(P(("row", "col"), None, None), P(), P(), P(), P(), P("row", "col", None)),
        out_specs=(
            P("row", "col", None),
            P(("row", "col"), None, None),
            P(("row", "col"), None),
            P(),
            P(),
        ),
        check_vma=False,
    )
```

profile of v0, /device:TPU:1, one launch (start us, length us, event | category | flops | bytes accessed | tf_op | source)
XLA Modules:
  0.0 755.6 jit_solution(1857481231155151446)
XLA Ops:
  16.1 47.5 %all-gather.3.cloned.1.call-done = bf16[16,1024,32]{1,2,0:T(8,128)(2,1)} async-done(((bf16[2,1024,32]{1,2,0:T(8,128)(2,1)}), bf16[16,1024,32]{1,2,0:T(8,128)(2,1)}) %all-gather.3.cloned.1.call-update) | async-done | bytes 1048592 | tf_op jit(solution)/shard_map/all_gather | solution.py:43
  63.6 5.9 copy.27
  69.5 7.4 reshape.87
  76.9 6.1 all-to-all-start
  83.3 8.3 %multiply_convert_fusion = bf16[8192,1024]{1,0:T(8,128)(2,1)} fusion(bf16[8192,128]{1,0:T(8,128)(2,1)S(1)} %bitcast.95, bf16[1024,128]{1,0:T(8,128)(2,1)S(1)} %copy-done.6), kind=kOutput, calls=%fused_computation | convolution fusion | flops 2164260864 | bytes 19136512 | tf_op jit(solution)/shard_map/dot_general | solution.py:64
  91.6 21.3 %copy.34 = bf16[8192,1024]{0,1:T(8,128)(2,1)} copy(bf16[8192,1024]{1,0:T(8,128)(2,1)} %multiply_convert_fusion) | data formatting | bytes 33554432 | tf_op jit(solution)/shard_map/convert_element_type | solution.py:65
  112.9 46.0 %reshape.75 = bf16[128,64,32,32]{1,0,3,2:T(8,128)(2,1)} reshape(bf16[8192,1024]{0,1:T(8,128)(2,1)} %copy.34) | data formatting | bytes 33554432 | tf_op jit(solution)/shard_map/reshape | solution.py:66
  158.9 3.5 reshape.88
  162.5 5.8 copy.28
  168.2 2.8 copy.35
  171.0 15.5 %bitcast_convert_fusion.1 = bf16[256,128,32]{1,0,2:T(8,128)(2,1)} fusion(bf16[128,64,32,32]{1,0,3,2:T(8,128)(2,1)} %reshape.75, bf16[256,64,32]{0,1,2:T(8,128)(2,1)S(1)} %copy.35), kind=kOutput, calls=%fused_computation.6 | convolution fusion | flops 4296015872 | bytes 19922944 | tf_op jit(solution)/shard_map/ijce,sje->sic/dot_general | solution.py:70
  186.6 12.5 %copy.30 = bf16[32,1024,32]{2,0,1:T(8,128)(2,1)} copy(bf16[32,1024,32]{1,2,0:T(8,128)(2,1)} %all-gather.5.cloned.1.call-done) | data formatting | bytes 4194304 | tf_op jit(solution)/shard_map/all_gather | solution.py:41
  199.1 11.2 %reshape.89 = bf16[8,2,65536]{2,1,0:T(2,128)(2,1)} reshape(bf16[1024,32,32]{2,1,0:T(8,128)(2,1)} %bitcast.97) | data formatting | bytes 4194304
  210.3 4.8 all-to-all-start.1
  215.4 3.5 copy.29
  218.9 4.1 copy.42
  223.0 25.1 %all-to-all-done.1 = bf16[8,2,65536]{2,1,0:T(2,128)(2,1)} async-done(((bf16[8,2,65536]{2,1,0:T(2,128)(2,1)}), bf16[8,2,65536]{2,1,0:T(2,128)(2,1)}, u32[]{:S(2)}, u32[]{:S(2)}) %all-to-all-start.1) | async-done | bytes 2097184 | tf_op jit(solution)/shard_map/all_to_all | solution.py:42
  248.0 8.7 %reshape.90 = bf16[1024,32,32]{2,1,0:T(8,128)(2,1)} reshape(bf16[8,2,65536]{2,1,0:T(2,128)(2,1)} %all-to-all-done.1) | data formatting | bytes 4194304
  256.7 13.2 %copy.31 = bf16[32,8,128,32]{2,0,1,3:T(8,128)(2,1)} copy(bf16[32,8,128,32]{3,0,2,1:T(8,128)(2,1)} %bitcast.98) | data formatting | bytes 4194304 | tf_op jit(solution)/shard_map/all_to_all | solution.py:42
  269.9 9.8 %fusion = bf16[128,64,32,32]{0,3,2,1:T(8,128)(2,1)} fusion(bf16[256,64,32,1]{0,2,3,1:T(8,128)(2,1)S(1)} %copy.42, bf16[256,128,32,1]{1,0,2,3:T(8,128)(2,1)} %bitcast.107), kind=kOutput, calls=%fused_computation.2 | convolution fusion | flops 4311744512 | bytes 19922944 | tf_op jit(solution)/shard_map/sic,sje->ijce/dot_general | solution.py:53
  279.8 34.1 %copy.33 = bf16[128,64,32,32]{1,0,3,2:T(8,128)(2,1)} copy(bf16[128,64,32,32]{0,3,2,1:T(8,128)(2,1)} %fusion) | data formatting | bytes 33554432 | tf_op jit(solution)/shard_map/convert_element_type | solution.py:56
  313.9 44.0 %reshape.72 = bf16[8192,1024]{0,1:T(8,128)(2,1)} reshape(bf16[128,64,32,32]{1,0,3,2:T(8,128)(2,1)} %copy.33) | data formatting | bytes 33554432 | tf_op jit(solution)/shard_map/reshape | solution.py:56
  357.9 8.9 %fusion.22 = f32[1024,128]{1,0:T(8,128)} fusion(bf16[8192,1024]{0,1:T(8,128)(2,1)} %reshape.72, bf16[8192,128]{1,0:T(8,128)(2,1)S(1)} %bitcast.96), kind=kOutput, calls=%fused_computation.39 | convolution fusion | flops 2147483648 | bytes 19398656 | tf_op jit(solution)/shard_map/dot_general | solution.py:62
  366.9 15.9 %bitcast_convert_fusion = bf16[256,64,32]{1,0,2:T(8,128)(2,1)} fusion(bf16[256,128,32,1]{1,0,3,2:T(8,128)(2,1)} %bitcast.108, bf16[128,64,32,32]{1,0,3,2:T(8,128)(2,1)} %reshape.75), kind=kOutput, calls=%fused_computation.5 | convolution fusion | flops 4295491584 | bytes 19922944 | tf_op jit(solution)/shard_map/ijce,sic->sje/dot_general | solution.py:80
  385.1 4.5 all-to-all-start.2
  389.6 9.7 %fusion.1 = bf16[8192,128]{1,0:T(8,128)(2,1)} fusion(bf16[8192,1024]{0,1:T(8,128)(2,1)} %reshape.72, bf16[1024,128]{1,0:T(8,128)(2,1)S(1)} %copy-done.7, f32[128]{0:T(128)S(1)} %convert_element_type.42), kind=kOutput, calls=%fused_computation.4 | convolution fusion | flops 2149580800 | bytes 19137024 | tf_op jit(solution)/shard_map/dot_general | solution.py:57
  399.3 111.6 %all-reduce.4.cloned.1.call-done = f32[1024,128]{1,0:T(8,128)} async-done(((f32[1024,128]{1,0:T(8,128)}), f32[1024,128]{1,0:T(8,128)}) %all-reduce.4.cloned.1.call-update) | async-done | bytes 524304 | tf_op jit(solution)/shard_map/psum | solution.py:95
  514.1 73.6 %reduce-scatter.5.cloned.1.call-done = bf16[32,64,32]{1,0,2:T(8,128)(2,1)} async-done(((bf16[256,64,32]{1,0,2:T(8,128)(2,1)}), bf16[32,64,32]{1,0,2:T(8,128)(2,1)}) %reduce-scatter.5.cloned.1.call-update) | async-done | bytes 131088 | tf_op jit(solution)/shard_map/reduce_scatter | solution.py:79
  589.7 6.7 all-to-all-start.3
  597.3 5.1 all-to-all-done.3
  610.4 4.0 fusion.10
  614.4 131.7 %all-reduce.6.cloned.1.call-done = (f32[256,32]{0,1:T(8,128)}, f32[256,32]{0,1:T(8,128)}) async-done(((f32[256,32]{0,1:T(8,128)}, f32[256,32]{0,1:T(8,128)}), (f32[256,32]{0,1:T(8,128)}, f32[256,32]{0,1:T(8,128)})) %all-reduce.6.cloned.1.call-update) | async-done | bytes 65552 | tf_op jit(solution)/shard_map/psum | solution.py:94
  (76 shorter events, 28.3 us)
Async XLA Ops:
  7.2 76.1 %copy-start = (bf16[128,64,128]{2,1,0:T(8,128)(2,1)S(1)}, bf16[128,64,128]{2,1,0:T(8,128)(2,1)}, u32[]{:S(2)}) copy-start(bf16[128,64,128]{2,1,0:T(8,128)(2,1)} %param.11) | copy-start | bytes 6291460
  7.2 3.7 copy-start.1
  7.2 5.5 copy-start.14
  7.2 56.4 %all-gather.3.cloned.1.call-start = ((), (), s32[]{:S(2)}) async-start(), calls=%async_computation.6 | async-start | bytes 1179648 | tf_op jit(solution)/shard_map/all_gather | solution.py:43
  9.0 2.7 copy-start.8
  9.0 4.8 copy-start.12
  10.9 0.7 copy-start.10
  11.7 1.0 copy-start.3
  13.8 172.8 %all-gather.5.cloned.1.call-start = ((), (), s32[]{:S(2)}) async-start(), calls=%async_computation.7 | async-start | bytes 2228224 | tf_op jit(solution)/shard_map/all_gather | solution.py:41
  76.9 6.3 copy-start.6
  76.9 82.0 %all-to-all-start = ((bf16[16,2,16384]{2,1,0:T(2,128)(2,1)}), bf16[16,2,16384]{2,1,0:T(2,128)(2,1)S(1)}, u32[]{:S(2)}, u32[]{:S(2)}) async-start(bf16[16,2,16384]{2,1,0:T(2,128)(2,1)} %reshape.87), calls=%async_computation | async-start | bytes 2097152 | tf_op jit(solution)/shard_map/all_to_all | solution.py:45
  83.0 300.5 %reduce-scatter.3.cloned.1.call-start = ((), (), s32[]{:S(2)}) async-start(), calls=%async_computation.8 | async-start | bytes 2228224 | tf_op jit(solution)/shard_map/reduce_scatter | solution.py:69
  210.3 37.7 %all-to-all-start.1 = ((bf16[8,2,65536]{2,1,0:T(2,128)(2,1)}), bf16[8,2,65536]{2,1,0:T(2,128)(2,1)}, u32[]{:S(2)}, u32[]{:S(2)}) async-start(bf16[8,2,65536]{2,1,0:T(2,128)(2,1)} %reshape.89), calls=%async_computation.1 | async-start | bytes 4194304 | tf_op jit(solution)/shard_map/all_to_all | solution.py:42
  215.1 295.8 %all-reduce.4.cloned.1.call-start = ((), (), s32[]{:S(2)}) async-start(), calls=%async_computation.10 | async-start | bytes 1048576 | tf_op jit(solution)/shard_map/psum | solution.py:95
  366.8 220.9 %reduce-scatter.5.cloned.1.call-start = ((), (), s32[]{:S(2)}) async-start(), calls=%async_computation.9 | async-start | bytes 2359296 | tf_op jit(solution)/shard_map/reduce_scatter | solution.py:79
  382.8 0.7 copy-start.16
  382.8 6.7 copy-start.7
  385.1 127.1 %all-to-all-start.2 = ((bf16[16,128,32]{1,2,0:T(8,128)(2,1)}), bf16[16,128,32]{1,2,0:T(8,128)(2,1)S(1)}, u32[]{:S(2)}, u32[]{:S(2)}) async-start(bf16[16,128,32]{1,2,0:T(8,128)(2,1)} %copy.37), calls=%async_computation.3 | async-start | bytes 262144 | tf_op jit(solution)/shard_map/all_to_all | solution.py:77
  389.6 122.7 %copy-start.13 = (bf16[256,32]{0,1:T(8,128)(2,1)S(1)}, bf16[256,32]{0,1:T(8,128)(2,1)}, u32[]{:S(2)}) copy-start(bf16[256,32]{0,1:T(8,128)(2,1)} %param.7) | copy-start | bytes 49156
  399.3 197.1 %copy-start.4 = (bf16[2,1024,256]{2,1,0:T(8,128)(2,1)S(1)}, bf16[2,1024,256]{2,1,0:T(8,128)(2,1)}, u32[]{:S(2)}) copy-start(bf16[2,1024,256]{2,1,0:T(8,128)(2,1)} %copy-done.3) | copy-start | bytes 3145732
  589.7 16.0 %copy-start.15 = (bf16[256,32]{0,1:T(8,128)(2,1)S(1)}, bf16[256,32]{0,1:T(8,128)(2,1)}, u32[]{:S(2)}) copy-start(bf16[256,32]{0,1:T(8,128)(2,1)} %param.8) | copy-start | bytes 49156
  589.7 12.8 %all-to-all-start.3 = ((bf16[16,2,2048]{2,1,0:T(2,128)(2,1)}), bf16[16,2,2048]{2,1,0:T(2,128)(2,1)S(1)}, u32[]{:S(2)}, u32[]{:S(2)}) async-start(bf16[16,2,2048]{2,1,0:T(2,128)(2,1)} %reshape.91), calls=%async_computation.5 | async-start | bytes 262144 | tf_op jit(solution)/shard_map/all_to_all | solution.py:87
  596.4 149.7 %all-reduce.6.cloned.1.call-start = ((), (), s32[]{:S(2)}) async-start(), calls=%async_computation.11 | async-start | bytes 131072 | tf_op jit(solution)/shard_map/psum | solution.py:94
  605.7 3.6 copy-start.2
  605.7 3.6 copy-start.9
  605.7 3.6 copy-start.11
  607.9 1.3 copy-start.5
Sparse Core Ops, SparseCore 0:
  13.9 49.7 all-gather.2
  65.3 42.6 all-gather.4
  186.7 65.6 reduce-scatter.2
  367.0 143.9 all-reduce.3
  515.0 72.6 reduce-scatter.4
  610.5 135.4 all-reduce.5
where the time goes:
time: 761 us; the launch traced here: 756 us
  waiting for transfers between devices  395 us (52%)
  local copies, waits for them, and re-layouts  237 us (31%)
  matrix products  77.5 us (10%)
  starting transfers between devices  22.6 us (3%)
  between operations  14.4 us (2%)
  other arithmetic  9.35 us (1%)
    psum x1, waiting for transfers between devices, body(): lax.psum((left_wgrad, right_wgrad), ('row', 'col'))  132 us
    psum x1, waiting for transfers between devices, body(): whole_grad = lax.psum(weight_term, ('row', 'col'))  112 us
    reduce_scatter x1, waiting for transfers between devices, body(): lax.psum_scatter(jnp.einsum('ijce,sic->sje', outer_grad, piece, preferred...  73.6 us
    all_gather x1, waiting for transfers between devices, body(): grid_col = lax.all_gather(right, 'row', axis=0, tiled=True)  47.5 us
    reshape x1, local copies, waits for them, and re-layouts, body(): outer_grad = outer_grad.reshape(row_block, col_block, width, width)  46 us
    reshape x1, local copies, waits for them, and re-layouts, body(): outer_mean.astype(jnp.bfloat16)  44 us
    unnamed x42, local copies, waits for them, and re-layouts  37.8 us
    convert_element_type x1, local copies, waits for them, and re-layouts, body(): outer_mean.astype(jnp.bfloat16)  34.1 us
  transfers between devices with their start and end apart: 10, of which 6 were waited for; matrix products, arithmetic and copies ran while one was open for 40% of the time, Pallas kernels for 0%

commit v1 on v0

v1 whole, which is shorter than its diff:
```python
import functools

import jax
import jax.numpy as jnp
from jax import lax
from jax.experimental import pallas as pl
from jax.experimental.pallas import tpu as pltpu
from jax.sharding import PartitionSpec as P

BOTH = ("row", "col")
TILE = 16
VMEM_BYTES = 48 * 1024 * 1024
NT = (((1,), (1,)), ((), ()))


def layer_norm(values):
    centered = values - jnp.mean(values, axis=-1, keepdims=True)
    inv_sigma = lax.rsqrt(jnp.mean(centered * centered, axis=-1, keepdims=True) + 1e-05)
    return (centered * inv_sigma, inv_sigma)


def norm_backward(upstream, normed, inv_sigma):
    first = jnp.mean(upstream, axis=-1, keepdims=True)
    second = jnp.mean(upstream * normed, axis=-1, keepdims=True)
    return inv_sigma * (upstream - first - normed * second)


def outer_grad_tile(weight_ref, cot_ref, grad_ref, width):
    tile, rows, pair_width = cot_ref.shape
    flat = cot_ref[...].reshape(tile * rows, pair_width)
    step = 2
    for j in range(0, tile, step):
        grads = lax.dot_general(
            weight_ref[...], flat[j * rows:(j + step) * rows], NT, preferred_element_type=jnp.float32
        ).astype(jnp.bfloat16)
        for k in range(step):
            for c in range(width):
                grad_ref[(j + k) * width:(j + k + 1) * width, c * rows:(c + 1) * rows] = grads[
                    c * width:(c + 1) * width, k * rows:(k + 1) * rows
                ]


def left_kernel(inverse, width, right_ref, weight_ref, cot_ref, out_ref, grad_ref, acc_ref):
    step = pl.program_id(0)
    outer_grad_tile(weight_ref, cot_ref, grad_ref, width)
    chunk = 1024

    @pl.when(step == 0)
    def _():
        acc_ref[...] = jnp.zeros_like(acc_ref)

    for n in range(0, acc_ref.shape[1], chunk):
        acc_ref[:, n:n + chunk] += jnp.dot(
            right_ref[...], grad_ref[:, n:n + chunk], preferred_element_type=jnp.float32
        )

    @pl.when(step == pl.num_programs(0) - 1)
    def _():
        out_ref[...] = (acc_ref[...] * inverse).astype(out_ref.dtype)


def right_kernel(inverse, width, left_ref, weight_ref, cot_ref, out_ref, grad_ref, left_t_ref):
    @pl.when(pl.program_id(0) == 0)
    def _():
        left_t_ref[...] = left_ref[...].T

    outer_grad_tile(weight_ref, cot_ref, grad_ref, width)
    grads = jnp.dot(grad_ref[...], left_t_ref[...], preferred_element_type=jnp.float32)
    out_ref[...] = (grads * inverse).T.astype(out_ref.dtype)


def forward_kernel(
    inverse, width, left_ref, right_ref, weight_t_ref, bias_ref, cot_ref, update_ref, wgrad_ref, outer_ref
):
    tile, rows, pair_width = cot_ref.shape
    right_t = right_ref[...].T
    step = 2
    for c in range(0, width, step):
        outer = jnp.dot(
            right_t, left_ref[:, c * rows:(c + step) * rows], preferred_element_type=jnp.float32
        ).astype(jnp.bfloat16)
        for k in range(step):
            for j in range(tile):
                outer_ref[(c + k) * width:(c + k + 1) * width, j * rows:(j + 1) * rows] = outer[
                    j * width:(j + 1) * width, k * rows:(k + 1) * rows
                ]
    for j in range(0, tile, step):
        update = jnp.dot(
            weight_t_ref[...], outer_ref[:, j * rows:(j + step) * rows], preferred_element_type=jnp.float32
        )
        for k in range(step):
            one = update[:, k * rows:(k + 1) * rows].T
            update_ref[j + k] = (one * inverse + bias_ref[...]).astype(update_ref.dtype)

    @pl.when(pl.program_id(0) == 0)
    def _():
        wgrad_ref[...] = jnp.zeros_like(wgrad_ref)

    flat = cot_ref[...].reshape(tile * rows, pair_width)
    wgrad_ref[...] += inverse * jnp.dot(outer_ref[...], flat, preferred_element_type=jnp.float32)


def whole(shape):
    return pl.BlockSpec(shape, lambda j: (0,) * len(shape))


def params():
    return pltpu.CompilerParams(dimension_semantics=("arbitrary",), vmem_limit_bytes=VMEM_BYTES)


def left_grads(right, weight, cot, width, interpret=False):
    seqs, cols, rows, pair_width = right.shape[0], cot.shape[0], cot.shape[1], cot.shape[2]
    flops = 2 * cols * rows * width * width * (pair_width + seqs)
    return pl.pallas_call(
        functools.partial(left_kernel, 1.0 / seqs, width),
        grid=(cols // TILE,),
        in_specs=[
            pl.BlockSpec((seqs, TILE * width), lambda j: (0, j)),
            whole(weight.shape),
            pl.BlockSpec((TILE, rows, pair_width), lambda j: (j, 0, 0)),
        ],
        out_specs=whole((seqs, width * rows)),
        out_shape=jax.ShapeDtypeStruct((seqs, width * rows), jnp.bfloat16),
        scratch_shapes=[
            pltpu.VMEM((TILE * width, width * rows), jnp.bfloat16),
            pltpu.VMEM((seqs, width * rows), jnp.float32),
        ],
        compiler_params=params(),
        cost_estimate=pl.CostEstimate(flops=flops, bytes_accessed=5 * 2**20, transcendentals=0),
        interpret=interpret,
        name="left_grads",
    )(right, weight, cot)


def right_grads(left, weight, cot, width, interpret=False):
    seqs, cols, rows, pair_width = left.shape[0], cot.shape[0], cot.shape[1], cot.shape[2]
    flops = 2 * cols * rows * width * width * (pair_width + seqs)
    return pl.pallas_call(
        functools.partial(right_kernel, 1.0 / seqs, width),
        grid=(cols // TILE,),
        in_specs=[
            whole(left.shape),
            whole(weight.shape),
            pl.BlockSpec((TILE, rows, pair_width), lambda j: (j, 0, 0)),
        ],
        out_specs=pl.BlockSpec((seqs, TILE * width), lambda j: (0, j)),
        out_shape=jax.ShapeDtypeStruct((seqs, cols * width), jnp.bfloat16),
        scratch_shapes=[
            pltpu.VMEM((TILE * width, width * rows), jnp.bfloat16),
            pltpu.VMEM((width * rows, seqs), jnp.bfloat16),
        ],
        compiler_params=params(),
        cost_estimate=pl.CostEstimate(flops=flops, bytes_accessed=5 * 2**20, transcendentals=0),
        interpret=interpret,
        name="right_grads",
    )(left, weight, cot)


def forward(left, right, weight_t, bias, cot, width, interpret=False):
    seqs, cols, rows, pair_width = left.shape[0], cot.shape[0], cot.shape[1], cot.shape[2]
    flops = 2 * cols * rows * width * width * (2 * pair_width + seqs)
    return pl.pallas_call(
        functools.partial(forward_kernel, 1.0 / seqs, width),
        grid=(cols // TILE,),
        in_specs=[
            whole(left.shape),
            pl.BlockSpec((seqs, TILE * width), lambda j: (0, j)),
            whole(weight_t.shape),
            whole(bias.shape),
            pl.BlockSpec((TILE, rows, pair_width), lambda j: (j, 0, 0)),
        ],
        out_specs=[
            pl.BlockSpec((TILE, rows, pair_width), lambda j: (j, 0, 0)),
            whole((width * width, pair_width)),
        ],
        out_shape=[
            jax.ShapeDtypeStruct((cols, rows, pair_width), jnp.bfloat16),
            jax.ShapeDtypeStruct((width * width, pair_width), jnp.float32),
        ],
        scratch_shapes=[pltpu.VMEM((width * width, TILE * rows), jnp.bfloat16)],
        compiler_params=params(),
        cost_estimate=pl.CostEstimate(flops=flops, bytes_accessed=8 * 2**20, transcendentals=0),
        interpret=interpret,
        name="forward",
    )(left, right, weight_t, bias, cot)


def exchange(blocks):
    return lax.all_to_all(blocks, BOTH, 0, 0, tiled=True)


def body(alignment, left_weight, right_weight, out_weight, out_bias, pair_cotangent):
    row_count = lax.axis_size("row")
    col_count = lax.axis_size("col")
    devices = row_count * col_count
    local, residues, model_width = alignment.shape
    width = left_weight.shape[1]
    row_block, col_block, pair_width = pair_cotangent.shape
    seqs = local * devices

    normed, inv_sigma = layer_norm(alignment.astype(jnp.float32))
    normed_low = normed.astype(jnp.bfloat16)
    left = jnp.einsum("src,ch->shr", normed_low, left_weight, preferred_element_type=jnp.float32).astype(
        jnp.bfloat16
    )
    right = jnp.einsum("src,ch->srh", normed_low, right_weight, preferred_element_type=jnp.float32).astype(
        jnp.bfloat16
    )
    left_out = left.reshape(local, width, row_count, row_block).transpose(2, 0, 1, 3)
    left_out = left_out.reshape(row_count, 1, local, width * row_block)
    left_out = jnp.broadcast_to(left_out, (row_count, col_count) + left_out.shape[2:])
    right_out = right.reshape(local, col_count, col_block * width).transpose(1, 0, 2)[None]
    right_out = jnp.broadcast_to(right_out, (row_count,) + right_out.shape[1:])
    right_panel = exchange(right_out.reshape(devices, local, col_block * width)).reshape(seqs, -1)
    left_panel = exchange(left_out.reshape(devices, local, width * row_block)).reshape(seqs, -1)

    cot = pair_cotangent.transpose(1, 0, 2)
    bias = out_bias.astype(jnp.float32).reshape(1, pair_width)
    left_part = left_grads(right_panel, out_weight, cot, width)
    left_back = exchange(left_part.reshape(devices, local, width * row_block))
    right_part = right_grads(left_panel, out_weight, cot, width)
    right_back = exchange(right_part.reshape(devices, local, col_block * width))
    update, weight_term = forward(left_panel, right_panel, out_weight.T, bias, cot, width)
    pair_update = update.transpose(1, 0, 2)
    share = weight_term.shape[0] // devices
    weight_parts = exchange(weight_term.reshape(devices, share, pair_width))
    grad_out_weight = jnp.sum(weight_parts, axis=0)

    left_back = left_back.reshape(row_count, col_count, local, width, row_block).astype(jnp.float32)
    left_grad = jnp.sum(left_back, axis=1).astype(jnp.bfloat16)
    left_grad = left_grad.transpose(1, 2, 0, 3).reshape(local, width, residues)
    right_back = right_back.reshape(row_count, col_count, local, col_block * width).astype(jnp.float32)
    right_grad = jnp.sum(right_back, axis=0).astype(jnp.bfloat16)
    right_grad = right_grad.transpose(1, 0, 2).reshape(local, residues, width)
    left_wgrad = jnp.einsum("src,shr->ch", normed_low, left_grad, preferred_element_type=jnp.float32)
    right_wgrad = jnp.einsum("src,srh->ch", normed_low, right_grad, preferred_element_type=jnp.float32)
    wgrads = jnp.concatenate([left_wgrad.reshape(devices, 1, -1), right_wgrad.reshape(devices, 1, -1)], axis=1)
    total = jnp.sum(exchange(wgrads), axis=0)
    wgrads = exchange(jnp.broadcast_to(total[None], wgrads.shape))
    grad_left_weight = wgrads[:, 0].reshape(model_width, width)
    grad_right_weight = wgrads[:, 1].reshape(model_width, width)

    upstream = jnp.einsum("shr,ch->src", left_grad, left_weight, preferred_element_type=jnp.float32)
    upstream += jnp.einsum("srh,ch->src", right_grad, right_weight, preferred_element_type=jnp.float32)
    grad_alignment = norm_backward(upstream, normed, inv_sigma).astype(jnp.bfloat16)
    return (pair_update, grad_alignment, grad_out_weight, grad_left_weight, grad_right_weight)


def solution(mesh):
    return jax.shard_map(
        body,
        mesh=mesh,
        in_specs=(P(("row", "col"), None, None), P(), P(), P(), P(), P("row", "col", None)),
        out_specs=(
            P("row", "col", None),
            P(("row", "col"), None, None),
            P(("row", "col"), None),
            P(),
            P(),
        ),
        check_vma=False,
    )
```

time: 761 us -> 240 us (0.32)
  waiting for transfers between devices: 395 us -> 75.6 us
  local copies, waits for them, and re-layouts: 237 us -> 50 us
  matrix products: 77.5 us -> 6.5 us
  Pallas kernels: 0 us -> 44.6 us
  starting transfers between devices: 22.6 us -> 50.8 us
  between operations: 14.4 us -> 1.03 us
    psum x2 -> x0, waiting for transfers between devices: 243 us -> none  [the longest x1 132 us: body(): lax.psum((left_wgrad, right_wgrad), ('row', 'col'))]
    reshape x5 -> x10, local copies, waits for them, and re-layouts: 98.9 us -> 18 us  [the longest x1 4.52 us: body(): left_back.reshape(row_count, col_count, local, width, row_block)]
    reduce_scatter x2 -> x0, waiting for transfers between devices: 73.6 us -> none  [the longest x1 73.6 us: body(): lax.psum_scatter(jnp.einsum('ijce,sic->sje', outer_grad, piece, preferred...]
    dot_general x11 -> x5, matrix products: 76.4 us -> 6.1 us  [the longest x1 2.03 us: body(): jnp.einsum('shr,ch->src', left_grad, left_weight, preferred_element_type=...]
    convert_element_type x2 -> x1, local copies, waits for them, and re-layouts: 55.5 us -> 0.28 us  [body(): jnp.einsum('src,ch->srh', normed_low, right_weight, preferred_element_typ...]
    all_gather x2 -> x0, waiting for transfers between devices: 47.5 us -> none  [the longest x1 47.5 us: body(): grid_col = lax.all_gather(right, 'row', axis=0, tiled=True)]
    all_to_all x4 -> x7, waiting for transfers between devices: 30.2 us -> 75.6 us  [exchange(): return lax.all_to_all(blocks, BOTH, 0, 0, tiled=True)]
    pallas_call x0 -> x3, Pallas kernels: none -> 44.6 us  [the longest x1 18.4 us: right_grads(): pl.pallas_call(functools.partial(right_kernel, 1.0 / seqs, width), grid=(...]
  transfers between devices with their start and end apart: 10 -> 7, of which waited for: 6 -> 5; matrix products, arithmetic and copies ran while one was open for 40% -> 12% of each run, Pallas kernels for 0% -> 13%
where the time goes in v1:
time: 240 us; the launch traced here: 239 us
  waiting for transfers between devices  75.6 us (31%)
  starting transfers between devices  50.8 us (21%)
  local copies, waits for them, and re-layouts  50 us (21%)
  Pallas kernels  44.6 us (19%)
  other arithmetic  10.5 us (4%)
  matrix products  6.5 us (3%)
    all_to_all x7, waiting for transfers between devices, exchange(): return lax.all_to_all(blocks, BOTH, 0, 0, tiled=True)  75.6 us
    all_to_all x7, starting transfers between devices, exchange(): return lax.all_to_all(blocks, BOTH, 0, 0, tiled=True)  50.8 us
    unnamed x43, local copies, waits for them, and re-layouts  25.1 us
    pallas_call x1, Pallas kernels, right_grads(): pl.pallas_call(functools.partial(right_kernel, 1.0 / seqs, width), grid=(...  18.4 us
    pallas_call x1, Pallas kernels, forward(): pl.pallas_call(functools.partial(forward_kernel, 1.0 / seqs, width), grid...  14.5 us
    pallas_call x1, Pallas kernels, left_grads(): pl.pallas_call(functools.partial(left_kernel, 1.0 / seqs, width), grid=(c...  11.7 us
  transfers between devices with their start and end apart: 7, of which 5 were waited for; matrix products, arithmetic and copies ran while one was open for 12% of the time, Pallas kernels for 13%

profile of v1, /device:TPU:1, one launch (start us, length us, event | category | flops | bytes accessed | tf_op | source)
XLA Modules:
  0.0 239.1 jit_solution(10356174644619382736)
XLA Ops:
  4.1 1.7 broadcast_in_dim.10
  5.8 11.5 %all-to-all-start.1 = ((bf16[128,2,2048]{2,1,0:T(2,128)(2,1)}), bf16[128,2,2048]{2,1,0:T(2,128)(2,1)S(1)}, u32[]{:S(2)}, u32[]{:S(2)}) async-start(bf16[128,2,2048]{2,1,0:T(2,128)(2,1)} %bitcast.6), calls=%async_computation.1 | async-start | bytes 2097152 | tf_op jit(solution)/shard_map/all_to_all | solution.py:189
  18.0 18.7 %all-to-all-done.1 = bf16[128,2,2048]{2,1,0:T(2,128)(2,1)S(1)} async-done(((bf16[128,2,2048]{2,1,0:T(2,128)(2,1)}), bf16[128,2,2048]{2,1,0:T(2,128)(2,1)S(1)}, u32[]{:S(2)}, u32[]{:S(2)}) %all-to-all-start.1) | async-done | bytes 1048608 | tf_op jit(solution)/shard_map/all_to_all | solution.py:189
  36.6 3.4 %broadcast_in_dim.9 = bf16[8,16,2,4096]{3,2,1,0:T(2,128)(2,1)} broadcast(bf16[8,2,4096]{2,1,0:T(2,128)(2,1)S(1)} %copy.63), dimensions={0,2,3} | broadcast | bytes 2228224 | tf_op jit(solution)/shard_map/broadcast_in_dim | solution.py:211
  40.1 4.3 %all-to-all-start = ((bf16[128,2,4096]{2,1,0:T(2,128)(2,1)}), bf16[128,2,4096]{2,1,0:T(2,128)(2,1)S(1)}, u32[]{:S(2)}, u32[]{:S(2)}) async-start(bf16[128,2,4096]{2,1,0:T(2,128)(2,1)} %bitcast.66), calls=%async_computation | async-start | bytes 4194304 | tf_op jit(solution)/shard_map/all_to_all | solution.py:189
  44.4 4.3 %copy.106 = bf16[128,64,128]{2,0,1:T(8,128)(2,1)} copy(bf16[128,64,128]{2,1,0:T(8,128)(2,1)} %param.11) | data formatting | bytes 4194304 | tf_op args[5]
  51.1 23.9 %all-to-all-done = bf16[128,2,4096]{2,1,0:T(2,128)(2,1)S(1)} async-done(((bf16[128,2,4096]{2,1,0:T(2,128)(2,1)}), bf16[128,2,4096]{2,1,0:T(2,128)(2,1)S(1)}, u32[]{:S(2)}, u32[]{:S(2)}) %all-to-all-start) | async-done | bytes 2097184 | tf_op jit(solution)/shard_map/all_to_all | solution.py:189
  75.0 2.2 reshape.86.left_ref
  77.2 1.6 copy-done.3
  79.8 14.5 %forward.1 = (bf16[64,128,128]{2,1,0:T(8,128)(2,1)S(1)}, f32[1024,128]{1,0:T(8,128)S(1)}) custom-call(bf16[256,4096]{1,0:T(8,128)(2,1)S(1)} %copy-done.3, bf16[256,2048]{1,0:T(8,128)(2,1)S(1)} %reshape.89.right_ref, bf16[128,1024]{1,0:T(8,128)(2,1)S(1)} %bitcast.65, f32[1,128]{1,0:T(1,128)S(1)} %bitcast_convert_fusion.bias_ref, bf16[64,128,128]{2,1,0:T(8,128)(2,1)} %bitcast.61), custom_call_target="tpu_custom_call" | custom-call | flops 8589934592 | bytes 8388608 | tf_op jit(solution)/shard_map/forward/pallas_call | solution.py:162
  95.1 5.4 %all-to-all-start.4 = ((f32[128,8,128]{2,1,0:T(8,128)}), f32[128,8,128]{2,1,0:T(8,128)}, u32[]{:S(2)}, u32[]{:S(2)}) async-start(f32[128,8,128]{2,1,0:T(8,128)} %bitcast.64), calls=%async_computation.4 | async-start | bytes 1048576 | tf_op jit(solution)/shard_map/all_to_all | solution.py:189
  100.5 1.6 copy-done.1
  102.1 1.6 copy-done.4
  103.7 18.4 %right_grads.1 = bf16[256,2048]{1,0:T(8,128)(2,1)S(1)} custom-call(bf16[256,4096]{1,0:T(8,128)(2,1)S(1)} %copy-done.4, bf16[1024,128]{1,0:T(8,128)(2,1)S(1)} %copy-done.8, bf16[64,128,128]{2,1,0:T(8,128)(2,1)S(1)} %bitcast.62), custom_call_target="tpu_custom_call" | custom-call | flops 6442450944 | bytes 5242880 | tf_op jit(solution)/shard_map/right_grads/pallas_call | solution.py:138
  123.0 2.6 %reshape.95 = bf16[128,2,2048]{2,1,0:T(2,128)(2,1)} reshape(bf16[256,2048]{1,0:T(8,128)(2,1)} %copy-done.6) | data formatting | bytes 2097152 | tf_op jit(solution)/shard_map/reshape | solution.py:222
  125.6 10.4 %all-to-all-start.3 = ((bf16[128,2,2048]{2,1,0:T(2,128)(2,1)}), bf16[128,2,2048]{2,1,0:T(2,128)(2,1)}, u32[]{:S(2)}, u32[]{:S(2)}) async-start(bf16[128,2,2048]{2,1,0:T(2,128)(2,1)} %reshape.95), calls=%async_computation.3 | async-start | bytes 2097152 | tf_op jit(solution)/shard_map/all_to_all | solution.py:189
  135.9 1.6 copy-done.2
  137.5 11.7 %left_grads.1 = bf16[256,4096]{1,0:T(8,128)(2,1)S(1)} custom-call(bf16[256,2048]{1,0:T(8,128)(2,1)S(1)} %reshape.89.right_ref, bf16[1024,128]{1,0:T(8,128)(2,1)S(1)} %copy-done.8, bf16[64,128,128]{2,1,0:T(8,128)(2,1)S(1)} %bitcast.63), custom_call_target="tpu_custom_call" | custom-call | flops 6442450944 | bytes 5242880 | tf_op jit(solution)/shard_map/left_grads/pallas_call | solution.py:114
  150.6 4.4 %reshape.92 = bf16[128,2,4096]{2,1,0:T(2,128)(2,1)} reshape(bf16[256,4096]{1,0:T(8,128)(2,1)} %copy-done.5) | data formatting | bytes 4194304 | tf_op jit(solution)/shard_map/reshape | solution.py:220
  155.0 10.2 %all-to-all-start.2 = ((bf16[128,2,4096]{2,1,0:T(2,128)(2,1)}), bf16[128,2,4096]{2,1,0:T(2,128)(2,1)}, u32[]{:S(2)}, u32[]{:S(2)}) async-start(bf16[128,2,4096]{2,1,0:T(2,128)(2,1)} %reshape.92), calls=%async_computation.2 | async-start | bytes 4194304 | tf_op jit(solution)/shard_map/all_to_all | solution.py:189
  165.2 2.7 %copy.78 = bf16[128,64,128]{2,1,0:T(8,128)(2,1)} copy(bf16[128,64,128]{2,0,1:T(8,128)(2,1)S(1)} %bitcast.60) | data formatting | bytes 4194304
  167.9 1.9 reduce_sum.84
  169.7 2.3 reduce_sum.81
  175.8 19.5 %all-to-all-done.2 = bf16[128,2,4096]{2,1,0:T(2,128)(2,1)} async-done(((bf16[128,2,4096]{2,1,0:T(2,128)(2,1)}), bf16[128,2,4096]{2,1,0:T(2,128)(2,1)}, u32[]{:S(2)}, u32[]{:S(2)}) %all-to-all-start.2) | async-done | bytes 2097184 | tf_op jit(solution)/shard_map/all_to_all | solution.py:189
  195.4 4.5 %reshape.93 = bf16[8,16,2,32,128]{4,3,2,1,0:T(8,128)(2,1)} reshape(bf16[128,2,4096]{2,1,0:T(2,128)(2,1)} %all-to-all-done.2) | data formatting | bytes 4194304 | tf_op jit(solution)/shard_map/reshape | solution.py:229
  199.9 1.9 reduce_sum.80
  205.8 4.4 %all-to-all-start.5 = ((f32[128,1,128]{2,1,0:T(1,128)}), f32[128,1,128]{2,1,0:T(1,128)S(1)}, u32[]{:S(2)}, u32[]{:S(2)}) async-start(f32[128,1,128]{2,1,0:T(1,128)} %reshape.119), calls=%async_computation.5 | async-start | bytes 131072 | tf_op jit(solution)/shard_map/all_to_all | solution.py:189
  210.2 2.0 fusion.24
  212.3 7.4 %all-to-all-done.5 = f32[128,1,128]{2,1,0:T(1,128)S(1)} async-done(((f32[128,1,128]{2,1,0:T(1,128)}), f32[128,1,128]{2,1,0:T(1,128)S(1)}, u32[]{:S(2)}, u32[]{:S(2)}) %all-to-all-start.5) | async-done | bytes 65568 | tf_op jit(solution)/shard_map/all_to_all | solution.py:189
  222.1 4.6 %all-to-all-start.6 = ((f32[128,1,128]{2,1,0:T(1,128)}), f32[128,1,128]{2,1,0:T(1,128)S(1)}, u32[]{:S(2)}, u32[]{:S(2)}) async-start(f32[128,1,128]{2,1,0:T(1,128)} %reshape.121), calls=%async_computation.6 | async-start | bytes 131072 | tf_op jit(solution)/shard_map/all_to_all | solution.py:189
  226.7 2.1 fusion.8
  230.2 6.1 %all-to-all-done.6 = f32[128,1,128]{2,1,0:T(1,128)S(1)} async-done(((f32[128,1,128]{2,1,0:T(1,128)}), f32[128,1,128]{2,1,0:T(1,128)S(1)}, u32[]{:S(2)}, u32[]{:S(2)}) %all-to-all-start.6) | async-done | bytes 65568 | tf_op jit(solution)/shard_map/all_to_all | solution.py:189
  (71 shorter events, 24.7 us)
Async XLA Ops:
  0.6 16.7 %copy-start = (bf16[256,32]{0,1:T(8,128)(2,1)S(1)}, bf16[256,32]{0,1:T(8,128)(2,1)}, u32[]{:S(2)}) copy-start(bf16[256,32]{0,1:T(8,128)(2,1)} %param.7) | copy-start | bytes 49156
  0.6 2.1 copy-start.14
  2.2 15.1 %copy-start.10 = (bf16[2,1024,256]{1,2,0:T(8,128)(2,1)}, bf16[2,1024,256]{1,2,0:T(8,128)(2,1)S(1)}, u32[]{:S(2)}) copy-start(bf16[2,1024,256]{1,2,0:T(8,128)(2,1)S(1)} %copy.60) | copy-start | bytes 3145732
  5.8 30.9 %all-to-all-start.1 = ((bf16[128,2,2048]{2,1,0:T(2,128)(2,1)}), bf16[128,2,2048]{2,1,0:T(2,128)(2,1)S(1)}, u32[]{:S(2)}, u32[]{:S(2)}) async-start(bf16[128,2,2048]{2,1,0:T(2,128)(2,1)} %bitcast.6), calls=%async_computation.1 | async-start | bytes 2097152 | tf_op jit(solution)/shard_map/all_to_all | solution.py:189
  36.6 3.4 %copy-start.12 = (bf16[128,2,2048]{2,1,0:T(2,128)(2,1)}, bf16[128,2,2048]{2,1,0:T(2,128)(2,1)S(1)}, u32[]{:S(2)}) copy-start(bf16[128,2,2048]{2,1,0:T(2,128)(2,1)S(1)} %all-to-all-done.1) | copy-start | bytes 3145732
  40.1 35.0 %all-to-all-start = ((bf16[128,2,4096]{2,1,0:T(2,128)(2,1)}), bf16[128,2,4096]{2,1,0:T(2,128)(2,1)S(1)}, u32[]{:S(2)}, u32[]{:S(2)}) async-start(bf16[128,2,4096]{2,1,0:T(2,128)(2,1)} %bitcast.66), calls=%async_computation | async-start | bytes 4194304 | tf_op jit(solution)/shard_map/all_to_all | solution.py:189
  44.4 4.4 %copy-start.8 = (bf16[1024,128]{1,0:T(8,128)(2,1)S(1)}, bf16[1024,128]{1,0:T(8,128)(2,1)}, u32[]{:S(2)}) copy-start(bf16[1024,128]{1,0:T(8,128)(2,1)} %weight_ref.3) | copy-start | bytes 786436
  44.4 5.2 %copy-start.15 = (bf16[128]{0:T(256)(128)(2,1)S(1)}, bf16[128]{0:T(256)(128)(2,1)}, u32[]{:S(2)}) copy-start(bf16[128]{0:T(256)(128)(2,1)} %param.10) | copy-start | bytes 772
  77.2 1.6 copy-start.3
  78.8 0.9 copy-start.9
  94.3 0.8 copy-start.7
  95.1 30.5 %all-to-all-start.4 = ((f32[128,8,128]{2,1,0:T(8,128)}), f32[128,8,128]{2,1,0:T(8,128)}, u32[]{:S(2)}, u32[]{:S(2)}) async-start(f32[128,8,128]{2,1,0:T(8,128)} %bitcast.64), calls=%async_computation.4 | async-start | bytes 1048576 | tf_op jit(solution)/shard_map/all_to_all | solution.py:189
  100.5 1.6 copy-start.1
  102.1 1.6 copy-start.4
  122.0 1.0 copy-start.6
  125.6 29.4 %all-to-all-start.3 = ((bf16[128,2,2048]{2,1,0:T(2,128)(2,1)}), bf16[128,2,2048]{2,1,0:T(2,128)(2,1)}, u32[]{:S(2)}, u32[]{:S(2)}) async-start(bf16[128,2,2048]{2,1,0:T(2,128)(2,1)} %reshape.95), calls=%async_computation.3 | async-start | bytes 2097152 | tf_op jit(solution)/shard_map/all_to_all | solution.py:189
  135.9 1.6 copy-start.2
  149.2 1.3 copy-start.5
  155.0 40.4 %all-to-all-start.2 = ((bf16[128,2,4096]{2,1,0:T(2,128)(2,1)}), bf16[128,2,4096]{2,1,0:T(2,128)(2,1)}, u32[]{:S(2)}, u32[]{:S(2)}) async-start(bf16[128,2,4096]{2,1,0:T(2,128)(2,1)} %reshape.92), calls=%async_computation.2 | async-start | bytes 4194304 | tf_op jit(solution)/shard_map/all_to_all | solution.py:189
  167.9 5.3 %copy-start.11 = (bf16[2,1024,256]{1,2,0:T(8,128)(2,1)S(1)}, bf16[2,1024,256]{1,2,0:T(8,128)(2,1)}, u32[]{:S(2)}) copy-start(bf16[2,1024,256]{1,2,0:T(8,128)(2,1)} %copy-done.10) | copy-start | bytes 3145732
  172.4 0.8 copy-start.13
  205.8 13.9 %all-to-all-start.5 = ((f32[128,1,128]{2,1,0:T(1,128)}), f32[128,1,128]{2,1,0:T(1,128)S(1)}, u32[]{:S(2)}, u32[]{:S(2)}) async-start(f32[128,1,128]{2,1,0:T(1,128)} %reshape.119), calls=%async_computation.5 | async-start | bytes 131072 | tf_op jit(solution)/shard_map/all_to_all | solution.py:189
  222.1 14.1 %all-to-all-start.6 = ((f32[128,1,128]{2,1,0:T(1,128)}), f32[128,1,128]{2,1,0:T(1,128)S(1)}, u32[]{:S(2)}, u32[]{:S(2)}) async-start(f32[128,1,128]{2,1,0:T(1,128)} %reshape.121), calls=%async_computation.6 | async-start | bytes 131072 | tf_op jit(solution)/shard_map/all_to_all | solution.py:189

commit v2 on v1

v2 whole, which is shorter than its diff:
```python
import functools

import jax
import jax.numpy as jnp
import numpy as np
from jax import lax
from jax.experimental import pallas as pl
from jax.experimental.pallas import tpu as pltpu
from jax.sharding import PartitionSpec as P

BOTH = ("row", "col")
TILE = 16
GRAD_TILE = 8
CORES = 2
VMEM_BYTES = 48 * 1024 * 1024
NT = (((1,), (1,)), ((), ()))


def layer_norm(values):
    centered = values - jnp.mean(values, axis=-1, keepdims=True)
    inv_sigma = lax.rsqrt(jnp.mean(centered * centered, axis=-1, keepdims=True) + 1e-05)
    return (centered * inv_sigma, inv_sigma)


def norm_backward(upstream, normed, inv_sigma):
    first = jnp.mean(upstream, axis=-1, keepdims=True)
    second = jnp.mean(upstream * normed, axis=-1, keepdims=True)
    return inv_sigma * (upstream - first - normed * second)


def outer_grad_kernel(width, weight_ref, cot_ref, grad_ref):
    tile, rows, pair_width = cot_ref.shape
    flat = cot_ref[...].reshape(tile * rows, pair_width)
    step = 2
    for j in range(0, tile, step):
        grads = lax.dot_general(
            weight_ref[...], flat[j * rows:(j + step) * rows], NT, preferred_element_type=jnp.float32
        ).astype(jnp.bfloat16)
        for k in range(step):
            for c in range(width):
                grad_ref[(j + k) * width:(j + k + 1) * width, c * rows:(c + 1) * rows] = grads[
                    c * width:(c + 1) * width, k * rows:(k + 1) * rows
                ]


def left_kernel(inverse, right_ref, grad_ref, out_ref):
    grads = jnp.dot(right_ref[...], grad_ref[...], preferred_element_type=jnp.float32)
    out_ref[...] = (grads * inverse).astype(out_ref.dtype)


def right_kernel(inverse, own_ref, other_ref, grad_ref, out_ref):
    half = own_ref.shape[1]
    grads = lax.dot_general(own_ref[...], grad_ref[:, :half], NT, preferred_element_type=jnp.float32)
    grads += lax.dot_general(other_ref[...], grad_ref[:, half:], NT, preferred_element_type=jnp.float32)
    out_ref[...] = (grads * inverse).astype(out_ref.dtype)


def forward_kernel(
    inverse, width, own_ref, other_ref, right_ref, weight_t_ref, bias_ref, cot_ref, update_ref, wgrad_ref, outer_ref
):
    tile, rows, pair_width = cot_ref.shape
    right_t = right_ref[...].T
    step = 2
    for c in range(0, width, step):
        half_ref, first = (own_ref, c) if c < width // 2 else (other_ref, c - width // 2)
        outer = jnp.dot(
            right_t, half_ref[:, first * rows:(first + step) * rows], preferred_element_type=jnp.float32
        ).astype(jnp.bfloat16)
        for k in range(step):
            for j in range(tile):
                outer_ref[(c + k) * width:(c + k + 1) * width, j * rows:(j + 1) * rows] = outer[
                    j * width:(j + 1) * width, k * rows:(k + 1) * rows
                ]
    for j in range(0, tile, step):
        update = jnp.dot(
            weight_t_ref[...], outer_ref[:, j * rows:(j + step) * rows], preferred_element_type=jnp.float32
        )
        for k in range(step):
            one = update[:, k * rows:(k + 1) * rows].T
            update_ref[j + k] = (one * inverse + bias_ref[...]).astype(update_ref.dtype)

    @pl.when(pl.program_id(0) == 0)
    def _():
        wgrad_ref[...] = jnp.zeros_like(wgrad_ref)

    flat = cot_ref[...].reshape(tile * rows, pair_width)
    wgrad_ref[...] += inverse * jnp.dot(outer_ref[...], flat, preferred_element_type=jnp.float32)


def whole(shape):
    return pl.BlockSpec(shape, lambda j: (0,) * len(shape))


def params():
    return pltpu.CompilerParams(dimension_semantics=("arbitrary",), vmem_limit_bytes=VMEM_BYTES)


def outer_grads(weight, cot, width, interpret=False):
    cols, rows, pair_width = cot.shape
    return pl.pallas_call(
        functools.partial(outer_grad_kernel, width),
        grid=(cols // GRAD_TILE,),
        in_specs=[whole(weight.shape), pl.BlockSpec((GRAD_TILE, rows, pair_width), lambda j: (j, 0, 0))],
        out_specs=pl.BlockSpec((GRAD_TILE * width, width * rows), lambda j: (j, 0)),
        out_shape=jax.ShapeDtypeStruct((cols * width, width * rows), jnp.bfloat16),
        compiler_params=params(),
        cost_estimate=pl.CostEstimate(
            flops=2 * cols * rows * width * width * pair_width, bytes_accessed=18 * 2**20, transcendentals=0
        ),
        interpret=interpret,
        name="outer_grads",
    )(weight, cot)


def left_grads(came, grads, interpret=False):
    seqs, (depth, columns) = came.shape[0], grads.shape
    block = 512
    last = came.shape[1] // depth - 1
    return pl.pallas_call(
        functools.partial(left_kernel, 1.0 / seqs),
        grid=(columns // block,),
        in_specs=[
            pl.BlockSpec((seqs, depth), lambda n: (0, last)),
            pl.BlockSpec((depth, block), lambda n: (0, n)),
        ],
        out_specs=pl.BlockSpec((seqs, block), lambda n: (0, n)),
        out_shape=jax.ShapeDtypeStruct((seqs, columns), jnp.bfloat16),
        compiler_params=params(),
        cost_estimate=pl.CostEstimate(flops=2 * seqs * depth * columns, bytes_accessed=19 * 2**20, transcendentals=0),
        interpret=interpret,
        name="left_grads",
    )(came, grads)


def right_grads(came, other, grads, interpret=False):
    seqs, (rows, depth) = came.shape[0], grads.shape
    block = 256
    return pl.pallas_call(
        functools.partial(right_kernel, 1.0 / seqs),
        grid=(rows // block,),
        in_specs=[
            pl.BlockSpec((seqs, depth // 2), lambda n: (0, 0)),
            whole((seqs, depth // 2)),
            pl.BlockSpec((block, depth), lambda n: (n, 0)),
        ],
        out_specs=pl.BlockSpec((seqs, block), lambda n: (0, n)),
        out_shape=jax.ShapeDtypeStruct((seqs, rows), jnp.bfloat16),
        compiler_params=params(),
        cost_estimate=pl.CostEstimate(flops=2 * seqs * depth * rows, bytes_accessed=19 * 2**20, transcendentals=0),
        interpret=interpret,
        name="right_grads",
    )(came, other, grads)


def forward(came, other, weight_t, bias, cot, width, interpret=False):
    seqs, cols, rows, pair_width = came.shape[0], cot.shape[0], cot.shape[1], cot.shape[2]
    flops = 2 * cols * rows * width * width * (2 * pair_width + seqs)
    first = other.shape[1] // (TILE * width)
    return pl.pallas_call(
        functools.partial(forward_kernel, 1.0 / seqs, width),
        grid=(cols // TILE,),
        in_specs=[
            pl.BlockSpec(other.shape, lambda j: (0, 0)),
            whole(other.shape),
            pl.BlockSpec((seqs, TILE * width), lambda j: (0, first + j)),
            whole(weight_t.shape),
            whole(bias.shape),
            pl.BlockSpec((TILE, rows, pair_width), lambda j: (j, 0, 0)),
        ],
        out_specs=[
            pl.BlockSpec((TILE, rows, pair_width), lambda j: (j, 0, 0)),
            whole((width * width, pair_width)),
        ],
        out_shape=[
            jax.ShapeDtypeStruct((cols, rows, pair_width), jnp.bfloat16),
            jax.ShapeDtypeStruct((width * width, pair_width), jnp.float32),
        ],
        scratch_shapes=[pltpu.VMEM((width * width, TILE * rows), jnp.bfloat16)],
        compiler_params=params(),
        cost_estimate=pl.CostEstimate(flops=flops, bytes_accessed=8 * 2**20, transcendentals=0),
        interpret=interpret,
        name="forward",
    )(came, other, came, weight_t, bias, cot)


def exchange(blocks):
    return lax.all_to_all(blocks, BOTH, 0, 0, tiled=True)


def swap_cores(values):
    return lax.ppermute(values, "col", [(i, i ^ 1) for i in range(lax.axis_size("col"))])


def own_first(values, core):
    half = values.shape[0] // CORES
    return jnp.where(core == 0, values, jnp.concatenate([values[half:], values[:half]], axis=0))


def sum_all(values):
    devices = lax.axis_size(BOTH)

    def partner(part, mask):
        return lax.ppermute(part, BOTH, [(i, i ^ mask) for i in range(devices)])

    core = lax.axis_index("col") % CORES
    half = values.shape[0] // CORES
    halves = own_first(values, core)
    part = halves[:half] + partner(halves[half:], 1)
    mask = CORES
    while mask < devices:
        if 4 * mask <= devices:
            others = [partner(part, mask), partner(part, 2 * mask), partner(part, 3 * mask)]
            part = (part + others[0]) + (others[1] + others[2])
        else:
            part = part + partner(part, mask)
        mask *= 4
    return own_first(jnp.concatenate([part, partner(part, 1)], axis=0), core)


def body(alignment, left_weight, right_weight, out_weight, out_bias, pair_cotangent):
    row_count = lax.axis_size("row")
    col_count = lax.axis_size("col")
    devices = row_count * col_count
    local, residues, model_width = alignment.shape
    width = left_weight.shape[1]
    row_block, col_block, pair_width = pair_cotangent.shape
    seqs = local * devices

    normed, inv_sigma = layer_norm(alignment.astype(jnp.float32))
    normed_low = normed.astype(jnp.bfloat16)
    left = jnp.einsum("src,ch->shr", normed_low, left_weight, preferred_element_type=jnp.float32).astype(
        jnp.bfloat16
    )
    right = jnp.einsum("src,ch->srh", normed_low, right_weight, preferred_element_type=jnp.float32).astype(
        jnp.bfloat16
    )
    chips = col_count // CORES
    core = lax.axis_index("col") % CORES
    panel = row_block * width // CORES
    left_out = left.reshape(local, CORES, width // CORES, row_count, row_block).transpose(3, 1, 0, 2, 4)
    left_out = left_out.reshape(row_count, 1, CORES, local, panel)
    right_out = right.reshape(local, chips, CORES, col_block * width).transpose(1, 2, 0, 3)[None]
    shape = (row_count, chips, CORES, local)
    sent = jnp.concatenate(
        [jnp.broadcast_to(left_out, shape + (panel,)), jnp.broadcast_to(right_out, shape + right_out.shape[4:])], axis=4
    )
    columns = sent.shape[4]
    cot = pair_cotangent.transpose(1, 0, 2)
    bias = out_bias.astype(jnp.float32).reshape(1, pair_width)
    weight = own_first(out_weight, core)
    came = exchange(sent.reshape(devices, local, columns))
    came, outer_grad = lax.optimization_barrier((came, outer_grads(weight, cot, width)))
    came = came.reshape(seqs, columns)
    left_other = swap_cores(came[:, :panel])
    left_part = left_grads(came, outer_grad)
    left_other, left_part = lax.optimization_barrier((left_other, left_part))
    left_share = swap_cores(left_part[:, panel:])
    right_part = right_grads(came, left_other, outer_grad)
    left_pair = (left_part[:, :panel].astype(jnp.float32) + left_share.astype(jnp.float32)).astype(jnp.bfloat16)
    sent = jnp.concatenate([left_pair, right_part], axis=1).reshape(devices, local, columns)
    sent, left_other = lax.optimization_barrier((sent, left_other))
    back = exchange(sent).reshape(seqs, columns)
    update, weight_term = forward(came, left_other, weight.T, bias, cot, width)
    pair_update = update.transpose(1, 0, 2)
    share = weight_term.shape[0] // devices
    weight_parts = exchange(own_first(weight_term, core).reshape(devices, share, pair_width))

    place = np.indices((row_count, chips, CORES, local)).reshape(4, -1)
    left_place = (place[3] * row_count + place[0]) * CORES + place[2]
    right_place = (place[3] * chips + place[1]) * CORES + place[2]
    left_rows, right_rows = local * row_count * CORES, local * chips * CORES
    left_pick = jnp.asarray(np.arange(left_rows)[:, None] == left_place[None], dtype=jnp.bfloat16)
    right_pick = jnp.asarray(np.arange(right_rows)[:, None] == right_place[None], dtype=jnp.bfloat16)
    left_grad = jnp.dot(left_pick, back[:, :panel], preferred_element_type=jnp.float32).astype(jnp.bfloat16)
    right_grad = jnp.dot(right_pick, back[:, panel:], preferred_element_type=jnp.float32).astype(jnp.bfloat16)
    left_grad = left_grad.reshape(local, row_count, width, row_block).transpose(0, 2, 1, 3)
    left_grad = left_grad.reshape(local, width, residues)
    right_grad = right_grad.reshape(local, residues, width)
    left_wgrad = jnp.einsum("src,shr->ch", normed_low, left_grad, preferred_element_type=jnp.float32)
    right_wgrad = jnp.einsum("src,srh->ch", normed_low, right_grad, preferred_element_type=jnp.float32)
    wgrads = sum_all(jnp.concatenate([left_wgrad, right_wgrad], axis=1).reshape(-1, 128))
    wgrads, weight_parts = lax.optimization_barrier((wgrads, weight_parts))
    grad_out_weight = jnp.sum(weight_parts, axis=0)
    wgrads = wgrads.reshape(model_width, 2 * width)

    upstream = jnp.einsum("shr,ch->src", left_grad, left_weight, preferred_element_type=jnp.float32)
    upstream += jnp.einsum("srh,ch->src", right_grad, right_weight, preferred_element_type=jnp.float32)
    grad_alignment = norm_backward(upstream, normed, inv_sigma).astype(jnp.bfloat16)
    return (pair_update, grad_alignment, grad_out_weight, wgrads[:, :width], wgrads[:, width:])


def solution(mesh):
    return jax.shard_map(
        body,
        mesh=mesh,
        in_specs=(P(("row", "col"), None, None), P(), P(), P(), P(), P("row", "col", None)),
        out_specs=(
            P("row", "col", None),
            P(("row", "col"), None, None),
            P(("row", "col"), None),
            P(),
            P(),
        ),
        check_vma=False,
    )
```

time: 240 us -> 180 us (0.75)
  waiting for transfers between devices: 75.6 us -> 38.5 us
  local copies, waits for them, and re-layouts: 50 us -> 36.2 us
  starting transfers between devices: 50.8 us -> 39.6 us
    all_to_all x7 -> x3, waiting for transfers between devices: 75.6 us -> 27.6 us  [exchange(): return lax.all_to_all(blocks, BOTH, 0, 0, tiled=True)]
    all_to_all x7 -> x3, starting transfers between devices: 50.8 us -> 21 us  [exchange(): return lax.all_to_all(blocks, BOTH, 0, 0, tiled=True)]
    ppermute x0 -> x13, starting transfers between devices: none -> 18.6 us  [the longest x11 17.5 us: partner(): return lax.ppermute(part, BOTH, [(i, i ^ mask) for i in range(devices)])]
    unnamed x43 -> x46, local copies, waits for them, and re-layouts: 25.1 us -> 13.1 us
    ppermute x0 -> x13, waiting for transfers between devices: none -> 10.9 us  [the longest x11 10.9 us: partner(): return lax.ppermute(part, BOTH, [(i, i ^ mask) for i in range(devices)])]
    concatenate x1 -> x4, other arithmetic: 0.01 us -> 6.64 us  [the longest x1 3.84 us: body(): jnp.concatenate([jnp.broadcast_to(left_out, shape + (panel,)), jnp.broadc...]
    reshape x10 -> x9, local copies, waits for them, and re-layouts: 18 us -> 13.2 us  [the longest x1 4.41 us: body(): jnp.concatenate([left_pair, right_part], axis=1)]
    reduce_sum x3 -> x0, other arithmetic: 4.34 us -> none  [the longest x1 2.25 us: body(): right_grad = jnp.sum(right_back, axis=0).astype(jnp.bfloat16)]
  transfers between devices with their start and end apart: 7 -> 16, of which waited for: 5 -> 8; matrix products, arithmetic and copies ran while one was open for 12% -> 8% of each run, Pallas kernels for 13% -> 25%
where the time goes in v2:
time: 180 us; the launch traced here: 179 us
  Pallas kernels  45.4 us (25%)
  starting transfers between devices  39.6 us (22%)
  waiting for transfers between devices  38.5 us (21%)
  local copies, waits for them, and re-layouts  36.2 us (20%)
  other arithmetic  10.8 us (6%)
  matrix products  7.05 us (4%)
    all_to_all x3, waiting for transfers between devices, exchange(): return lax.all_to_all(blocks, BOTH, 0, 0, tiled=True)  27.6 us
    all_to_all x3, starting transfers between devices, exchange(): return lax.all_to_all(blocks, BOTH, 0, 0, tiled=True)  21 us
    ppermute x11, starting transfers between devices, partner(): return lax.ppermute(part, BOTH, [(i, i ^ mask) for i in range(devices)])  17.5 us
    pallas_call x1, Pallas kernels, forward(): pl.pallas_call(functools.partial(forward_kernel, 1.0 / seqs, width), grid...  14.6 us
    unnamed x46, local copies, waits for them, and re-layouts  13.1 us
    ppermute x11, waiting for transfers between devices, partner(): return lax.ppermute(part, BOTH, [(i, i ^ mask) for i in range(devices)])  10.9 us
    pallas_call x1, Pallas kernels, right_grads(): pl.pallas_call(functools.partial(right_kernel, 1.0 / seqs), grid=(rows //...  10.7 us
    pallas_call x1, Pallas kernels, left_grads(): pl.pallas_call(functools.partial(left_kernel, 1.0 / seqs), grid=(columns...  10.5 us
  transfers between devices with their start and end apart: 16, of which 8 were waited for; matrix products, arithmetic and copies ran while one was open for 8% of the time, Pallas kernels for 25%

profile of v2, /device:TPU:1, one launch (start us, length us, event | category | flops | bytes accessed | tf_op | source)
XLA Modules:
  0.0 178.8 jit_solution(16624103876164663187)
XLA Ops:
  0.7 1.5 copy.31
  6.8 3.8 %pad_maximum_fusion = bf16[8,8,2,2,4096]{4,3,2,1,0:T(2,128)(2,1)} fusion(bf16[8,8,2,2,2048]{4,3,2,1,0:T(2,128)(2,1)S(1)} %broadcast_in_dim.8, bf16[8,8,2,2,2048]{4,3,2,1,0:T(2,128)(2,1)S(1)} %broadcast_in_dim.7), kind=kLoop, calls=%fused_computation.16 | loop fusion | flops 4194304 | bytes 4194304 | tf_op jit(solution)/shard_map/concatenate | solution.py:244
  10.7 12.0 %all-to-all-start = ((bf16[128,2,4096]{2,1,0:T(2,128)(2,1)}), bf16[128,2,4096]{2,1,0:T(2,128)(2,1)}, u32[]{:S(2)}, u32[]{:S(2)}) async-start(bf16[128,2,4096]{2,1,0:T(2,128)(2,1)} %bitcast.5), calls=%async_computation | async-start | bytes 4194304 | tf_op jit(solution)/shard_map/all_to_all | solution.py:187
  24.2 1.4 copy.79
  25.6 9.7 %outer_grads.1.grad_ref = bf16[2048,4096]{1,0:T(8,128)(2,1)} custom-call(bf16[1024,128]{1,0:T(8,128)(2,1)S(1)} %copy.42.weight_ref, bf16[64,128,128]{2,1,0:T(8,128)(2,1)S(1)} %bitcast.62), custom_call_target="tpu_custom_call" | custom-call | flops 2147483648 | bytes 18874368 | tf_op jit(solution)/shard_map/outer_grads/pallas_call | solution.py:100
  35.2 1.3 copy-done.1
  36.6 16.2 %all-to-all-done = bf16[128,2,4096]{2,1,0:T(2,128)(2,1)} async-done(((bf16[128,2,4096]{2,1,0:T(2,128)(2,1)}), bf16[128,2,4096]{2,1,0:T(2,128)(2,1)}, u32[]{:S(2)}, u32[]{:S(2)}) %all-to-all-start) | async-done | bytes 2097184 | tf_op jit(solution)/shard_map/all_to_all | solution.py:187
  52.8 2.7 %reshape.79.right_ref.own_ref = bf16[256,4096]{1,0:T(8,128)(2,1)S(1)} reshape(bf16[128,2,4096]{2,1,0:T(2,128)(2,1)} %all-to-all-done) | data formatting | bytes 4194304 | tf_op jit(solution)/shard_map/reshape | solution.py:253
  56.6 10.5 %left_grads.1 = bf16[256,4096]{1,0:T(8,128)(2,1)S(1)} custom-call(bf16[256,4096]{1,0:T(8,128)(2,1)S(1)} %reshape.79.right_ref.own_ref, bf16[2048,4096]{1,0:T(8,128)(2,1)} %outer_grads.1.grad_ref), custom_call_target="tpu_custom_call" | custom-call | flops 4294967296 | bytes 19922944 | tf_op jit(solution)/shard_map/left_grads/pallas_call | solution.py:119
  67.4 10.7 %right_grads.1 = bf16[256,2048]{1,0:T(8,128)(2,1)S(1)} custom-call(bf16[256,4096]{1,0:T(8,128)(2,1)S(1)} %reshape.79.right_ref.own_ref, bf16[256,2048]{1,0:T(8,128)(2,1)S(1)} %collective-permute-done.other_ref, bf16[2048,4096]{1,0:T(8,128)(2,1)} %outer_grads.1.grad_ref), custom_call_target="tpu_custom_call" | custom-call | flops 4294967296 | bytes 19922944 | tf_op jit(solution)/shard_map/right_grads/pallas_call | solution.py:138
  78.4 1.5 pad_maximum_fusion.1
  80.0 4.4 %reshape.80 = bf16[128,2,4096]{2,1,0:T(2,128)(2,1)} reshape(bf16[256,4096]{1,0:T(8,128)(2,1)} %pad_maximum_fusion.1) | data formatting | bytes 4194304 | tf_op jit(solution)/shard_map/reshape | solution.py:260
  84.4 5.3 %all-to-all-start.1 = ((bf16[128,2,4096]{2,1,0:T(2,128)(2,1)}), bf16[128,2,4096]{2,1,0:T(2,128)(2,1)}, u32[]{:S(2)}, u32[]{:S(2)}) async-start(bf16[128,2,4096]{2,1,0:T(2,128)(2,1)} %reshape.80), calls=%async_computation.1 | async-start | bytes 4194304 | tf_op jit(solution)/shard_map/all_to_all | solution.py:187
  89.7 14.6 %forward.1 = (bf16[64,128,128]{2,1,0:T(8,128)(2,1)S(1)}, f32[1024,128]{1,0:T(8,128)S(1)}) custom-call(bf16[256,4096]{1,0:T(8,128)(2,1)S(1)} %reshape.79.right_ref.own_ref, bf16[256,2048]{1,0:T(8,128)(2,1)S(1)} %collective-permute-done.other_ref, bf16[256,4096]{1,0:T(8,128)(2,1)S(1)} %reshape.79.right_ref.own_ref, bf16[128,1024]{1,0:T(8,128)(2,1)S(1)} %bitcast.65, ...), custom_call_target="tpu_custom_call" | custom-call | flops 8589934592 | bytes 8388608 | tf_op jit(solution)/shard_map/forward/pallas_call | solution.py:159
  104.3 1.3 copy-done.2
  108.6 11.4 %all-to-all-done.1 = bf16[128,2,4096]{2,1,0:T(2,128)(2,1)} async-done(((bf16[128,2,4096]{2,1,0:T(2,128)(2,1)}), bf16[128,2,4096]{2,1,0:T(2,128)(2,1)}, u32[]{:S(2)}, u32[]{:S(2)}) %all-to-all-start.1) | async-done | bytes 2097184 | tf_op jit(solution)/shard_map/all_to_all | solution.py:187
  120.0 2.7 %reshape.83 = bf16[256,4096]{1,0:T(8,128)(2,1)S(1)} reshape(bf16[128,2,4096]{2,1,0:T(2,128)(2,1)} %all-to-all-done.1) | data formatting | bytes 4194304 | tf_op jit(solution)/shard_map/reshape | solution.py:262
  126.8 1.5 convolution_bitcast_fusion
  128.3 1.5 convolution_bitcast_fusion.1
  134.6 1.8 %collective-permute-start.2 = (f32[64,128]{1,0:T(8,128)S(1)}, f32[64,128]{1,0:T(8,128)S(1)}, u32[]{:S(2)}, u32[]{:S(2)}) collective-permute-start(f32[64,128]{1,0:T(8,128)S(1)} %slice.78), channel_id=1, source_target_pairs={{0,1},{1,0},{2,3},{3,2},{4,5},{5,4},{6,7},{7,6},{8,9},{9,8},{10,11... | collective-permute-start | bytes 98312 | tf_op jit(solution)/shard_map/ppermute | solution.py:203
  136.5 1.8 %maximum_select_fusion = f32[1024,128]{0,1:T(8,128)} fusion(f32[1024,128]{0,1:T(8,128)} %copy-done.7, f32[512,128]{0,1:T(8,128)} %get-tuple-element.38, f32[512,128]{0,1:T(8,128)S(1)} %get-tuple-element.37, pred[]{:T(512)S(6)} %eq.5), kind=kLoop, calls=%fused_computation.27 | loop fusion | flops 262144 | bytes 1572865 | tf_op jit(solution)/shard_map/jit(_where)/select_n | solution.py:196
  138.3 2.7 %copy.55 = bf16[128,64,128]{2,1,0:T(8,128)(2,1)} copy(bf16[128,64,128]{2,0,1:T(8,128)(2,1)S(1)} %bitcast.64) | data formatting | bytes 4194304
  141.0 2.1 %copy.54 = f32[1024,128]{1,0:T(8,128)} copy(f32[1024,128]{0,1:T(8,128)} %maximum_select_fusion) | data formatting | bytes 1048576 | tf_op jit(solution)/shard_map/jit(_where)/select_n | solution.py:196
  143.1 3.7 %all-to-all-start.2 = ((f32[128,8,128]{2,1,0:T(8,128)}), f32[128,8,128]{2,1,0:T(8,128)S(1)}, u32[]{:S(2)}, u32[]{:S(2)}) async-start(f32[128,8,128]{2,1,0:T(8,128)} %bitcast.15), calls=%async_computation.2 | async-start | bytes 1048576 | tf_op jit(solution)/shard_map/all_to_all | solution.py:187
  146.8 3.0 %collective-permute-start.4 = (f32[64,128]{1,0:T(8,128)S(1)}, f32[64,128]{1,0:T(8,128)S(1)}, u32[]{:S(2)}, u32[]{:S(2)}) collective-permute-start(f32[64,128]{1,0:T(8,128)S(1)} %slice_add_fusion), channel_id=1, source_target_pairs={{0,4},{1,5},{2,6},{3,7},{4,0},{5,1},{6,2},{7,3},{8,12},{9,13},{10,... | collective-permute-start | bytes 98312 | tf_op jit(solution)/shard_map/ppermute | solution.py:203
  151.2 5.0 %collective-permute-done.4 = f32[64,128]{1,0:T(8,128)S(1)} collective-permute-done((f32[64,128]{1,0:T(8,128)S(1)}, f32[64,128]{1,0:T(8,128)S(1)}, u32[]{:S(2)}, u32[]{:S(2)}) %collective-permute-start.4) | collective-permute-done | bytes 32800 | tf_op jit(solution)/shard_map/ppermute | solution.py:203
  156.2 3.3 %collective-permute-start.7 = (f32[64,128]{1,0:T(8,128)S(1)}, f32[64,128]{1,0:T(8,128)S(1)}, u32[]{:S(2)}, u32[]{:S(2)}) collective-permute-start(f32[64,128]{1,0:T(8,128)S(1)} %add_add_fusion.2), channel_id=1, source_target_pairs={{0,16},{1,17},{2,18},{3,19},{4,20},{5,21},{6,22},{7,23},{8,24},{9,... | collective-permute-start | bytes 98312 | tf_op jit(solution)/shard_map/ppermute | solution.py:203
  161.2 2.3 %collective-permute-done.8 = f32[64,128]{1,0:T(8,128)S(1)} collective-permute-done((f32[64,128]{1,0:T(8,128)S(1)}, f32[64,128]{1,0:T(8,128)S(1)}, u32[]{:S(2)}, u32[]{:S(2)}) %collective-permute-start.8) | collective-permute-done | bytes 32800 | tf_op jit(solution)/shard_map/ppermute | solution.py:203
  163.5 2.9 %collective-permute-start.10 = (f32[64,128]{1,0:T(8,128)S(1)}, f32[64,128]{1,0:T(8,128)S(1)}, u32[]{:S(2)}, u32[]{:S(2)}) collective-permute-start(f32[64,128]{1,0:T(8,128)S(1)} %add_add_fusion.1), channel_id=1, source_target_pairs={{0,64},{1,65},{2,66},{3,67},{4,68},{5,69},{6,70},{7,71},{8,72},{9,... | collective-permute-start | bytes 98312 | tf_op jit(solution)/shard_map/ppermute | solution.py:203
  167.9 2.5 %collective-permute-done.11 = f32[64,128]{1,0:T(8,128)S(1)} collective-permute-done((f32[64,128]{1,0:T(8,128)S(1)}, f32[64,128]{1,0:T(8,128)S(1)}, u32[]{:S(2)}, u32[]{:S(2)}) %collective-permute-start.11) | collective-permute-done | bytes 32800 | tf_op jit(solution)/shard_map/ppermute | solution.py:203
  170.4 4.1 %collective-permute-start.12 = (f32[64,128]{1,0:T(8,128)S(1)}, f32[64,128]{1,0:T(8,128)S(1)}, u32[]{:S(2)}, u32[]{:S(2)}) collective-permute-start(f32[64,128]{1,0:T(8,128)S(1)} %add_add_fusion), channel_id=1, source_target_pairs={{0,1},{1,0},{2,3},{3,2},{4,5},{5,4},{6,7},{7,6},{8,9},{9,8},{10,11... | collective-permute-start | bytes 98312 | tf_op jit(solution)/shard_map/ppermute | solution.py:203
  175.1 1.3 copy.56
  (108 shorter events, 26.9 us)
Async XLA Ops:
  0.6 3.5 %copy-start = (bf16[256,32]{0,1:T(8,128)(2,1)S(1)}, bf16[256,32]{0,1:T(8,128)(2,1)}, u32[]{:S(2)}) copy-start(bf16[256,32]{0,1:T(8,128)(2,1)} %param.9) | copy-start | bytes 49156
  0.6 2.1 %copy-start.16 = (bf16[256,32]{0,1:T(8,128)(2,1)S(1)}, bf16[256,32]{0,1:T(8,128)(2,1)}, u32[]{:S(2)}) copy-start(bf16[256,32]{0,1:T(8,128)(2,1)} %param.10) | copy-start | bytes 49156
  2.2 1.9 %copy-start.5 = (bf16[2,1024,256]{1,2,0:T(8,128)(2,1)}, bf16[2,1024,256]{1,2,0:T(8,128)(2,1)S(1)}, u32[]{:S(2)}) copy-start(bf16[2,1024,256]{1,2,0:T(8,128)(2,1)S(1)} %copy.31) | copy-start | bytes 3145732
  2.4 1.7 copy-start.12
  2.7 1.8 copy-start.14
  10.7 12.0 %copy-start.11 = (bf16[1024,128]{1,0:T(8,128)(2,1)S(1)}, bf16[1024,128]{1,0:T(8,128)(2,1)}, u32[]{:S(2)}) copy-start(bf16[1024,128]{1,0:T(8,128)(2,1)} %param.11) | copy-start | bytes 786436
  10.7 42.1 %all-to-all-start = ((bf16[128,2,4096]{2,1,0:T(2,128)(2,1)}), bf16[128,2,4096]{2,1,0:T(2,128)(2,1)}, u32[]{:S(2)}, u32[]{:S(2)}) async-start(bf16[128,2,4096]{2,1,0:T(2,128)(2,1)} %bitcast.5), calls=%async_computation | async-start | bytes 4194304 | tf_op jit(solution)/shard_map/all_to_all | solution.py:187
  22.6 1.6 copy-start.9
  55.6 11.5 %collective-permute-start = (bf16[256,2048]{1,0:T(8,128)(2,1)S(1)}, bf16[256,2048]{1,0:T(8,128)(2,1)S(1)}, u32[]{:S(2)}, u32[]{:S(2)}) collective-permute-start(bf16[256,2048]{1,0:T(8,128)(2,1)S(1)} %slice.70), channel_id=1, source_target_pairs={{0,1},{1,0},{2,3},{3,2},{4,5},{5,4},{6,7},{7,6},{8,9},{9,8},{10,11... | collective-permute-start | bytes 3145736 | tf_op jit(solution)/shard_map/ppermute | solution.py:191
  67.2 10.8 %collective-permute-start.1 = (bf16[256,2048]{1,0:T(8,128)(2,1)S(1)}, bf16[256,2048]{1,0:T(8,128)(2,1)S(1)}, u32[]{:S(2)}, u32[]{:S(2)}) collective-permute-start(bf16[256,2048]{1,0:T(8,128)(2,1)S(1)} %slice.55), channel_id=1, source_target_pairs={{0,1},{1,0},{2,3},{3,2},{4,5},{5,4},{6,7},{7,6},{8,9},{9,8},{10,11... | collective-permute-start | bytes 3145736 | tf_op jit(solution)/shard_map/ppermute | solution.py:191
  84.4 5.3 %copy-start.18 = (bf16[128]{0:T(256)(128)(2,1)S(1)}, bf16[128]{0:T(256)(128)(2,1)}, u32[]{:S(2)}) copy-start(bf16[128]{0:T(256)(128)(2,1)} %param.12) | copy-start | bytes 772
  84.4 35.6 %all-to-all-start.1 = ((bf16[128,2,4096]{2,1,0:T(2,128)(2,1)}), bf16[128,2,4096]{2,1,0:T(2,128)(2,1)}, u32[]{:S(2)}, u32[]{:S(2)}) async-start(bf16[128,2,4096]{2,1,0:T(2,128)(2,1)} %reshape.80), calls=%async_computation.1 | async-start | bytes 4194304 | tf_op jit(solution)/shard_map/all_to_all | solution.py:187
  107.7 12.3 %copy-start.7 = (f32[1024,128]{0,1:T(8,128)}, f32[1024,128]{0,1:T(8,128)S(1)}, u32[]{:S(2)}) copy-start(f32[1024,128]{0,1:T(8,128)S(1)} %copy.53) | copy-start | bytes 1572868
  122.7 4.0 %copy-start.6 = (bf16[2,1024,256]{1,2,0:T(8,128)(2,1)S(1)}, bf16[2,1024,256]{1,2,0:T(8,128)(2,1)}, u32[]{:S(2)}) copy-start(bf16[2,1024,256]{1,2,0:T(8,128)(2,1)} %copy-done.5) | copy-start | bytes 3145732
  128.3 10.0 %copy-start.3 = (bf16[64,128,128]{2,1,0:T(8,128)(2,1)S(1)}, bf16[64,128,128]{2,1,0:T(8,128)(2,1)}, u32[]{:S(2)}) copy-start(bf16[64,128,128]{2,1,0:T(8,128)(2,1)} %copy-done.2) | copy-start | bytes 6291460
  134.6 12.2 %collective-permute-start.2 = (f32[64,128]{1,0:T(8,128)S(1)}, f32[64,128]{1,0:T(8,128)S(1)}, u32[]{:S(2)}, u32[]{:S(2)}) collective-permute-start(f32[64,128]{1,0:T(8,128)S(1)} %slice.78), channel_id=1, source_target_pairs={{0,1},{1,0},{2,3},{3,2},{4,5},{5,4},{6,7},{7,6},{8,9},{9,8},{10,11... | collective-permute-start | bytes 98312 | tf_op jit(solution)/shard_map/ppermute | solution.py:203
  141.0 9.7 %copy-start.8 = (bf16[2,1024,32]{2,1,0:T(8,128)(2,1)S(1)}, bf16[2,1024,32]{2,1,0:T(8,128)(2,1)}, u32[]{:S(2)}) copy-start(bf16[2,1024,32]{2,1,0:T(8,128)(2,1)} %reshape.86) | copy-start | bytes 393220
  141.0 9.7 %copy-start.17 = (bf16[256,32]{0,1:T(8,128)(2,1)S(1)}, bf16[256,32]{0,1:T(8,128)(2,1)}, u32[]{:S(2)}) copy-start(bf16[256,32]{0,1:T(8,128)(2,1)} %param.10) | copy-start | bytes 49156
  143.1 17.1 %copy-start.10 = (bf16[2,8,32,128]{3,2,1,0:T(8,128)(2,1)S(1)}, bf16[2,8,32,128]{3,2,1,0:T(8,128)(2,1)}, u32[]{:S(2)}) copy-start(bf16[2,8,32,128]{3,2,1,0:T(8,128)(2,1)} %reshape.84) | copy-start | bytes 393220
  143.1 17.1 %copy-start.13 = (f32[2,1024]{1,0:T(2,128)S(1)}, f32[2,1024]{1,0:T(2,128)}, u32[]{:S(2)}) copy-start(f32[2,1024]{1,0:T(2,128)} %copy-done.12) | copy-start | bytes 24580
  143.1 17.1 %copy-start.15 = (f32[2,1024]{1,0:T(2,128)S(1)}, f32[2,1024]{1,0:T(2,128)}, u32[]{:S(2)}) copy-start(f32[2,1024]{1,0:T(2,128)} %copy-done.14) | copy-start | bytes 24580
  143.1 33.4 %all-to-all-start.2 = ((f32[128,8,128]{2,1,0:T(8,128)}), f32[128,8,128]{2,1,0:T(8,128)S(1)}, u32[]{:S(2)}, u32[]{:S(2)}) async-start(f32[128,8,128]{2,1,0:T(8,128)} %bitcast.15), calls=%async_computation.2 | async-start | bytes 1048576 | tf_op jit(solution)/shard_map/all_to_all | solution.py:187
  146.8 9.3 %collective-permute-start.4 = (f32[64,128]{1,0:T(8,128)S(1)}, f32[64,128]{1,0:T(8,128)S(1)}, u32[]{:S(2)}, u32[]{:S(2)}) collective-permute-start(f32[64,128]{1,0:T(8,128)S(1)} %slice_add_fusion), channel_id=1, source_target_pairs={{0,4},{1,5},{2,6},{3,7},{4,0},{5,1},{6,2},{7,3},{8,12},{9,13},{10,... | collective-permute-start | bytes 98312 | tf_op jit(solution)/shard_map/ppermute | solution.py:203
  149.8 6.4 %collective-permute-start.5 = (f32[64,128]{1,0:T(8,128)S(1)}, f32[64,128]{1,0:T(8,128)S(1)}, u32[]{:S(2)}, u32[]{:S(2)}) collective-permute-start(f32[64,128]{1,0:T(8,128)S(1)} %slice_add_fusion), channel_id=1, source_target_pairs={{0,6},{1,7},{2,4},{3,5},{4,2},{5,3},{6,0},{7,1},{8,14},{9,15},{10,... | collective-permute-start | bytes 98312 | tf_op jit(solution)/shard_map/ppermute | solution.py:203
  150.7 5.6 %collective-permute-start.3 = (f32[64,128]{1,0:T(8,128)S(1)}, f32[64,128]{1,0:T(8,128)S(1)}, u32[]{:S(2)}, u32[]{:S(2)}) collective-permute-start(f32[64,128]{1,0:T(8,128)S(1)} %slice_add_fusion), channel_id=1, source_target_pairs={{0,2},{1,3},{2,0},{3,1},{4,6},{5,7},{6,4},{7,5},{8,10},{9,11},{10,... | collective-permute-start | bytes 98312 | tf_op jit(solution)/shard_map/ppermute | solution.py:203
  156.2 4.9 %collective-permute-start.7 = (f32[64,128]{1,0:T(8,128)S(1)}, f32[64,128]{1,0:T(8,128)S(1)}, u32[]{:S(2)}, u32[]{:S(2)}) collective-permute-start(f32[64,128]{1,0:T(8,128)S(1)} %add_add_fusion.2), channel_id=1, source_target_pairs={{0,16},{1,17},{2,18},{3,19},{4,20},{5,21},{6,22},{7,23},{8,24},{9,... | collective-permute-start | bytes 98312 | tf_op jit(solution)/shard_map/ppermute | solution.py:203
  159.6 4.0 %collective-permute-start.8 = (f32[64,128]{1,0:T(8,128)S(1)}, f32[64,128]{1,0:T(8,128)S(1)}, u32[]{:S(2)}, u32[]{:S(2)}) collective-permute-start(f32[64,128]{1,0:T(8,128)S(1)} %add_add_fusion.2), channel_id=1, source_target_pairs={{0,24},{1,25},{2,26},{3,27},{4,28},{5,29},{6,30},{7,31},{8,16},{9,... | collective-permute-start | bytes 98312 | tf_op jit(solution)/shard_map/ppermute | solution.py:203
  160.2 3.4 %collective-permute-start.6 = (f32[64,128]{1,0:T(8,128)S(1)}, f32[64,128]{1,0:T(8,128)S(1)}, u32[]{:S(2)}, u32[]{:S(2)}) collective-permute-start(f32[64,128]{1,0:T(8,128)S(1)} %add_add_fusion.2), channel_id=1, source_target_pairs={{0,8},{1,9},{2,10},{3,11},{4,12},{5,13},{6,14},{7,15},{8,0},{9,1},... | collective-permute-start | bytes 98312 | tf_op jit(solution)/shard_map/ppermute | solution.py:203
  163.5 4.3 %collective-permute-start.10 = (f32[64,128]{1,0:T(8,128)S(1)}, f32[64,128]{1,0:T(8,128)S(1)}, u32[]{:S(2)}, u32[]{:S(2)}) collective-permute-start(f32[64,128]{1,0:T(8,128)S(1)} %add_add_fusion.1), channel_id=1, source_target_pairs={{0,64},{1,65},{2,66},{3,67},{4,68},{5,69},{6,70},{7,71},{8,72},{9,... | collective-permute-start | bytes 98312 | tf_op jit(solution)/shard_map/ppermute | solution.py:203
  166.4 4.0 %collective-permute-start.11 = (f32[64,128]{1,0:T(8,128)S(1)}, f32[64,128]{1,0:T(8,128)S(1)}, u32[]{:S(2)}, u32[]{:S(2)}) collective-permute-start(f32[64,128]{1,0:T(8,128)S(1)} %add_add_fusion.1), channel_id=1, source_target_pairs={{0,96},{1,97},{2,98},{3,99},{4,100},{5,101},{6,102},{7,103},{8,104... | collective-permute-start | bytes 98312 | tf_op jit(solution)/shard_map/ppermute | solution.py:203
  167.3 3.2 %collective-permute-start.9 = (f32[64,128]{1,0:T(8,128)S(1)}, f32[64,128]{1,0:T(8,128)S(1)}, u32[]{:S(2)}, u32[]{:S(2)}) collective-permute-start(f32[64,128]{1,0:T(8,128)S(1)} %add_add_fusion.1), channel_id=1, source_target_pairs={{0,32},{1,33},{2,34},{3,35},{4,36},{5,37},{6,38},{7,39},{8,40},{9,... | collective-permute-start | bytes 98312 | tf_op jit(solution)/shard_map/ppermute | solution.py:203
  170.4 6.0 %collective-permute-start.12 = (f32[64,128]{1,0:T(8,128)S(1)}, f32[64,128]{1,0:T(8,128)S(1)}, u32[]{:S(2)}, u32[]{:S(2)}) collective-permute-start(f32[64,128]{1,0:T(8,128)S(1)} %add_add_fusion), channel_id=1, source_target_pairs={{0,1},{1,0},{2,3},{3,2},{4,5},{5,4},{6,7},{7,6},{8,9},{9,8},{10,11... | collective-permute-start | bytes 98312 | tf_op jit(solution)/shard_map/ppermute | solution.py:203
  (3 other events, 3.5 us)

commit v3 on v2

--- a/solution.py
+++ b/solution.py
@@ -11,6 +11,7 @@
 BOTH = ("row", "col")
 TILE = 16
 GRAD_TILE = 8
+STREAMS = 4
 CORES = 2
 VMEM_BYTES = 48 * 1024 * 1024
 NT = (((1,), (1,)), ((), ()))
@@ -43,20 +44,32 @@
                 ]
 
 
-def left_kernel(inverse, right_ref, grad_ref, out_ref):
-    grads = jnp.dot(right_ref[...], grad_ref[...], preferred_element_type=jnp.float32)
+def left_kernel(inverse, right_ref, *refs):
+    grad_refs, out_ref = refs[:-1], refs[-1]
+    depth = grad_refs[0].shape[0]
+    grads = 0.0
+    for k, grad_ref in enumerate(grad_refs):
+        grads += jnp.dot(
+            right_ref[:, k * depth:(k + 1) * depth], grad_ref[...], preferred_element_type=jnp.float32
+        )
     out_ref[...] = (grads * inverse).astype(out_ref.dtype)
 
 
-def right_kernel(inverse, own_ref, other_ref, grad_ref, out_ref):
-    half = own_ref.shape[1]
-    grads = lax.dot_general(own_ref[...], grad_ref[:, :half], NT, preferred_element_type=jnp.float32)
-    grads += lax.dot_general(other_ref[...], grad_ref[:, half:], NT, preferred_element_type=jnp.float32)
+def right_kernel(inverse, own_ref, other_ref, *refs):
+    grad_refs, out_ref = refs[:-1], refs[-1]
+    depth = grad_refs[0].shape[1]
+    each = own_ref.shape[1] // depth
+    grads = 0.0
+    for k, grad_ref in enumerate(grad_refs):
+        half_ref, first = (own_ref, k) if k < each else (other_ref, k - each)
+        grads += lax.dot_general(
+            half_ref[:, first * depth:(first + 1) * depth], grad_ref[...], NT, preferred_element_type=jnp.float32
+        )
     out_ref[...] = (grads * inverse).astype(out_ref.dtype)
 
 
 def forward_kernel(
-    inverse, width, own_ref, other_ref, right_ref, weight_t_ref, bias_ref, cot_ref, update_ref, wgrad_ref, outer_ref
+    inverse, width, core_ref, own_ref, other_ref, right_ref, weight_t_ref, bias_ref, cot_ref, update_ref, wgrad_ref, outer_ref
 ):
     tile, rows, pair_width = cot_ref.shape
     right_t = right_ref[...].T
@@ -84,7 +97,12 @@
         wgrad_ref[...] = jnp.zeros_like(wgrad_ref)
 
     flat = cot_ref[...].reshape(tile * rows, pair_width)
-    wgrad_ref[...] += inverse * jnp.dot(outer_ref[...], flat, preferred_element_type=jnp.float32)
+    half = wgrad_ref.shape[0] // CORES
+    for k in range(CORES):
+        place = pl.ds(pl.multiple_of((core_ref[0] ^ k) * half, half), half)
+        wgrad_ref[place] += inverse * jnp.dot(
+            outer_ref[k * half:(k + 1) * half], flat, preferred_element_type=jnp.float32
+        )
 
 
 def whole(shape):
@@ -121,7 +139,7 @@
         grid=(columns // block,),
         in_specs=[
             pl.BlockSpec((seqs, depth), lambda n: (0, last)),
-            pl.BlockSpec((depth, block), lambda n: (0, n)),
+            *[pl.BlockSpec((depth // STREAMS, block), lambda n, k=k: (k, n)) for k in range(STREAMS)],
         ],
         out_specs=pl.BlockSpec((seqs, block), lambda n: (0, n)),
         out_shape=jax.ShapeDtypeStruct((seqs, columns), jnp.bfloat16),
@@ -129,7 +147,7 @@
         cost_estimate=pl.CostEstimate(flops=2 * seqs * depth * columns, bytes_accessed=19 * 2**20, transcendentals=0),
         interpret=interpret,
         name="left_grads",
-    )(came, grads)
+    )(came, *[grads] * STREAMS)
 
 
 def right_grads(came, other, grads, interpret=False):
@@ -141,7 +159,7 @@
         in_specs=[
             pl.BlockSpec((seqs, depth // 2), lambda n: (0, 0)),
             whole((seqs, depth // 2)),
-            pl.BlockSpec((block, depth), lambda n: (n, 0)),
+            *[pl.BlockSpec((block, depth // STREAMS), lambda n, k=k: (n, k)) for k in range(STREAMS)],
         ],
         out_specs=pl.BlockSpec((seqs, block), lambda n: (0, n)),
         out_shape=jax.ShapeDtypeStruct((seqs, rows), jnp.bfloat16),
@@ -149,10 +167,10 @@
         cost_estimate=pl.CostEstimate(flops=2 * seqs * depth * rows, bytes_accessed=19 * 2**20, transcendentals=0),
         interpret=interpret,
         name="right_grads",
-    )(came, other, grads)
-
-
-def forward(came, other, weight_t, bias, cot, width, interpret=False):
+    )(came, other, *[grads] * STREAMS)
+
+
+def forward(core, came, other, weight_t, bias, cot, width, interpret=False):
     seqs, cols, rows, pair_width = came.shape[0], cot.shape[0], cot.shape[1], cot.shape[2]
     flops = 2 * cols * rows * width * width * (2 * pair_width + seqs)
     first = other.shape[1] // (TILE * width)
@@ -160,6 +178,7 @@
         functools.partial(forward_kernel, 1.0 / seqs, width),
         grid=(cols // TILE,),
         in_specs=[
+            pl.BlockSpec(memory_space=pltpu.SMEM),
             pl.BlockSpec(other.shape, lambda j: (0, 0)),
             whole(other.shape),
             pl.BlockSpec((seqs, TILE * width), lambda j: (0, first + j)),
@@ -180,7 +199,7 @@
         cost_estimate=pl.CostEstimate(flops=flops, bytes_accessed=8 * 2**20, transcendentals=0),
         interpret=interpret,
         name="forward",
-    )(came, other, came, weight_t, bias, cot)
+    )(core.reshape(1), came, other, came, weight_t, bias, cot)
 
 
 def exchange(blocks):
@@ -196,25 +215,58 @@
     return jnp.where(core == 0, values, jnp.concatenate([values[half:], values[:half]], axis=0))
 
 
-def sum_all(values):
+def permute_groups():
     devices = lax.axis_size(BOTH)
-
-    def partner(part, mask):
-        return lax.ppermute(part, BOTH, [(i, i ^ mask) for i in range(devices)])
-
-    core = lax.axis_index("col") % CORES
-    half = values.shape[0] // CORES
-    halves = own_first(values, core)
-    part = halves[:half] + partner(halves[half:], 1)
-    mask = CORES
-    while mask < devices:
-        if 4 * mask <= devices:
-            others = [partner(part, mask), partner(part, 2 * mask), partner(part, 3 * mask)]
-            part = (part + others[0]) + (others[1] + others[2])
-        else:
-            part = part + partner(part, mask)
-        mask *= 4
-    return own_first(jnp.concatenate([part, partner(part, 1)], axis=0), core)
+    groups = [(1, CORES)]
+    while groups[-1][0] * groups[-1][1] < devices:
+        low = groups[-1][0] * groups[-1][1]
+        groups.append((low, min(4, devices // low)))
+    return groups
+
+
+def partner(part, mask):
+    return lax.ppermute(part, BOTH, [(i, i ^ mask) for i in range(lax.axis_size(BOTH))])
+
+
+def add_parts(parts):
+    while len(parts) > 1:
+        parts = [parts[k] + parts[k + 1] for k in range(0, len(parts), 2)]
+    return parts[0]
+
+
+def scatter_pieces(values, low, size):
+    values = values.reshape((-1, size) + values.shape[1:])
+    mine = lax.axis_index(BOTH) // low % size
+    return [lax.dynamic_index_in_dim(values, mine ^ mask, 1, keepdims=False) for mask in range(size)]
+
+
+def sum_scatter(values, groups):
+    for low, size in groups:
+        kept, *pieces = scatter_pieces(values, low, size)
+        values = add_parts([kept] + [partner(piece, low * (k + 1)) for k, piece in enumerate(pieces)])
+    return values
+
+
+def sum_all(first, second, values, early):
+    core = lax.axis_index(BOTH) % CORES
+    own, other = jnp.where(core == 0, first, second), jnp.where(core == 0, second, first)
+    part = own + partner(other, 1)
+    rows, columns = part.shape
+    for step, (low, size) in enumerate(permute_groups()):
+        if step == 0:
+            continue
+        if step < early:
+            part = add_parts([part] + [partner(part, low * mask) for mask in range(1, size)])
+            continue
+        share, lanes = values.shape[1:]
+        pieces = [piece.reshape(-1, lanes) for piece in scatter_pieces(values, low, size)]
+        used = pieces[0].shape[0]
+        pieces = [jnp.pad(piece, ((0, rows - used), (0, 0))) for piece in pieces]
+        sent = [jnp.concatenate([part, piece], axis=1) for piece in pieces]
+        both = add_parts(sent[:1] + [partner(sent[mask], low * mask) for mask in range(1, size)])
+        part, values = both[:, :columns], both[:used, columns:].reshape(-1, share, lanes)
+    other = partner(part, 1)
+    return jnp.where(core == 0, part, other), jnp.where(core == 0, other, part), values
 
 
 def body(alignment, left_weight, right_weight, out_weight, out_bias, pair_cotangent):
@@ -260,10 +312,12 @@
     sent = jnp.concatenate([left_pair, right_part], axis=1).reshape(devices, local, columns)
     sent, left_other = lax.optimization_barrier((sent, left_other))
     back = exchange(sent).reshape(seqs, columns)
-    update, weight_term = forward(came, left_other, weight.T, bias, cot, width)
+    update, weight_term = forward(core, came, left_other, weight.T, bias, cot, width)
     pair_update = update.transpose(1, 0, 2)
-    share = weight_term.shape[0] // devices
-    weight_parts = exchange(own_first(weight_term, core).reshape(devices, share, pair_width))
+    early = 2
+    weight_term = weight_term.reshape(devices, -1, pair_width)
+    weight_term = sum_scatter(weight_term, permute_groups()[:early])
+    back, weight_term = lax.optimization_barrier((back, weight_term))
 
     place = np.indices((row_count, chips, CORES, local)).reshape(4, -1)
     left_place = (place[3] * row_count + place[0]) * CORES + place[2]
@@ -276,17 +330,15 @@
     left_grad = left_grad.reshape(local, row_count, width, row_block).transpose(0, 2, 1, 3)
     left_grad = left_grad.reshape(local, width, residues)
     right_grad = right_grad.reshape(local, residues, width)
-    left_wgrad = jnp.einsum("src,shr->ch", normed_low, left_grad, preferred_element_type=jnp.float32)
-    right_wgrad = jnp.einsum("src,srh->ch", normed_low, right_grad, preferred_element_type=jnp.float32)
-    wgrads = sum_all(jnp.concatenate([left_wgrad, right_wgrad], axis=1).reshape(-1, 128))
-    wgrads, weight_parts = lax.optimization_barrier((wgrads, weight_parts))
-    grad_out_weight = jnp.sum(weight_parts, axis=0)
-    wgrads = wgrads.reshape(model_width, 2 * width)
+    left_wgrad = jnp.einsum("src,shr->hc", normed_low, left_grad, preferred_element_type=jnp.float32)
+    right_wgrad = jnp.einsum("src,srh->hc", normed_low, right_grad, preferred_element_type=jnp.float32)
+    left_wgrad, right_wgrad, weight_term = sum_all(left_wgrad, right_wgrad, weight_term, early)
+    grad_out_weight = weight_term.reshape(-1, pair_width)
 
     upstream = jnp.einsum("shr,ch->src", left_grad, left_weight, preferred_element_type=jnp.float32)
     upstream += jnp.einsum("srh,ch->src", right_grad, right_weight, preferred_element_type=jnp.float32)
     grad_alignment = norm_backward(upstream, normed, inv_sigma).astype(jnp.bfloat16)
-    return (pair_update, grad_alignment, grad_out_weight, wgrads[:, :width], wgrads[:, width:])
+    return (pair_update, grad_alignment, grad_out_weight, left_wgrad.T, right_wgrad.T)
 
 
 def solution(mesh):

time: 180 us -> 158 us (0.88)
  waiting for transfers between devices: 38.5 us -> 28.4 us
  local copies, waits for them, and re-layouts: 36.2 us -> 28.6 us
  matrix products: 7.05 us -> 4.42 us
  other arithmetic: 10.8 us -> 8.64 us
    all_to_all x3 -> x2, waiting for transfers between devices: 27.6 us -> 17.2 us  [exchange(): return lax.all_to_all(blocks, BOTH, 0, 0, tiled=True)]
    ppermute x11 -> x15, starting transfers between devices: 17.5 us -> 22.2 us  [partner(): lax.ppermute(part, BOTH, [(i, i ^ mask) for i in range(lax.axis_size(BOTH...]
    all_to_all x3 -> x2, starting transfers between devices: 21 us -> 17.2 us  [exchange(): return lax.all_to_all(blocks, BOTH, 0, 0, tiled=True)]
    select_n x2 -> x1, local copies, waits for them, and re-layouts: 2.27 us -> 0.17 us  [own_first(): jnp.where(core == 0, values, jnp.concatenate([values[half:], values[:half...]
    select_n x4 -> x1, other arithmetic: 1.9 us -> 0.07 us  [own_first(): jnp.where(core == 0, values, jnp.concatenate([values[half:], values[:half...]
    ppermute x11 -> x15, waiting for transfers between devices: 10.9 us -> 11.2 us  [partner(): lax.ppermute(part, BOTH, [(i, i ^ mask) for i in range(lax.axis_size(BOTH...]
    unnamed x46 -> x32, local copies, waits for them, and re-layouts: 13.1 us -> 13.3 us
  transfers between devices with their start and end apart: 16 -> 19, of which waited for: 8 -> 10; matrix products, arithmetic and copies ran while one was open for 8% -> 7% of each run, Pallas kernels for 25% -> 29%
where the time goes in v3:
time: 158 us; the launch traced here: 157 us
  Pallas kernels  45 us (28%)
  starting transfers between devices  40.6 us (26%)
  local copies, waits for them, and re-layouts  28.6 us (18%)
  waiting for transfers between devices  28.4 us (18%)
  other arithmetic  8.64 us (5%)
  matrix products  4.42 us (3%)
    ppermute x15, starting transfers between devices, partner(): lax.ppermute(part, BOTH, [(i, i ^ mask) for i in range(lax.axis_size(BOTH...  22.2 us
    all_to_all x2, starting transfers between devices, exchange(): return lax.all_to_all(blocks, BOTH, 0, 0, tiled=True)  17.2 us
    all_to_all x2, waiting for transfers between devices, exchange(): return lax.all_to_all(blocks, BOTH, 0, 0, tiled=True)  17.2 us
    pallas_call x1, Pallas kernels, forward(): pl.pallas_call(functools.partial(forward_kernel, 1.0 / seqs, width), grid...  14.7 us
    unnamed x32, local copies, waits for them, and re-layouts  13.3 us
    ppermute x15, waiting for transfers between devices, partner(): lax.ppermute(part, BOTH, [(i, i ^ mask) for i in range(lax.axis_size(BOTH...  11.2 us
    pallas_call x1, Pallas kernels, right_grads(): pl.pallas_call(functools.partial(right_kernel, 1.0 / seqs), grid=(rows //...  10.4 us
    pallas_call x1, Pallas kernels, left_grads(): pl.pallas_call(functools.partial(left_kernel, 1.0 / seqs), grid=(columns...  10.3 us
  transfers between devices with their start and end apart: 19, of which 10 were waited for; matrix products, arithmetic and copies ran while one was open for 7% of the time, Pallas kernels for 29%

profile of v3, /device:TPU:1, one launch (start us, length us, event | category | flops | bytes accessed | tf_op | source)
XLA Modules:
  0.0 156.9 jit_solution(3814355263897510672)
XLA Ops:
  0.7 1.5 copy.47
  6.8 3.8 %pad_maximum_fusion = bf16[8,8,2,2,4096]{4,3,2,1,0:T(2,128)(2,1)} fusion(bf16[8,8,2,2,2048]{4,3,2,1,0:T(2,128)(2,1)S(1)} %broadcast_in_dim.8, bf16[8,8,2,2,2048]{4,3,2,1,0:T(2,128)(2,1)S(1)} %broadcast_in_dim.7), kind=kLoop, calls=%fused_computation.16 | loop fusion | flops 4194304 | bytes 4194304 | tf_op jit(solution)/shard_map/concatenate | solution.py:296
  10.6 12.0 %all-to-all-start = ((bf16[128,2,4096]{2,1,0:T(2,128)(2,1)}), bf16[128,2,4096]{2,1,0:T(2,128)(2,1)}, u32[]{:S(2)}, u32[]{:S(2)}) async-start(bf16[128,2,4096]{2,1,0:T(2,128)(2,1)} %bitcast.6), calls=%async_computation | async-start | bytes 4194304 | tf_op jit(solution)/shard_map/all_to_all | solution.py:206
  24.2 1.4 copy.86
  25.5 9.6 %outer_grads.1.refs_0_.refs_1_.refs_2_.refs_3_ = bf16[2048,4096]{1,0:T(8,128)(2,1)} custom-call(bf16[1024,128]{1,0:T(8,128)(2,1)S(1)} %copy.58.weight_ref, bf16[64,128,128]{2,1,0:T(8,128)(2,1)S(1)} %bitcast.101), custom_call_target="tpu_custom_call" | custom-call | flops 2147483648 | bytes 18874368 | tf_op jit(solution)/shard_map/outer_grads/pallas_call | solution.py:118
  35.2 1.4 copy-done.1
  36.5 16.2 %all-to-all-done = bf16[128,2,4096]{2,1,0:T(2,128)(2,1)} async-done(((bf16[128,2,4096]{2,1,0:T(2,128)(2,1)}), bf16[128,2,4096]{2,1,0:T(2,128)(2,1)}, u32[]{:S(2)}, u32[]{:S(2)}) %all-to-all-start) | async-done | bytes 2097184 | tf_op jit(solution)/shard_map/all_to_all | solution.py:206
  52.8 2.7 %reshape.110.right_ref.own_ref = bf16[256,4096]{1,0:T(8,128)(2,1)S(1)} reshape(bf16[128,2,4096]{2,1,0:T(2,128)(2,1)} %all-to-all-done) | data formatting | bytes 4194304 | tf_op jit(solution)/shard_map/reshape | solution.py:305
  56.6 10.3 %left_grads.1 = bf16[256,4096]{1,0:T(8,128)(2,1)S(1)} custom-call(bf16[256,4096]{1,0:T(8,128)(2,1)S(1)} %reshape.110.right_ref.own_ref, bf16[2048,4096]{1,0:T(8,128)(2,1)} %outer_grads.1.refs_0_.refs_1_.refs_2_.refs_3_, bf16[2048,4096]{1,0:T(8,128)(2,1)} %outer_grads.1.refs_0_.refs_1_.refs_2_.refs_3_, ...), custom_call_target="tpu_custom_call" | custom-call | flops 4294967296 | bytes 19922944 | tf_op jit(solution)/shard_map/left_grads/pallas_call | solution.py:137
  67.1 10.4 %right_grads.1 = bf16[256,2048]{1,0:T(8,128)(2,1)S(1)} custom-call(bf16[256,4096]{1,0:T(8,128)(2,1)S(1)} %reshape.110.right_ref.own_ref, bf16[256,2048]{1,0:T(8,128)(2,1)S(1)} %collective-permute-done.other_ref, bf16[2048,4096]{1,0:T(8,128)(2,1)} %outer_grads.1.refs_0_.refs_1_.refs_2_.refs_3_, bf16[2048,4096]{1,0:T(8,128)(2,1)} %outer_grads.1.refs_0_.refs_1_.refs_2_.refs_3_, ...), custom_call_target="tpu_custom_call" | custom-call | flops 4294967296 | bytes 19922944 | tf_op jit(solution)/shard_map/right_grads/pallas_call | solution.py:156
  77.9 1.5 pad_maximum_fusion.1
  79.4 4.4 %reshape.111 = bf16[128,2,4096]{2,1,0:T(2,128)(2,1)} reshape(bf16[256,4096]{1,0:T(8,128)(2,1)} %pad_maximum_fusion.1) | data formatting | bytes 4194304 | tf_op jit(solution)/shard_map/reshape | solution.py:312
  83.8 5.3 %all-to-all-start.1 = ((bf16[128,2,4096]{2,1,0:T(2,128)(2,1)}), bf16[128,2,4096]{2,1,0:T(2,128)(2,1)}, u32[]{:S(2)}, u32[]{:S(2)}) async-start(bf16[128,2,4096]{2,1,0:T(2,128)(2,1)} %reshape.111), calls=%async_computation.1 | async-start | bytes 4194304 | tf_op jit(solution)/shard_map/all_to_all | solution.py:206
  89.2 14.7 %forward.1 = (bf16[64,128,128]{2,1,0:T(8,128)(2,1)S(1)}, f32[1024,128]{1,0:T(8,128)S(1)}) custom-call(s32[1]{0:T(128)} %bitcast.core_ref, bf16[256,4096]{1,0:T(8,128)(2,1)S(1)} %reshape.110.right_ref.own_ref, bf16[256,2048]{1,0:T(8,128)(2,1)S(1)} %collective-permute-done.other_ref, bf16[256,4096]{1,0:T(8,128)(2,1)S(1)} %reshape.110.right_ref.own_ref, ...), custom_call_target="tpu_custom_call" | custom-call | flops 8589934592 | bytes 8388608 | tf_op jit(solution)/shard_map/forward/pallas_call | solution.py:177
  103.9 1.4 copy-done.2
  106.1 1.4 collective-permute-start.2
  110.2 2.4 %collective-permute-start.4 = (f32[16,8,128]{2,1,0:T(8,128)S(1)}, f32[16,8,128]{2,1,0:T(8,128)S(1)}, u32[]{:S(2)}, u32[]{:S(2)}) collective-permute-start(f32[16,8,128]{2,1,0:T(8,128)S(1)} %get-tuple-element.43), channel_id=1, source_target_pairs={{0,4},{1,5},{2,6},{3,7},{4,0},{5,1},{6,2},{7,3},{8,12},{9,13},{10,... | collective-permute-start | bytes 196616 | tf_op jit(solution)/shard_map/ppermute | solution.py:228
  113.6 4.3 %copy.64 = bf16[128,64,128]{2,1,0:T(8,128)(2,1)} copy(bf16[128,64,128]{2,0,1:T(8,128)(2,1)} %bitcast.103) | data formatting | bytes 4194304
  119.4 2.7 %reshape.114 = bf16[256,4096]{1,0:T(8,128)(2,1)S(1)} reshape(bf16[128,2,4096]{2,1,0:T(2,128)(2,1)} %all-to-all-done.1) | data formatting | bytes 4194304 | tf_op jit(solution)/shard_map/reshape | solution.py:314
  124.5 1.5 broadcast_select_fusion
  126.0 1.5 collective-permute-start.6
  128.3 2.7 %collective-permute-start.9 = (f32[32,256]{1,0:T(8,128)S(1)}, f32[32,256]{1,0:T(8,128)S(1)}, u32[]{:S(2)}, u32[]{:S(2)}) collective-permute-start(f32[32,256]{1,0:T(8,128)S(1)} %select_add_fusion), channel_id=1, source_target_pairs={{0,6},{1,7},{2,4},{3,5},{4,2},{5,3},{6,0},{7,1},{8,14},{9,15},{10,... | collective-permute-start | bytes 98312 | tf_op jit(solution)/shard_map/ppermute | solution.py:228
  131.0 1.7 %collective-permute-done.8 = f32[32,256]{1,0:T(8,128)S(1)} collective-permute-done((f32[32,256]{1,0:T(8,128)S(1)}, f32[32,256]{1,0:T(8,128)S(1)}, u32[]{:S(2)}, u32[]{:S(2)}) %collective-permute-start.8) | collective-permute-done | bytes 32800 | tf_op jit(solution)/shard_map/ppermute | solution.py:228
  134.0 2.2 %collective-permute-start.11 = (f32[32,384]{1,0:T(8,128)S(1)}, f32[32,384]{1,0:T(8,128)S(1)}, u32[]{:S(2)}, u32[]{:S(2)}) collective-permute-start(f32[32,384]{1,0:T(8,128)S(1)} %get-tuple-element.58), channel_id=1, source_target_pairs={{0,16},{1,17},{2,18},{3,19},{4,20},{5,21},{6,22},{7,23},{8,24},{9,... | collective-permute-start | bytes 147464 | tf_op jit(solution)/shard_map/ppermute | solution.py:228
  136.3 1.6 %collective-permute-start.12 = (f32[32,384]{1,0:T(8,128)S(1)}, f32[32,384]{1,0:T(8,128)S(1)}, u32[]{:S(2)}, u32[]{:S(2)}) collective-permute-start(f32[32,384]{1,0:T(8,128)S(1)} %get-tuple-element.56), channel_id=1, source_target_pairs={{0,24},{1,25},{2,26},{3,27},{4,28},{5,29},{6,30},{7,31},{8,16},{9,... | collective-permute-start | bytes 147464 | tf_op jit(solution)/shard_map/ppermute | solution.py:228
  138.6 2.1 %collective-permute-done.12 = f32[32,384]{1,0:T(8,128)S(1)} collective-permute-done((f32[32,384]{1,0:T(8,128)S(1)}, f32[32,384]{1,0:T(8,128)S(1)}, u32[]{:S(2)}, u32[]{:S(2)}) %collective-permute-start.12) | collective-permute-done | bytes 49184 | tf_op jit(solution)/shard_map/ppermute | solution.py:228
  140.8 1.6 collective-permute-start.13
  142.4 2.5 %collective-permute-start.14 = (f32[32,384]{1,0:T(8,128)S(1)}, f32[32,384]{1,0:T(8,128)S(1)}, u32[]{:S(2)}, u32[]{:S(2)}) collective-permute-start(f32[32,384]{1,0:T(8,128)S(1)} %get-tuple-element.55), channel_id=1, source_target_pairs={{0,64},{1,65},{2,66},{3,67},{4,68},{5,69},{6,70},{7,71},{8,72},{9,... | collective-permute-start | bytes 147464 | tf_op jit(solution)/shard_map/ppermute | solution.py:228
  144.9 2.0 %collective-permute-done.14 = f32[32,384]{1,0:T(8,128)S(1)} collective-permute-done((f32[32,384]{1,0:T(8,128)S(1)}, f32[32,384]{1,0:T(8,128)S(1)}, u32[]{:S(2)}, u32[]{:S(2)}) %collective-permute-start.14) | collective-permute-done | bytes 49184 | tf_op jit(solution)/shard_map/ppermute | solution.py:228
  146.9 2.1 %collective-permute-done.15 = f32[32,384]{1,0:T(8,128)S(1)} collective-permute-done((f32[32,384]{1,0:T(8,128)S(1)}, f32[32,384]{1,0:T(8,128)S(1)}, u32[]{:S(2)}, u32[]{:S(2)}) %collective-permute-start.15) | collective-permute-done | bytes 49184 | tf_op jit(solution)/shard_map/ppermute | solution.py:228
  149.1 4.7 %collective-permute-start.16 = (f32[32,256]{1,0:T(8,128)S(1)}, f32[32,256]{1,0:T(8,128)S(1)}, u32[]{:S(2)}, u32[]{:S(2)}) collective-permute-start(f32[32,256]{1,0:T(8,128)S(1)} %slice.50), channel_id=1, source_target_pairs={{0,1},{1,0},{2,3},{3,2},{4,5},{5,4},{6,7},{7,6},{8,9},{9,8},{10,11... | collective-permute-start | bytes 98312 | tf_op jit(solution)/shard_map/ppermute | solution.py:228
  154.4 1.3 copy.65
  (95 shorter events, 20.8 us)
Async XLA Ops:
  0.6 3.5 %copy-start = (bf16[256,32]{0,1:T(8,128)(2,1)S(1)}, bf16[256,32]{0,1:T(8,128)(2,1)}, u32[]{:S(2)}) copy-start(bf16[256,32]{0,1:T(8,128)(2,1)} %param.9) | copy-start | bytes 49156
  0.6 2.1 %copy-start.9 = (bf16[256,32]{0,1:T(8,128)(2,1)S(1)}, bf16[256,32]{0,1:T(8,128)(2,1)}, u32[]{:S(2)}) copy-start(bf16[256,32]{0,1:T(8,128)(2,1)} %param.10) | copy-start | bytes 49156
  2.2 1.9 %copy-start.4 = (bf16[2,1024,256]{1,2,0:T(8,128)(2,1)}, bf16[2,1024,256]{1,2,0:T(8,128)(2,1)S(1)}, u32[]{:S(2)}) copy-start(bf16[2,1024,256]{1,2,0:T(8,128)(2,1)S(1)} %copy.47) | copy-start | bytes 3145732
  10.6 12.0 %copy-start.8 = (bf16[1024,128]{1,0:T(8,128)(2,1)S(1)}, bf16[1024,128]{1,0:T(8,128)(2,1)}, u32[]{:S(2)}) copy-start(bf16[1024,128]{1,0:T(8,128)(2,1)} %param.11) | copy-start | bytes 786436
  10.6 42.1 %all-to-all-start = ((bf16[128,2,4096]{2,1,0:T(2,128)(2,1)}), bf16[128,2,4096]{2,1,0:T(2,128)(2,1)}, u32[]{:S(2)}, u32[]{:S(2)}) async-start(bf16[128,2,4096]{2,1,0:T(2,128)(2,1)} %bitcast.6), calls=%async_computation | async-start | bytes 4194304 | tf_op jit(solution)/shard_map/all_to_all | solution.py:206
  22.6 1.6 %copy-start.7 = (bf16[128,64,128]{2,1,0:T(8,128)(2,1)S(1)}, bf16[128,64,128]{2,1,0:T(8,128)(2,1)}, u32[]{:S(2)}) copy-start(bf16[128,64,128]{2,1,0:T(8,128)(2,1)} %param.13) | copy-start | bytes 6291460
  35.2 1.4 copy-start.1
  55.6 11.3 %collective-permute-start = (bf16[256,2048]{1,0:T(8,128)(2,1)S(1)}, bf16[256,2048]{1,0:T(8,128)(2,1)S(1)}, u32[]{:S(2)}, u32[]{:S(2)}) collective-permute-start(bf16[256,2048]{1,0:T(8,128)(2,1)S(1)} %slice.46), channel_id=1, source_target_pairs={{0,1},{1,0},{2,3},{3,2},{4,5},{5,4},{6,7},{7,6},{8,9},{9,8},{10,11... | collective-permute-start | bytes 3145736 | tf_op jit(solution)/shard_map/ppermute | solution.py:210
  67.0 10.5 %collective-permute-start.1 = (bf16[256,2048]{1,0:T(8,128)(2,1)S(1)}, bf16[256,2048]{1,0:T(8,128)(2,1)S(1)}, u32[]{:S(2)}, u32[]{:S(2)}) collective-permute-start(bf16[256,2048]{1,0:T(8,128)(2,1)S(1)} %slice.37), channel_id=1, source_target_pairs={{0,1},{1,0},{2,3},{3,2},{4,5},{5,4},{6,7},{7,6},{8,9},{9,8},{10,11... | collective-permute-start | bytes 3145736 | tf_op jit(solution)/shard_map/ppermute | solution.py:210
  83.8 5.3 %copy-start.12 = (bf16[128]{0:T(256)(128)(2,1)S(1)}, bf16[128]{0:T(256)(128)(2,1)}, u32[]{:S(2)}) copy-start(bf16[128]{0:T(256)(128)(2,1)} %param.12) | copy-start | bytes 772
  83.8 35.6 %all-to-all-start.1 = ((bf16[128,2,4096]{2,1,0:T(2,128)(2,1)}), bf16[128,2,4096]{2,1,0:T(2,128)(2,1)}, u32[]{:S(2)}, u32[]{:S(2)}) async-start(bf16[128,2,4096]{2,1,0:T(2,128)(2,1)} %reshape.111), calls=%async_computation.1 | async-start | bytes 4194304 | tf_op jit(solution)/shard_map/all_to_all | solution.py:206
  103.9 1.4 copy-start.2
  105.3 0.8 copy-start.3
  106.1 2.5 %collective-permute-start.2 = (f32[64,8,128]{2,1,0:T(8,128)S(1)}, f32[64,8,128]{2,1,0:T(8,128)S(1)}, u32[]{:S(2)}, u32[]{:S(2)}) collective-permute-start(f32[64,8,128]{2,1,0:T(8,128)S(1)} %dynamic-slice_bitcast_fusion), channel_id=1, source_target_pairs={{0,1},{1,0},{2,3},{3,2},{4,5},{5,4},{6,7},{7,6},{8,9},{9,8},{10,11... | collective-permute-start | bytes 786440 | tf_op jit(solution)/shard_map/ppermute | solution.py:228
  109.7 8.2 %collective-permute-start.3 = (f32[16,8,128]{2,1,0:T(8,128)S(1)}, f32[16,8,128]{2,1,0:T(8,128)S(1)}, u32[]{:S(2)}, u32[]{:S(2)}) collective-permute-start(f32[16,8,128]{2,1,0:T(8,128)S(1)} %get-tuple-element.44), channel_id=1, source_target_pairs={{0,2},{1,3},{2,0},{3,1},{4,6},{5,7},{6,4},{7,5},{8,10},{9,11},{10,... | collective-permute-start | bytes 196616 | tf_op jit(solution)/shard_map/ppermute | solution.py:228
  110.2 7.7 %collective-permute-start.4 = (f32[16,8,128]{2,1,0:T(8,128)S(1)}, f32[16,8,128]{2,1,0:T(8,128)S(1)}, u32[]{:S(2)}, u32[]{:S(2)}) collective-permute-start(f32[16,8,128]{2,1,0:T(8,128)S(1)} %get-tuple-element.43), channel_id=1, source_target_pairs={{0,4},{1,5},{2,6},{3,7},{4,0},{5,1},{6,2},{7,3},{8,12},{9,13},{10,... | collective-permute-start | bytes 196616 | tf_op jit(solution)/shard_map/ppermute | solution.py:228
  112.7 5.7 %collective-permute-start.5 = (f32[16,8,128]{2,1,0:T(8,128)S(1)}, f32[16,8,128]{2,1,0:T(8,128)S(1)}, u32[]{:S(2)}, u32[]{:S(2)}) collective-permute-start(f32[16,8,128]{2,1,0:T(8,128)S(1)} %get-tuple-element.42), channel_id=1, source_target_pairs={{0,6},{1,7},{2,4},{3,5},{4,2},{5,3},{6,0},{7,1},{8,14},{9,15},{10,... | collective-permute-start | bytes 196616 | tf_op jit(solution)/shard_map/ppermute | solution.py:228
  118.4 3.8 %copy-start.11 = (bf16[32,256]{1,0:T(8,128)(2,1)S(1)}, bf16[32,256]{1,0:T(8,128)(2,1)}, u32[]{:S(2)}) copy-start(bf16[32,256]{1,0:T(8,128)(2,1)} %constant.145.clone) | copy-start | bytes 49156
  118.4 5.2 %copy-start.10 = (bf16[32,256]{1,0:T(8,128)(2,1)S(1)}, bf16[32,256]{1,0:T(8,128)(2,1)}, u32[]{:S(2)}) copy-start(bf16[32,256]{1,0:T(8,128)(2,1)} %constant.144.clone) | copy-start | bytes 49156
  122.2 1.8 %copy-start.5 = (bf16[2,1024,256]{1,2,0:T(8,128)(2,1)S(1)}, bf16[2,1024,256]{1,2,0:T(8,128)(2,1)}, u32[]{:S(2)}) copy-start(bf16[2,1024,256]{1,2,0:T(8,128)(2,1)} %copy-done.4) | copy-start | bytes 3145732
  124.0 3.5 %copy-start.6 = (bf16[2,1024,32]{2,1,0:T(8,128)(2,1)S(1)}, bf16[2,1024,32]{2,1,0:T(8,128)(2,1)}, u32[]{:S(2)}) copy-start(bf16[2,1024,32]{2,1,0:T(8,128)(2,1)} %reshape.118) | copy-start | bytes 393220
  126.0 2.3 %collective-permute-start.6 = (f32[32,256]{1,0:T(8,128)S(1)}, f32[32,256]{1,0:T(8,128)S(1)}, u32[]{:S(2)}, u32[]{:S(2)}) collective-permute-start(f32[32,256]{1,0:T(8,128)S(1)} %get-tuple-element.64), channel_id=1, source_target_pairs={{0,1},{1,0},{2,3},{3,2},{4,5},{5,4},{6,7},{7,6},{8,9},{9,8},{10,11... | collective-permute-start | bytes 98312 | tf_op jit(solution)/shard_map/ppermute | solution.py:228
  128.3 4.4 %collective-permute-start.8 = (f32[32,256]{1,0:T(8,128)S(1)}, f32[32,256]{1,0:T(8,128)S(1)}, u32[]{:S(2)}, u32[]{:S(2)}) collective-permute-start(f32[32,256]{1,0:T(8,128)S(1)} %select_add_fusion), channel_id=1, source_target_pairs={{0,4},{1,5},{2,6},{3,7},{4,0},{5,1},{6,2},{7,3},{8,12},{9,13},{10,... | collective-permute-start | bytes 98312 | tf_op jit(solution)/shard_map/ppermute | solution.py:228
  128.3 4.4 %collective-permute-start.9 = (f32[32,256]{1,0:T(8,128)S(1)}, f32[32,256]{1,0:T(8,128)S(1)}, u32[]{:S(2)}, u32[]{:S(2)}) collective-permute-start(f32[32,256]{1,0:T(8,128)S(1)} %select_add_fusion), channel_id=1, source_target_pairs={{0,6},{1,7},{2,4},{3,5},{4,2},{5,3},{6,0},{7,1},{8,14},{9,15},{10,... | collective-permute-start | bytes 98312 | tf_op jit(solution)/shard_map/ppermute | solution.py:228
  131.0 2.9 %collective-permute-start.7 = (f32[32,256]{1,0:T(8,128)S(1)}, f32[32,256]{1,0:T(8,128)S(1)}, u32[]{:S(2)}, u32[]{:S(2)}) collective-permute-start(f32[32,256]{1,0:T(8,128)S(1)} %select_add_fusion), channel_id=1, source_target_pairs={{0,2},{1,3},{2,0},{3,1},{4,6},{5,7},{6,4},{7,5},{8,10},{9,11},{10,... | collective-permute-start | bytes 98312 | tf_op jit(solution)/shard_map/ppermute | solution.py:228
  134.0 4.6 %collective-permute-start.10 = (f32[32,384]{1,0:T(8,128)S(1)}, f32[32,384]{1,0:T(8,128)S(1)}, u32[]{:S(2)}, u32[]{:S(2)}) collective-permute-start(f32[32,384]{1,0:T(8,128)S(1)} %get-tuple-element.57), channel_id=1, source_target_pairs={{0,8},{1,9},{2,10},{3,11},{4,12},{5,13},{6,14},{7,15},{8,0},{9,1},... | collective-permute-start | bytes 147464 | tf_op jit(solution)/shard_map/ppermute | solution.py:228
  134.0 4.6 %collective-permute-start.11 = (f32[32,384]{1,0:T(8,128)S(1)}, f32[32,384]{1,0:T(8,128)S(1)}, u32[]{:S(2)}, u32[]{:S(2)}) collective-permute-start(f32[32,384]{1,0:T(8,128)S(1)} %get-tuple-element.58), channel_id=1, source_target_pairs={{0,16},{1,17},{2,18},{3,19},{4,20},{5,21},{6,22},{7,23},{8,24},{9,... | collective-permute-start | bytes 147464 | tf_op jit(solution)/shard_map/ppermute | solution.py:228
  136.3 4.4 %collective-permute-start.12 = (f32[32,384]{1,0:T(8,128)S(1)}, f32[32,384]{1,0:T(8,128)S(1)}, u32[]{:S(2)}, u32[]{:S(2)}) collective-permute-start(f32[32,384]{1,0:T(8,128)S(1)} %get-tuple-element.56), channel_id=1, source_target_pairs={{0,24},{1,25},{2,26},{3,27},{4,28},{5,29},{6,30},{7,31},{8,16},{9,... | collective-permute-start | bytes 147464 | tf_op jit(solution)/shard_map/ppermute | solution.py:228
  140.8 4.1 %collective-permute-start.13 = (f32[32,384]{1,0:T(8,128)S(1)}, f32[32,384]{1,0:T(8,128)S(1)}, u32[]{:S(2)}, u32[]{:S(2)}) collective-permute-start(f32[32,384]{1,0:T(8,128)S(1)} %get-tuple-element.54), channel_id=1, source_target_pairs={{0,32},{1,33},{2,34},{3,35},{4,36},{5,37},{6,38},{7,39},{8,40},{9,... | collective-permute-start | bytes 147464 | tf_op jit(solution)/shard_map/ppermute | solution.py:228
  142.4 4.5 %collective-permute-start.14 = (f32[32,384]{1,0:T(8,128)S(1)}, f32[32,384]{1,0:T(8,128)S(1)}, u32[]{:S(2)}, u32[]{:S(2)}) collective-permute-start(f32[32,384]{1,0:T(8,128)S(1)} %get-tuple-element.55), channel_id=1, source_target_pairs={{0,64},{1,65},{2,66},{3,67},{4,68},{5,69},{6,70},{7,71},{8,72},{9,... | collective-permute-start | bytes 147464 | tf_op jit(solution)/shard_map/ppermute | solution.py:228
  144.9 4.2 %collective-permute-start.15 = (f32[32,384]{1,0:T(8,128)S(1)}, f32[32,384]{1,0:T(8,128)S(1)}, u32[]{:S(2)}, u32[]{:S(2)}) collective-permute-start(f32[32,384]{1,0:T(8,128)S(1)} %get-tuple-element.53), channel_id=1, source_target_pairs={{0,96},{1,97},{2,98},{3,99},{4,100},{5,101},{6,102},{7,103},{8,104... | collective-permute-start | bytes 147464 | tf_op jit(solution)/shard_map/ppermute | solution.py:228
  149.1 7.2 %collective-permute-start.16 = (f32[32,256]{1,0:T(8,128)S(1)}, f32[32,256]{1,0:T(8,128)S(1)}, u32[]{:S(2)}, u32[]{:S(2)}) collective-permute-start(f32[32,256]{1,0:T(8,128)S(1)} %slice.50), channel_id=1, source_target_pairs={{0,1},{1,0},{2,3},{3,2},{4,5},{5,4},{6,7},{7,6},{8,9},{9,8},{10,11... | collective-permute-start | bytes 98312 | tf_op jit(solution)/shard_map/ppermute | solution.py:228

commit v4 on v3

--- a/solution.py
+++ b/solution.py
@@ -11,7 +11,6 @@
 BOTH = ("row", "col")
 TILE = 16
 GRAD_TILE = 8
-STREAMS = 4
 CORES = 2
 VMEM_BYTES = 48 * 1024 * 1024
 NT = (((1,), (1,)), ((), ()))
@@ -44,28 +43,40 @@
                 ]
 
 
-def left_kernel(inverse, right_ref, *refs):
-    grad_refs, out_ref = refs[:-1], refs[-1]
-    depth = grad_refs[0].shape[0]
-    grads = 0.0
-    for k, grad_ref in enumerate(grad_refs):
-        grads += jnp.dot(
-            right_ref[:, k * depth:(k + 1) * depth], grad_ref[...], preferred_element_type=jnp.float32
-        )
+def left_kernel(inverse, right_ref, own_ref, grad_ref, out_ref, partial_ref):
+    step = pl.program_id(0)
+    grads = jnp.dot(right_ref[...], grad_ref[...], preferred_element_type=jnp.float32)
     out_ref[...] = (grads * inverse).astype(out_ref.dtype)
 
-
-def right_kernel(inverse, own_ref, other_ref, *refs):
-    grad_refs, out_ref = refs[:-1], refs[-1]
-    depth = grad_refs[0].shape[1]
-    each = own_ref.shape[1] // depth
-    grads = 0.0
-    for k, grad_ref in enumerate(grad_refs):
-        half_ref, first = (own_ref, k) if k < each else (other_ref, k - each)
-        grads += lax.dot_general(
-            half_ref[:, first * depth:(first + 1) * depth], grad_ref[...], NT, preferred_element_type=jnp.float32
-        )
-    out_ref[...] = (grads * inverse).astype(out_ref.dtype)
+    @pl.when(step == 0)
+    def _():
+        partial_ref[...] = lax.dot_general(own_ref[...], grad_ref[...], NT, preferred_element_type=jnp.float32)
+
+    @pl.when((step > 0) & (step < pl.num_programs(0) // CORES))
+    def _():
+        partial_ref[...] += lax.dot_general(own_ref[...], grad_ref[...], NT, preferred_element_type=jnp.float32)
+
+
+def right_kernel(inverse, other_ref, partial_ref, grad_ref, out_ref):
+    grads = lax.dot_general(other_ref[...], grad_ref[...], NT, preferred_element_type=jnp.float32)
+    out_ref[...] = ((partial_ref[...] + grads) * inverse).astype(out_ref.dtype)
+
+
+def pack_kernel(left_ref, right_ref, out_ref, sems):
+    rows, chips = out_ref.shape[:2]
+    panel = left_ref.shape[-1]
+    copies = [
+        pltpu.make_async_copy(right_ref, out_ref.at[k, :, :, :, pl.ds(panel, right_ref.shape[-1])], sems.at[k])
+        for k in range(rows)
+    ]
+    copies += [
+        pltpu.make_async_copy(left_ref, out_ref.at[:, k, :, :, pl.ds(0, panel)], sems.at[rows + k])
+        for k in range(chips)
+    ]
+    for copy in copies:
+        copy.start()
+    for copy in copies:
+        copy.wait()
 
 
 def forward_kernel(
@@ -133,41 +144,60 @@
 def left_grads(came, grads, interpret=False):
     seqs, (depth, columns) = came.shape[0], grads.shape
     block = 512
+    own = columns // CORES // block
     last = came.shape[1] // depth - 1
     return pl.pallas_call(
         functools.partial(left_kernel, 1.0 / seqs),
         grid=(columns // block,),
         in_specs=[
             pl.BlockSpec((seqs, depth), lambda n: (0, last)),
-            *[pl.BlockSpec((depth // STREAMS, block), lambda n, k=k: (k, n)) for k in range(STREAMS)],
-        ],
-        out_specs=pl.BlockSpec((seqs, block), lambda n: (0, n)),
-        out_shape=jax.ShapeDtypeStruct((seqs, columns), jnp.bfloat16),
+            pl.BlockSpec((seqs, block), lambda n: (0, jnp.minimum(n, own - 1))),
+            pl.BlockSpec((depth, block), lambda n: (0, n)),
+        ],
+        out_specs=[pl.BlockSpec((seqs, block), lambda n: (0, n)), whole((seqs, depth))],
+        out_shape=[
+            jax.ShapeDtypeStruct((seqs, columns), jnp.bfloat16),
+            jax.ShapeDtypeStruct((seqs, depth), jnp.float32),
+        ],
         compiler_params=params(),
-        cost_estimate=pl.CostEstimate(flops=2 * seqs * depth * columns, bytes_accessed=19 * 2**20, transcendentals=0),
+        cost_estimate=pl.CostEstimate(flops=3 * seqs * depth * columns, bytes_accessed=21 * 2**20, transcendentals=0),
         interpret=interpret,
         name="left_grads",
-    )(came, *[grads] * STREAMS)
-
-
-def right_grads(came, other, grads, interpret=False):
-    seqs, (rows, depth) = came.shape[0], grads.shape
+    )(came, came, grads)
+
+
+def right_grads(other, partial, grads, interpret=False):
+    seqs, (rows, depth) = other.shape[0], grads.shape
     block = 256
     return pl.pallas_call(
         functools.partial(right_kernel, 1.0 / seqs),
         grid=(rows // block,),
         in_specs=[
-            pl.BlockSpec((seqs, depth // 2), lambda n: (0, 0)),
-            whole((seqs, depth // 2)),
-            *[pl.BlockSpec((block, depth // STREAMS), lambda n, k=k: (n, k)) for k in range(STREAMS)],
+            whole(other.shape),
+            pl.BlockSpec((seqs, block), lambda n: (0, n)),
+            pl.BlockSpec((block, depth // CORES), lambda n: (n, 1)),
         ],
         out_specs=pl.BlockSpec((seqs, block), lambda n: (0, n)),
         out_shape=jax.ShapeDtypeStruct((seqs, rows), jnp.bfloat16),
         compiler_params=params(),
-        cost_estimate=pl.CostEstimate(flops=2 * seqs * depth * rows, bytes_accessed=19 * 2**20, transcendentals=0),
+        cost_estimate=pl.CostEstimate(flops=seqs * depth * rows, bytes_accessed=12 * 2**20, transcendentals=0),
         interpret=interpret,
         name="right_grads",
-    )(came, other, *[grads] * STREAMS)
+    )(other, partial, grads)
+
+
+def pack(left, right, interpret=False):
+    shape = (left.shape[0],) + right.shape[:-1] + (left.shape[-1] + right.shape[-1],)
+    return pl.pallas_call(
+        pack_kernel,
+        in_specs=[pl.BlockSpec(memory_space=pltpu.VMEM)] * 2,
+        out_specs=pl.BlockSpec(memory_space=pl.ANY),
+        out_shape=jax.ShapeDtypeStruct(shape, left.dtype),
+        scratch_shapes=[pltpu.SemaphoreType.DMA((shape[0] + shape[1],))],
+        cost_estimate=pl.CostEstimate(flops=0, bytes_accessed=2 * 2**20, transcendentals=0),
+        interpret=interpret,
+        name="pack",
+    )(left, right)
 
 
 def forward(core, came, other, weight_t, bias, cot, width, interpret=False):
@@ -290,12 +320,9 @@
     core = lax.axis_index("col") % CORES
     panel = row_block * width // CORES
     left_out = left.reshape(local, CORES, width // CORES, row_count, row_block).transpose(3, 1, 0, 2, 4)
-    left_out = left_out.reshape(row_count, 1, CORES, local, panel)
-    right_out = right.reshape(local, chips, CORES, col_block * width).transpose(1, 2, 0, 3)[None]
-    shape = (row_count, chips, CORES, local)
-    sent = jnp.concatenate(
-        [jnp.broadcast_to(left_out, shape + (panel,)), jnp.broadcast_to(right_out, shape + right_out.shape[4:])], axis=4
-    )
+    left_out = left_out.reshape(row_count, CORES, local, panel)
+    right_out = right.reshape(local, chips, CORES, col_block * width).transpose(1, 2, 0, 3)
+    sent = pack(left_out, right_out)
     columns = sent.shape[4]
     cot = pair_cotangent.transpose(1, 0, 2)
     bias = out_bias.astype(jnp.float32).reshape(1, pair_width)
@@ -304,10 +331,10 @@
     came, outer_grad = lax.optimization_barrier((came, outer_grads(weight, cot, width)))
     came = came.reshape(seqs, columns)
     left_other = swap_cores(came[:, :panel])
-    left_part = left_grads(came, outer_grad)
+    left_part, right_partial = left_grads(came, outer_grad)
     left_other, left_part = lax.optimization_barrier((left_other, left_part))
     left_share = swap_cores(left_part[:, panel:])
-    right_part = right_grads(came, left_other, outer_grad)
+    right_part = right_grads(left_other, right_partial, outer_grad)
     left_pair = (left_part[:, :panel].astype(jnp.float32) + left_share.astype(jnp.float32)).astype(jnp.bfloat16)
     sent = jnp.concatenate([left_pair, right_part], axis=1).reshape(devices, local, columns)
     sent, left_other = lax.optimization_barrier((sent, left_other))

time: 158 us -> 153 us (0.968)
  other arithmetic: 8.64 us -> 3.4 us
  local copies, waits for them, and re-layouts: 28.6 us -> 25.3 us
  Pallas kernels: 45 us -> 47.3 us
    concatenate x1 -> x0, other arithmetic: 3.84 us -> none  [body(): jnp.concatenate([jnp.broadcast_to(left_out, shape + (panel,)), jnp.broadc...]
    pallas_call x1, Pallas kernels: 10.4 us -> 7.68 us  [right_grads(): pl.pallas_call(functools.partial(right_kernel, 1.0 / seqs), grid=(rows //...]
    pallas_call x1, Pallas kernels: 10.3 us -> 12.9 us  [left_grads(): pl.pallas_call(functools.partial(left_kernel, 1.0 / seqs), grid=(columns...]
    pallas_call x0 -> x1, Pallas kernels: none -> 2.4 us  [pack(): pl.pallas_call(pack_kernel, in_specs=[pl.BlockSpec(memory_space=pltpu.VME...]
    broadcast_in_dim x4 -> x0, local copies, waits for them, and re-layouts: 2.21 us -> none  [the longest x3 1.2 us: body(): jnp.broadcast_to(left_out, shape + (panel,))]
    reshape x1, local copies, waits for them, and re-layouts: 4.39 us -> 2.65 us  [body(): jnp.concatenate([left_pair, right_part], axis=1)]
    unnamed x32 -> x34, local copies, waits for them, and re-layouts: 13.3 us -> 12.6 us
  transfers between devices with their start and end apart: 19 -> 19, of which waited for: 10 -> 10; matrix products, arithmetic and copies ran while one was open for 7% -> 8% of each run, Pallas kernels for 29% -> 30%
where the time goes in v4:
time: 153 us; the launch traced here: 152 us
  Pallas kernels  47.3 us (31%)
  starting transfers between devices  41.1 us (27%)
  waiting for transfers between devices  29.2 us (19%)
  local copies, waits for them, and re-layouts  25.3 us (17%)
  matrix products  4.41 us (3%)
  other arithmetic  3.4 us (2%)
    ppermute x15, starting transfers between devices, partner(): lax.ppermute(part, BOTH, [(i, i ^ mask) for i in range(lax.axis_size(BOTH...  22 us
    all_to_all x2, waiting for transfers between devices, exchange(): return lax.all_to_all(blocks, BOTH, 0, 0, tiled=True)  18.1 us
    all_to_all x2, starting transfers between devices, exchange(): return lax.all_to_all(blocks, BOTH, 0, 0, tiled=True)  17 us
    pallas_call x1, Pallas kernels, forward(): pl.pallas_call(functools.partial(forward_kernel, 1.0 / seqs, width), grid...  14.7 us
    pallas_call x1, Pallas kernels, left_grads(): pl.pallas_call(functools.partial(left_kernel, 1.0 / seqs), grid=(columns...  12.9 us
    unnamed x34, local copies, waits for them, and re-layouts  12.6 us
    ppermute x15, waiting for transfers between devices, partner(): lax.ppermute(part, BOTH, [(i, i ^ mask) for i in range(lax.axis_size(BOTH...  11 us
    pallas_call x1, Pallas kernels, outer_grads(): pl.pallas_call(functools.partial(outer_grad_kernel, width), grid=(cols //...  9.63 us
  transfers between devices with their start and end apart: 19, of which 10 were waited for; matrix products, arithmetic and copies ran while one was open for 8% of the time, Pallas kernels for 30%

profile of v4, /device:TPU:1, one launch (start us, length us, event | category | flops | bytes accessed | tf_op | source)
XLA Modules:
  0.0 151.8 jit_solution(12608046382441448503)
XLA Ops:
  0.6 1.5 copy.47
  5.8 2.4 %pack.1 = bf16[8,8,2,2,4096]{4,3,2,1,0:T(2,128)(2,1)} custom-call(bf16[8,2,2,2048]{3,2,1,0:T(2,128)(2,1)} %reshape.108.left_ref, bf16[8,2,2,2048]{3,2,1,0:T(2,128)(2,1)} %bitcast.110), custom_call_target="tpu_custom_call" | custom-call | bytes 2097152 | tf_op jit(solution)/shard_map/pack/pallas_call | solution.py:191
  8.3 12.0 %all-to-all-start = ((bf16[128,2,4096]{2,1,0:T(2,128)(2,1)}), bf16[128,2,4096]{2,1,0:T(2,128)(2,1)}, u32[]{:S(2)}, u32[]{:S(2)}) async-start(bf16[128,2,4096]{2,1,0:T(2,128)(2,1)} %bitcast.107), calls=%async_computation | async-start | bytes 4194304 | tf_op jit(solution)/shard_map/all_to_all | solution.py:236
  20.7 2.9 %copy.86 = bf16[128,64,128]{2,0,1:T(8,128)(2,1)S(1)} copy(bf16[128,64,128]{2,1,0:T(8,128)(2,1)} %param.13) | data formatting | bytes 4194304 | tf_op args[5]
  23.6 9.6 %outer_grads.1.grad_ref = bf16[2048,4096]{1,0:T(8,128)(2,1)} custom-call(bf16[1024,128]{1,0:T(8,128)(2,1)S(1)} %copy.57.weight_ref, bf16[64,128,128]{2,1,0:T(8,128)(2,1)S(1)} %bitcast.101), custom_call_target="tpu_custom_call" | custom-call | flops 2147483648 | bytes 18874368 | tf_op jit(solution)/shard_map/outer_grads/pallas_call | solution.py:129
  33.3 17.1 %all-to-all-done = bf16[128,2,4096]{2,1,0:T(2,128)(2,1)} async-done(((bf16[128,2,4096]{2,1,0:T(2,128)(2,1)}), bf16[128,2,4096]{2,1,0:T(2,128)(2,1)}, u32[]{:S(2)}, u32[]{:S(2)}) %all-to-all-start) | async-done | bytes 2097184 | tf_op jit(solution)/shard_map/all_to_all | solution.py:236
  50.4 2.7 %reshape.111.right_ref.own_ref = bf16[256,4096]{1,0:T(8,128)(2,1)S(1)} reshape(bf16[128,2,4096]{2,1,0:T(2,128)(2,1)} %all-to-all-done) | data formatting | bytes 4194304 | tf_op jit(solution)/shard_map/reshape | solution.py:332
  54.5 12.9 %left_grads.1 = (bf16[256,4096]{1,0:T(8,128)(2,1)S(1)}, f32[256,2048]{1,0:T(8,128)S(1)}) custom-call(bf16[256,4096]{1,0:T(8,128)(2,1)} %copy-done.2, bf16[256,4096]{1,0:T(8,128)(2,1)} %copy-done.2, bf16[2048,4096]{1,0:T(8,128)(2,1)} %outer_grads.1.grad_ref), custom_call_target="tpu_custom_call" | custom-call | flops 6442450944 | bytes 22020096 | tf_op jit(solution)/shard_map/left_grads/pallas_call | solution.py:149
  68.5 7.7 %right_grads.1 = bf16[256,2048]{1,0:T(8,128)(2,1)S(1)} custom-call(bf16[256,2048]{1,0:T(8,128)(2,1)S(1)} %collective-permute-done.other_ref, f32[256,2048]{1,0:T(8,128)S(1)} %get-tuple-element.22.partial_ref, bf16[2048,4096]{1,0:T(8,128)(2,1)} %outer_grads.1.grad_ref), custom_call_target="tpu_custom_call" | custom-call | flops 2147483648 | bytes 12582912 | tf_op jit(solution)/shard_map/right_grads/pallas_call | solution.py:172
  76.7 2.7 %reshape.112 = bf16[128,2,4096]{2,1,0:T(2,128)(2,1)} reshape(bf16[256,4096]{1,0:T(8,128)(2,1)S(1)} %pad_maximum_fusion) | data formatting | bytes 4194304 | tf_op jit(solution)/shard_map/reshape | solution.py:339
  79.4 5.0 %all-to-all-start.1 = ((bf16[128,2,4096]{2,1,0:T(2,128)(2,1)}), bf16[128,2,4096]{2,1,0:T(2,128)(2,1)}, u32[]{:S(2)}, u32[]{:S(2)}) async-start(bf16[128,2,4096]{2,1,0:T(2,128)(2,1)} %reshape.112), calls=%async_computation.1 | async-start | bytes 4194304 | tf_op jit(solution)/shard_map/all_to_all | solution.py:236
  84.5 14.7 %forward.1 = (bf16[64,128,128]{2,1,0:T(8,128)(2,1)S(1)}, f32[1024,128]{1,0:T(8,128)S(1)}) custom-call(s32[1]{0:T(128)} %bitcast.core_ref, bf16[256,4096]{1,0:T(8,128)(2,1)S(1)} %copy-done.3, bf16[256,2048]{1,0:T(8,128)(2,1)S(1)} %collective-permute-done.other_ref, bf16[256,4096]{1,0:T(8,128)(2,1)S(1)} %copy-done.3, bf16[128,1024]{1,0:T(8,128)(2,1)S(1)} %bitcast.104, ...), custom_call_target="tpu_custom_call" | custom-call | flops 8589934592 | bytes 8388608 | tf_op jit(solution)/shard_map/forward/pallas_call | solution.py:207
  99.2 1.4 copy-done.4
  101.4 1.2 collective-permute-start.2
  102.6 1.2 collective-permute-done.2
  105.2 2.4 %collective-permute-start.4 = (f32[16,8,128]{2,1,0:T(8,128)S(1)}, f32[16,8,128]{2,1,0:T(8,128)S(1)}, u32[]{:S(2)}, u32[]{:S(2)}) collective-permute-start(f32[16,8,128]{2,1,0:T(8,128)S(1)} %get-tuple-element.47), channel_id=1, source_target_pairs={{0,4},{1,5},{2,6},{3,7},{4,0},{5,1},{6,2},{7,3},{8,12},{9,13},{10,... | collective-permute-start | bytes 196616 | tf_op jit(solution)/shard_map/ppermute | solution.py:258
  108.7 4.3 %copy.63 = bf16[128,64,128]{2,1,0:T(8,128)(2,1)} copy(bf16[128,64,128]{2,0,1:T(8,128)(2,1)} %bitcast.103) | data formatting | bytes 4194304
  114.4 2.7 %reshape.115 = bf16[256,4096]{1,0:T(8,128)(2,1)S(1)} reshape(bf16[128,2,4096]{2,1,0:T(2,128)(2,1)} %all-to-all-done.1) | data formatting | bytes 4194304 | tf_op jit(solution)/shard_map/reshape | solution.py:341
  119.4 1.5 broadcast_select_fusion
  120.9 1.5 collective-permute-start.6
  123.2 2.7 %collective-permute-start.9 = (f32[32,256]{1,0:T(8,128)S(1)}, f32[32,256]{1,0:T(8,128)S(1)}, u32[]{:S(2)}, u32[]{:S(2)}) collective-permute-start(f32[32,256]{1,0:T(8,128)S(1)} %select_add_fusion), channel_id=1, source_target_pairs={{0,6},{1,7},{2,4},{3,5},{4,2},{5,3},{6,0},{7,1},{8,14},{9,15},{10,... | collective-permute-start | bytes 98312 | tf_op jit(solution)/shard_map/ppermute | solution.py:258
  125.9 1.7 %collective-permute-done.8 = f32[32,256]{1,0:T(8,128)S(1)} collective-permute-done((f32[32,256]{1,0:T(8,128)S(1)}, f32[32,256]{1,0:T(8,128)S(1)}, u32[]{:S(2)}, u32[]{:S(2)}) %collective-permute-start.8) | collective-permute-done | bytes 32800 | tf_op jit(solution)/shard_map/ppermute | solution.py:258
  127.7 1.2 collective-permute-done.7
  129.0 2.2 %collective-permute-start.11 = (f32[32,384]{1,0:T(8,128)S(1)}, f32[32,384]{1,0:T(8,128)S(1)}, u32[]{:S(2)}, u32[]{:S(2)}) collective-permute-start(f32[32,384]{1,0:T(8,128)S(1)} %get-tuple-element.62), channel_id=1, source_target_pairs={{0,16},{1,17},{2,18},{3,19},{4,20},{5,21},{6,22},{7,23},{8,24},{9,... | collective-permute-start | bytes 147464 | tf_op jit(solution)/shard_map/ppermute | solution.py:258
  131.2 1.6 %collective-permute-start.12 = (f32[32,384]{1,0:T(8,128)S(1)}, f32[32,384]{1,0:T(8,128)S(1)}, u32[]{:S(2)}, u32[]{:S(2)}) collective-permute-start(f32[32,384]{1,0:T(8,128)S(1)} %get-tuple-element.60), channel_id=1, source_target_pairs={{0,24},{1,25},{2,26},{3,27},{4,28},{5,29},{6,30},{7,31},{8,16},{9,... | collective-permute-start | bytes 147464 | tf_op jit(solution)/shard_map/ppermute | solution.py:258
  133.5 2.1 %collective-permute-done.12 = f32[32,384]{1,0:T(8,128)S(1)} collective-permute-done((f32[32,384]{1,0:T(8,128)S(1)}, f32[32,384]{1,0:T(8,128)S(1)}, u32[]{:S(2)}, u32[]{:S(2)}) %collective-permute-start.12) | collective-permute-done | bytes 49184 | tf_op jit(solution)/shard_map/ppermute | solution.py:258
  135.7 1.5 %collective-permute-start.13 = (f32[32,384]{1,0:T(8,128)S(1)}, f32[32,384]{1,0:T(8,128)S(1)}, u32[]{:S(2)}, u32[]{:S(2)}) collective-permute-start(f32[32,384]{1,0:T(8,128)S(1)} %get-tuple-element.58), channel_id=1, source_target_pairs={{0,32},{1,33},{2,34},{3,35},{4,36},{5,37},{6,38},{7,39},{8,40},{9,... | collective-permute-start | bytes 147464 | tf_op jit(solution)/shard_map/ppermute | solution.py:258
  137.3 2.5 %collective-permute-start.14 = (f32[32,384]{1,0:T(8,128)S(1)}, f32[32,384]{1,0:T(8,128)S(1)}, u32[]{:S(2)}, u32[]{:S(2)}) collective-permute-start(f32[32,384]{1,0:T(8,128)S(1)} %get-tuple-element.59), channel_id=1, source_target_pairs={{0,64},{1,65},{2,66},{3,67},{4,68},{5,69},{6,70},{7,71},{8,72},{9,... | collective-permute-start | bytes 147464 | tf_op jit(solution)/shard_map/ppermute | solution.py:258
  139.8 2.0 %collective-permute-done.14 = f32[32,384]{1,0:T(8,128)S(1)} collective-permute-done((f32[32,384]{1,0:T(8,128)S(1)}, f32[32,384]{1,0:T(8,128)S(1)}, u32[]{:S(2)}, u32[]{:S(2)}) %collective-permute-start.14) | collective-permute-done | bytes 49184 | tf_op jit(solution)/shard_map/ppermute | solution.py:258
  141.8 2.1 %collective-permute-done.15 = f32[32,384]{1,0:T(8,128)S(1)} collective-permute-done((f32[32,384]{1,0:T(8,128)S(1)}, f32[32,384]{1,0:T(8,128)S(1)}, u32[]{:S(2)}, u32[]{:S(2)}) %collective-permute-start.15) | collective-permute-done | bytes 49184 | tf_op jit(solution)/shard_map/ppermute | solution.py:258
  144.0 4.7 %collective-permute-start.16 = (f32[32,256]{1,0:T(8,128)S(1)}, f32[32,256]{1,0:T(8,128)S(1)}, u32[]{:S(2)}, u32[]{:S(2)}) collective-permute-start(f32[32,256]{1,0:T(8,128)S(1)} %slice.50), channel_id=1, source_target_pairs={{0,1},{1,0},{2,3},{3,2},{4,5},{5,4},{6,7},{7,6},{8,9},{9,8},{10,11... | collective-permute-start | bytes 98312 | tf_op jit(solution)/shard_map/ppermute | solution.py:258
  149.3 1.3 copy.64
  (94 shorter events, 17.5 us)
Async XLA Ops:
  0.6 2.1 %copy-start = (bf16[256,32]{0,1:T(8,128)(2,1)S(1)}, bf16[256,32]{0,1:T(8,128)(2,1)}, u32[]{:S(2)}) copy-start(bf16[256,32]{0,1:T(8,128)(2,1)} %param.9) | copy-start | bytes 49156
  2.1 1.7 %copy-start.6 = (bf16[2,1024,256]{1,2,0:T(8,128)(2,1)}, bf16[2,1024,256]{1,2,0:T(8,128)(2,1)S(1)}, u32[]{:S(2)}) copy-start(bf16[2,1024,256]{1,2,0:T(8,128)(2,1)S(1)} %copy.47) | copy-start | bytes 3145732
  2.2 1.7 %copy-start.10 = (bf16[256,32]{0,1:T(8,128)(2,1)S(1)}, bf16[256,32]{0,1:T(8,128)(2,1)}, u32[]{:S(2)}) copy-start(bf16[256,32]{0,1:T(8,128)(2,1)} %param.10) | copy-start | bytes 49156
  8.2 12.0 %copy-start.9 = (bf16[1024,128]{1,0:T(8,128)(2,1)S(1)}, bf16[1024,128]{1,0:T(8,128)(2,1)}, u32[]{:S(2)}) copy-start(bf16[1024,128]{1,0:T(8,128)(2,1)} %param.11) | copy-start | bytes 786436
  8.3 42.1 %all-to-all-start = ((bf16[128,2,4096]{2,1,0:T(2,128)(2,1)}), bf16[128,2,4096]{2,1,0:T(2,128)(2,1)}, u32[]{:S(2)}, u32[]{:S(2)}) async-start(bf16[128,2,4096]{2,1,0:T(2,128)(2,1)} %bitcast.107), calls=%async_computation | async-start | bytes 4194304 | tf_op jit(solution)/shard_map/all_to_all | solution.py:236
  23.6 9.6 %copy-start.1 = (bf16[128,64,128]{2,0,1:T(8,128)(2,1)}, bf16[128,64,128]{2,0,1:T(8,128)(2,1)S(1)}, u32[]{:S(2)}) copy-start(bf16[128,64,128]{2,0,1:T(8,128)(2,1)S(1)} %copy.86) | copy-start | bytes 6291460
  53.1 1.3 copy-start.2
  53.2 14.1 %collective-permute-start = (bf16[256,2048]{1,0:T(8,128)(2,1)S(1)}, bf16[256,2048]{1,0:T(8,128)(2,1)S(1)}, u32[]{:S(2)}, u32[]{:S(2)}) collective-permute-start(bf16[256,2048]{1,0:T(8,128)(2,1)S(1)} %slice.46), channel_id=1, source_target_pairs={{0,1},{1,0},{2,3},{3,2},{4,5},{5,4},{6,7},{7,6},{8,9},{9,8},{10,11... | collective-permute-start | bytes 3145736 | tf_op jit(solution)/shard_map/ppermute | solution.py:240
  67.5 8.7 %collective-permute-start.1 = (bf16[256,2048]{1,0:T(8,128)(2,1)S(1)}, bf16[256,2048]{1,0:T(8,128)(2,1)S(1)}, u32[]{:S(2)}, u32[]{:S(2)}) collective-permute-start(bf16[256,2048]{1,0:T(8,128)(2,1)S(1)} %slice.37), channel_id=1, source_target_pairs={{0,1},{1,0},{2,3},{3,2},{4,5},{5,4},{6,7},{7,6},{8,9},{9,8},{10,11... | collective-permute-start | bytes 3145736 | tf_op jit(solution)/shard_map/ppermute | solution.py:240
  79.4 5.1 %copy-start.13 = (bf16[128]{0:T(256)(128)(2,1)S(1)}, bf16[128]{0:T(256)(128)(2,1)}, u32[]{:S(2)}) copy-start(bf16[128]{0:T(256)(128)(2,1)} %param.12) | copy-start | bytes 772
  79.4 5.1 %copy-start.3 = (bf16[256,4096]{1,0:T(8,128)(2,1)S(1)}, bf16[256,4096]{1,0:T(8,128)(2,1)}, u32[]{:S(2)}) copy-start(bf16[256,4096]{1,0:T(8,128)(2,1)} %copy-done.2) | copy-start | bytes 6291460
  79.4 35.0 %all-to-all-start.1 = ((bf16[128,2,4096]{2,1,0:T(2,128)(2,1)}), bf16[128,2,4096]{2,1,0:T(2,128)(2,1)}, u32[]{:S(2)}, u32[]{:S(2)}) async-start(bf16[128,2,4096]{2,1,0:T(2,128)(2,1)} %reshape.112), calls=%async_computation.1 | async-start | bytes 4194304 | tf_op jit(solution)/shard_map/all_to_all | solution.py:236
  99.2 1.4 copy-start.4
  101.4 2.3 %collective-permute-start.2 = (f32[64,8,128]{2,1,0:T(8,128)S(1)}, f32[64,8,128]{2,1,0:T(8,128)S(1)}, u32[]{:S(2)}, u32[]{:S(2)}) collective-permute-start(f32[64,8,128]{2,1,0:T(8,128)S(1)} %dynamic-slice_bitcast_fusion), channel_id=1, source_target_pairs={{0,1},{1,0},{2,3},{3,2},{4,5},{5,4},{6,7},{7,6},{8,9},{9,8},{10,11... | collective-permute-start | bytes 786440 | tf_op jit(solution)/shard_map/ppermute | solution.py:258
  104.8 8.2 %collective-permute-start.3 = (f32[16,8,128]{2,1,0:T(8,128)S(1)}, f32[16,8,128]{2,1,0:T(8,128)S(1)}, u32[]{:S(2)}, u32[]{:S(2)}) collective-permute-start(f32[16,8,128]{2,1,0:T(8,128)S(1)} %get-tuple-element.48), channel_id=1, source_target_pairs={{0,2},{1,3},{2,0},{3,1},{4,6},{5,7},{6,4},{7,5},{8,10},{9,11},{10,... | collective-permute-start | bytes 196616 | tf_op jit(solution)/shard_map/ppermute | solution.py:258
  105.2 7.8 %collective-permute-start.4 = (f32[16,8,128]{2,1,0:T(8,128)S(1)}, f32[16,8,128]{2,1,0:T(8,128)S(1)}, u32[]{:S(2)}, u32[]{:S(2)}) collective-permute-start(f32[16,8,128]{2,1,0:T(8,128)S(1)} %get-tuple-element.47), channel_id=1, source_target_pairs={{0,4},{1,5},{2,6},{3,7},{4,0},{5,1},{6,2},{7,3},{8,12},{9,13},{10,... | collective-permute-start | bytes 196616 | tf_op jit(solution)/shard_map/ppermute | solution.py:258
  107.6 5.7 %collective-permute-start.5 = (f32[16,8,128]{2,1,0:T(8,128)S(1)}, f32[16,8,128]{2,1,0:T(8,128)S(1)}, u32[]{:S(2)}, u32[]{:S(2)}) collective-permute-start(f32[16,8,128]{2,1,0:T(8,128)S(1)} %get-tuple-element.46), channel_id=1, source_target_pairs={{0,6},{1,7},{2,4},{3,5},{4,2},{5,3},{6,0},{7,1},{8,14},{9,15},{10,... | collective-permute-start | bytes 196616 | tf_op jit(solution)/shard_map/ppermute | solution.py:258
  113.3 3.8 %copy-start.12 = (bf16[32,256]{1,0:T(8,128)(2,1)S(1)}, bf16[32,256]{1,0:T(8,128)(2,1)}, u32[]{:S(2)}) copy-start(bf16[32,256]{1,0:T(8,128)(2,1)} %constant.145.clone) | copy-start | bytes 49156
  113.3 5.2 %copy-start.11 = (bf16[32,256]{1,0:T(8,128)(2,1)S(1)}, bf16[32,256]{1,0:T(8,128)(2,1)}, u32[]{:S(2)}) copy-start(bf16[32,256]{1,0:T(8,128)(2,1)} %constant.144.clone) | copy-start | bytes 49156
  117.1 1.8 %copy-start.7 = (bf16[2,1024,256]{1,2,0:T(8,128)(2,1)S(1)}, bf16[2,1024,256]{1,2,0:T(8,128)(2,1)}, u32[]{:S(2)}) copy-start(bf16[2,1024,256]{1,2,0:T(8,128)(2,1)} %copy-done.6) | copy-start | bytes 3145732
  118.9 3.5 %copy-start.8 = (bf16[2,1024,32]{2,1,0:T(8,128)(2,1)S(1)}, bf16[2,1024,32]{2,1,0:T(8,128)(2,1)}, u32[]{:S(2)}) copy-start(bf16[2,1024,32]{2,1,0:T(8,128)(2,1)} %reshape.119) | copy-start | bytes 393220
  120.9 2.3 %collective-permute-start.6 = (f32[32,256]{1,0:T(8,128)S(1)}, f32[32,256]{1,0:T(8,128)S(1)}, u32[]{:S(2)}, u32[]{:S(2)}) collective-permute-start(f32[32,256]{1,0:T(8,128)S(1)} %get-tuple-element.68), channel_id=1, source_target_pairs={{0,1},{1,0},{2,3},{3,2},{4,5},{5,4},{6,7},{7,6},{8,9},{9,8},{10,11... | collective-permute-start | bytes 98312 | tf_op jit(solution)/shard_map/ppermute | solution.py:258
  123.2 4.4 %collective-permute-start.8 = (f32[32,256]{1,0:T(8,128)S(1)}, f32[32,256]{1,0:T(8,128)S(1)}, u32[]{:S(2)}, u32[]{:S(2)}) collective-permute-start(f32[32,256]{1,0:T(8,128)S(1)} %select_add_fusion), channel_id=1, source_target_pairs={{0,4},{1,5},{2,6},{3,7},{4,0},{5,1},{6,2},{7,3},{8,12},{9,13},{10,... | collective-permute-start | bytes 98312 | tf_op jit(solution)/shard_map/ppermute | solution.py:258
  123.2 4.4 %collective-permute-start.9 = (f32[32,256]{1,0:T(8,128)S(1)}, f32[32,256]{1,0:T(8,128)S(1)}, u32[]{:S(2)}, u32[]{:S(2)}) collective-permute-start(f32[32,256]{1,0:T(8,128)S(1)} %select_add_fusion), channel_id=1, source_target_pairs={{0,6},{1,7},{2,4},{3,5},{4,2},{5,3},{6,0},{7,1},{8,14},{9,15},{10,... | collective-permute-start | bytes 98312 | tf_op jit(solution)/shard_map/ppermute | solution.py:258
  125.9 2.9 %collective-permute-start.7 = (f32[32,256]{1,0:T(8,128)S(1)}, f32[32,256]{1,0:T(8,128)S(1)}, u32[]{:S(2)}, u32[]{:S(2)}) collective-permute-start(f32[32,256]{1,0:T(8,128)S(1)} %select_add_fusion), channel_id=1, source_target_pairs={{0,2},{1,3},{2,0},{3,1},{4,6},{5,7},{6,4},{7,5},{8,10},{9,11},{10,... | collective-permute-start | bytes 98312 | tf_op jit(solution)/shard_map/ppermute | solution.py:258
  128.9 4.6 %collective-permute-start.10 = (f32[32,384]{1,0:T(8,128)S(1)}, f32[32,384]{1,0:T(8,128)S(1)}, u32[]{:S(2)}, u32[]{:S(2)}) collective-permute-start(f32[32,384]{1,0:T(8,128)S(1)} %get-tuple-element.61), channel_id=1, source_target_pairs={{0,8},{1,9},{2,10},{3,11},{4,12},{5,13},{6,14},{7,15},{8,0},{9,1},... | collective-permute-start | bytes 147464 | tf_op jit(solution)/shard_map/ppermute | solution.py:258
  129.0 4.6 %collective-permute-start.11 = (f32[32,384]{1,0:T(8,128)S(1)}, f32[32,384]{1,0:T(8,128)S(1)}, u32[]{:S(2)}, u32[]{:S(2)}) collective-permute-start(f32[32,384]{1,0:T(8,128)S(1)} %get-tuple-element.62), channel_id=1, source_target_pairs={{0,16},{1,17},{2,18},{3,19},{4,20},{5,21},{6,22},{7,23},{8,24},{9,... | collective-permute-start | bytes 147464 | tf_op jit(solution)/shard_map/ppermute | solution.py:258
  131.2 4.5 %collective-permute-start.12 = (f32[32,384]{1,0:T(8,128)S(1)}, f32[32,384]{1,0:T(8,128)S(1)}, u32[]{:S(2)}, u32[]{:S(2)}) collective-permute-start(f32[32,384]{1,0:T(8,128)S(1)} %get-tuple-element.60), channel_id=1, source_target_pairs={{0,24},{1,25},{2,26},{3,27},{4,28},{5,29},{6,30},{7,31},{8,16},{9,... | collective-permute-start | bytes 147464 | tf_op jit(solution)/shard_map/ppermute | solution.py:258
  135.7 4.1 %collective-permute-start.13 = (f32[32,384]{1,0:T(8,128)S(1)}, f32[32,384]{1,0:T(8,128)S(1)}, u32[]{:S(2)}, u32[]{:S(2)}) collective-permute-start(f32[32,384]{1,0:T(8,128)S(1)} %get-tuple-element.58), channel_id=1, source_target_pairs={{0,32},{1,33},{2,34},{3,35},{4,36},{5,37},{6,38},{7,39},{8,40},{9,... | collective-permute-start | bytes 147464 | tf_op jit(solution)/shard_map/ppermute | solution.py:258
  137.3 4.5 %collective-permute-start.14 = (f32[32,384]{1,0:T(8,128)S(1)}, f32[32,384]{1,0:T(8,128)S(1)}, u32[]{:S(2)}, u32[]{:S(2)}) collective-permute-start(f32[32,384]{1,0:T(8,128)S(1)} %get-tuple-element.59), channel_id=1, source_target_pairs={{0,64},{1,65},{2,66},{3,67},{4,68},{5,69},{6,70},{7,71},{8,72},{9,... | collective-permute-start | bytes 147464 | tf_op jit(solution)/shard_map/ppermute | solution.py:258
  139.8 4.2 %collective-permute-start.15 = (f32[32,384]{1,0:T(8,128)S(1)}, f32[32,384]{1,0:T(8,128)S(1)}, u32[]{:S(2)}, u32[]{:S(2)}) collective-permute-start(f32[32,384]{1,0:T(8,128)S(1)} %get-tuple-element.57), channel_id=1, source_target_pairs={{0,96},{1,97},{2,98},{3,99},{4,100},{5,101},{6,102},{7,103},{8,104... | collective-permute-start | bytes 147464 | tf_op jit(solution)/shard_map/ppermute | solution.py:258
  144.0 7.2 %collective-permute-start.16 = (f32[32,256]{1,0:T(8,128)S(1)}, f32[32,256]{1,0:T(8,128)S(1)}, u32[]{:S(2)}, u32[]{:S(2)}) collective-permute-start(f32[32,256]{1,0:T(8,128)S(1)} %slice.50), channel_id=1, source_target_pairs={{0,1},{1,0},{2,3},{3,2},{4,5},{5,4},{6,7},{7,6},{8,9},{9,8},{10,11... | collective-permute-start | bytes 98312 | tf_op jit(solution)/shard_map/ppermute | solution.py:258
  (1 other events, 0.8 us)

commit v5 on v4

--- a/solution.py
+++ b/solution.py
@@ -11,6 +11,7 @@
 BOTH = ("row", "col")
 TILE = 16
 GRAD_TILE = 8
+BLOCKS = 4
 CORES = 2
 VMEM_BYTES = 48 * 1024 * 1024
 NT = (((1,), (1,)), ((), ()))
@@ -43,23 +44,44 @@
                 ]
 
 
-def left_kernel(inverse, right_ref, own_ref, grad_ref, out_ref, partial_ref):
-    step = pl.program_id(0)
-    grads = jnp.dot(right_ref[...], grad_ref[...], preferred_element_type=jnp.float32)
-    out_ref[...] = (grads * inverse).astype(out_ref.dtype)
-
-    @pl.when(step == 0)
-    def _():
-        partial_ref[...] = lax.dot_general(own_ref[...], grad_ref[...], NT, preferred_element_type=jnp.float32)
-
-    @pl.when((step > 0) & (step < pl.num_programs(0) // CORES))
-    def _():
-        partial_ref[...] += lax.dot_general(own_ref[...], grad_ref[...], NT, preferred_element_type=jnp.float32)
-
-
-def right_kernel(inverse, other_ref, partial_ref, grad_ref, out_ref):
-    grads = lax.dot_general(other_ref[...], grad_ref[...], NT, preferred_element_type=jnp.float32)
-    out_ref[...] = ((partial_ref[...] + grads) * inverse).astype(out_ref.dtype)
+def left_kernel(inverse, came_ref, grad_ref, out_ref, partial_ref, panel_ref, held_ref, sems):
+    blocks = sems.shape[0] - 1
+    depth, columns = held_ref.shape
+    block, half = columns // blocks, columns // CORES
+    panel = pltpu.make_async_copy(came_ref, panel_ref, sems.at[blocks])
+    panel.start()
+    parts = [pl.ds(n * block, block) for n in range(blocks)]
+    copies = [
+        pltpu.make_async_copy(grad_ref.at[:, part], held_ref.at[:, part], sems.at[n]) for n, part in enumerate(parts)
+    ]
+    for copy in copies:
+        copy.start()
+    panel.wait()
+    for n, part in enumerate(parts):
+        if n == blocks // CORES:
+            partial_ref[...] = lax.dot_general(
+                panel_ref[:, :half], held_ref[:, :half], NT, preferred_element_type=jnp.float32
+            )
+        copies[n].wait()
+        grads = jnp.dot(panel_ref[:, -depth:], held_ref[:, part], preferred_element_type=jnp.float32)
+        out_ref[:, part] = (grads * inverse).astype(out_ref.dtype)
+
+
+def right_kernel(inverse, other_ref, partial_ref, grad_ref, out_ref, held_ref, sems):
+    blocks = sems.shape[0]
+    rows, depth = held_ref.shape
+    block = rows // blocks
+    parts = [pl.ds(n * block, block) for n in range(blocks)]
+    copies = [
+        pltpu.make_async_copy(grad_ref.at[part, pl.ds(depth, depth)], held_ref.at[part], sems.at[n])
+        for n, part in enumerate(parts)
+    ]
+    for copy in copies:
+        copy.start()
+    for n, part in enumerate(parts):
+        copies[n].wait()
+        grads = lax.dot_general(other_ref[...], held_ref[part], NT, preferred_element_type=jnp.float32)
+        out_ref[:, part] = ((partial_ref[:, part] + grads) * inverse).astype(out_ref.dtype)
 
 
 def pack_kernel(left_ref, right_ref, out_ref, sems):
@@ -143,43 +165,35 @@
 
 def left_grads(came, grads, interpret=False):
     seqs, (depth, columns) = came.shape[0], grads.shape
-    block = 512
-    own = columns // CORES // block
-    last = came.shape[1] // depth - 1
     return pl.pallas_call(
         functools.partial(left_kernel, 1.0 / seqs),
-        grid=(columns // block,),
-        in_specs=[
-            pl.BlockSpec((seqs, depth), lambda n: (0, last)),
-            pl.BlockSpec((seqs, block), lambda n: (0, jnp.minimum(n, own - 1))),
-            pl.BlockSpec((depth, block), lambda n: (0, n)),
-        ],
-        out_specs=[pl.BlockSpec((seqs, block), lambda n: (0, n)), whole((seqs, depth))],
+        in_specs=[pl.BlockSpec(memory_space=pl.ANY)] * 2,
+        out_specs=[pl.BlockSpec(memory_space=pltpu.VMEM)] * 2,
         out_shape=[
             jax.ShapeDtypeStruct((seqs, columns), jnp.bfloat16),
             jax.ShapeDtypeStruct((seqs, depth), jnp.float32),
         ],
-        compiler_params=params(),
+        scratch_shapes=[
+            pltpu.VMEM(came.shape, jnp.bfloat16),
+            pltpu.VMEM(grads.shape, jnp.bfloat16),
+            pltpu.SemaphoreType.DMA((BLOCKS + 1,)),
+        ],
+        compiler_params=pltpu.CompilerParams(vmem_limit_bytes=VMEM_BYTES),
         cost_estimate=pl.CostEstimate(flops=3 * seqs * depth * columns, bytes_accessed=21 * 2**20, transcendentals=0),
         interpret=interpret,
         name="left_grads",
-    )(came, came, grads)
+    )(came, grads)
 
 
 def right_grads(other, partial, grads, interpret=False):
     seqs, (rows, depth) = other.shape[0], grads.shape
-    block = 256
     return pl.pallas_call(
         functools.partial(right_kernel, 1.0 / seqs),
-        grid=(rows // block,),
-        in_specs=[
-            whole(other.shape),
-            pl.BlockSpec((seqs, block), lambda n: (0, n)),
-            pl.BlockSpec((block, depth // CORES), lambda n: (n, 1)),
-        ],
-        out_specs=pl.BlockSpec((seqs, block), lambda n: (0, n)),
+        in_specs=[pl.BlockSpec(memory_space=pltpu.VMEM)] * 2 + [pl.BlockSpec(memory_space=pl.ANY)],
+        out_specs=pl.BlockSpec(memory_space=pltpu.VMEM),
         out_shape=jax.ShapeDtypeStruct((seqs, rows), jnp.bfloat16),
-        compiler_params=params(),
+        scratch_shapes=[pltpu.VMEM((rows, depth // CORES), jnp.bfloat16), pltpu.SemaphoreType.DMA((BLOCKS,))],
+        compiler_params=pltpu.CompilerParams(vmem_limit_bytes=VMEM_BYTES),
         cost_estimate=pl.CostEstimate(flops=seqs * depth * rows, bytes_accessed=12 * 2**20, transcendentals=0),
         interpret=interpret,
         name="right_grads",

time: 153 us -> 147 us (0.961)
  Pallas kernels: 47.3 us -> 41.4 us
    pallas_call x2, Pallas kernels: 20.6 us -> 14.6 us  [the longest x1 10 us: left_grads(): pl.pallas_call(functools.partial(left_kernel, 1.0 / seqs), in_specs=[pl.B...]
  transfers between devices with their start and end apart: 19 -> 19, of which waited for: 10 -> 11; matrix products, arithmetic and copies ran while one was open for 8% -> 8% of each run, Pallas kernels for 30% -> 27%
where the time goes in v5:
time: 147 us; the launch traced here: 146 us
  Pallas kernels  41.4 us (28%)
  starting transfers between devices  41 us (28%)
  waiting for transfers between devices  29.4 us (20%)
  local copies, waits for them, and re-layouts  25.3 us (17%)
  matrix products  4.41 us (3%)
  other arithmetic  3.4 us (2%)
    ppermute x15, starting transfers between devices, partner(): lax.ppermute(part, BOTH, [(i, i ^ mask) for i in range(lax.axis_size(BOTH...  22 us
    all_to_all x2, waiting for transfers between devices, exchange(): return lax.all_to_all(blocks, BOTH, 0, 0, tiled=True)  18.1 us
    all_to_all x2, starting transfers between devices, exchange(): return lax.all_to_all(blocks, BOTH, 0, 0, tiled=True)  16.8 us
    pallas_call x1, Pallas kernels, forward(): pl.pallas_call(functools.partial(forward_kernel, 1.0 / seqs, width), grid...  14.7 us
    unnamed x34, local copies, waits for them, and re-layouts  12.6 us
    ppermute x15, waiting for transfers between devices, partner(): lax.ppermute(part, BOTH, [(i, i ^ mask) for i in range(lax.axis_size(BOTH...  11.3 us
    pallas_call x1, Pallas kernels, left_grads(): pl.pallas_call(functools.partial(left_kernel, 1.0 / seqs), in_specs=[pl.B...  10 us
    pallas_call x1, Pallas kernels, outer_grads(): pl.pallas_call(functools.partial(outer_grad_kernel, width), grid=(cols //...  9.63 us
  transfers between devices with their start and end apart: 19, of which 11 were waited for; matrix products, arithmetic and copies ran while one was open for 8% of the time, Pallas kernels for 27%

profile of v5, /device:TPU:1, one launch (start us, length us, event | category | flops | bytes accessed | tf_op | source)
XLA Modules:
  0.0 146.1 jit_solution(14673892556748931186)
XLA Ops:
  0.6 1.5 %copy.47 = bf16[2,1024,256]{1,2,0:T(8,128)(2,1)S(1)} copy(bf16[2,1024,256]{2,1,0:T(8,128)(2,1)} %param.8) | data formatting | bytes 2097152 | tf_op args[0]
  5.8 2.4 %pack.1 = bf16[8,8,2,2,4096]{4,3,2,1,0:T(2,128)(2,1)} custom-call(bf16[8,2,2,2048]{3,2,1,0:T(2,128)(2,1)} %reshape.108.left_ref, bf16[8,2,2,2048]{3,2,1,0:T(2,128)(2,1)} %bitcast.110), custom_call_target="tpu_custom_call" | custom-call | bytes 2097152 | tf_op jit(solution)/shard_map/pack/pallas_call | solution.py:205
  8.3 12.0 %all-to-all-start = ((bf16[128,2,4096]{2,1,0:T(2,128)(2,1)}), bf16[128,2,4096]{2,1,0:T(2,128)(2,1)}, u32[]{:S(2)}, u32[]{:S(2)}) async-start(bf16[128,2,4096]{2,1,0:T(2,128)(2,1)} %bitcast.107), calls=%async_computation | async-start | bytes 4194304 | tf_op jit(solution)/shard_map/all_to_all | solution.py:250
  20.7 2.9 %copy.86 = bf16[128,64,128]{2,0,1:T(8,128)(2,1)S(1)} copy(bf16[128,64,128]{2,1,0:T(8,128)(2,1)} %param.13) | data formatting | bytes 4194304 | tf_op args[5]
  23.6 9.6 %outer_grads.1.grad_ref = bf16[2048,4096]{1,0:T(8,128)(2,1)} custom-call(bf16[1024,128]{1,0:T(8,128)(2,1)S(1)} %copy.57.weight_ref, bf16[64,128,128]{2,1,0:T(8,128)(2,1)S(1)} %bitcast.101), custom_call_target="tpu_custom_call" | custom-call | flops 2147483648 | bytes 18874368 | tf_op jit(solution)/shard_map/outer_grads/pallas_call | solution.py:151
  33.3 17.1 %all-to-all-done = bf16[128,2,4096]{2,1,0:T(2,128)(2,1)} async-done(((bf16[128,2,4096]{2,1,0:T(2,128)(2,1)}), bf16[128,2,4096]{2,1,0:T(2,128)(2,1)}, u32[]{:S(2)}, u32[]{:S(2)}) %all-to-all-start) | async-done | bytes 2097184 | tf_op jit(solution)/shard_map/all_to_all | solution.py:250
  50.4 2.7 %reshape.111.came_ref.own_ref.right_ref = bf16[256,4096]{1,0:T(8,128)(2,1)S(1)} reshape(bf16[128,2,4096]{2,1,0:T(2,128)(2,1)} %all-to-all-done) | data formatting | bytes 4194304 | tf_op jit(solution)/shard_map/reshape | solution.py:346
  54.5 10.0 %left_grads.1 = (bf16[256,4096]{1,0:T(8,128)(2,1)S(1)}, f32[256,2048]{1,0:T(8,128)S(1)}) custom-call(bf16[256,4096]{1,0:T(8,128)(2,1)} %copy-done.2, bf16[2048,4096]{1,0:T(8,128)(2,1)} %outer_grads.1.grad_ref), custom_call_target="tpu_custom_call" | custom-call | flops 6442450944 | bytes 22020096 | tf_op jit(solution)/shard_map/left_grads/pallas_call | solution.py:168
  64.6 1.2 collective-permute-start.1
  65.8 4.6 %right_grads.1 = bf16[256,2048]{1,0:T(8,128)(2,1)S(1)} custom-call(bf16[256,2048]{1,0:T(8,128)(2,1)S(1)} %collective-permute-done.other_ref, f32[256,2048]{1,0:T(8,128)S(1)} %get-tuple-element.22.partial_ref, bf16[2048,4096]{1,0:T(8,128)(2,1)} %outer_grads.1.grad_ref), custom_call_target="tpu_custom_call" | custom-call | flops 2147483648 | bytes 12582912 | tf_op jit(solution)/shard_map/right_grads/pallas_call | solution.py:190
  71.0 2.7 %reshape.112 = bf16[128,2,4096]{2,1,0:T(2,128)(2,1)} reshape(bf16[256,4096]{1,0:T(8,128)(2,1)S(1)} %pad_maximum_fusion) | data formatting | bytes 4194304 | tf_op jit(solution)/shard_map/reshape | solution.py:353
  73.6 4.8 %all-to-all-start.1 = ((bf16[128,2,4096]{2,1,0:T(2,128)(2,1)}), bf16[128,2,4096]{2,1,0:T(2,128)(2,1)}, u32[]{:S(2)}, u32[]{:S(2)}) async-start(bf16[128,2,4096]{2,1,0:T(2,128)(2,1)} %reshape.112), calls=%async_computation.1 | async-start | bytes 4194304 | tf_op jit(solution)/shard_map/all_to_all | solution.py:250
  78.5 14.7 %forward.1 = (bf16[64,128,128]{2,1,0:T(8,128)(2,1)S(1)}, f32[1024,128]{1,0:T(8,128)S(1)}) custom-call(s32[1]{0:T(128)} %bitcast.core_ref, bf16[256,4096]{1,0:T(8,128)(2,1)S(1)} %copy-done.3, bf16[256,2048]{1,0:T(8,128)(2,1)S(1)} %collective-permute-done.other_ref, bf16[256,4096]{1,0:T(8,128)(2,1)S(1)} %copy-done.3, bf16[128,1024]{1,0:T(8,128)(2,1)S(1)} %bitcast.104, ...), custom_call_target="tpu_custom_call" | custom-call | flops 8589934592 | bytes 8388608 | tf_op jit(solution)/shard_map/forward/pallas_call | solution.py:221
  93.3 1.4 copy-done.4
  95.4 1.2 collective-permute-start.2
  96.6 1.2 collective-permute-done.2
  99.4 2.4 %collective-permute-start.4 = (f32[16,8,128]{2,1,0:T(8,128)S(1)}, f32[16,8,128]{2,1,0:T(8,128)S(1)}, u32[]{:S(2)}, u32[]{:S(2)}) collective-permute-start(f32[16,8,128]{2,1,0:T(8,128)S(1)} %get-tuple-element.47), channel_id=1, source_target_pairs={{0,4},{1,5},{2,6},{3,7},{4,0},{5,1},{6,2},{7,3},{8,12},{9,13},{10,... | collective-permute-start | bytes 196616 | tf_op jit(solution)/shard_map/ppermute | solution.py:272
  102.7 4.3 %copy.63 = bf16[128,64,128]{2,1,0:T(8,128)(2,1)} copy(bf16[128,64,128]{2,0,1:T(8,128)(2,1)} %bitcast.103) | data formatting | bytes 4194304
  108.6 2.7 %reshape.115 = bf16[256,4096]{1,0:T(8,128)(2,1)S(1)} reshape(bf16[128,2,4096]{2,1,0:T(2,128)(2,1)} %all-to-all-done.1) | data formatting | bytes 4194304 | tf_op jit(solution)/shard_map/reshape | solution.py:355
  113.6 1.5 %broadcast_select_fusion = (f32[32,256]{1,0:T(8,128)S(1)}, f32[32,256]{1,0:T(8,128)S(1)}) fusion(f32[32,256]{1,0:T(8,128)S(1)} %convolution_bitcast_fusion.1, pred[]{:T(512)S(6)} %eq.17, bf16[2,1024,32]{2,1,0:T(8,128)(2,1)} %reshape.119, bf16[2,1024,256]{1,2,0:T(8,128)(2,1)S(1)} %copy-done.7, f32[2,1024]{1,0:T(2,128)S(1)} %add_rsqrt_fusion, ...), kind=kOutput, calls=%fused_computation.67 | convolution fusion | flops 35659776 | bytes 1294337 | tf_op jit(solution)/shard_map/src,srh->hc/dot_general | solution.py:375
  115.1 1.5 %collective-permute-start.6 = (f32[32,256]{1,0:T(8,128)S(1)}, f32[32,256]{1,0:T(8,128)S(1)}, u32[]{:S(2)}, u32[]{:S(2)}) collective-permute-start(f32[32,256]{1,0:T(8,128)S(1)} %get-tuple-element.68), channel_id=1, source_target_pairs={{0,1},{1,0},{2,3},{3,2},{4,5},{5,4},{6,7},{7,6},{8,9},{9,8},{10,11... | collective-permute-start | bytes 98312 | tf_op jit(solution)/shard_map/ppermute | solution.py:272
  117.5 2.7 %collective-permute-start.9 = (f32[32,256]{1,0:T(8,128)S(1)}, f32[32,256]{1,0:T(8,128)S(1)}, u32[]{:S(2)}, u32[]{:S(2)}) collective-permute-start(f32[32,256]{1,0:T(8,128)S(1)} %select_add_fusion), channel_id=1, source_target_pairs={{0,6},{1,7},{2,4},{3,5},{4,2},{5,3},{6,0},{7,1},{8,14},{9,15},{10,... | collective-permute-start | bytes 98312 | tf_op jit(solution)/shard_map/ppermute | solution.py:272
  120.2 1.6 %collective-permute-done.8 = f32[32,256]{1,0:T(8,128)S(1)} collective-permute-done((f32[32,256]{1,0:T(8,128)S(1)}, f32[32,256]{1,0:T(8,128)S(1)}, u32[]{:S(2)}, u32[]{:S(2)}) %collective-permute-start.8) | collective-permute-done | bytes 32800 | tf_op jit(solution)/shard_map/ppermute | solution.py:272
  123.3 2.1 %collective-permute-start.11 = (f32[32,384]{1,0:T(8,128)S(1)}, f32[32,384]{1,0:T(8,128)S(1)}, u32[]{:S(2)}, u32[]{:S(2)}) collective-permute-start(f32[32,384]{1,0:T(8,128)S(1)} %get-tuple-element.62), channel_id=1, source_target_pairs={{0,16},{1,17},{2,18},{3,19},{4,20},{5,21},{6,22},{7,23},{8,24},{9,... | collective-permute-start | bytes 147464 | tf_op jit(solution)/shard_map/ppermute | solution.py:272
  125.4 1.7 %collective-permute-start.12 = (f32[32,384]{1,0:T(8,128)S(1)}, f32[32,384]{1,0:T(8,128)S(1)}, u32[]{:S(2)}, u32[]{:S(2)}) collective-permute-start(f32[32,384]{1,0:T(8,128)S(1)} %get-tuple-element.60), channel_id=1, source_target_pairs={{0,24},{1,25},{2,26},{3,27},{4,28},{5,29},{6,30},{7,31},{8,16},{9,... | collective-permute-start | bytes 147464 | tf_op jit(solution)/shard_map/ppermute | solution.py:272
  127.9 2.0 %collective-permute-done.12 = f32[32,384]{1,0:T(8,128)S(1)} collective-permute-done((f32[32,384]{1,0:T(8,128)S(1)}, f32[32,384]{1,0:T(8,128)S(1)}, u32[]{:S(2)}, u32[]{:S(2)}) %collective-permute-start.12) | collective-permute-done | bytes 49184 | tf_op jit(solution)/shard_map/ppermute | solution.py:272
  130.0 1.5 %collective-permute-start.13 = (f32[32,384]{1,0:T(8,128)S(1)}, f32[32,384]{1,0:T(8,128)S(1)}, u32[]{:S(2)}, u32[]{:S(2)}) collective-permute-start(f32[32,384]{1,0:T(8,128)S(1)} %get-tuple-element.58), channel_id=1, source_target_pairs={{0,32},{1,33},{2,34},{3,35},{4,36},{5,37},{6,38},{7,39},{8,40},{9,... | collective-permute-start | bytes 147464 | tf_op jit(solution)/shard_map/ppermute | solution.py:272
  131.5 2.5 %collective-permute-start.14 = (f32[32,384]{1,0:T(8,128)S(1)}, f32[32,384]{1,0:T(8,128)S(1)}, u32[]{:S(2)}, u32[]{:S(2)}) collective-permute-start(f32[32,384]{1,0:T(8,128)S(1)} %get-tuple-element.59), channel_id=1, source_target_pairs={{0,64},{1,65},{2,66},{3,67},{4,68},{5,69},{6,70},{7,71},{8,72},{9,... | collective-permute-start | bytes 147464 | tf_op jit(solution)/shard_map/ppermute | solution.py:272
  134.1 2.0 %collective-permute-done.14 = f32[32,384]{1,0:T(8,128)S(1)} collective-permute-done((f32[32,384]{1,0:T(8,128)S(1)}, f32[32,384]{1,0:T(8,128)S(1)}, u32[]{:S(2)}, u32[]{:S(2)}) %collective-permute-start.14) | collective-permute-done | bytes 49184 | tf_op jit(solution)/shard_map/ppermute | solution.py:272
  136.0 2.1 %collective-permute-done.15 = f32[32,384]{1,0:T(8,128)S(1)} collective-permute-done((f32[32,384]{1,0:T(8,128)S(1)}, f32[32,384]{1,0:T(8,128)S(1)}, u32[]{:S(2)}, u32[]{:S(2)}) %collective-permute-start.15) | collective-permute-done | bytes 49184 | tf_op jit(solution)/shard_map/ppermute | solution.py:272
  138.2 4.7 %collective-permute-start.16 = (f32[32,256]{1,0:T(8,128)S(1)}, f32[32,256]{1,0:T(8,128)S(1)}, u32[]{:S(2)}, u32[]{:S(2)}) collective-permute-start(f32[32,256]{1,0:T(8,128)S(1)} %slice.50), channel_id=1, source_target_pairs={{0,1},{1,0},{2,3},{3,2},{4,5},{5,4},{6,7},{7,6},{8,9},{9,8},{10,11... | collective-permute-start | bytes 98312 | tf_op jit(solution)/shard_map/ppermute | solution.py:272
  143.5 1.3 copy.64
  (94 shorter events, 18.1 us)
Async XLA Ops:
  0.6 2.1 %copy-start = (bf16[256,32]{0,1:T(8,128)(2,1)S(1)}, bf16[256,32]{0,1:T(8,128)(2,1)}, u32[]{:S(2)}) copy-start(bf16[256,32]{0,1:T(8,128)(2,1)} %param.9) | copy-start | bytes 49156
  2.1 1.7 %copy-start.6 = (bf16[2,1024,256]{1,2,0:T(8,128)(2,1)}, bf16[2,1024,256]{1,2,0:T(8,128)(2,1)S(1)}, u32[]{:S(2)}) copy-start(bf16[2,1024,256]{1,2,0:T(8,128)(2,1)S(1)} %copy.47) | copy-start | bytes 3145732
  2.2 1.7 %copy-start.10 = (bf16[256,32]{0,1:T(8,128)(2,1)S(1)}, bf16[256,32]{0,1:T(8,128)(2,1)}, u32[]{:S(2)}) copy-start(bf16[256,32]{0,1:T(8,128)(2,1)} %param.10) | copy-start | bytes 49156
  8.2 12.0 %copy-start.9 = (bf16[1024,128]{1,0:T(8,128)(2,1)S(1)}, bf16[1024,128]{1,0:T(8,128)(2,1)}, u32[]{:S(2)}) copy-start(bf16[1024,128]{1,0:T(8,128)(2,1)} %param.11) | copy-start | bytes 786436
  8.3 42.1 %all-to-all-start = ((bf16[128,2,4096]{2,1,0:T(2,128)(2,1)}), bf16[128,2,4096]{2,1,0:T(2,128)(2,1)}, u32[]{:S(2)}, u32[]{:S(2)}) async-start(bf16[128,2,4096]{2,1,0:T(2,128)(2,1)} %bitcast.107), calls=%async_computation | async-start | bytes 4194304 | tf_op jit(solution)/shard_map/all_to_all | solution.py:250
  23.6 9.6 %copy-start.1 = (bf16[128,64,128]{2,0,1:T(8,128)(2,1)}, bf16[128,64,128]{2,0,1:T(8,128)(2,1)S(1)}, u32[]{:S(2)}) copy-start(bf16[128,64,128]{2,0,1:T(8,128)(2,1)S(1)} %copy.86) | copy-start | bytes 6291460
  53.1 1.3 copy-start.2
  53.2 11.3 %collective-permute-start = (bf16[256,2048]{1,0:T(8,128)(2,1)S(1)}, bf16[256,2048]{1,0:T(8,128)(2,1)S(1)}, u32[]{:S(2)}, u32[]{:S(2)}) collective-permute-start(bf16[256,2048]{1,0:T(8,128)(2,1)S(1)} %slice.46), channel_id=1, source_target_pairs={{0,1},{1,0},{2,3},{3,2},{4,5},{5,4},{6,7},{7,6},{8,9},{9,8},{10,11... | collective-permute-start | bytes 3145736 | tf_op jit(solution)/shard_map/ppermute | solution.py:254
  64.6 5.8 %collective-permute-start.1 = (bf16[256,2048]{1,0:T(8,128)(2,1)S(1)}, bf16[256,2048]{1,0:T(8,128)(2,1)S(1)}, u32[]{:S(2)}, u32[]{:S(2)}) collective-permute-start(bf16[256,2048]{1,0:T(8,128)(2,1)S(1)} %slice.37), channel_id=1, source_target_pairs={{0,1},{1,0},{2,3},{3,2},{4,5},{5,4},{6,7},{7,6},{8,9},{9,8},{10,11... | collective-permute-start | bytes 3145736 | tf_op jit(solution)/shard_map/ppermute | solution.py:254
  73.6 4.9 %copy-start.13 = (bf16[128]{0:T(256)(128)(2,1)S(1)}, bf16[128]{0:T(256)(128)(2,1)}, u32[]{:S(2)}) copy-start(bf16[128]{0:T(256)(128)(2,1)} %param.12) | copy-start | bytes 772
  73.6 4.9 %copy-start.3 = (bf16[256,4096]{1,0:T(8,128)(2,1)S(1)}, bf16[256,4096]{1,0:T(8,128)(2,1)}, u32[]{:S(2)}) copy-start(bf16[256,4096]{1,0:T(8,128)(2,1)} %copy-done.2) | copy-start | bytes 6291460
  73.6 35.0 %all-to-all-start.1 = ((bf16[128,2,4096]{2,1,0:T(2,128)(2,1)}), bf16[128,2,4096]{2,1,0:T(2,128)(2,1)}, u32[]{:S(2)}, u32[]{:S(2)}) async-start(bf16[128,2,4096]{2,1,0:T(2,128)(2,1)} %reshape.112), calls=%async_computation.1 | async-start | bytes 4194304 | tf_op jit(solution)/shard_map/all_to_all | solution.py:250
  93.3 1.4 copy-start.4
  95.4 2.3 %collective-permute-start.2 = (f32[64,8,128]{2,1,0:T(8,128)S(1)}, f32[64,8,128]{2,1,0:T(8,128)S(1)}, u32[]{:S(2)}, u32[]{:S(2)}) collective-permute-start(f32[64,8,128]{2,1,0:T(8,128)S(1)} %dynamic-slice_bitcast_fusion), channel_id=1, source_target_pairs={{0,1},{1,0},{2,3},{3,2},{4,5},{5,4},{6,7},{7,6},{8,9},{9,8},{10,11... | collective-permute-start | bytes 786440 | tf_op jit(solution)/shard_map/ppermute | solution.py:272
  98.8 8.2 %collective-permute-start.3 = (f32[16,8,128]{2,1,0:T(8,128)S(1)}, f32[16,8,128]{2,1,0:T(8,128)S(1)}, u32[]{:S(2)}, u32[]{:S(2)}) collective-permute-start(f32[16,8,128]{2,1,0:T(8,128)S(1)} %get-tuple-element.48), channel_id=1, source_target_pairs={{0,2},{1,3},{2,0},{3,1},{4,6},{5,7},{6,4},{7,5},{8,10},{9,11},{10,... | collective-permute-start | bytes 196616 | tf_op jit(solution)/shard_map/ppermute | solution.py:272
  99.4 7.6 %collective-permute-start.4 = (f32[16,8,128]{2,1,0:T(8,128)S(1)}, f32[16,8,128]{2,1,0:T(8,128)S(1)}, u32[]{:S(2)}, u32[]{:S(2)}) collective-permute-start(f32[16,8,128]{2,1,0:T(8,128)S(1)} %get-tuple-element.47), channel_id=1, source_target_pairs={{0,4},{1,5},{2,6},{3,7},{4,0},{5,1},{6,2},{7,3},{8,12},{9,13},{10,... | collective-permute-start | bytes 196616 | tf_op jit(solution)/shard_map/ppermute | solution.py:272
  101.8 5.8 %collective-permute-start.5 = (f32[16,8,128]{2,1,0:T(8,128)S(1)}, f32[16,8,128]{2,1,0:T(8,128)S(1)}, u32[]{:S(2)}, u32[]{:S(2)}) collective-permute-start(f32[16,8,128]{2,1,0:T(8,128)S(1)} %get-tuple-element.46), channel_id=1, source_target_pairs={{0,6},{1,7},{2,4},{3,5},{4,2},{5,3},{6,0},{7,1},{8,14},{9,15},{10,... | collective-permute-start | bytes 196616 | tf_op jit(solution)/shard_map/ppermute | solution.py:272
  107.6 3.8 %copy-start.12 = (bf16[32,256]{1,0:T(8,128)(2,1)S(1)}, bf16[32,256]{1,0:T(8,128)(2,1)}, u32[]{:S(2)}) copy-start(bf16[32,256]{1,0:T(8,128)(2,1)} %constant.145.clone) | copy-start | bytes 49156
  107.6 5.2 %copy-start.11 = (bf16[32,256]{1,0:T(8,128)(2,1)S(1)}, bf16[32,256]{1,0:T(8,128)(2,1)}, u32[]{:S(2)}) copy-start(bf16[32,256]{1,0:T(8,128)(2,1)} %constant.144.clone) | copy-start | bytes 49156
  111.3 1.8 %copy-start.7 = (bf16[2,1024,256]{1,2,0:T(8,128)(2,1)S(1)}, bf16[2,1024,256]{1,2,0:T(8,128)(2,1)}, u32[]{:S(2)}) copy-start(bf16[2,1024,256]{1,2,0:T(8,128)(2,1)} %copy-done.6) | copy-start | bytes 3145732
  113.1 3.5 %copy-start.8 = (bf16[2,1024,32]{2,1,0:T(8,128)(2,1)S(1)}, bf16[2,1024,32]{2,1,0:T(8,128)(2,1)}, u32[]{:S(2)}) copy-start(bf16[2,1024,32]{2,1,0:T(8,128)(2,1)} %reshape.119) | copy-start | bytes 393220
  115.1 2.3 %collective-permute-start.6 = (f32[32,256]{1,0:T(8,128)S(1)}, f32[32,256]{1,0:T(8,128)S(1)}, u32[]{:S(2)}, u32[]{:S(2)}) collective-permute-start(f32[32,256]{1,0:T(8,128)S(1)} %get-tuple-element.68), channel_id=1, source_target_pairs={{0,1},{1,0},{2,3},{3,2},{4,5},{5,4},{6,7},{7,6},{8,9},{9,8},{10,11... | collective-permute-start | bytes 98312 | tf_op jit(solution)/shard_map/ppermute | solution.py:272
  117.5 4.3 %collective-permute-start.8 = (f32[32,256]{1,0:T(8,128)S(1)}, f32[32,256]{1,0:T(8,128)S(1)}, u32[]{:S(2)}, u32[]{:S(2)}) collective-permute-start(f32[32,256]{1,0:T(8,128)S(1)} %select_add_fusion), channel_id=1, source_target_pairs={{0,4},{1,5},{2,6},{3,7},{4,0},{5,1},{6,2},{7,3},{8,12},{9,13},{10,... | collective-permute-start | bytes 98312 | tf_op jit(solution)/shard_map/ppermute | solution.py:272
  117.5 4.6 %collective-permute-start.9 = (f32[32,256]{1,0:T(8,128)S(1)}, f32[32,256]{1,0:T(8,128)S(1)}, u32[]{:S(2)}, u32[]{:S(2)}) collective-permute-start(f32[32,256]{1,0:T(8,128)S(1)} %select_add_fusion), channel_id=1, source_target_pairs={{0,6},{1,7},{2,4},{3,5},{4,2},{5,3},{6,0},{7,1},{8,14},{9,15},{10,... | collective-permute-start | bytes 98312 | tf_op jit(solution)/shard_map/ppermute | solution.py:272
  120.1 3.0 %collective-permute-start.7 = (f32[32,256]{1,0:T(8,128)S(1)}, f32[32,256]{1,0:T(8,128)S(1)}, u32[]{:S(2)}, u32[]{:S(2)}) collective-permute-start(f32[32,256]{1,0:T(8,128)S(1)} %select_add_fusion), channel_id=1, source_target_pairs={{0,2},{1,3},{2,0},{3,1},{4,6},{5,7},{6,4},{7,5},{8,10},{9,11},{10,... | collective-permute-start | bytes 98312 | tf_op jit(solution)/shard_map/ppermute | solution.py:272
  123.2 4.6 %collective-permute-start.10 = (f32[32,384]{1,0:T(8,128)S(1)}, f32[32,384]{1,0:T(8,128)S(1)}, u32[]{:S(2)}, u32[]{:S(2)}) collective-permute-start(f32[32,384]{1,0:T(8,128)S(1)} %get-tuple-element.61), channel_id=1, source_target_pairs={{0,8},{1,9},{2,10},{3,11},{4,12},{5,13},{6,14},{7,15},{8,0},{9,1},... | collective-permute-start | bytes 147464 | tf_op jit(solution)/shard_map/ppermute | solution.py:272
  123.3 4.6 %collective-permute-start.11 = (f32[32,384]{1,0:T(8,128)S(1)}, f32[32,384]{1,0:T(8,128)S(1)}, u32[]{:S(2)}, u32[]{:S(2)}) collective-permute-start(f32[32,384]{1,0:T(8,128)S(1)} %get-tuple-element.62), channel_id=1, source_target_pairs={{0,16},{1,17},{2,18},{3,19},{4,20},{5,21},{6,22},{7,23},{8,24},{9,... | collective-permute-start | bytes 147464 | tf_op jit(solution)/shard_map/ppermute | solution.py:272
  125.4 4.5 %collective-permute-start.12 = (f32[32,384]{1,0:T(8,128)S(1)}, f32[32,384]{1,0:T(8,128)S(1)}, u32[]{:S(2)}, u32[]{:S(2)}) collective-permute-start(f32[32,384]{1,0:T(8,128)S(1)} %get-tuple-element.60), channel_id=1, source_target_pairs={{0,24},{1,25},{2,26},{3,27},{4,28},{5,29},{6,30},{7,31},{8,16},{9,... | collective-permute-start | bytes 147464 | tf_op jit(solution)/shard_map/ppermute | solution.py:272
  130.0 4.1 %collective-permute-start.13 = (f32[32,384]{1,0:T(8,128)S(1)}, f32[32,384]{1,0:T(8,128)S(1)}, u32[]{:S(2)}, u32[]{:S(2)}) collective-permute-start(f32[32,384]{1,0:T(8,128)S(1)} %get-tuple-element.58), channel_id=1, source_target_pairs={{0,32},{1,33},{2,34},{3,35},{4,36},{5,37},{6,38},{7,39},{8,40},{9,... | collective-permute-start | bytes 147464 | tf_op jit(solution)/shard_map/ppermute | solution.py:272
  131.5 4.5 %collective-permute-start.14 = (f32[32,384]{1,0:T(8,128)S(1)}, f32[32,384]{1,0:T(8,128)S(1)}, u32[]{:S(2)}, u32[]{:S(2)}) collective-permute-start(f32[32,384]{1,0:T(8,128)S(1)} %get-tuple-element.59), channel_id=1, source_target_pairs={{0,64},{1,65},{2,66},{3,67},{4,68},{5,69},{6,70},{7,71},{8,72},{9,... | collective-permute-start | bytes 147464 | tf_op jit(solution)/shard_map/ppermute | solution.py:272
  134.0 4.2 %collective-permute-start.15 = (f32[32,384]{1,0:T(8,128)S(1)}, f32[32,384]{1,0:T(8,128)S(1)}, u32[]{:S(2)}, u32[]{:S(2)}) collective-permute-start(f32[32,384]{1,0:T(8,128)S(1)} %get-tuple-element.57), channel_id=1, source_target_pairs={{0,96},{1,97},{2,98},{3,99},{4,100},{5,101},{6,102},{7,103},{8,104... | collective-permute-start | bytes 147464 | tf_op jit(solution)/shard_map/ppermute | solution.py:272
  138.2 7.2 %collective-permute-start.16 = (f32[32,256]{1,0:T(8,128)S(1)}, f32[32,256]{1,0:T(8,128)S(1)}, u32[]{:S(2)}, u32[]{:S(2)}) collective-permute-start(f32[32,256]{1,0:T(8,128)S(1)} %slice.50), channel_id=1, source_target_pairs={{0,1},{1,0},{2,3},{3,2},{4,5},{5,4},{6,7},{7,6},{8,9},{9,8},{10,11... | collective-permute-start | bytes 98312 | tf_op jit(solution)/shard_map/ppermute | solution.py:272
  (1 other events, 0.8 us)

commit v6 on v5

--- a/solution.py
+++ b/solution.py
@@ -4,6 +4,7 @@
 import jax.numpy as jnp
 import numpy as np
 from jax import lax
+from jax.experimental import layout
 from jax.experimental import pallas as pl
 from jax.experimental.pallas import tpu as pltpu
 from jax.sharding import PartitionSpec as P
@@ -259,6 +260,10 @@
     return jnp.where(core == 0, values, jnp.concatenate([values[half:], values[:half]], axis=0))
 
 
+def row_major(values):
+    return layout.with_layout_constraint(values, layout.Layout(major_to_minor=tuple(range(values.ndim))))
+
+
 def permute_groups():
     devices = lax.axis_size(BOTH)
     groups = [(1, CORES)]
@@ -291,7 +296,7 @@
     return values
 
 
-def sum_all(first, second, values, early):
+def sum_all(first, second, values, early, beside):
     core = lax.axis_index(BOTH) % CORES
     own, other = jnp.where(core == 0, first, second), jnp.where(core == 0, second, first)
     part = own + partner(other, 1)
@@ -302,6 +307,8 @@
         if step < early:
             part = add_parts([part] + [partner(part, low * mask) for mask in range(1, size)])
             continue
+        if step == len(permute_groups()) - 1:
+            part, beside = lax.optimization_barrier((part, beside))
         share, lanes = values.shape[1:]
         pieces = [piece.reshape(-1, lanes) for piece in scatter_pieces(values, low, size)]
         used = pieces[0].shape[0]
@@ -310,7 +317,7 @@
         both = add_parts(sent[:1] + [partner(sent[mask], low * mask) for mask in range(1, size)])
         part, values = both[:, :columns], both[:used, columns:].reshape(-1, share, lanes)
     other = partner(part, 1)
-    return jnp.where(core == 0, part, other), jnp.where(core == 0, other, part), values
+    return jnp.where(core == 0, part, other), jnp.where(core == 0, other, part), values, beside
 
 
 def body(alignment, left_weight, right_weight, out_weight, out_bias, pair_cotangent):
@@ -354,11 +361,11 @@
     sent, left_other = lax.optimization_barrier((sent, left_other))
     back = exchange(sent).reshape(seqs, columns)
     update, weight_term = forward(core, came, left_other, weight.T, bias, cot, width)
-    pair_update = update.transpose(1, 0, 2)
+    pair_update = row_major(update.transpose(1, 0, 2))
     early = 2
     weight_term = weight_term.reshape(devices, -1, pair_width)
     weight_term = sum_scatter(weight_term, permute_groups()[:early])
-    back, weight_term = lax.optimization_barrier((back, weight_term))
+    back, weight_term, pair_update = lax.optimization_barrier((back, weight_term, pair_update))
 
     place = np.indices((row_count, chips, CORES, local)).reshape(4, -1)
     left_place = (place[3] * row_count + place[0]) * CORES + place[2]
@@ -373,12 +380,14 @@
     right_grad = right_grad.reshape(local, residues, width)
     left_wgrad = jnp.einsum("src,shr->hc", normed_low, left_grad, preferred_element_type=jnp.float32)
     right_wgrad = jnp.einsum("src,srh->hc", normed_low, right_grad, preferred_element_type=jnp.float32)
-    left_wgrad, right_wgrad, weight_term = sum_all(left_wgrad, right_wgrad, weight_term, early)
-    grad_out_weight = weight_term.reshape(-1, pair_width)
-
     upstream = jnp.einsum("shr,ch->src", left_grad, left_weight, preferred_element_type=jnp.float32)
     upstream += jnp.einsum("srh,ch->src", right_grad, right_weight, preferred_element_type=jnp.float32)
     grad_alignment = norm_backward(upstream, normed, inv_sigma).astype(jnp.bfloat16)
+    grad_alignment = row_major(grad_alignment)
+    left_wgrad, right_wgrad, weight_term, grad_alignment = sum_all(
+        left_wgrad, right_wgrad, weight_term, early, grad_alignment
+    )
+    grad_out_weight = weight_term.reshape(-1, pair_width)
     return (pair_update, grad_alignment, grad_out_weight, left_wgrad.T, right_wgrad.T)
 
 

time: 147 us -> 149 us (1.014)
  other arithmetic: 3.4 us -> 8.2 us
  local copies, waits for them, and re-layouts: 25.3 us -> 21.7 us
  matrix products: 4.41 us -> 6.9 us
  waiting for transfers between devices: 29.4 us -> 27.6 us
    unnamed x34 -> x27, local copies, waits for them, and re-layouts: 12.6 us -> 5.56 us
    pallas_call x0 -> x1, local copies, waits for them, and re-layouts: none -> 4.26 us  [forward(): pl.pallas_call(functools.partial(forward_kernel, 1.0 / seqs, width), grid...]
    ppermute x15, waiting for transfers between devices: 11.3 us -> 9.48 us  [partner(): lax.ppermute(part, BOTH, [(i, i ^ mask) for i in range(lax.axis_size(BOTH...]
    convert_element_type x1, other arithmetic: 0.57 us -> 2.35 us  [body(): norm_backward(upstream, normed, inv_sigma).astype(jnp.bfloat16)]
    reduce_sum x1, other arithmetic: 0.3 us -> 1.87 us  [layer_norm(): jnp.mean(centered * centered, axis=-1, keepdims=True) + 1e-05]
  transfers between devices with their start and end apart: 19 -> 19, of which waited for: 11 -> 11; matrix products, arithmetic and copies ran while one was open for 8% -> 9% of each run, Pallas kernels for 27% -> 26%
where the time goes in v6:
time: 149 us; the launch traced here: 148 us
  Pallas kernels  41.4 us (28%)
  starting transfers between devices  41.1 us (28%)
  waiting for transfers between devices  27.6 us (19%)
  local copies, waits for them, and re-layouts  21.7 us (15%)
  other arithmetic  8.2 us (6%)
  matrix products  6.9 us (5%)
    ppermute x15, starting transfers between devices, partner(): lax.ppermute(part, BOTH, [(i, i ^ mask) for i in range(lax.axis_size(BOTH...  22 us
    all_to_all x2, waiting for transfers between devices, exchange(): return lax.all_to_all(blocks, BOTH, 0, 0, tiled=True)  18.1 us
    all_to_all x2, starting transfers between devices, exchange(): return lax.all_to_all(blocks, BOTH, 0, 0, tiled=True)  16.8 us
    pallas_call x1, Pallas kernels, forward(): pl.pallas_call(functools.partial(forward_kernel, 1.0 / seqs, width), grid...  14.7 us
    pallas_call x1, Pallas kernels, left_grads(): pl.pallas_call(functools.partial(left_kernel, 1.0 / seqs), in_specs=[pl.B...  10 us
    pallas_call x1, Pallas kernels, outer_grads(): pl.pallas_call(functools.partial(outer_grad_kernel, width), grid=(cols //...  9.65 us
    ppermute x15, waiting for transfers between devices, partner(): lax.ppermute(part, BOTH, [(i, i ^ mask) for i in range(lax.axis_size(BOTH...  9.48 us
    unnamed x27, local copies, waits for them, and re-layouts  5.56 us
  transfers between devices with their start and end apart: 19, of which 11 were waited for; matrix products, arithmetic and copies ran while one was open for 9% of the time, Pallas kernels for 26%

profile of v6, /device:TPU:1, one launch (start us, length us, event | category | flops | bytes accessed | tf_op | source)
XLA Modules:
  0.0 148.1 jit_solution(9231571418934463230)
XLA Ops:
  0.7 1.7 %convert_reduce_fusion = f32[2,1024]{1,0:T(2,128)S(1)} fusion(bf16[2,1024,256]{2,1,0:T(8,128)(2,1)} %param.8), kind=kLoop, calls=%fused_computation.1 | loop fusion | flops 1046528 | bytes 1056768 | tf_op jit(solution)/shard_map/reduce_sum | solution.py:22
  2.4 1.9 %fusion.11 = f32[2,1024]{1,0:T(2,128)S(1)} fusion(bf16[2,1024,256]{2,1,0:T(8,128)(2,1)} %param.8, f32[2,1024]{1,0:T(2,128)S(1)} %broadcast_multiply_fusion.2), kind=kLoop, calls=%fused_computation.15 | loop fusion | flops 2095104 | bytes 1064960 | tf_op jit(solution)/shard_map/reduce_sum | solution.py:23
  8.5 2.4 %pack.1 = bf16[8,8,2,2,4096]{4,3,2,1,0:T(2,128)(2,1)} custom-call(bf16[8,2,2,2048]{3,2,1,0:T(2,128)(2,1)} %reshape.107.left_ref, bf16[8,2,2,2048]{3,2,1,0:T(2,128)(2,1)} %bitcast.112), custom_call_target="tpu_custom_call" | custom-call | bytes 2097152 | tf_op jit(solution)/shard_map/pack/pallas_call | solution.py:206
  10.9 12.0 %all-to-all-start = ((bf16[128,2,4096]{2,1,0:T(2,128)(2,1)}), bf16[128,2,4096]{2,1,0:T(2,128)(2,1)}, u32[]{:S(2)}, u32[]{:S(2)}) async-start(bf16[128,2,4096]{2,1,0:T(2,128)(2,1)} %bitcast.108), calls=%async_computation | async-start | bytes 4194304 | tf_op jit(solution)/shard_map/all_to_all | solution.py:251
  23.3 2.9 %copy.74 = bf16[128,64,128]{2,0,1:T(8,128)(2,1)S(1)} copy(bf16[128,64,128]{2,1,0:T(8,128)(2,1)} %param.13) | data formatting | bytes 4194304 | tf_op args[5]
  26.3 9.6 %outer_grads.1.grad_ref = bf16[2048,4096]{1,0:T(8,128)(2,1)} custom-call(bf16[1024,128]{1,0:T(8,128)(2,1)S(1)} %copy.46.weight_ref, bf16[64,128,128]{2,1,0:T(8,128)(2,1)S(1)} %bitcast.103), custom_call_target="tpu_custom_call" | custom-call | flops 2147483648 | bytes 18874368 | tf_op jit(solution)/shard_map/outer_grads/pallas_call | solution.py:152
  36.0 17.1 %all-to-all-done = bf16[128,2,4096]{2,1,0:T(2,128)(2,1)} async-done(((bf16[128,2,4096]{2,1,0:T(2,128)(2,1)}), bf16[128,2,4096]{2,1,0:T(2,128)(2,1)}, u32[]{:S(2)}, u32[]{:S(2)}) %all-to-all-start) | async-done | bytes 2097184 | tf_op jit(solution)/shard_map/all_to_all | solution.py:251
  53.0 2.7 %reshape.110.came_ref.own_ref.right_ref = bf16[256,4096]{1,0:T(8,128)(2,1)S(1)} reshape(bf16[128,2,4096]{2,1,0:T(2,128)(2,1)} %all-to-all-done) | data formatting | bytes 4194304 | tf_op jit(solution)/shard_map/reshape | solution.py:353
  57.1 10.0 %left_grads.1 = (bf16[256,4096]{1,0:T(8,128)(2,1)S(1)}, f32[256,2048]{1,0:T(8,128)S(1)}) custom-call(bf16[256,4096]{1,0:T(8,128)(2,1)} %copy-done.2, bf16[2048,4096]{1,0:T(8,128)(2,1)} %outer_grads.1.grad_ref), custom_call_target="tpu_custom_call" | custom-call | flops 6442450944 | bytes 22020096 | tf_op jit(solution)/shard_map/left_grads/pallas_call | solution.py:169
  67.3 1.2 collective-permute-start.1
  68.5 4.6 %right_grads.1 = bf16[256,2048]{1,0:T(8,128)(2,1)S(1)} custom-call(bf16[256,2048]{1,0:T(8,128)(2,1)S(1)} %collective-permute-done.other_ref, f32[256,2048]{1,0:T(8,128)S(1)} %get-tuple-element.25.partial_ref, bf16[2048,4096]{1,0:T(8,128)(2,1)} %outer_grads.1.grad_ref), custom_call_target="tpu_custom_call" | custom-call | flops 2147483648 | bytes 12582912 | tf_op jit(solution)/shard_map/right_grads/pallas_call | solution.py:191
  73.6 2.6 %reshape.111 = bf16[128,2,4096]{2,1,0:T(2,128)(2,1)} reshape(bf16[256,4096]{1,0:T(8,128)(2,1)S(1)} %pad_maximum_fusion) | data formatting | bytes 4194304 | tf_op jit(solution)/shard_map/reshape | solution.py:360
  76.3 4.8 %all-to-all-start.1 = ((bf16[128,2,4096]{2,1,0:T(2,128)(2,1)}), bf16[128,2,4096]{2,1,0:T(2,128)(2,1)}, u32[]{:S(2)}, u32[]{:S(2)}) async-start(bf16[128,2,4096]{2,1,0:T(2,128)(2,1)} %reshape.111), calls=%async_computation.1 | async-start | bytes 4194304 | tf_op jit(solution)/shard_map/all_to_all | solution.py:251
  81.2 14.7 %forward.1 = (bf16[64,128,128]{2,1,0:T(8,128)(2,1)S(1)}, f32[1024,128]{1,0:T(8,128)S(1)}) custom-call(s32[1]{0:T(128)} %bitcast.7.core_ref, bf16[256,4096]{1,0:T(8,128)(2,1)S(1)} %copy-done.3, bf16[256,2048]{1,0:T(8,128)(2,1)S(1)} %collective-permute-done.other_ref, bf16[256,4096]{1,0:T(8,128)(2,1)S(1)} %copy-done.3, bf16[128,1024]{1,0:T(8,128)(2,1)S(1)} %bitcast.105, ...), custom_call_target="tpu_custom_call" | custom-call | flops 8589934592 | bytes 8388608 | tf_op jit(solution)/shard_map/forward/pallas_call | solution.py:222
  95.9 1.4 copy-done.4
  98.1 1.2 collective-permute-start.2
  99.3 1.2 collective-permute-done.2
  102.0 2.4 %collective-permute-start.4 = (f32[16,8,128]{2,1,0:T(8,128)S(1)}, f32[16,8,128]{2,1,0:T(8,128)S(1)}, u32[]{:S(2)}, u32[]{:S(2)}) collective-permute-start(f32[16,8,128]{2,1,0:T(8,128)S(1)} %get-tuple-element.38), channel_id=1, source_target_pairs={{0,4},{1,5},{2,6},{3,7},{4,0},{5,1},{6,2},{7,3},{8,12},{9,13},{10,... | collective-permute-start | bytes 196616 | tf_op jit(solution)/shard_map/ppermute | solution.py:277
  105.4 4.3 %copy.73 = bf16[64,128,128]{2,0,1:T(8,128)(2,1)} copy(bf16[64,128,128]{2,1,0:T(8,128)(2,1)} %copy-done.4) | data formatting | bytes 4194304 | tf_op jit(solution)/shard_map/forward/pallas_call | solution.py:222
  111.2 2.7 %reshape.112 = bf16[256,4096]{1,0:T(8,128)(2,1)S(1)} reshape(bf16[128,2,4096]{2,1,0:T(2,128)(2,1)} %all-to-all-done.1) | data formatting | bytes 4194304 | tf_op jit(solution)/shard_map/reshape | solution.py:362
  117.7 1.6 %collective-permute-start.6 = (f32[32,256]{1,0:T(8,128)S(1)}, f32[32,256]{1,0:T(8,128)S(1)}, u32[]{:S(2)}, u32[]{:S(2)}) collective-permute-start(f32[32,256]{1,0:T(8,128)S(1)} %get-tuple-element.58), channel_id=1, source_target_pairs={{0,1},{1,0},{2,3},{3,2},{4,5},{5,4},{6,7},{7,6},{8,9},{9,8},{10,11... | collective-permute-start | bytes 98312 | tf_op jit(solution)/shard_map/ppermute | solution.py:277
  119.4 1.8 %fusion.32 = (f32[2,1024]{1,0:T(2,128)S(1)}, f32[2,1024]{1,0:T(2,128)S(1)}, f32[2,1024,256]{2,1,0:T(8,128)S(1)}) fusion(f32[2,1024]{1,0:T(2,128)S(1)} %add_rsqrt_fusion, f32[2,1024]{1,0:T(2,128)S(1)} %broadcast_multiply_fusion.2, bf16[2,1024,256]{2,1,0:T(8,128)(2,1)S(1)} %copy-done.7, f32[2,1024,256]{2,1,0:T(8,128)S(1)} %fusion.27, ...), kind=kOutput, calls=%fused_computation.78 | convolution fusion | flops 37220352 | bytes 5423104 | tf_op jit(solution)/shard_map/shr,ch->src/dot_general | solution.py:383
  121.3 2.7 %collective-permute-start.9 = (f32[32,256]{1,0:T(8,128)S(1)}, f32[32,256]{1,0:T(8,128)S(1)}, u32[]{:S(2)}, u32[]{:S(2)}) collective-permute-start(f32[32,256]{1,0:T(8,128)S(1)} %select_add_fusion), channel_id=1, source_target_pairs={{0,6},{1,7},{2,4},{3,5},{4,2},{5,3},{6,0},{7,1},{8,14},{9,15},{10,... | collective-permute-start | bytes 98312 | tf_op jit(solution)/shard_map/ppermute | solution.py:277
  124.0 1.7 %collective-permute-done.8 = f32[32,256]{1,0:T(8,128)S(1)} collective-permute-done((f32[32,256]{1,0:T(8,128)S(1)}, f32[32,256]{1,0:T(8,128)S(1)}, u32[]{:S(2)}, u32[]{:S(2)}) %collective-permute-start.8) | collective-permute-done | bytes 32800 | tf_op jit(solution)/shard_map/ppermute | solution.py:277
  126.9 2.5 %collective-permute-start.11 = (f32[32,384]{1,0:T(8,128)S(1)}, f32[32,384]{1,0:T(8,128)S(1)}, u32[]{:S(2)}, u32[]{:S(2)}) collective-permute-start(f32[32,384]{1,0:T(8,128)S(1)} %get-tuple-element.53), channel_id=1, source_target_pairs={{0,16},{1,17},{2,18},{3,19},{4,20},{5,21},{6,22},{7,23},{8,24},{9,... | collective-permute-start | bytes 147464 | tf_op jit(solution)/shard_map/ppermute | solution.py:277
  129.4 1.3 collective-permute-start.12
  130.7 2.4 %fusion.10 = bf16[2,1024,256]{2,1,0:T(8,128)(2,1)} fusion(bf16[2,1024,256]{2,1,0:T(8,128)(2,1)S(1)} %copy-done.7, f32[2,1024,256]{2,1,0:T(8,128)S(1)} %get-tuple-element.60, f32[2,1024]{1,0:T(2,128)S(1)} %get-tuple-element.61, f32[2,1024]{1,0:T(2,128)S(1)} %get-tuple-element.62, f32[2,1024]{1,0:T(2,128)S(1)} %add_rsqrt_fusion, ...), kind=kLoop, calls=%fused_computation.14 | loop fusion | flops 4194304 | bytes 4227072 | tf_op jit(solution)/shard_map/convert_element_type | solution.py:385
  134.2 1.0 collective-permute-start.13
  135.2 2.5 %collective-permute-start.14 = (f32[32,384]{1,0:T(8,128)S(1)}, f32[32,384]{1,0:T(8,128)S(1)}, u32[]{:S(2)}, u32[]{:S(2)}) collective-permute-start(f32[32,384]{1,0:T(8,128)S(1)} %get-tuple-element.50), channel_id=1, source_target_pairs={{0,64},{1,65},{2,66},{3,67},{4,68},{5,69},{6,70},{7,71},{8,72},{9,... | collective-permute-start | bytes 147464 | tf_op jit(solution)/shard_map/ppermute | solution.py:277
  138.1 1.6 %collective-permute-done.14 = f32[32,384]{1,0:T(8,128)S(1)} collective-permute-done((f32[32,384]{1,0:T(8,128)S(1)}, f32[32,384]{1,0:T(8,128)S(1)}, u32[]{:S(2)}, u32[]{:S(2)}) %collective-permute-start.14) | collective-permute-done | bytes 49184 | tf_op jit(solution)/shard_map/ppermute | solution.py:277
  139.7 2.1 %collective-permute-done.15 = f32[32,384]{1,0:T(8,128)S(1)} collective-permute-done((f32[32,384]{1,0:T(8,128)S(1)}, f32[32,384]{1,0:T(8,128)S(1)}, u32[]{:S(2)}, u32[]{:S(2)}) %collective-permute-start.15) | collective-permute-done | bytes 49184 | tf_op jit(solution)/shard_map/ppermute | solution.py:277
  141.9 4.7 %collective-permute-start.16 = (f32[32,256]{1,0:T(8,128)S(1)}, f32[32,256]{1,0:T(8,128)S(1)}, u32[]{:S(2)}, u32[]{:S(2)}) collective-permute-start(f32[32,256]{1,0:T(8,128)S(1)} %slice.50), channel_id=1, source_target_pairs={{0,1},{1,0},{2,3},{3,2},{4,5},{5,4},{6,7},{7,6},{8,9},{9,8},{10,11... | collective-permute-start | bytes 98312 | tf_op jit(solution)/shard_map/ppermute | solution.py:277
  (88 shorter events, 19.4 us)
Async XLA Ops:
  0.6 3.6 %copy-start = (bf16[256,32]{0,1:T(8,128)(2,1)S(1)}, bf16[256,32]{0,1:T(8,128)(2,1)}, u32[]{:S(2)}) copy-start(bf16[256,32]{0,1:T(8,128)(2,1)} %param.9) | copy-start | bytes 49156
  0.6 3.6 %copy-start.6 = (bf16[2,1024,256]{2,1,0:T(8,128)(2,1)S(1)}, bf16[2,1024,256]{2,1,0:T(8,128)(2,1)}, u32[]{:S(2)}) copy-start(bf16[2,1024,256]{2,1,0:T(8,128)(2,1)} %param.8) | copy-start | bytes 3145732
  2.3 3.6 %copy-start.9 = (bf16[256,32]{0,1:T(8,128)(2,1)S(1)}, bf16[256,32]{0,1:T(8,128)(2,1)}, u32[]{:S(2)}) copy-start(bf16[256,32]{0,1:T(8,128)(2,1)} %param.10) | copy-start | bytes 49156
  10.9 12.0 %copy-start.8 = (bf16[1024,128]{1,0:T(8,128)(2,1)S(1)}, bf16[1024,128]{1,0:T(8,128)(2,1)}, u32[]{:S(2)}) copy-start(bf16[1024,128]{1,0:T(8,128)(2,1)} %param.11) | copy-start | bytes 786436
  10.9 42.1 %all-to-all-start = ((bf16[128,2,4096]{2,1,0:T(2,128)(2,1)}), bf16[128,2,4096]{2,1,0:T(2,128)(2,1)}, u32[]{:S(2)}, u32[]{:S(2)}) async-start(bf16[128,2,4096]{2,1,0:T(2,128)(2,1)} %bitcast.108), calls=%async_computation | async-start | bytes 4194304 | tf_op jit(solution)/shard_map/all_to_all | solution.py:251
  26.3 9.7 %copy-start.1 = (bf16[128,64,128]{2,0,1:T(8,128)(2,1)}, bf16[128,64,128]{2,0,1:T(8,128)(2,1)S(1)}, u32[]{:S(2)}) copy-start(bf16[128,64,128]{2,0,1:T(8,128)(2,1)S(1)} %copy.74) | copy-start | bytes 6291460
  55.8 1.3 copy-start.2
  55.9 11.3 %collective-permute-start = (bf16[256,2048]{1,0:T(8,128)(2,1)S(1)}, bf16[256,2048]{1,0:T(8,128)(2,1)S(1)}, u32[]{:S(2)}, u32[]{:S(2)}) collective-permute-start(bf16[256,2048]{1,0:T(8,128)(2,1)S(1)} %slice.46), channel_id=1, source_target_pairs={{0,1},{1,0},{2,3},{3,2},{4,5},{5,4},{6,7},{7,6},{8,9},{9,8},{10,11... | collective-permute-start | bytes 3145736 | tf_op jit(solution)/shard_map/ppermute | solution.py:255
  67.3 5.8 %collective-permute-start.1 = (bf16[256,2048]{1,0:T(8,128)(2,1)S(1)}, bf16[256,2048]{1,0:T(8,128)(2,1)S(1)}, u32[]{:S(2)}, u32[]{:S(2)}) collective-permute-start(bf16[256,2048]{1,0:T(8,128)(2,1)S(1)} %slice.37), channel_id=1, source_target_pairs={{0,1},{1,0},{2,3},{3,2},{4,5},{5,4},{6,7},{7,6},{8,9},{9,8},{10,11... | collective-permute-start | bytes 3145736 | tf_op jit(solution)/shard_map/ppermute | solution.py:255
  76.3 4.9 %copy-start.11 = (bf16[128]{0:T(256)(128)(2,1)S(1)}, bf16[128]{0:T(256)(128)(2,1)}, u32[]{:S(2)}) copy-start(bf16[128]{0:T(256)(128)(2,1)} %param.12) | copy-start | bytes 772
  76.3 4.9 %copy-start.3 = (bf16[256,4096]{1,0:T(8,128)(2,1)S(1)}, bf16[256,4096]{1,0:T(8,128)(2,1)}, u32[]{:S(2)}) copy-start(bf16[256,4096]{1,0:T(8,128)(2,1)} %copy-done.2) | copy-start | bytes 6291460
  76.3 35.0 %all-to-all-start.1 = ((bf16[128,2,4096]{2,1,0:T(2,128)(2,1)}), bf16[128,2,4096]{2,1,0:T(2,128)(2,1)}, u32[]{:S(2)}, u32[]{:S(2)}) async-start(bf16[128,2,4096]{2,1,0:T(2,128)(2,1)} %reshape.111), calls=%async_computation.1 | async-start | bytes 4194304 | tf_op jit(solution)/shard_map/all_to_all | solution.py:251
  95.9 1.4 copy-start.4
  97.3 0.8 copy-start.5
  98.1 2.3 %collective-permute-start.2 = (f32[64,8,128]{2,1,0:T(8,128)S(1)}, f32[64,8,128]{2,1,0:T(8,128)S(1)}, u32[]{:S(2)}, u32[]{:S(2)}) collective-permute-start(f32[64,8,128]{2,1,0:T(8,128)S(1)} %dynamic-slice_bitcast_fusion), channel_id=1, source_target_pairs={{0,1},{1,0},{2,3},{3,2},{4,5},{5,4},{6,7},{7,6},{8,9},{9,8},{10,11... | collective-permute-start | bytes 786440 | tf_op jit(solution)/shard_map/ppermute | solution.py:277
  101.5 8.2 %collective-permute-start.3 = (f32[16,8,128]{2,1,0:T(8,128)S(1)}, f32[16,8,128]{2,1,0:T(8,128)S(1)}, u32[]{:S(2)}, u32[]{:S(2)}) collective-permute-start(f32[16,8,128]{2,1,0:T(8,128)S(1)} %get-tuple-element.39), channel_id=1, source_target_pairs={{0,2},{1,3},{2,0},{3,1},{4,6},{5,7},{6,4},{7,5},{8,10},{9,11},{10,... | collective-permute-start | bytes 196616 | tf_op jit(solution)/shard_map/ppermute | solution.py:277
  102.0 7.6 %collective-permute-start.4 = (f32[16,8,128]{2,1,0:T(8,128)S(1)}, f32[16,8,128]{2,1,0:T(8,128)S(1)}, u32[]{:S(2)}, u32[]{:S(2)}) collective-permute-start(f32[16,8,128]{2,1,0:T(8,128)S(1)} %get-tuple-element.38), channel_id=1, source_target_pairs={{0,4},{1,5},{2,6},{3,7},{4,0},{5,1},{6,2},{7,3},{8,12},{9,13},{10,... | collective-permute-start | bytes 196616 | tf_op jit(solution)/shard_map/ppermute | solution.py:277
  104.5 5.7 %collective-permute-start.5 = (f32[16,8,128]{2,1,0:T(8,128)S(1)}, f32[16,8,128]{2,1,0:T(8,128)S(1)}, u32[]{:S(2)}, u32[]{:S(2)}) collective-permute-start(f32[16,8,128]{2,1,0:T(8,128)S(1)} %get-tuple-element.37), channel_id=1, source_target_pairs={{0,6},{1,7},{2,4},{3,5},{4,2},{5,3},{6,0},{7,1},{8,14},{9,15},{10,... | collective-permute-start | bytes 196616 | tf_op jit(solution)/shard_map/ppermute | solution.py:277
  110.2 3.8 %copy-start.10 = (bf16[32,256]{1,0:T(8,128)(2,1)S(1)}, bf16[32,256]{1,0:T(8,128)(2,1)}, u32[]{:S(2)}) copy-start(bf16[32,256]{1,0:T(8,128)(2,1)} %constant.144.clone) | copy-start | bytes 49156
  110.2 4.1 %copy-start.7 = (bf16[2,1024,256]{2,1,0:T(8,128)(2,1)S(1)}, bf16[2,1024,256]{2,1,0:T(8,128)(2,1)}, u32[]{:S(2)}) copy-start(bf16[2,1024,256]{2,1,0:T(8,128)(2,1)} %param.8) | copy-start | bytes 3145732
  117.7 3.5 %collective-permute-start.6 = (f32[32,256]{1,0:T(8,128)S(1)}, f32[32,256]{1,0:T(8,128)S(1)}, u32[]{:S(2)}, u32[]{:S(2)}) collective-permute-start(f32[32,256]{1,0:T(8,128)S(1)} %get-tuple-element.58), channel_id=1, source_target_pairs={{0,1},{1,0},{2,3},{3,2},{4,5},{5,4},{6,7},{7,6},{8,9},{9,8},{10,11... | collective-permute-start | bytes 98312 | tf_op jit(solution)/shard_map/ppermute | solution.py:277
  121.2 4.5 %collective-permute-start.8 = (f32[32,256]{1,0:T(8,128)S(1)}, f32[32,256]{1,0:T(8,128)S(1)}, u32[]{:S(2)}, u32[]{:S(2)}) collective-permute-start(f32[32,256]{1,0:T(8,128)S(1)} %select_add_fusion), channel_id=1, source_target_pairs={{0,4},{1,5},{2,6},{3,7},{4,0},{5,1},{6,2},{7,3},{8,12},{9,13},{10,... | collective-permute-start | bytes 98312 | tf_op jit(solution)/shard_map/ppermute | solution.py:277
  121.3 5.1 %collective-permute-start.9 = (f32[32,256]{1,0:T(8,128)S(1)}, f32[32,256]{1,0:T(8,128)S(1)}, u32[]{:S(2)}, u32[]{:S(2)}) collective-permute-start(f32[32,256]{1,0:T(8,128)S(1)} %select_add_fusion), channel_id=1, source_target_pairs={{0,6},{1,7},{2,4},{3,5},{4,2},{5,3},{6,0},{7,1},{8,14},{9,15},{10,... | collective-permute-start | bytes 98312 | tf_op jit(solution)/shard_map/ppermute | solution.py:277
  124.0 2.8 %collective-permute-start.7 = (f32[32,256]{1,0:T(8,128)S(1)}, f32[32,256]{1,0:T(8,128)S(1)}, u32[]{:S(2)}, u32[]{:S(2)}) collective-permute-start(f32[32,256]{1,0:T(8,128)S(1)} %select_add_fusion), channel_id=1, source_target_pairs={{0,2},{1,3},{2,0},{3,1},{4,6},{5,7},{6,4},{7,5},{8,10},{9,11},{10,... | collective-permute-start | bytes 98312 | tf_op jit(solution)/shard_map/ppermute | solution.py:277
  126.8 6.3 %collective-permute-start.10 = (f32[32,384]{1,0:T(8,128)S(1)}, f32[32,384]{1,0:T(8,128)S(1)}, u32[]{:S(2)}, u32[]{:S(2)}) collective-permute-start(f32[32,384]{1,0:T(8,128)S(1)} %get-tuple-element.52), channel_id=1, source_target_pairs={{0,8},{1,9},{2,10},{3,11},{4,12},{5,13},{6,14},{7,15},{8,0},{9,1},... | collective-permute-start | bytes 147464 | tf_op jit(solution)/shard_map/ppermute | solution.py:277
  126.9 6.2 %collective-permute-start.11 = (f32[32,384]{1,0:T(8,128)S(1)}, f32[32,384]{1,0:T(8,128)S(1)}, u32[]{:S(2)}, u32[]{:S(2)}) collective-permute-start(f32[32,384]{1,0:T(8,128)S(1)} %get-tuple-element.53), channel_id=1, source_target_pairs={{0,16},{1,17},{2,18},{3,19},{4,20},{5,21},{6,22},{7,23},{8,24},{9,... | collective-permute-start | bytes 147464 | tf_op jit(solution)/shard_map/ppermute | solution.py:277
  129.4 4.7 %collective-permute-start.12 = (f32[32,384]{1,0:T(8,128)S(1)}, f32[32,384]{1,0:T(8,128)S(1)}, u32[]{:S(2)}, u32[]{:S(2)}) collective-permute-start(f32[32,384]{1,0:T(8,128)S(1)} %get-tuple-element.51), channel_id=1, source_target_pairs={{0,24},{1,25},{2,26},{3,27},{4,28},{5,29},{6,30},{7,31},{8,16},{9,... | collective-permute-start | bytes 147464 | tf_op jit(solution)/shard_map/ppermute | solution.py:277
  134.2 3.9 %collective-permute-start.13 = (f32[32,384]{1,0:T(8,128)S(1)}, f32[32,384]{1,0:T(8,128)S(1)}, u32[]{:S(2)}, u32[]{:S(2)}) collective-permute-start(f32[32,384]{1,0:T(8,128)S(1)} %get-tuple-element.49), channel_id=1, source_target_pairs={{0,32},{1,33},{2,34},{3,35},{4,36},{5,37},{6,38},{7,39},{8,40},{9,... | collective-permute-start | bytes 147464 | tf_op jit(solution)/shard_map/ppermute | solution.py:277
  135.2 4.5 %collective-permute-start.14 = (f32[32,384]{1,0:T(8,128)S(1)}, f32[32,384]{1,0:T(8,128)S(1)}, u32[]{:S(2)}, u32[]{:S(2)}) collective-permute-start(f32[32,384]{1,0:T(8,128)S(1)} %get-tuple-element.50), channel_id=1, source_target_pairs={{0,64},{1,65},{2,66},{3,67},{4,68},{5,69},{6,70},{7,71},{8,72},{9,... | collective-permute-start | bytes 147464 | tf_op jit(solution)/shard_map/ppermute | solution.py:277
  137.7 4.2 %collective-permute-start.15 = (f32[32,384]{1,0:T(8,128)S(1)}, f32[32,384]{1,0:T(8,128)S(1)}, u32[]{:S(2)}, u32[]{:S(2)}) collective-permute-start(f32[32,384]{1,0:T(8,128)S(1)} %get-tuple-element.48), channel_id=1, source_target_pairs={{0,96},{1,97},{2,98},{3,99},{4,100},{5,101},{6,102},{7,103},{8,104... | collective-permute-start | bytes 147464 | tf_op jit(solution)/shard_map/ppermute | solution.py:277
  141.9 5.5 %collective-permute-start.16 = (f32[32,256]{1,0:T(8,128)S(1)}, f32[32,256]{1,0:T(8,128)S(1)}, u32[]{:S(2)}, u32[]{:S(2)}) collective-permute-start(f32[32,256]{1,0:T(8,128)S(1)} %slice.50), channel_id=1, source_target_pairs={{0,1},{1,0},{2,3},{3,2},{4,5},{5,4},{6,7},{7,6},{8,9},{9,8},{10,11... | collective-permute-start | bytes 98312 | tf_op jit(solution)/shard_map/ppermute | solution.py:277

commit v7 on v6

--- a/solution.py
+++ b/solution.py
@@ -365,7 +365,7 @@
     early = 2
     weight_term = weight_term.reshape(devices, -1, pair_width)
     weight_term = sum_scatter(weight_term, permute_groups()[:early])
-    back, weight_term, pair_update = lax.optimization_barrier((back, weight_term, pair_update))
+    back, weight_term = lax.optimization_barrier((back, weight_term))
 
     place = np.indices((row_count, chips, CORES, local)).reshape(4, -1)
     left_place = (place[3] * row_count + place[0]) * CORES + place[2]
@@ -383,9 +383,8 @@
     upstream = jnp.einsum("shr,ch->src", left_grad, left_weight, preferred_element_type=jnp.float32)
     upstream += jnp.einsum("srh,ch->src", right_grad, right_weight, preferred_element_type=jnp.float32)
     grad_alignment = norm_backward(upstream, normed, inv_sigma).astype(jnp.bfloat16)
-    grad_alignment = row_major(grad_alignment)
-    left_wgrad, right_wgrad, weight_term, grad_alignment = sum_all(
-        left_wgrad, right_wgrad, weight_term, early, grad_alignment
+    left_wgrad, right_wgrad, weight_term, pair_update = sum_all(
+        left_wgrad, right_wgrad, weight_term, early, pair_update
     )
     grad_out_weight = weight_term.reshape(-1, pair_width)
     return (pair_update, grad_alignment, grad_out_weight, left_wgrad.T, right_wgrad.T)

time: 149 us -> 146 us (0.980)
  other arithmetic: 8.2 us -> 3.4 us
  matrix products: 6.9 us -> 4.08 us
  local copies, waits for them, and re-layouts: 21.7 us -> 24.5 us
  waiting for transfers between devices: 27.6 us -> 29.4 us
    unnamed x27 -> x29, local copies, waits for them, and re-layouts: 5.56 us -> 8.36 us
    ppermute x15, waiting for transfers between devices: 9.48 us -> 11.3 us  [partner(): lax.ppermute(part, BOTH, [(i, i ^ mask) for i in range(lax.axis_size(BOTH...]
    convert_element_type x1, other arithmetic: 2.35 us -> 0.57 us  [body(): norm_backward(upstream, normed, inv_sigma).astype(jnp.bfloat16)]
    reduce_sum x1, other arithmetic: 1.87 us -> 0.3 us  [layer_norm(): jnp.mean(centered * centered, axis=-1, keepdims=True) + 1e-05]
  transfers between devices with their start and end apart: 19 -> 19, of which waited for: 11 -> 11; matrix products, arithmetic and copies ran while one was open for 9% -> 8% of each run, Pallas kernels for 26% -> 27%
where the time goes in v7:
time: 146 us; the launch traced here: 145 us
  Pallas kernels  41.4 us (28%)
  starting transfers between devices  41 us (28%)
  waiting for transfers between devices  29.4 us (20%)
  local copies, waits for them, and re-layouts  24.5 us (17%)
  matrix products  4.08 us (3%)
  other arithmetic  3.4 us (2%)
    ppermute x15, starting transfers between devices, partner(): lax.ppermute(part, BOTH, [(i, i ^ mask) for i in range(lax.axis_size(BOTH...  22 us
    all_to_all x2, waiting for transfers between devices, exchange(): return lax.all_to_all(blocks, BOTH, 0, 0, tiled=True)  18.1 us
    all_to_all x2, starting transfers between devices, exchange(): return lax.all_to_all(blocks, BOTH, 0, 0, tiled=True)  16.8 us
    pallas_call x1, Pallas kernels, forward(): pl.pallas_call(functools.partial(forward_kernel, 1.0 / seqs, width), grid...  14.7 us
    ppermute x15, waiting for transfers between devices, partner(): lax.ppermute(part, BOTH, [(i, i ^ mask) for i in range(lax.axis_size(BOTH...  11.3 us
    pallas_call x1, Pallas kernels, left_grads(): pl.pallas_call(functools.partial(left_kernel, 1.0 / seqs), in_specs=[pl.B...  10 us
    pallas_call x1, Pallas kernels, outer_grads(): pl.pallas_call(functools.partial(outer_grad_kernel, width), grid=(cols //...  9.65 us
    unnamed x29, local copies, waits for them, and re-layouts  8.36 us
  transfers between devices with their start and end apart: 19, of which 11 were waited for; matrix products, arithmetic and copies ran while one was open for 8% of the time, Pallas kernels for 27%

profile of v7, /device:TPU:1, one launch (start us, length us, event | category | flops | bytes accessed | tf_op | source)
XLA Modules:
  0.0 145.0 jit_solution(3054545470949499539)
XLA Ops:
  0.6 1.5 %copy.47 = bf16[2,1024,256]{1,2,0:T(8,128)(2,1)S(1)} copy(bf16[2,1024,256]{2,1,0:T(8,128)(2,1)} %param.8) | data formatting | bytes 2097152 | tf_op args[0]
  5.8 2.4 %pack.1 = bf16[8,8,2,2,4096]{4,3,2,1,0:T(2,128)(2,1)} custom-call(bf16[8,2,2,2048]{3,2,1,0:T(2,128)(2,1)} %reshape.107.left_ref, bf16[8,2,2,2048]{3,2,1,0:T(2,128)(2,1)} %bitcast.112), custom_call_target="tpu_custom_call" | custom-call | bytes 2097152 | tf_op jit(solution)/shard_map/pack/pallas_call | solution.py:206
  8.3 12.0 %all-to-all-start = ((bf16[128,2,4096]{2,1,0:T(2,128)(2,1)}), bf16[128,2,4096]{2,1,0:T(2,128)(2,1)}, u32[]{:S(2)}, u32[]{:S(2)}) async-start(bf16[128,2,4096]{2,1,0:T(2,128)(2,1)} %bitcast.108), calls=%async_computation | async-start | bytes 4194304 | tf_op jit(solution)/shard_map/all_to_all | solution.py:251
  20.7 2.9 %copy.88 = bf16[128,64,128]{2,0,1:T(8,128)(2,1)S(1)} copy(bf16[128,64,128]{2,1,0:T(8,128)(2,1)} %param.13) | data formatting | bytes 4194304 | tf_op args[5]
  23.7 9.7 %outer_grads.1.grad_ref = bf16[2048,4096]{1,0:T(8,128)(2,1)} custom-call(bf16[1024,128]{1,0:T(8,128)(2,1)S(1)} %copy.57.weight_ref, bf16[64,128,128]{2,1,0:T(8,128)(2,1)S(1)} %bitcast.103), custom_call_target="tpu_custom_call" | custom-call | flops 2147483648 | bytes 18874368 | tf_op jit(solution)/shard_map/outer_grads/pallas_call | solution.py:152
  33.3 17.1 %all-to-all-done = bf16[128,2,4096]{2,1,0:T(2,128)(2,1)} async-done(((bf16[128,2,4096]{2,1,0:T(2,128)(2,1)}), bf16[128,2,4096]{2,1,0:T(2,128)(2,1)}, u32[]{:S(2)}, u32[]{:S(2)}) %all-to-all-start) | async-done | bytes 2097184 | tf_op jit(solution)/shard_map/all_to_all | solution.py:251
  50.4 2.7 %reshape.110.came_ref.own_ref.right_ref = bf16[256,4096]{1,0:T(8,128)(2,1)S(1)} reshape(bf16[128,2,4096]{2,1,0:T(2,128)(2,1)} %all-to-all-done) | data formatting | bytes 4194304 | tf_op jit(solution)/shard_map/reshape | solution.py:353
  54.5 10.0 %left_grads.1 = (bf16[256,4096]{1,0:T(8,128)(2,1)S(1)}, f32[256,2048]{1,0:T(8,128)S(1)}) custom-call(bf16[256,4096]{1,0:T(8,128)(2,1)} %copy-done.2, bf16[2048,4096]{1,0:T(8,128)(2,1)} %outer_grads.1.grad_ref), custom_call_target="tpu_custom_call" | custom-call | flops 6442450944 | bytes 22020096 | tf_op jit(solution)/shard_map/left_grads/pallas_call | solution.py:169
  64.6 1.2 collective-permute-start.1
  65.8 4.6 %right_grads.1 = bf16[256,2048]{1,0:T(8,128)(2,1)S(1)} custom-call(bf16[256,2048]{1,0:T(8,128)(2,1)S(1)} %collective-permute-done.other_ref, f32[256,2048]{1,0:T(8,128)S(1)} %get-tuple-element.24.partial_ref, bf16[2048,4096]{1,0:T(8,128)(2,1)} %outer_grads.1.grad_ref), custom_call_target="tpu_custom_call" | custom-call | flops 2147483648 | bytes 12582912 | tf_op jit(solution)/shard_map/right_grads/pallas_call | solution.py:191
  71.0 2.6 %reshape.111 = bf16[128,2,4096]{2,1,0:T(2,128)(2,1)} reshape(bf16[256,4096]{1,0:T(8,128)(2,1)S(1)} %pad_maximum_fusion) | data formatting | bytes 4194304 | tf_op jit(solution)/shard_map/reshape | solution.py:360
  73.6 4.8 %all-to-all-start.1 = ((bf16[128,2,4096]{2,1,0:T(2,128)(2,1)}), bf16[128,2,4096]{2,1,0:T(2,128)(2,1)}, u32[]{:S(2)}, u32[]{:S(2)}) async-start(bf16[128,2,4096]{2,1,0:T(2,128)(2,1)} %reshape.111), calls=%async_computation.1 | async-start | bytes 4194304 | tf_op jit(solution)/shard_map/all_to_all | solution.py:251
  78.5 14.7 %forward.1 = (bf16[64,128,128]{2,1,0:T(8,128)(2,1)S(1)}, f32[1024,128]{1,0:T(8,128)S(1)}) custom-call(s32[1]{0:T(128)} %bitcast.7.core_ref, bf16[256,4096]{1,0:T(8,128)(2,1)S(1)} %copy-done.3, bf16[256,2048]{1,0:T(8,128)(2,1)S(1)} %collective-permute-done.other_ref, bf16[256,4096]{1,0:T(8,128)(2,1)S(1)} %copy-done.3, bf16[128,1024]{1,0:T(8,128)(2,1)S(1)} %bitcast.105, ...), custom_call_target="tpu_custom_call" | custom-call | flops 8589934592 | bytes 8388608 | tf_op jit(solution)/shard_map/forward/pallas_call | solution.py:222
  93.3 1.4 copy-done.4
  95.5 1.2 collective-permute-start.2
  96.6 1.2 collective-permute-done.2
  99.4 2.4 %collective-permute-start.4 = (f32[16,8,128]{2,1,0:T(8,128)S(1)}, f32[16,8,128]{2,1,0:T(8,128)S(1)}, u32[]{:S(2)}, u32[]{:S(2)}) collective-permute-start(f32[16,8,128]{2,1,0:T(8,128)S(1)} %get-tuple-element.51), channel_id=1, source_target_pairs={{0,4},{1,5},{2,6},{3,7},{4,0},{5,1},{6,2},{7,3},{8,12},{9,13},{10,... | collective-permute-start | bytes 196616 | tf_op jit(solution)/shard_map/ppermute | solution.py:277
  102.8 4.3 %copy.87 = bf16[64,128,128]{2,0,1:T(8,128)(2,1)} copy(bf16[64,128,128]{2,1,0:T(8,128)(2,1)} %copy-done.4) | data formatting | bytes 4194304 | tf_op jit(solution)/shard_map/forward/pallas_call | solution.py:222
  108.6 2.7 %reshape.112 = bf16[256,4096]{1,0:T(8,128)(2,1)S(1)} reshape(bf16[128,2,4096]{2,1,0:T(2,128)(2,1)} %all-to-all-done.1) | data formatting | bytes 4194304 | tf_op jit(solution)/shard_map/reshape | solution.py:362
  114.0 1.5 %collective-permute-start.6 = (f32[32,256]{1,0:T(8,128)S(1)}, f32[32,256]{1,0:T(8,128)S(1)}, u32[]{:S(2)}, u32[]{:S(2)}) collective-permute-start(f32[32,256]{1,0:T(8,128)S(1)} %get-tuple-element.71), channel_id=1, source_target_pairs={{0,1},{1,0},{2,3},{3,2},{4,5},{5,4},{6,7},{7,6},{8,9},{9,8},{10,11... | collective-permute-start | bytes 98312 | tf_op jit(solution)/shard_map/ppermute | solution.py:277
  116.3 2.7 %collective-permute-start.9 = (f32[32,256]{1,0:T(8,128)S(1)}, f32[32,256]{1,0:T(8,128)S(1)}, u32[]{:S(2)}, u32[]{:S(2)}) collective-permute-start(f32[32,256]{1,0:T(8,128)S(1)} %select_add_fusion), channel_id=1, source_target_pairs={{0,6},{1,7},{2,4},{3,5},{4,2},{5,3},{6,0},{7,1},{8,14},{9,15},{10,... | collective-permute-start | bytes 98312 | tf_op jit(solution)/shard_map/ppermute | solution.py:277
  119.0 1.6 %collective-permute-done.8 = f32[32,256]{1,0:T(8,128)S(1)} collective-permute-done((f32[32,256]{1,0:T(8,128)S(1)}, f32[32,256]{1,0:T(8,128)S(1)}, u32[]{:S(2)}, u32[]{:S(2)}) %collective-permute-start.8) | collective-permute-done | bytes 32800 | tf_op jit(solution)/shard_map/ppermute | solution.py:277
  120.9 1.1 collective-permute-done.7
  122.2 2.2 %collective-permute-start.11 = (f32[32,384]{1,0:T(8,128)S(1)}, f32[32,384]{1,0:T(8,128)S(1)}, u32[]{:S(2)}, u32[]{:S(2)}) collective-permute-start(f32[32,384]{1,0:T(8,128)S(1)} %get-tuple-element.66), channel_id=1, source_target_pairs={{0,16},{1,17},{2,18},{3,19},{4,20},{5,21},{6,22},{7,23},{8,24},{9,... | collective-permute-start | bytes 147464 | tf_op jit(solution)/shard_map/ppermute | solution.py:277
  124.4 1.6 %collective-permute-start.12 = (f32[32,384]{1,0:T(8,128)S(1)}, f32[32,384]{1,0:T(8,128)S(1)}, u32[]{:S(2)}, u32[]{:S(2)}) collective-permute-start(f32[32,384]{1,0:T(8,128)S(1)} %get-tuple-element.64), channel_id=1, source_target_pairs={{0,24},{1,25},{2,26},{3,27},{4,28},{5,29},{6,30},{7,31},{8,16},{9,... | collective-permute-start | bytes 147464 | tf_op jit(solution)/shard_map/ppermute | solution.py:277
  126.7 2.1 %collective-permute-done.12 = f32[32,384]{1,0:T(8,128)S(1)} collective-permute-done((f32[32,384]{1,0:T(8,128)S(1)}, f32[32,384]{1,0:T(8,128)S(1)}, u32[]{:S(2)}, u32[]{:S(2)}) %collective-permute-start.12) | collective-permute-done | bytes 49184 | tf_op jit(solution)/shard_map/ppermute | solution.py:277
  128.9 1.6 %collective-permute-start.13 = (f32[32,384]{1,0:T(8,128)S(1)}, f32[32,384]{1,0:T(8,128)S(1)}, u32[]{:S(2)}, u32[]{:S(2)}) collective-permute-start(f32[32,384]{1,0:T(8,128)S(1)} %get-tuple-element.62), channel_id=1, source_target_pairs={{0,32},{1,33},{2,34},{3,35},{4,36},{5,37},{6,38},{7,39},{8,40},{9,... | collective-permute-start | bytes 147464 | tf_op jit(solution)/shard_map/ppermute | solution.py:277
  130.5 2.5 %collective-permute-start.14 = (f32[32,384]{1,0:T(8,128)S(1)}, f32[32,384]{1,0:T(8,128)S(1)}, u32[]{:S(2)}, u32[]{:S(2)}) collective-permute-start(f32[32,384]{1,0:T(8,128)S(1)} %get-tuple-element.63), channel_id=1, source_target_pairs={{0,64},{1,65},{2,66},{3,67},{4,68},{5,69},{6,70},{7,71},{8,72},{9,... | collective-permute-start | bytes 147464 | tf_op jit(solution)/shard_map/ppermute | solution.py:277
  133.0 2.0 %collective-permute-done.14 = f32[32,384]{1,0:T(8,128)S(1)} collective-permute-done((f32[32,384]{1,0:T(8,128)S(1)}, f32[32,384]{1,0:T(8,128)S(1)}, u32[]{:S(2)}, u32[]{:S(2)}) %collective-permute-start.14) | collective-permute-done | bytes 49184 | tf_op jit(solution)/shard_map/ppermute | solution.py:277
  135.0 2.1 %collective-permute-done.15 = f32[32,384]{1,0:T(8,128)S(1)} collective-permute-done((f32[32,384]{1,0:T(8,128)S(1)}, f32[32,384]{1,0:T(8,128)S(1)}, u32[]{:S(2)}, u32[]{:S(2)}) %collective-permute-start.15) | collective-permute-done | bytes 49184 | tf_op jit(solution)/shard_map/ppermute | solution.py:277
  137.2 4.7 %collective-permute-start.16 = (f32[32,256]{1,0:T(8,128)S(1)}, f32[32,256]{1,0:T(8,128)S(1)}, u32[]{:S(2)}, u32[]{:S(2)}) collective-permute-start(f32[32,256]{1,0:T(8,128)S(1)} %slice.50), channel_id=1, source_target_pairs={{0,1},{1,0},{2,3},{3,2},{4,5},{5,4},{6,7},{7,6},{8,9},{9,8},{10,11... | collective-permute-start | bytes 98312 | tf_op jit(solution)/shard_map/ppermute | solution.py:277
  142.5 1.3 copy.64
  (90 shorter events, 17.4 us)
Async XLA Ops:
  0.6 2.1 %copy-start = (bf16[256,32]{0,1:T(8,128)(2,1)S(1)}, bf16[256,32]{0,1:T(8,128)(2,1)}, u32[]{:S(2)}) copy-start(bf16[256,32]{0,1:T(8,128)(2,1)} %param.9) | copy-start | bytes 49156
  2.1 1.7 %copy-start.6 = (bf16[2,1024,256]{1,2,0:T(8,128)(2,1)}, bf16[2,1024,256]{1,2,0:T(8,128)(2,1)S(1)}, u32[]{:S(2)}) copy-start(bf16[2,1024,256]{1,2,0:T(8,128)(2,1)S(1)} %copy.47) | copy-start | bytes 3145732
  2.2 1.7 %copy-start.9 = (bf16[256,32]{0,1:T(8,128)(2,1)S(1)}, bf16[256,32]{0,1:T(8,128)(2,1)}, u32[]{:S(2)}) copy-start(bf16[256,32]{0,1:T(8,128)(2,1)} %param.10) | copy-start | bytes 49156
  8.3 12.0 %copy-start.8 = (bf16[1024,128]{1,0:T(8,128)(2,1)S(1)}, bf16[1024,128]{1,0:T(8,128)(2,1)}, u32[]{:S(2)}) copy-start(bf16[1024,128]{1,0:T(8,128)(2,1)} %param.11) | copy-start | bytes 786436
  8.3 42.1 %all-to-all-start = ((bf16[128,2,4096]{2,1,0:T(2,128)(2,1)}), bf16[128,2,4096]{2,1,0:T(2,128)(2,1)}, u32[]{:S(2)}, u32[]{:S(2)}) async-start(bf16[128,2,4096]{2,1,0:T(2,128)(2,1)} %bitcast.108), calls=%async_computation | async-start | bytes 4194304 | tf_op jit(solution)/shard_map/all_to_all | solution.py:251
  23.7 9.7 %copy-start.1 = (bf16[128,64,128]{2,0,1:T(8,128)(2,1)}, bf16[128,64,128]{2,0,1:T(8,128)(2,1)S(1)}, u32[]{:S(2)}) copy-start(bf16[128,64,128]{2,0,1:T(8,128)(2,1)S(1)} %copy.88) | copy-start | bytes 6291460
  53.2 1.3 copy-start.2
  53.2 11.3 %collective-permute-start = (bf16[256,2048]{1,0:T(8,128)(2,1)S(1)}, bf16[256,2048]{1,0:T(8,128)(2,1)S(1)}, u32[]{:S(2)}, u32[]{:S(2)}) collective-permute-start(bf16[256,2048]{1,0:T(8,128)(2,1)S(1)} %slice.46), channel_id=1, source_target_pairs={{0,1},{1,0},{2,3},{3,2},{4,5},{5,4},{6,7},{7,6},{8,9},{9,8},{10,11... | collective-permute-start | bytes 3145736 | tf_op jit(solution)/shard_map/ppermute | solution.py:255
  64.6 5.8 %collective-permute-start.1 = (bf16[256,2048]{1,0:T(8,128)(2,1)S(1)}, bf16[256,2048]{1,0:T(8,128)(2,1)S(1)}, u32[]{:S(2)}, u32[]{:S(2)}) collective-permute-start(bf16[256,2048]{1,0:T(8,128)(2,1)S(1)} %slice.37), channel_id=1, source_target_pairs={{0,1},{1,0},{2,3},{3,2},{4,5},{5,4},{6,7},{7,6},{8,9},{9,8},{10,11... | collective-permute-start | bytes 3145736 | tf_op jit(solution)/shard_map/ppermute | solution.py:255
  73.6 4.9 %copy-start.11 = (bf16[128]{0:T(256)(128)(2,1)S(1)}, bf16[128]{0:T(256)(128)(2,1)}, u32[]{:S(2)}) copy-start(bf16[128]{0:T(256)(128)(2,1)} %param.12) | copy-start | bytes 772
  73.6 4.9 %copy-start.3 = (bf16[256,4096]{1,0:T(8,128)(2,1)S(1)}, bf16[256,4096]{1,0:T(8,128)(2,1)}, u32[]{:S(2)}) copy-start(bf16[256,4096]{1,0:T(8,128)(2,1)} %copy-done.2) | copy-start | bytes 6291460
  73.6 35.0 %all-to-all-start.1 = ((bf16[128,2,4096]{2,1,0:T(2,128)(2,1)}), bf16[128,2,4096]{2,1,0:T(2,128)(2,1)}, u32[]{:S(2)}, u32[]{:S(2)}) async-start(bf16[128,2,4096]{2,1,0:T(2,128)(2,1)} %reshape.111), calls=%async_computation.1 | async-start | bytes 4194304 | tf_op jit(solution)/shard_map/all_to_all | solution.py:251
  93.3 1.4 copy-start.4
  94.7 0.8 copy-start.5
  95.5 2.3 %collective-permute-start.2 = (f32[64,8,128]{2,1,0:T(8,128)S(1)}, f32[64,8,128]{2,1,0:T(8,128)S(1)}, u32[]{:S(2)}, u32[]{:S(2)}) collective-permute-start(f32[64,8,128]{2,1,0:T(8,128)S(1)} %dynamic-slice_bitcast_fusion), channel_id=1, source_target_pairs={{0,1},{1,0},{2,3},{3,2},{4,5},{5,4},{6,7},{7,6},{8,9},{9,8},{10,11... | collective-permute-start | bytes 786440 | tf_op jit(solution)/shard_map/ppermute | solution.py:277
  98.8 8.2 %collective-permute-start.3 = (f32[16,8,128]{2,1,0:T(8,128)S(1)}, f32[16,8,128]{2,1,0:T(8,128)S(1)}, u32[]{:S(2)}, u32[]{:S(2)}) collective-permute-start(f32[16,8,128]{2,1,0:T(8,128)S(1)} %get-tuple-element.52), channel_id=1, source_target_pairs={{0,2},{1,3},{2,0},{3,1},{4,6},{5,7},{6,4},{7,5},{8,10},{9,11},{10,... | collective-permute-start | bytes 196616 | tf_op jit(solution)/shard_map/ppermute | solution.py:277
  99.4 7.6 %collective-permute-start.4 = (f32[16,8,128]{2,1,0:T(8,128)S(1)}, f32[16,8,128]{2,1,0:T(8,128)S(1)}, u32[]{:S(2)}, u32[]{:S(2)}) collective-permute-start(f32[16,8,128]{2,1,0:T(8,128)S(1)} %get-tuple-element.51), channel_id=1, source_target_pairs={{0,4},{1,5},{2,6},{3,7},{4,0},{5,1},{6,2},{7,3},{8,12},{9,13},{10,... | collective-permute-start | bytes 196616 | tf_op jit(solution)/shard_map/ppermute | solution.py:277
  101.8 5.7 %collective-permute-start.5 = (f32[16,8,128]{2,1,0:T(8,128)S(1)}, f32[16,8,128]{2,1,0:T(8,128)S(1)}, u32[]{:S(2)}, u32[]{:S(2)}) collective-permute-start(f32[16,8,128]{2,1,0:T(8,128)S(1)} %get-tuple-element.50), channel_id=1, source_target_pairs={{0,6},{1,7},{2,4},{3,5},{4,2},{5,3},{6,0},{7,1},{8,14},{9,15},{10,... | collective-permute-start | bytes 196616 | tf_op jit(solution)/shard_map/ppermute | solution.py:277
  107.6 3.8 %copy-start.10 = (bf16[32,256]{1,0:T(8,128)(2,1)S(1)}, bf16[32,256]{1,0:T(8,128)(2,1)}, u32[]{:S(2)}) copy-start(bf16[32,256]{1,0:T(8,128)(2,1)} %constant.144.clone) | copy-start | bytes 49156
  107.6 4.1 %copy-start.7 = (bf16[2,1024,256]{1,2,0:T(8,128)(2,1)S(1)}, bf16[2,1024,256]{1,2,0:T(8,128)(2,1)}, u32[]{:S(2)}) copy-start(bf16[2,1024,256]{1,2,0:T(8,128)(2,1)} %copy-done.6) | copy-start | bytes 3145732
  114.0 2.3 %collective-permute-start.6 = (f32[32,256]{1,0:T(8,128)S(1)}, f32[32,256]{1,0:T(8,128)S(1)}, u32[]{:S(2)}, u32[]{:S(2)}) collective-permute-start(f32[32,256]{1,0:T(8,128)S(1)} %get-tuple-element.71), channel_id=1, source_target_pairs={{0,1},{1,0},{2,3},{3,2},{4,5},{5,4},{6,7},{7,6},{8,9},{9,8},{10,11... | collective-permute-start | bytes 98312 | tf_op jit(solution)/shard_map/ppermute | solution.py:277
  116.3 4.3 %collective-permute-start.8 = (f32[32,256]{1,0:T(8,128)S(1)}, f32[32,256]{1,0:T(8,128)S(1)}, u32[]{:S(2)}, u32[]{:S(2)}) collective-permute-start(f32[32,256]{1,0:T(8,128)S(1)} %select_add_fusion), channel_id=1, source_target_pairs={{0,4},{1,5},{2,6},{3,7},{4,0},{5,1},{6,2},{7,3},{8,12},{9,13},{10,... | collective-permute-start | bytes 98312 | tf_op jit(solution)/shard_map/ppermute | solution.py:277
  116.3 4.6 %collective-permute-start.9 = (f32[32,256]{1,0:T(8,128)S(1)}, f32[32,256]{1,0:T(8,128)S(1)}, u32[]{:S(2)}, u32[]{:S(2)}) collective-permute-start(f32[32,256]{1,0:T(8,128)S(1)} %select_add_fusion), channel_id=1, source_target_pairs={{0,6},{1,7},{2,4},{3,5},{4,2},{5,3},{6,0},{7,1},{8,14},{9,15},{10,... | collective-permute-start | bytes 98312 | tf_op jit(solution)/shard_map/ppermute | solution.py:277
  119.0 3.0 %collective-permute-start.7 = (f32[32,256]{1,0:T(8,128)S(1)}, f32[32,256]{1,0:T(8,128)S(1)}, u32[]{:S(2)}, u32[]{:S(2)}) collective-permute-start(f32[32,256]{1,0:T(8,128)S(1)} %select_add_fusion), channel_id=1, source_target_pairs={{0,2},{1,3},{2,0},{3,1},{4,6},{5,7},{6,4},{7,5},{8,10},{9,11},{10,... | collective-permute-start | bytes 98312 | tf_op jit(solution)/shard_map/ppermute | solution.py:277
  122.1 4.6 %collective-permute-start.10 = (f32[32,384]{1,0:T(8,128)S(1)}, f32[32,384]{1,0:T(8,128)S(1)}, u32[]{:S(2)}, u32[]{:S(2)}) collective-permute-start(f32[32,384]{1,0:T(8,128)S(1)} %get-tuple-element.65), channel_id=1, source_target_pairs={{0,8},{1,9},{2,10},{3,11},{4,12},{5,13},{6,14},{7,15},{8,0},{9,1},... | collective-permute-start | bytes 147464 | tf_op jit(solution)/shard_map/ppermute | solution.py:277
  122.2 4.6 %collective-permute-start.11 = (f32[32,384]{1,0:T(8,128)S(1)}, f32[32,384]{1,0:T(8,128)S(1)}, u32[]{:S(2)}, u32[]{:S(2)}) collective-permute-start(f32[32,384]{1,0:T(8,128)S(1)} %get-tuple-element.66), channel_id=1, source_target_pairs={{0,16},{1,17},{2,18},{3,19},{4,20},{5,21},{6,22},{7,23},{8,24},{9,... | collective-permute-start | bytes 147464 | tf_op jit(solution)/shard_map/ppermute | solution.py:277
  124.4 4.5 %collective-permute-start.12 = (f32[32,384]{1,0:T(8,128)S(1)}, f32[32,384]{1,0:T(8,128)S(1)}, u32[]{:S(2)}, u32[]{:S(2)}) collective-permute-start(f32[32,384]{1,0:T(8,128)S(1)} %get-tuple-element.64), channel_id=1, source_target_pairs={{0,24},{1,25},{2,26},{3,27},{4,28},{5,29},{6,30},{7,31},{8,16},{9,... | collective-permute-start | bytes 147464 | tf_op jit(solution)/shard_map/ppermute | solution.py:277
  128.9 4.1 %collective-permute-start.13 = (f32[32,384]{1,0:T(8,128)S(1)}, f32[32,384]{1,0:T(8,128)S(1)}, u32[]{:S(2)}, u32[]{:S(2)}) collective-permute-start(f32[32,384]{1,0:T(8,128)S(1)} %get-tuple-element.62), channel_id=1, source_target_pairs={{0,32},{1,33},{2,34},{3,35},{4,36},{5,37},{6,38},{7,39},{8,40},{9,... | collective-permute-start | bytes 147464 | tf_op jit(solution)/shard_map/ppermute | solution.py:277
  130.5 4.5 %collective-permute-start.14 = (f32[32,384]{1,0:T(8,128)S(1)}, f32[32,384]{1,0:T(8,128)S(1)}, u32[]{:S(2)}, u32[]{:S(2)}) collective-permute-start(f32[32,384]{1,0:T(8,128)S(1)} %get-tuple-element.63), channel_id=1, source_target_pairs={{0,64},{1,65},{2,66},{3,67},{4,68},{5,69},{6,70},{7,71},{8,72},{9,... | collective-permute-start | bytes 147464 | tf_op jit(solution)/shard_map/ppermute | solution.py:277
  133.0 4.2 %collective-permute-start.15 = (f32[32,384]{1,0:T(8,128)S(1)}, f32[32,384]{1,0:T(8,128)S(1)}, u32[]{:S(2)}, u32[]{:S(2)}) collective-permute-start(f32[32,384]{1,0:T(8,128)S(1)} %get-tuple-element.61), channel_id=1, source_target_pairs={{0,96},{1,97},{2,98},{3,99},{4,100},{5,101},{6,102},{7,103},{8,104... | collective-permute-start | bytes 147464 | tf_op jit(solution)/shard_map/ppermute | solution.py:277
  137.2 7.2 %collective-permute-start.16 = (f32[32,256]{1,0:T(8,128)S(1)}, f32[32,256]{1,0:T(8,128)S(1)}, u32[]{:S(2)}, u32[]{:S(2)}) collective-permute-start(f32[32,256]{1,0:T(8,128)S(1)} %slice.50), channel_id=1, source_target_pairs={{0,1},{1,0},{2,3},{3,2},{4,5},{5,4},{6,7},{7,6},{8,9},{9,8},{10,11... | collective-permute-start | bytes 98312 | tf_op jit(solution)/shard_map/ppermute | solution.py:277

commit v8 on v7

--- a/solution.py
+++ b/solution.py
@@ -247,6 +247,25 @@
     )(core.reshape(1), came, other, came, weight_t, bias, cot)
 
 
+def flip_kernel(in_ref, out_ref):
+    for k in range(in_ref.shape[0]):
+        out_ref[k] = in_ref[k].T
+
+
+def flip(values, interpret=False):
+    shape = (values.shape[0], values.shape[2], values.shape[1])
+    return pl.pallas_call(
+        flip_kernel,
+        in_specs=[pl.BlockSpec(memory_space=pltpu.VMEM)],
+        out_specs=pl.BlockSpec(memory_space=pltpu.VMEM),
+        out_shape=jax.ShapeDtypeStruct(shape, values.dtype),
+        compiler_params=pltpu.CompilerParams(vmem_limit_bytes=VMEM_BYTES),
+        cost_estimate=pl.CostEstimate(flops=0, bytes_accessed=2 * 2**20, transcendentals=0),
+        interpret=interpret,
+        name="flip",
+    )(values)
+
+
 def exchange(blocks):
     return lax.all_to_all(blocks, BOTH, 0, 0, tiled=True)
 
@@ -308,7 +327,7 @@
             part = add_parts([part] + [partner(part, low * mask) for mask in range(1, size)])
             continue
         if step == len(permute_groups()) - 1:
-            part, beside = lax.optimization_barrier((part, beside))
+            part, beside[0] = lax.optimization_barrier((part, beside[0]))
         share, lanes = values.shape[1:]
         pieces = [piece.reshape(-1, lanes) for piece in scatter_pieces(values, low, size)]
         used = pieces[0].shape[0]
@@ -316,6 +335,7 @@
         sent = [jnp.concatenate([part, piece], axis=1) for piece in pieces]
         both = add_parts(sent[:1] + [partner(sent[mask], low * mask) for mask in range(1, size)])
         part, values = both[:, :columns], both[:used, columns:].reshape(-1, share, lanes)
+    part, beside[1] = lax.optimization_barrier((part, beside[1]))
     other = partner(part, 1)
     return jnp.where(core == 0, part, other), jnp.where(core == 0, other, part), values, beside
 
@@ -361,11 +381,11 @@
     sent, left_other = lax.optimization_barrier((sent, left_other))
     back = exchange(sent).reshape(seqs, columns)
     update, weight_term = forward(core, came, left_other, weight.T, bias, cot, width)
-    pair_update = row_major(update.transpose(1, 0, 2))
     early = 2
     weight_term = weight_term.reshape(devices, -1, pair_width)
     weight_term = sum_scatter(weight_term, permute_groups()[:early])
-    back, weight_term = lax.optimization_barrier((back, weight_term))
+    back, weight_term, update = lax.optimization_barrier((back, weight_term, update))
+    pair_update = row_major(update.transpose(1, 0, 2))
 
     place = np.indices((row_count, chips, CORES, local)).reshape(4, -1)
     left_place = (place[3] * row_count + place[0]) * CORES + place[2]
@@ -383,8 +403,9 @@
     upstream = jnp.einsum("shr,ch->src", left_grad, left_weight, preferred_element_type=jnp.float32)
     upstream += jnp.einsum("srh,ch->src", right_grad, right_weight, preferred_element_type=jnp.float32)
     grad_alignment = norm_backward(upstream, normed, inv_sigma).astype(jnp.bfloat16)
-    left_wgrad, right_wgrad, weight_term, pair_update = sum_all(
-        left_wgrad, right_wgrad, weight_term, early, pair_update
+    grad_alignment = flip(grad_alignment.transpose(0, 2, 1))
+    left_wgrad, right_wgrad, weight_term, (grad_alignment, pair_update) = sum_all(
+        left_wgrad, right_wgrad, weight_term, early, [grad_alignment, pair_update]
     )
     grad_out_weight = weight_term.reshape(-1, pair_width)
     return (pair_update, grad_alignment, grad_out_weight, left_wgrad.T, right_wgrad.T)

time: 146 us -> 144 us (0.986)
  local copies, waits for them, and re-layouts: 24.5 us -> 21.6 us
    pallas_call x1 -> x0, local copies, waits for them, and re-layouts: 4.26 us -> none  [forward(): pl.pallas_call(functools.partial(forward_kernel, 1.0 / seqs, width), grid...]
    optimization_barrier x0 -> x1, local copies, waits for them, and re-layouts: none -> 2.67 us  [body(): lax.optimization_barrier((back, weight_term, update))]
    unnamed x29 -> x30, local copies, waits for them, and re-layouts: 8.36 us -> 7.02 us
  transfers between devices with their start and end apart: 19 -> 19, of which waited for: 11 -> 12; matrix products, arithmetic and copies ran while one was open for 8% -> 6% of each run, Pallas kernels for 27% -> 28%
where the time goes in v8:
time: 144 us
  Pallas kernels  42.7 us (30%)
  starting transfers between devices  41.3 us (29%)
  waiting for transfers between devices  29.6 us (21%)
  local copies, waits for them, and re-layouts  21.6 us (15%)
  matrix products  4.08 us (3%)
  other arithmetic  3.4 us (2%)
    ppermute x15, starting transfers between devices, partner(): lax.ppermute(part, BOTH, [(i, i ^ mask) for i in range(lax.axis_size(BOTH...  22.3 us
    all_to_all x2, waiting for transfers between devices, exchange(): return lax.all_to_all(blocks, BOTH, 0, 0, tiled=True)  18.1 us
    all_to_all x2, starting transfers between devices, exchange(): return lax.all_to_all(blocks, BOTH, 0, 0, tiled=True)  16.8 us
    pallas_call x1, Pallas kernels, forward(): pl.pallas_call(functools.partial(forward_kernel, 1.0 / seqs, width), grid...  14.7 us
    ppermute x15, waiting for transfers between devices, partner(): lax.ppermute(part, BOTH, [(i, i ^ mask) for i in range(lax.axis_size(BOTH...  11.5 us
    pallas_call x1, Pallas kernels, left_grads(): pl.pallas_call(functools.partial(left_kernel, 1.0 / seqs), in_specs=[pl.B...  10 us
    pallas_call x1, Pallas kernels, outer_grads(): pl.pallas_call(functools.partial(outer_grad_kernel, width), grid=(cols //...  9.63 us
    unnamed x30, local copies, waits for them, and re-layouts  7.02 us
  transfers between devices with their start and end apart: 19, of which 12 were waited for; matrix products, arithmetic and copies ran while one was open for 6% of the time, Pallas kernels for 28%

profile of v8, /device:TPU:1, one launch (start us, length us, event | category | flops | bytes accessed | tf_op | source)
XLA Modules:
  0.0 143.8 jit_solution(8631536379704862992)
XLA Ops:
  0.6 1.5 %copy.45 = bf16[2,1024,256]{1,2,0:T(8,128)(2,1)S(1)} copy(bf16[2,1024,256]{2,1,0:T(8,128)(2,1)} %param.8) | data formatting | bytes 2097152 | tf_op args[0]
  5.8 2.4 %pack.1 = bf16[8,8,2,2,4096]{4,3,2,1,0:T(2,128)(2,1)} custom-call(bf16[8,2,2,2048]{3,2,1,0:T(2,128)(2,1)} %reshape.107.left_ref, bf16[8,2,2,2048]{3,2,1,0:T(2,128)(2,1)} %bitcast.114), custom_call_target="tpu_custom_call" | custom-call | bytes 2097152 | tf_op jit(solution)/shard_map/pack/pallas_call | solution.py:206
  8.3 12.0 %all-to-all-start = ((bf16[128,2,4096]{2,1,0:T(2,128)(2,1)}), bf16[128,2,4096]{2,1,0:T(2,128)(2,1)}, u32[]{:S(2)}, u32[]{:S(2)}) async-start(bf16[128,2,4096]{2,1,0:T(2,128)(2,1)} %bitcast.110), calls=%async_computation | async-start | bytes 4194304 | tf_op jit(solution)/shard_map/all_to_all | solution.py:270
  20.7 2.9 %copy.85 = bf16[128,64,128]{2,0,1:T(8,128)(2,1)S(1)} copy(bf16[128,64,128]{2,1,0:T(8,128)(2,1)} %param.13) | data formatting | bytes 4194304 | tf_op args[5]
  23.7 9.6 %outer_grads.1.grad_ref = bf16[2048,4096]{1,0:T(8,128)(2,1)} custom-call(bf16[1024,128]{1,0:T(8,128)(2,1)S(1)} %copy.55.weight_ref, bf16[64,128,128]{2,1,0:T(8,128)(2,1)S(1)} %bitcast.105), custom_call_target="tpu_custom_call" | custom-call | flops 2147483648 | bytes 18874368 | tf_op jit(solution)/shard_map/outer_grads/pallas_call | solution.py:152
  33.3 17.1 %all-to-all-done = bf16[128,2,4096]{2,1,0:T(2,128)(2,1)} async-done(((bf16[128,2,4096]{2,1,0:T(2,128)(2,1)}), bf16[128,2,4096]{2,1,0:T(2,128)(2,1)}, u32[]{:S(2)}, u32[]{:S(2)}) %all-to-all-start) | async-done | bytes 2097184 | tf_op jit(solution)/shard_map/all_to_all | solution.py:270
  50.4 2.7 %reshape.110.came_ref.own_ref.right_ref = bf16[256,4096]{1,0:T(8,128)(2,1)S(1)} reshape(bf16[128,2,4096]{2,1,0:T(2,128)(2,1)} %all-to-all-done) | data formatting | bytes 4194304 | tf_op jit(solution)/shard_map/reshape | solution.py:373
  54.5 10.0 %left_grads.1 = (bf16[256,4096]{1,0:T(8,128)(2,1)S(1)}, f32[256,2048]{1,0:T(8,128)S(1)}) custom-call(bf16[256,4096]{1,0:T(8,128)(2,1)} %copy-done.2, bf16[2048,4096]{1,0:T(8,128)(2,1)} %outer_grads.1.grad_ref), custom_call_target="tpu_custom_call" | custom-call | flops 6442450944 | bytes 22020096 | tf_op jit(solution)/shard_map/left_grads/pallas_call | solution.py:169
  64.6 1.2 collective-permute-start.1
  65.8 4.6 %right_grads.1 = bf16[256,2048]{1,0:T(8,128)(2,1)S(1)} custom-call(bf16[256,2048]{1,0:T(8,128)(2,1)S(1)} %collective-permute-done.other_ref, f32[256,2048]{1,0:T(8,128)S(1)} %get-tuple-element.27.partial_ref, bf16[2048,4096]{1,0:T(8,128)(2,1)} %outer_grads.1.grad_ref), custom_call_target="tpu_custom_call" | custom-call | flops 2147483648 | bytes 12582912 | tf_op jit(solution)/shard_map/right_grads/pallas_call | solution.py:191
  71.0 2.6 %reshape.111 = bf16[128,2,4096]{2,1,0:T(2,128)(2,1)} reshape(bf16[256,4096]{1,0:T(8,128)(2,1)S(1)} %pad_maximum_fusion) | data formatting | bytes 4194304 | tf_op jit(solution)/shard_map/reshape | solution.py:380
  73.6 4.8 %all-to-all-start.1 = ((bf16[128,2,4096]{2,1,0:T(2,128)(2,1)}), bf16[128,2,4096]{2,1,0:T(2,128)(2,1)}, u32[]{:S(2)}, u32[]{:S(2)}) async-start(bf16[128,2,4096]{2,1,0:T(2,128)(2,1)} %reshape.111), calls=%async_computation.1 | async-start | bytes 4194304 | tf_op jit(solution)/shard_map/all_to_all | solution.py:270
  78.5 14.7 %forward.1 = (bf16[64,128,128]{2,1,0:T(8,128)(2,1)S(1)}, f32[1024,128]{1,0:T(8,128)S(1)}) custom-call(s32[1]{0:T(128)} %bitcast.7.core_ref, bf16[256,4096]{1,0:T(8,128)(2,1)S(1)} %copy-done.3, bf16[256,2048]{1,0:T(8,128)(2,1)S(1)} %collective-permute-done.other_ref, bf16[256,4096]{1,0:T(8,128)(2,1)S(1)} %copy-done.3, bf16[128,1024]{1,0:T(8,128)(2,1)S(1)} %bitcast.107, ...), custom_call_target="tpu_custom_call" | custom-call | flops 8589934592 | bytes 8388608 | tf_op jit(solution)/shard_map/forward/pallas_call | solution.py:222
  93.3 1.3 copy-done.4
  95.4 1.2 collective-permute-start.2
  96.6 1.2 collective-permute-done.2
  99.3 2.4 %collective-permute-start.4 = (f32[16,8,128]{2,1,0:T(8,128)S(1)}, f32[16,8,128]{2,1,0:T(8,128)S(1)}, u32[]{:S(2)}, u32[]{:S(2)}) collective-permute-start(f32[16,8,128]{2,1,0:T(8,128)S(1)} %get-tuple-element.42), channel_id=1, source_target_pairs={{0,4},{1,5},{2,6},{3,7},{4,0},{5,1},{6,2},{7,3},{8,12},{9,13},{10,... | collective-permute-start | bytes 196616 | tf_op jit(solution)/shard_map/ppermute | solution.py:296
  103.3 2.9 %collective-permute-done.4 = f32[16,8,128]{2,1,0:T(8,128)S(1)} collective-permute-done((f32[16,8,128]{2,1,0:T(8,128)S(1)}, f32[16,8,128]{2,1,0:T(8,128)S(1)}, u32[]{:S(2)}, u32[]{:S(2)}) %collective-permute-start.4) | collective-permute-done | bytes 65568 | tf_op jit(solution)/shard_map/ppermute | solution.py:296
  106.2 1.4 collective-permute-done.5
  108.6 2.7 %reshape.112 = bf16[256,4096]{1,0:T(8,128)(2,1)S(1)} reshape(bf16[128,2,4096]{2,1,0:T(2,128)(2,1)} %all-to-all-done.1) | data formatting | bytes 4194304 | tf_op jit(solution)/shard_map/reshape | solution.py:382
  114.4 1.5 %collective-permute-start.6 = (f32[32,256]{1,0:T(8,128)S(1)}, f32[32,256]{1,0:T(8,128)S(1)}, u32[]{:S(2)}, u32[]{:S(2)}) collective-permute-start(f32[32,256]{1,0:T(8,128)S(1)} %get-tuple-element.62), channel_id=1, source_target_pairs={{0,1},{1,0},{2,3},{3,2},{4,5},{5,4},{6,7},{7,6},{8,9},{9,8},{10,11... | collective-permute-start | bytes 98312 | tf_op jit(solution)/shard_map/ppermute | solution.py:296
  116.8 2.7 %collective-permute-start.9 = (f32[32,256]{1,0:T(8,128)S(1)}, f32[32,256]{1,0:T(8,128)S(1)}, u32[]{:S(2)}, u32[]{:S(2)}) collective-permute-start(f32[32,256]{1,0:T(8,128)S(1)} %select_add_fusion), channel_id=1, source_target_pairs={{0,6},{1,7},{2,4},{3,5},{4,2},{5,3},{6,0},{7,1},{8,14},{9,15},{10,... | collective-permute-start | bytes 98312 | tf_op jit(solution)/shard_map/ppermute | solution.py:296
  119.5 1.7 %collective-permute-done.8 = f32[32,256]{1,0:T(8,128)S(1)} collective-permute-done((f32[32,256]{1,0:T(8,128)S(1)}, f32[32,256]{1,0:T(8,128)S(1)}, u32[]{:S(2)}, u32[]{:S(2)}) %collective-permute-start.8) | collective-permute-done | bytes 32800 | tf_op jit(solution)/shard_map/ppermute | solution.py:296
  121.2 1.2 collective-permute-done.7
  122.5 2.3 %collective-permute-start.11 = (f32[32,384]{1,0:T(8,128)S(1)}, f32[32,384]{1,0:T(8,128)S(1)}, u32[]{:S(2)}, u32[]{:S(2)}) collective-permute-start(f32[32,384]{1,0:T(8,128)S(1)} %get-tuple-element.57), channel_id=1, source_target_pairs={{0,16},{1,17},{2,18},{3,19},{4,20},{5,21},{6,22},{7,23},{8,24},{9,... | collective-permute-start | bytes 147464 | tf_op jit(solution)/shard_map/ppermute | solution.py:296
  124.8 1.6 %collective-permute-start.12 = (f32[32,384]{1,0:T(8,128)S(1)}, f32[32,384]{1,0:T(8,128)S(1)}, u32[]{:S(2)}, u32[]{:S(2)}) collective-permute-start(f32[32,384]{1,0:T(8,128)S(1)} %get-tuple-element.55), channel_id=1, source_target_pairs={{0,24},{1,25},{2,26},{3,27},{4,28},{5,29},{6,30},{7,31},{8,16},{9,... | collective-permute-start | bytes 147464 | tf_op jit(solution)/shard_map/ppermute | solution.py:296
  126.9 1.3 flip.1
  129.1 1.9 %collective-permute-start.13 = (f32[32,384]{1,0:T(8,128)S(1)}, f32[32,384]{1,0:T(8,128)S(1)}, u32[]{:S(2)}, u32[]{:S(2)}) collective-permute-start(f32[32,384]{1,0:T(8,128)S(1)} %get-tuple-element.53), channel_id=1, source_target_pairs={{0,32},{1,33},{2,34},{3,35},{4,36},{5,37},{6,38},{7,39},{8,40},{9,... | collective-permute-start | bytes 147464 | tf_op jit(solution)/shard_map/ppermute | solution.py:296
  130.9 2.5 %collective-permute-start.14 = (f32[32,384]{1,0:T(8,128)S(1)}, f32[32,384]{1,0:T(8,128)S(1)}, u32[]{:S(2)}, u32[]{:S(2)}) collective-permute-start(f32[32,384]{1,0:T(8,128)S(1)} %get-tuple-element.54), channel_id=1, source_target_pairs={{0,64},{1,65},{2,66},{3,67},{4,68},{5,69},{6,70},{7,71},{8,72},{9,... | collective-permute-start | bytes 147464 | tf_op jit(solution)/shard_map/ppermute | solution.py:296
  133.4 2.7 %copy.84 = bf16[64,128,128]{2,0,1:T(8,128)(2,1)} copy(bf16[64,128,128]{2,1,0:T(8,128)(2,1)S(1)} %copy-done.5) | data formatting | bytes 4194304 | tf_op jit(solution)/shard_map/optimization_barrier | solution.py:387
  136.1 1.5 %collective-permute-done.15 = f32[32,384]{1,0:T(8,128)S(1)} collective-permute-done((f32[32,384]{1,0:T(8,128)S(1)}, f32[32,384]{1,0:T(8,128)S(1)}, u32[]{:S(2)}, u32[]{:S(2)}) %collective-permute-start.15) | collective-permute-done | bytes 49184 | tf_op jit(solution)/shard_map/ppermute | solution.py:296
  137.6 4.7 %collective-permute-start.16 = (f32[32,256]{1,0:T(8,128)S(1)}, f32[32,256]{1,0:T(8,128)S(1)}, u32[]{:S(2)}, u32[]{:S(2)}) collective-permute-start(f32[32,256]{1,0:T(8,128)S(1)} %slice.49), channel_id=1, source_target_pairs={{0,1},{1,0},{2,3},{3,2},{4,5},{5,4},{6,7},{7,6},{8,9},{9,8},{10,11... | collective-permute-start | bytes 98312 | tf_op jit(solution)/shard_map/ppermute | solution.py:296
  (92 shorter events, 17.9 us)
Async XLA Ops:
  0.6 2.1 %copy-start = (bf16[256,32]{0,1:T(8,128)(2,1)S(1)}, bf16[256,32]{0,1:T(8,128)(2,1)}, u32[]{:S(2)}) copy-start(bf16[256,32]{0,1:T(8,128)(2,1)} %param.9) | copy-start | bytes 49156
  2.1 1.7 %copy-start.7 = (bf16[2,1024,256]{1,2,0:T(8,128)(2,1)}, bf16[2,1024,256]{1,2,0:T(8,128)(2,1)S(1)}, u32[]{:S(2)}) copy-start(bf16[2,1024,256]{1,2,0:T(8,128)(2,1)S(1)} %copy.45) | copy-start | bytes 3145732
  2.2 1.7 %copy-start.10 = (bf16[256,32]{0,1:T(8,128)(2,1)S(1)}, bf16[256,32]{0,1:T(8,128)(2,1)}, u32[]{:S(2)}) copy-start(bf16[256,32]{0,1:T(8,128)(2,1)} %param.10) | copy-start | bytes 49156
  8.3 12.0 %copy-start.9 = (bf16[1024,128]{1,0:T(8,128)(2,1)S(1)}, bf16[1024,128]{1,0:T(8,128)(2,1)}, u32[]{:S(2)}) copy-start(bf16[1024,128]{1,0:T(8,128)(2,1)} %param.11) | copy-start | bytes 786436
  8.3 42.1 %all-to-all-start = ((bf16[128,2,4096]{2,1,0:T(2,128)(2,1)}), bf16[128,2,4096]{2,1,0:T(2,128)(2,1)}, u32[]{:S(2)}, u32[]{:S(2)}) async-start(bf16[128,2,4096]{2,1,0:T(2,128)(2,1)} %bitcast.110), calls=%async_computation | async-start | bytes 4194304 | tf_op jit(solution)/shard_map/all_to_all | solution.py:270
  23.6 9.6 %copy-start.1 = (bf16[128,64,128]{2,0,1:T(8,128)(2,1)}, bf16[128,64,128]{2,0,1:T(8,128)(2,1)S(1)}, u32[]{:S(2)}) copy-start(bf16[128,64,128]{2,0,1:T(8,128)(2,1)S(1)} %copy.85) | copy-start | bytes 6291460
  53.2 1.3 copy-start.2
  53.2 11.3 %collective-permute-start = (bf16[256,2048]{1,0:T(8,128)(2,1)S(1)}, bf16[256,2048]{1,0:T(8,128)(2,1)S(1)}, u32[]{:S(2)}, u32[]{:S(2)}) collective-permute-start(bf16[256,2048]{1,0:T(8,128)(2,1)S(1)} %slice.46), channel_id=1, source_target_pairs={{0,1},{1,0},{2,3},{3,2},{4,5},{5,4},{6,7},{7,6},{8,9},{9,8},{10,11... | collective-permute-start | bytes 3145736 | tf_op jit(solution)/shard_map/ppermute | solution.py:274
  64.6 5.8 %collective-permute-start.1 = (bf16[256,2048]{1,0:T(8,128)(2,1)S(1)}, bf16[256,2048]{1,0:T(8,128)(2,1)S(1)}, u32[]{:S(2)}, u32[]{:S(2)}) collective-permute-start(bf16[256,2048]{1,0:T(8,128)(2,1)S(1)} %slice.37), channel_id=1, source_target_pairs={{0,1},{1,0},{2,3},{3,2},{4,5},{5,4},{6,7},{7,6},{8,9},{9,8},{10,11... | collective-permute-start | bytes 3145736 | tf_op jit(solution)/shard_map/ppermute | solution.py:274
  73.6 4.9 %copy-start.12 = (bf16[128]{0:T(256)(128)(2,1)S(1)}, bf16[128]{0:T(256)(128)(2,1)}, u32[]{:S(2)}) copy-start(bf16[128]{0:T(256)(128)(2,1)} %param.12) | copy-start | bytes 772
  73.6 4.9 %copy-start.3 = (bf16[256,4096]{1,0:T(8,128)(2,1)S(1)}, bf16[256,4096]{1,0:T(8,128)(2,1)}, u32[]{:S(2)}) copy-start(bf16[256,4096]{1,0:T(8,128)(2,1)} %copy-done.2) | copy-start | bytes 6291460
  73.6 35.0 %all-to-all-start.1 = ((bf16[128,2,4096]{2,1,0:T(2,128)(2,1)}), bf16[128,2,4096]{2,1,0:T(2,128)(2,1)}, u32[]{:S(2)}, u32[]{:S(2)}) async-start(bf16[128,2,4096]{2,1,0:T(2,128)(2,1)} %reshape.111), calls=%async_computation.1 | async-start | bytes 4194304 | tf_op jit(solution)/shard_map/all_to_all | solution.py:270
  93.2 1.3 copy-start.4
  94.6 0.8 copy-start.6
  95.4 2.3 %collective-permute-start.2 = (f32[64,8,128]{2,1,0:T(8,128)S(1)}, f32[64,8,128]{2,1,0:T(8,128)S(1)}, u32[]{:S(2)}, u32[]{:S(2)}) collective-permute-start(f32[64,8,128]{2,1,0:T(8,128)S(1)} %dynamic-slice_bitcast_fusion), channel_id=1, source_target_pairs={{0,1},{1,0},{2,3},{3,2},{4,5},{5,4},{6,7},{7,6},{8,9},{9,8},{10,11... | collective-permute-start | bytes 786440 | tf_op jit(solution)/shard_map/ppermute | solution.py:296
  98.8 4.5 %collective-permute-start.3 = (f32[16,8,128]{2,1,0:T(8,128)S(1)}, f32[16,8,128]{2,1,0:T(8,128)S(1)}, u32[]{:S(2)}, u32[]{:S(2)}) collective-permute-start(f32[16,8,128]{2,1,0:T(8,128)S(1)} %get-tuple-element.43), channel_id=1, source_target_pairs={{0,2},{1,3},{2,0},{3,1},{4,6},{5,7},{6,4},{7,5},{8,10},{9,11},{10,... | collective-permute-start | bytes 196616 | tf_op jit(solution)/shard_map/ppermute | solution.py:296
  99.3 6.9 %collective-permute-start.4 = (f32[16,8,128]{2,1,0:T(8,128)S(1)}, f32[16,8,128]{2,1,0:T(8,128)S(1)}, u32[]{:S(2)}, u32[]{:S(2)}) collective-permute-start(f32[16,8,128]{2,1,0:T(8,128)S(1)} %get-tuple-element.42), channel_id=1, source_target_pairs={{0,4},{1,5},{2,6},{3,7},{4,0},{5,1},{6,2},{7,3},{8,12},{9,13},{10,... | collective-permute-start | bytes 196616 | tf_op jit(solution)/shard_map/ppermute | solution.py:296
  101.8 5.8 %collective-permute-start.5 = (f32[16,8,128]{2,1,0:T(8,128)S(1)}, f32[16,8,128]{2,1,0:T(8,128)S(1)}, u32[]{:S(2)}, u32[]{:S(2)}) collective-permute-start(f32[16,8,128]{2,1,0:T(8,128)S(1)} %get-tuple-element.41), channel_id=1, source_target_pairs={{0,6},{1,7},{2,4},{3,5},{4,2},{5,3},{6,0},{7,1},{8,14},{9,15},{10,... | collective-permute-start | bytes 196616 | tf_op jit(solution)/shard_map/ppermute | solution.py:296
  107.6 3.7 %copy-start.11 = (bf16[32,256]{1,0:T(8,128)(2,1)S(1)}, bf16[32,256]{1,0:T(8,128)(2,1)}, u32[]{:S(2)}) copy-start(bf16[32,256]{1,0:T(8,128)(2,1)} %constant.144.clone) | copy-start | bytes 49156
  107.6 4.1 %copy-start.8 = (bf16[2,1024,256]{1,2,0:T(8,128)(2,1)S(1)}, bf16[2,1024,256]{1,2,0:T(8,128)(2,1)}, u32[]{:S(2)}) copy-start(bf16[2,1024,256]{1,2,0:T(8,128)(2,1)} %copy-done.7) | copy-start | bytes 3145732
  114.4 2.3 %collective-permute-start.6 = (f32[32,256]{1,0:T(8,128)S(1)}, f32[32,256]{1,0:T(8,128)S(1)}, u32[]{:S(2)}, u32[]{:S(2)}) collective-permute-start(f32[32,256]{1,0:T(8,128)S(1)} %get-tuple-element.62), channel_id=1, source_target_pairs={{0,1},{1,0},{2,3},{3,2},{4,5},{5,4},{6,7},{7,6},{8,9},{9,8},{10,11... | collective-permute-start | bytes 98312 | tf_op jit(solution)/shard_map/ppermute | solution.py:296
  116.8 4.4 %collective-permute-start.8 = (f32[32,256]{1,0:T(8,128)S(1)}, f32[32,256]{1,0:T(8,128)S(1)}, u32[]{:S(2)}, u32[]{:S(2)}) collective-permute-start(f32[32,256]{1,0:T(8,128)S(1)} %select_add_fusion), channel_id=1, source_target_pairs={{0,4},{1,5},{2,6},{3,7},{4,0},{5,1},{6,2},{7,3},{8,12},{9,13},{10,... | collective-permute-start | bytes 98312 | tf_op jit(solution)/shard_map/ppermute | solution.py:296
  116.8 4.4 %collective-permute-start.9 = (f32[32,256]{1,0:T(8,128)S(1)}, f32[32,256]{1,0:T(8,128)S(1)}, u32[]{:S(2)}, u32[]{:S(2)}) collective-permute-start(f32[32,256]{1,0:T(8,128)S(1)} %select_add_fusion), channel_id=1, source_target_pairs={{0,6},{1,7},{2,4},{3,5},{4,2},{5,3},{6,0},{7,1},{8,14},{9,15},{10,... | collective-permute-start | bytes 98312 | tf_op jit(solution)/shard_map/ppermute | solution.py:296
  119.5 2.9 %collective-permute-start.7 = (f32[32,256]{1,0:T(8,128)S(1)}, f32[32,256]{1,0:T(8,128)S(1)}, u32[]{:S(2)}, u32[]{:S(2)}) collective-permute-start(f32[32,256]{1,0:T(8,128)S(1)} %select_add_fusion), channel_id=1, source_target_pairs={{0,2},{1,3},{2,0},{3,1},{4,6},{5,7},{6,4},{7,5},{8,10},{9,11},{10,... | collective-permute-start | bytes 98312 | tf_op jit(solution)/shard_map/ppermute | solution.py:296
  122.4 5.8 %collective-permute-start.10 = (f32[32,384]{1,0:T(8,128)S(1)}, f32[32,384]{1,0:T(8,128)S(1)}, u32[]{:S(2)}, u32[]{:S(2)}) collective-permute-start(f32[32,384]{1,0:T(8,128)S(1)} %get-tuple-element.56), channel_id=1, source_target_pairs={{0,8},{1,9},{2,10},{3,11},{4,12},{5,13},{6,14},{7,15},{8,0},{9,1},... | collective-permute-start | bytes 147464 | tf_op jit(solution)/shard_map/ppermute | solution.py:296
  122.5 5.7 %collective-permute-start.11 = (f32[32,384]{1,0:T(8,128)S(1)}, f32[32,384]{1,0:T(8,128)S(1)}, u32[]{:S(2)}, u32[]{:S(2)}) collective-permute-start(f32[32,384]{1,0:T(8,128)S(1)} %get-tuple-element.57), channel_id=1, source_target_pairs={{0,16},{1,17},{2,18},{3,19},{4,20},{5,21},{6,22},{7,23},{8,24},{9,... | collective-permute-start | bytes 147464 | tf_op jit(solution)/shard_map/ppermute | solution.py:296
  124.8 4.2 %collective-permute-start.12 = (f32[32,384]{1,0:T(8,128)S(1)}, f32[32,384]{1,0:T(8,128)S(1)}, u32[]{:S(2)}, u32[]{:S(2)}) collective-permute-start(f32[32,384]{1,0:T(8,128)S(1)} %get-tuple-element.55), channel_id=1, source_target_pairs={{0,24},{1,25},{2,26},{3,27},{4,28},{5,29},{6,30},{7,31},{8,16},{9,... | collective-permute-start | bytes 147464 | tf_op jit(solution)/shard_map/ppermute | solution.py:296
  126.9 6.5 %copy-start.5 = (bf16[64,128,128]{2,1,0:T(8,128)(2,1)S(1)}, bf16[64,128,128]{2,1,0:T(8,128)(2,1)}, u32[]{:S(2)}) copy-start(bf16[64,128,128]{2,1,0:T(8,128)(2,1)} %copy-done.4) | copy-start | bytes 6291460
  129.1 7.1 %collective-permute-start.13 = (f32[32,384]{1,0:T(8,128)S(1)}, f32[32,384]{1,0:T(8,128)S(1)}, u32[]{:S(2)}, u32[]{:S(2)}) collective-permute-start(f32[32,384]{1,0:T(8,128)S(1)} %get-tuple-element.53), channel_id=1, source_target_pairs={{0,32},{1,33},{2,34},{3,35},{4,36},{5,37},{6,38},{7,39},{8,40},{9,... | collective-permute-start | bytes 147464 | tf_op jit(solution)/shard_map/ppermute | solution.py:296
  130.9 5.2 %collective-permute-start.14 = (f32[32,384]{1,0:T(8,128)S(1)}, f32[32,384]{1,0:T(8,128)S(1)}, u32[]{:S(2)}, u32[]{:S(2)}) collective-permute-start(f32[32,384]{1,0:T(8,128)S(1)} %get-tuple-element.54), channel_id=1, source_target_pairs={{0,64},{1,65},{2,66},{3,67},{4,68},{5,69},{6,70},{7,71},{8,72},{9,... | collective-permute-start | bytes 147464 | tf_op jit(solution)/shard_map/ppermute | solution.py:296
  133.4 4.2 %collective-permute-start.15 = (f32[32,384]{1,0:T(8,128)S(1)}, f32[32,384]{1,0:T(8,128)S(1)}, u32[]{:S(2)}, u32[]{:S(2)}) collective-permute-start(f32[32,384]{1,0:T(8,128)S(1)} %get-tuple-element.52), channel_id=1, source_target_pairs={{0,96},{1,97},{2,98},{3,99},{4,100},{5,101},{6,102},{7,103},{8,104... | collective-permute-start | bytes 147464 | tf_op jit(solution)/shard_map/ppermute | solution.py:296
  137.6 5.6 %collective-permute-start.16 = (f32[32,256]{1,0:T(8,128)S(1)}, f32[32,256]{1,0:T(8,128)S(1)}, u32[]{:S(2)}, u32[]{:S(2)}) collective-permute-start(f32[32,256]{1,0:T(8,128)S(1)} %slice.49), channel_id=1, source_target_pairs={{0,1},{1,0},{2,3},{3,2},{4,5},{5,4},{6,7},{7,6},{8,9},{9,8},{10,11... | collective-permute-start | bytes 98312 | tf_op jit(solution)/shard_map/ppermute | solution.py:296

commit v9 on v8

--- a/solution.py
+++ b/solution.py
@@ -326,6 +326,9 @@
         if step < early:
             part = add_parts([part] + [partner(part, low * mask) for mask in range(1, size)])
             continue
+        if step == early:
+            part, values = lax.optimization_barrier((part, values))
+            values = add_parts(values)
         if step == len(permute_groups()) - 1:
             part, beside[0] = lax.optimization_barrier((part, beside[0]))
         share, lanes = values.shape[1:]
@@ -383,8 +386,11 @@
     update, weight_term = forward(core, came, left_other, weight.T, bias, cot, width)
     early = 2
     weight_term = weight_term.reshape(devices, -1, pair_width)
-    weight_term = sum_scatter(weight_term, permute_groups()[:early])
-    back, weight_term, update = lax.optimization_barrier((back, weight_term, update))
+    weight_term = sum_scatter(weight_term, permute_groups()[:early - 1])
+    low, size = permute_groups()[early - 1]
+    kept, *pieces = scatter_pieces(weight_term, low, size)
+    weight_parts = [kept] + [partner(piece, low * (k + 1)) for k, piece in enumerate(pieces)]
+    back, update = lax.optimization_barrier((back, update))
     pair_update = row_major(update.transpose(1, 0, 2))
 
     place = np.indices((row_count, chips, CORES, local)).reshape(4, -1)
@@ -405,7 +411,7 @@
     grad_alignment = norm_backward(upstream, normed, inv_sigma).astype(jnp.bfloat16)
     grad_alignment = flip(grad_alignment.transpose(0, 2, 1))
     left_wgrad, right_wgrad, weight_term, (grad_alignment, pair_update) = sum_all(
-        left_wgrad, right_wgrad, weight_term, early, [grad_alignment, pair_update]
+        left_wgrad, right_wgrad, weight_parts, early, [grad_alignment, pair_update]
     )
     grad_out_weight = weight_term.reshape(-1, pair_width)
     return (pair_update, grad_alignment, grad_out_weight, left_wgrad.T, right_wgrad.T)

time: 144 us -> 146 us (1.014)
    all_to_all x2, waiting for transfers between devices: 18.1 us -> 23.3 us  [exchange(): return lax.all_to_all(blocks, BOTH, 0, 0, tiled=True)]
    ppermute x15, waiting for transfers between devices: 11.5 us -> 6.87 us  [partner(): lax.ppermute(part, BOTH, [(i, i ^ mask) for i in range(lax.axis_size(BOTH...]
    unnamed x30 -> x32, local copies, waits for them, and re-layouts: 7.02 us -> 7.02 us
  transfers between devices with their start and end apart: 19 -> 19, of which waited for: 12 -> 8; matrix products, arithmetic and copies ran while one was open for 6% -> 11% of each run, Pallas kernels for 28% -> 28%
where the time goes in v9:
time: 146 us; the launch traced here: 145 us
  Pallas kernels  42.7 us (29%)
  starting transfers between devices  40.5 us (28%)
  waiting for transfers between devices  30.2 us (21%)
  local copies, waits for them, and re-layouts  22.3 us (15%)
  other arithmetic  4.27 us (3%)
  matrix products  4.08 us (3%)
    all_to_all x2, waiting for transfers between devices, exchange(): return lax.all_to_all(blocks, BOTH, 0, 0, tiled=True)  23.3 us
    ppermute x15, starting transfers between devices, partner(): lax.ppermute(part, BOTH, [(i, i ^ mask) for i in range(lax.axis_size(BOTH...  21.5 us
    all_to_all x2, starting transfers between devices, exchange(): return lax.all_to_all(blocks, BOTH, 0, 0, tiled=True)  16.8 us
    pallas_call x1, Pallas kernels, forward(): pl.pallas_call(functools.partial(forward_kernel, 1.0 / seqs, width), grid...  14.7 us
    pallas_call x1, Pallas kernels, left_grads(): pl.pallas_call(functools.partial(left_kernel, 1.0 / seqs), in_specs=[pl.B...  10 us
    pallas_call x1, Pallas kernels, outer_grads(): pl.pallas_call(functools.partial(outer_grad_kernel, width), grid=(cols //...  9.63 us
    unnamed x32, local copies, waits for them, and re-layouts  7.02 us
    ppermute x15, waiting for transfers between devices, partner(): lax.ppermute(part, BOTH, [(i, i ^ mask) for i in range(lax.axis_size(BOTH...  6.87 us
  transfers between devices with their start and end apart: 19, of which 8 were waited for; matrix products, arithmetic and copies ran while one was open for 11% of the time, Pallas kernels for 28%

profile of v9, /device:TPU:1, one launch (start us, length us, event | category | flops | bytes accessed | tf_op | source)
XLA Modules:
  0.0 145.2 jit_solution(10350155377938879672)
XLA Ops:
  0.6 1.5 %copy.45 = bf16[2,1024,256]{1,2,0:T(8,128)(2,1)S(1)} copy(bf16[2,1024,256]{2,1,0:T(8,128)(2,1)} %param.8) | data formatting | bytes 2097152 | tf_op args[0]
  5.8 2.4 %pack.1 = bf16[8,8,2,2,4096]{4,3,2,1,0:T(2,128)(2,1)} custom-call(bf16[8,2,2,2048]{3,2,1,0:T(2,128)(2,1)} %reshape.107.left_ref, bf16[8,2,2,2048]{3,2,1,0:T(2,128)(2,1)} %bitcast.111), custom_call_target="tpu_custom_call" | custom-call | bytes 2097152 | tf_op jit(solution)/shard_map/pack/pallas_call | solution.py:206
  8.3 12.0 %all-to-all-start = ((bf16[128,2,4096]{2,1,0:T(2,128)(2,1)}), bf16[128,2,4096]{2,1,0:T(2,128)(2,1)}, u32[]{:S(2)}, u32[]{:S(2)}) async-start(bf16[128,2,4096]{2,1,0:T(2,128)(2,1)} %bitcast.108), calls=%async_computation | async-start | bytes 4194304 | tf_op jit(solution)/shard_map/all_to_all | solution.py:270
  20.7 2.9 %copy.85 = bf16[128,64,128]{2,0,1:T(8,128)(2,1)S(1)} copy(bf16[128,64,128]{2,1,0:T(8,128)(2,1)} %param.13) | data formatting | bytes 4194304 | tf_op args[5]
  23.6 9.6 %outer_grads.1.grad_ref = bf16[2048,4096]{1,0:T(8,128)(2,1)} custom-call(bf16[1024,128]{1,0:T(8,128)(2,1)S(1)} %copy.55.weight_ref, bf16[64,128,128]{2,1,0:T(8,128)(2,1)S(1)} %bitcast.103), custom_call_target="tpu_custom_call" | custom-call | flops 2147483648 | bytes 18874368 | tf_op jit(solution)/shard_map/outer_grads/pallas_call | solution.py:152
  33.3 17.1 %all-to-all-done = bf16[128,2,4096]{2,1,0:T(2,128)(2,1)} async-done(((bf16[128,2,4096]{2,1,0:T(2,128)(2,1)}), bf16[128,2,4096]{2,1,0:T(2,128)(2,1)}, u32[]{:S(2)}, u32[]{:S(2)}) %all-to-all-start) | async-done | bytes 2097184 | tf_op jit(solution)/shard_map/all_to_all | solution.py:270
  50.4 2.7 %reshape.110.came_ref.own_ref.right_ref = bf16[256,4096]{1,0:T(8,128)(2,1)S(1)} reshape(bf16[128,2,4096]{2,1,0:T(2,128)(2,1)} %all-to-all-done) | data formatting | bytes 4194304 | tf_op jit(solution)/shard_map/reshape | solution.py:376
  53.2 1.0 collective-permute-start
  54.5 10.0 %left_grads.1 = (bf16[256,4096]{1,0:T(8,128)(2,1)S(1)}, f32[256,2048]{1,0:T(8,128)S(1)}) custom-call(bf16[256,4096]{1,0:T(8,128)(2,1)} %copy-done.2, bf16[2048,4096]{1,0:T(8,128)(2,1)} %outer_grads.1.grad_ref), custom_call_target="tpu_custom_call" | custom-call | flops 6442450944 | bytes 22020096 | tf_op jit(solution)/shard_map/left_grads/pallas_call | solution.py:169
  64.6 1.2 collective-permute-start.1
  65.8 4.6 %right_grads.1 = bf16[256,2048]{1,0:T(8,128)(2,1)S(1)} custom-call(bf16[256,2048]{1,0:T(8,128)(2,1)S(1)} %collective-permute-done.other_ref, f32[256,2048]{1,0:T(8,128)S(1)} %get-tuple-element.31.partial_ref, bf16[2048,4096]{1,0:T(8,128)(2,1)} %outer_grads.1.grad_ref), custom_call_target="tpu_custom_call" | custom-call | flops 2147483648 | bytes 12582912 | tf_op jit(solution)/shard_map/right_grads/pallas_call | solution.py:191
  71.0 2.7 %reshape.111 = bf16[128,2,4096]{2,1,0:T(2,128)(2,1)} reshape(bf16[256,4096]{1,0:T(8,128)(2,1)S(1)} %pad_maximum_fusion) | data formatting | bytes 4194304 | tf_op jit(solution)/shard_map/reshape | solution.py:383
  73.6 4.8 %all-to-all-start.1 = ((bf16[128,2,4096]{2,1,0:T(2,128)(2,1)}), bf16[128,2,4096]{2,1,0:T(2,128)(2,1)}, u32[]{:S(2)}, u32[]{:S(2)}) async-start(bf16[128,2,4096]{2,1,0:T(2,128)(2,1)} %reshape.111), calls=%async_computation.1 | async-start | bytes 4194304 | tf_op jit(solution)/shard_map/all_to_all | solution.py:270
  78.5 14.7 %forward.1 = (bf16[64,128,128]{2,1,0:T(8,128)(2,1)S(1)}, f32[1024,128]{1,0:T(8,128)S(1)}) custom-call(s32[1]{0:T(128)} %bitcast.7.core_ref, bf16[256,4096]{1,0:T(8,128)(2,1)S(1)} %copy-done.3, bf16[256,2048]{1,0:T(8,128)(2,1)S(1)} %collective-permute-done.other_ref, bf16[256,4096]{1,0:T(8,128)(2,1)S(1)} %copy-done.3, bf16[128,1024]{1,0:T(8,128)(2,1)S(1)} %bitcast.105, ...), custom_call_target="tpu_custom_call" | custom-call | flops 8589934592 | bytes 8388608 | tf_op jit(solution)/shard_map/forward/pallas_call | solution.py:222
  93.3 1.3 copy-done.4
  95.4 1.2 collective-permute-start.6
  96.6 1.2 collective-permute-done.6
  99.9 2.4 %collective-permute-start.8 = (f32[16,8,128]{2,1,0:T(8,128)}, f32[16,8,128]{2,1,0:T(8,128)}, u32[]{:S(2)}, u32[]{:S(2)}) collective-permute-start(f32[16,8,128]{2,1,0:T(8,128)} %get-tuple-element.50), channel_id=1, source_target_pairs={{0,4},{1,5},{2,6},{3,7},{4,0},{5,1},{6,2},{7,3},{8,12},{9,13},{10,... | collective-permute-start | bytes 196616 | tf_op jit(solution)/shard_map/ppermute | solution.py:296
  102.4 6.2 %all-to-all-done.1 = bf16[128,2,4096]{2,1,0:T(2,128)(2,1)} async-done(((bf16[128,2,4096]{2,1,0:T(2,128)(2,1)}), bf16[128,2,4096]{2,1,0:T(2,128)(2,1)}, u32[]{:S(2)}, u32[]{:S(2)}) %all-to-all-start.1) | async-done | bytes 2097184 | tf_op jit(solution)/shard_map/all_to_all | solution.py:270
  108.6 2.7 %reshape.112 = bf16[256,4096]{1,0:T(8,128)(2,1)S(1)} reshape(bf16[128,2,4096]{2,1,0:T(2,128)(2,1)} %all-to-all-done.1) | data formatting | bytes 4194304 | tf_op jit(solution)/shard_map/reshape | solution.py:385
  112.1 1.0 fusion.6
  114.5 1.0 collective-permute-start.2
  116.8 2.5 %collective-permute-start.5 = (f32[32,256]{1,0:T(8,128)S(1)}, f32[32,256]{1,0:T(8,128)S(1)}, u32[]{:S(2)}, u32[]{:S(2)}) collective-permute-start(f32[32,256]{1,0:T(8,128)S(1)} %select_add_fusion), channel_id=1, source_target_pairs={{0,6},{1,7},{2,4},{3,5},{4,2},{5,3},{6,0},{7,1},{8,14},{9,15},{10,... | collective-permute-start | bytes 98312 | tf_op jit(solution)/shard_map/ppermute | solution.py:296
  119.3 1.3 collective-permute-done.4
  121.0 1.2 collective-permute-done.3
  122.2 2.7 %collective-permute-done.9 = f32[16,8,128]{2,1,0:T(8,128)S(1)} collective-permute-done((f32[16,8,128]{2,1,0:T(8,128)S(1)}, f32[16,8,128]{2,1,0:T(8,128)S(1)}, u32[]{:S(2)}, u32[]{:S(2)}) %collective-permute-start.9) | collective-permute-done | bytes 65568 | tf_op jit(solution)/shard_map/ppermute | solution.py:296
  127.0 2.8 %collective-permute-start.12 = (f32[32,384]{1,0:T(8,128)S(1)}, f32[32,384]{1,0:T(8,128)S(1)}, u32[]{:S(2)}, u32[]{:S(2)}) collective-permute-start(f32[32,384]{1,0:T(8,128)S(1)} %get-tuple-element.64), channel_id=1, source_target_pairs={{0,24},{1,25},{2,26},{3,27},{4,28},{5,29},{6,30},{7,31},{8,16},{9,... | collective-permute-start | bytes 147464 | tf_op jit(solution)/shard_map/ppermute | solution.py:296
  130.4 1.3 flip.1
  131.9 1.7 %collective-permute-start.14 = (f32[32,384]{1,0:T(8,128)S(1)}, f32[32,384]{1,0:T(8,128)S(1)}, u32[]{:S(2)}, u32[]{:S(2)}) collective-permute-start(f32[32,384]{1,0:T(8,128)S(1)} %get-tuple-element.63), channel_id=1, source_target_pairs={{0,64},{1,65},{2,66},{3,67},{4,68},{5,69},{6,70},{7,71},{8,72},{9,... | collective-permute-start | bytes 147464 | tf_op jit(solution)/shard_map/ppermute | solution.py:296
  133.6 2.1 %collective-permute-start.15 = (f32[32,384]{1,0:T(8,128)S(1)}, f32[32,384]{1,0:T(8,128)S(1)}, u32[]{:S(2)}, u32[]{:S(2)}) collective-permute-start(f32[32,384]{1,0:T(8,128)S(1)} %get-tuple-element.61), channel_id=1, source_target_pairs={{0,96},{1,97},{2,98},{3,99},{4,100},{5,101},{6,102},{7,103},{8,104... | collective-permute-start | bytes 147464 | tf_op jit(solution)/shard_map/ppermute | solution.py:296
  135.7 2.7 %copy.84 = bf16[64,128,128]{2,0,1:T(8,128)(2,1)} copy(bf16[64,128,128]{2,1,0:T(8,128)(2,1)S(1)} %copy-done.5) | data formatting | bytes 4194304 | tf_op jit(solution)/shard_map/optimization_barrier | solution.py:393
  138.5 5.2 %collective-permute-start.16 = (f32[32,256]{1,0:T(8,128)S(1)}, f32[32,256]{1,0:T(8,128)S(1)}, u32[]{:S(2)}, u32[]{:S(2)}) collective-permute-start(f32[32,256]{1,0:T(8,128)S(1)} %slice.49), channel_id=1, source_target_pairs={{0,1},{1,0},{2,3},{3,2},{4,5},{5,4},{6,7},{7,6},{8,9},{9,8},{10,11... | collective-permute-start | bytes 98312 | tf_op jit(solution)/shard_map/ppermute | solution.py:296
  (94 shorter events, 16.1 us)
Async XLA Ops:
  0.6 2.1 %copy-start = (bf16[256,32]{0,1:T(8,128)(2,1)S(1)}, bf16[256,32]{0,1:T(8,128)(2,1)}, u32[]{:S(2)}) copy-start(bf16[256,32]{0,1:T(8,128)(2,1)} %param.9) | copy-start | bytes 49156
  2.1 1.7 %copy-start.7 = (bf16[2,1024,256]{1,2,0:T(8,128)(2,1)}, bf16[2,1024,256]{1,2,0:T(8,128)(2,1)S(1)}, u32[]{:S(2)}) copy-start(bf16[2,1024,256]{1,2,0:T(8,128)(2,1)S(1)} %copy.45) | copy-start | bytes 3145732
  2.2 1.7 %copy-start.11 = (bf16[256,32]{0,1:T(8,128)(2,1)S(1)}, bf16[256,32]{0,1:T(8,128)(2,1)}, u32[]{:S(2)}) copy-start(bf16[256,32]{0,1:T(8,128)(2,1)} %param.10) | copy-start | bytes 49156
  8.2 12.0 %copy-start.9 = (bf16[1024,128]{1,0:T(8,128)(2,1)S(1)}, bf16[1024,128]{1,0:T(8,128)(2,1)}, u32[]{:S(2)}) copy-start(bf16[1024,128]{1,0:T(8,128)(2,1)} %param.11) | copy-start | bytes 786436
  8.3 42.1 %all-to-all-start = ((bf16[128,2,4096]{2,1,0:T(2,128)(2,1)}), bf16[128,2,4096]{2,1,0:T(2,128)(2,1)}, u32[]{:S(2)}, u32[]{:S(2)}) async-start(bf16[128,2,4096]{2,1,0:T(2,128)(2,1)} %bitcast.108), calls=%async_computation | async-start | bytes 4194304 | tf_op jit(solution)/shard_map/all_to_all | solution.py:270
  23.6 9.6 %copy-start.1 = (bf16[128,64,128]{2,0,1:T(8,128)(2,1)}, bf16[128,64,128]{2,0,1:T(8,128)(2,1)S(1)}, u32[]{:S(2)}) copy-start(bf16[128,64,128]{2,0,1:T(8,128)(2,1)S(1)} %copy.85) | copy-start | bytes 6291460
  53.1 1.3 copy-start.2
  53.2 11.3 %collective-permute-start = (bf16[256,2048]{1,0:T(8,128)(2,1)S(1)}, bf16[256,2048]{1,0:T(8,128)(2,1)S(1)}, u32[]{:S(2)}, u32[]{:S(2)}) collective-permute-start(bf16[256,2048]{1,0:T(8,128)(2,1)S(1)} %slice.46), channel_id=1, source_target_pairs={{0,1},{1,0},{2,3},{3,2},{4,5},{5,4},{6,7},{7,6},{8,9},{9,8},{10,11... | collective-permute-start | bytes 3145736 | tf_op jit(solution)/shard_map/ppermute | solution.py:274
  64.6 5.8 %collective-permute-start.1 = (bf16[256,2048]{1,0:T(8,128)(2,1)S(1)}, bf16[256,2048]{1,0:T(8,128)(2,1)S(1)}, u32[]{:S(2)}, u32[]{:S(2)}) collective-permute-start(bf16[256,2048]{1,0:T(8,128)(2,1)S(1)} %slice.37), channel_id=1, source_target_pairs={{0,1},{1,0},{2,3},{3,2},{4,5},{5,4},{6,7},{7,6},{8,9},{9,8},{10,11... | collective-permute-start | bytes 3145736 | tf_op jit(solution)/shard_map/ppermute | solution.py:274
  73.6 4.9 %copy-start.13 = (bf16[128]{0:T(256)(128)(2,1)S(1)}, bf16[128]{0:T(256)(128)(2,1)}, u32[]{:S(2)}) copy-start(bf16[128]{0:T(256)(128)(2,1)} %param.12) | copy-start | bytes 772
  73.6 4.9 %copy-start.3 = (bf16[256,4096]{1,0:T(8,128)(2,1)S(1)}, bf16[256,4096]{1,0:T(8,128)(2,1)}, u32[]{:S(2)}) copy-start(bf16[256,4096]{1,0:T(8,128)(2,1)} %copy-done.2) | copy-start | bytes 6291460
  73.6 35.0 %all-to-all-start.1 = ((bf16[128,2,4096]{2,1,0:T(2,128)(2,1)}), bf16[128,2,4096]{2,1,0:T(2,128)(2,1)}, u32[]{:S(2)}, u32[]{:S(2)}) async-start(bf16[128,2,4096]{2,1,0:T(2,128)(2,1)} %reshape.111), calls=%async_computation.1 | async-start | bytes 4194304 | tf_op jit(solution)/shard_map/all_to_all | solution.py:270
  93.3 1.3 copy-start.4
  95.4 2.3 %collective-permute-start.6 = (f32[64,8,128]{2,1,0:T(8,128)S(1)}, f32[64,8,128]{2,1,0:T(8,128)S(1)}, u32[]{:S(2)}, u32[]{:S(2)}) collective-permute-start(f32[64,8,128]{2,1,0:T(8,128)S(1)} %dynamic-slice_bitcast_fusion), channel_id=1, source_target_pairs={{0,1},{1,0},{2,3},{3,2},{4,5},{5,4},{6,7},{7,6},{8,9},{9,8},{10,11... | collective-permute-start | bytes 786440 | tf_op jit(solution)/shard_map/ppermute | solution.py:296
  99.4 22.8 %collective-permute-start.7 = (f32[16,8,128]{2,1,0:T(8,128)}, f32[16,8,128]{2,1,0:T(8,128)}, u32[]{:S(2)}, u32[]{:S(2)}) collective-permute-start(f32[16,8,128]{2,1,0:T(8,128)} %get-tuple-element.51), channel_id=1, source_target_pairs={{0,2},{1,3},{2,0},{3,1},{4,6},{5,7},{6,4},{7,5},{8,10},{9,11},{10,... | collective-permute-start | bytes 196616 | tf_op jit(solution)/shard_map/ppermute | solution.py:296
  99.9 11.4 %copy-start.12 = (bf16[32,256]{1,0:T(8,128)(2,1)S(1)}, bf16[32,256]{1,0:T(8,128)(2,1)}, u32[]{:S(2)}) copy-start(bf16[32,256]{1,0:T(8,128)(2,1)} %constant.144.clone) | copy-start | bytes 49156
  99.9 11.8 %copy-start.8 = (bf16[2,1024,256]{1,2,0:T(8,128)(2,1)S(1)}, bf16[2,1024,256]{1,2,0:T(8,128)(2,1)}, u32[]{:S(2)}) copy-start(bf16[2,1024,256]{1,2,0:T(8,128)(2,1)} %copy-done.7) | copy-start | bytes 3145732
  99.9 22.3 %collective-permute-start.8 = (f32[16,8,128]{2,1,0:T(8,128)}, f32[16,8,128]{2,1,0:T(8,128)}, u32[]{:S(2)}, u32[]{:S(2)}) collective-permute-start(f32[16,8,128]{2,1,0:T(8,128)} %get-tuple-element.50), channel_id=1, source_target_pairs={{0,4},{1,5},{2,6},{3,7},{4,0},{5,1},{6,2},{7,3},{8,12},{9,13},{10,... | collective-permute-start | bytes 196616 | tf_op jit(solution)/shard_map/ppermute | solution.py:296
  114.4 6.2 %copy-start.10 = (f32[16,8,128]{2,1,0:T(8,128)S(1)}, f32[16,8,128]{2,1,0:T(8,128)}, u32[]{:S(2)}) copy-start(f32[16,8,128]{2,1,0:T(8,128)} %get-tuple-element.49) | copy-start | bytes 196612
  114.5 1.9 %collective-permute-start.2 = (f32[32,256]{1,0:T(8,128)S(1)}, f32[32,256]{1,0:T(8,128)S(1)}, u32[]{:S(2)}, u32[]{:S(2)}) collective-permute-start(f32[32,256]{1,0:T(8,128)S(1)} %get-tuple-element.71), channel_id=1, source_target_pairs={{0,1},{1,0},{2,3},{3,2},{4,5},{5,4},{6,7},{7,6},{8,9},{9,8},{10,11... | collective-permute-start | bytes 98312 | tf_op jit(solution)/shard_map/ppermute | solution.py:296
  116.3 4.3 %collective-permute-start.4 = (f32[32,256]{1,0:T(8,128)S(1)}, f32[32,256]{1,0:T(8,128)S(1)}, u32[]{:S(2)}, u32[]{:S(2)}) collective-permute-start(f32[32,256]{1,0:T(8,128)S(1)} %select_add_fusion), channel_id=1, source_target_pairs={{0,4},{1,5},{2,6},{3,7},{4,0},{5,1},{6,2},{7,3},{8,12},{9,13},{10,... | collective-permute-start | bytes 98312 | tf_op jit(solution)/shard_map/ppermute | solution.py:296
  116.8 4.1 %collective-permute-start.5 = (f32[32,256]{1,0:T(8,128)S(1)}, f32[32,256]{1,0:T(8,128)S(1)}, u32[]{:S(2)}, u32[]{:S(2)}) collective-permute-start(f32[32,256]{1,0:T(8,128)S(1)} %select_add_fusion), channel_id=1, source_target_pairs={{0,6},{1,7},{2,4},{3,5},{4,2},{5,3},{6,0},{7,1},{8,14},{9,15},{10,... | collective-permute-start | bytes 98312 | tf_op jit(solution)/shard_map/ppermute | solution.py:296
  119.3 2.9 %collective-permute-start.3 = (f32[32,256]{1,0:T(8,128)S(1)}, f32[32,256]{1,0:T(8,128)S(1)}, u32[]{:S(2)}, u32[]{:S(2)}) collective-permute-start(f32[32,256]{1,0:T(8,128)S(1)} %select_add_fusion), channel_id=1, source_target_pairs={{0,2},{1,3},{2,0},{3,1},{4,6},{5,7},{6,4},{7,5},{8,10},{9,11},{10,... | collective-permute-start | bytes 98312 | tf_op jit(solution)/shard_map/ppermute | solution.py:296
  120.6 4.3 %collective-permute-start.9 = (f32[16,8,128]{2,1,0:T(8,128)S(1)}, f32[16,8,128]{2,1,0:T(8,128)S(1)}, u32[]{:S(2)}, u32[]{:S(2)}) collective-permute-start(f32[16,8,128]{2,1,0:T(8,128)S(1)} %copy-done.10), channel_id=1, source_target_pairs={{0,6},{1,7},{2,4},{3,5},{4,2},{5,3},{6,0},{7,1},{8,14},{9,15},{10,... | collective-permute-start | bytes 196616 | tf_op jit(solution)/shard_map/ppermute | solution.py:296
  125.9 5.8 %collective-permute-start.10 = (f32[32,384]{1,0:T(8,128)S(1)}, f32[32,384]{1,0:T(8,128)S(1)}, u32[]{:S(2)}, u32[]{:S(2)}) collective-permute-start(f32[32,384]{1,0:T(8,128)S(1)} %get-tuple-element.65), channel_id=1, source_target_pairs={{0,8},{1,9},{2,10},{3,11},{4,12},{5,13},{6,14},{7,15},{8,0},{9,1},... | collective-permute-start | bytes 147464 | tf_op jit(solution)/shard_map/ppermute | solution.py:296
  126.1 5.6 %collective-permute-start.11 = (f32[32,384]{1,0:T(8,128)S(1)}, f32[32,384]{1,0:T(8,128)S(1)}, u32[]{:S(2)}, u32[]{:S(2)}) collective-permute-start(f32[32,384]{1,0:T(8,128)S(1)} %get-tuple-element.66), channel_id=1, source_target_pairs={{0,16},{1,17},{2,18},{3,19},{4,20},{5,21},{6,22},{7,23},{8,24},{9,... | collective-permute-start | bytes 147464 | tf_op jit(solution)/shard_map/ppermute | solution.py:296
  127.0 4.7 %collective-permute-start.12 = (f32[32,384]{1,0:T(8,128)S(1)}, f32[32,384]{1,0:T(8,128)S(1)}, u32[]{:S(2)}, u32[]{:S(2)}) collective-permute-start(f32[32,384]{1,0:T(8,128)S(1)} %get-tuple-element.64), channel_id=1, source_target_pairs={{0,24},{1,25},{2,26},{3,27},{4,28},{5,29},{6,30},{7,31},{8,16},{9,... | collective-permute-start | bytes 147464 | tf_op jit(solution)/shard_map/ppermute | solution.py:296
  130.4 5.4 %copy-start.5 = (bf16[64,128,128]{2,1,0:T(8,128)(2,1)S(1)}, bf16[64,128,128]{2,1,0:T(8,128)(2,1)}, u32[]{:S(2)}) copy-start(bf16[64,128,128]{2,1,0:T(8,128)(2,1)} %copy-done.4) | copy-start | bytes 6291460
  131.8 6.6 %collective-permute-start.13 = (f32[32,384]{1,0:T(8,128)S(1)}, f32[32,384]{1,0:T(8,128)S(1)}, u32[]{:S(2)}, u32[]{:S(2)}) collective-permute-start(f32[32,384]{1,0:T(8,128)S(1)} %get-tuple-element.62), channel_id=1, source_target_pairs={{0,32},{1,33},{2,34},{3,35},{4,36},{5,37},{6,38},{7,39},{8,40},{9,... | collective-permute-start | bytes 147464 | tf_op jit(solution)/shard_map/ppermute | solution.py:296
  131.9 6.5 %collective-permute-start.14 = (f32[32,384]{1,0:T(8,128)S(1)}, f32[32,384]{1,0:T(8,128)S(1)}, u32[]{:S(2)}, u32[]{:S(2)}) collective-permute-start(f32[32,384]{1,0:T(8,128)S(1)} %get-tuple-element.63), channel_id=1, source_target_pairs={{0,64},{1,65},{2,66},{3,67},{4,68},{5,69},{6,70},{7,71},{8,72},{9,... | collective-permute-start | bytes 147464 | tf_op jit(solution)/shard_map/ppermute | solution.py:296
  133.6 4.8 %collective-permute-start.15 = (f32[32,384]{1,0:T(8,128)S(1)}, f32[32,384]{1,0:T(8,128)S(1)}, u32[]{:S(2)}, u32[]{:S(2)}) collective-permute-start(f32[32,384]{1,0:T(8,128)S(1)} %get-tuple-element.61), channel_id=1, source_target_pairs={{0,96},{1,97},{2,98},{3,99},{4,100},{5,101},{6,102},{7,103},{8,104... | collective-permute-start | bytes 147464 | tf_op jit(solution)/shard_map/ppermute | solution.py:296
  138.5 6.1 %collective-permute-start.16 = (f32[32,256]{1,0:T(8,128)S(1)}, f32[32,256]{1,0:T(8,128)S(1)}, u32[]{:S(2)}, u32[]{:S(2)}) collective-permute-start(f32[32,256]{1,0:T(8,128)S(1)} %slice.49), channel_id=1, source_target_pairs={{0,1},{1,0},{2,3},{3,2},{4,5},{5,4},{6,7},{7,6},{8,9},{9,8},{10,11... | collective-permute-start | bytes 98312 | tf_op jit(solution)/shard_map/ppermute | solution.py:296
  (1 other events, 0.8 us)

commit v10 on v8

--- a/solution.py
+++ b/solution.py
@@ -46,12 +46,13 @@
 
 
 def left_kernel(inverse, came_ref, grad_ref, out_ref, partial_ref, panel_ref, held_ref, sems):
-    blocks = sems.shape[0] - 1
+    blocks = sems.shape[0] - 2
     depth, columns = held_ref.shape
     block, half = columns // blocks, columns // CORES
-    panel = pltpu.make_async_copy(came_ref, panel_ref, sems.at[blocks])
+    panel = pltpu.make_async_copy(came_ref, panel_ref, sems.at[blocks + 1])
     panel.start()
-    parts = [pl.ds(n * block, block) for n in range(blocks)]
+    parts = [pl.ds(0, block // 2), pl.ds(block // 2, block // 2)]
+    parts += [pl.ds(n * block, block) for n in range(1, blocks)]
     copies = [
         pltpu.make_async_copy(grad_ref.at[:, part], held_ref.at[:, part], sems.at[n]) for n, part in enumerate(parts)
     ]
@@ -59,7 +60,7 @@
         copy.start()
     panel.wait()
     for n, part in enumerate(parts):
-        if n == blocks // CORES:
+        if n == blocks // CORES + 1:
             partial_ref[...] = lax.dot_general(
                 panel_ref[:, :half], held_ref[:, :half], NT, preferred_element_type=jnp.float32
             )
@@ -177,7 +178,7 @@
         scratch_shapes=[
             pltpu.VMEM(came.shape, jnp.bfloat16),
             pltpu.VMEM(grads.shape, jnp.bfloat16),
-            pltpu.SemaphoreType.DMA((BLOCKS + 1,)),
+            pltpu.SemaphoreType.DMA((BLOCKS + 2,)),
         ],
         compiler_params=pltpu.CompilerParams(vmem_limit_bytes=VMEM_BYTES),
         cost_estimate=pl.CostEstimate(flops=3 * seqs * depth * columns, bytes_accessed=21 * 2**20, transcendentals=0),

time: 144 us -> 144 us (level)
  no operation moved by 1% of the time
where the time goes in v10:
time: 144 us
  Pallas kernels  42.7 us (30%)
  starting transfers between devices  41.3 us (29%)
  waiting for transfers between devices  29.6 us (21%)
  local copies, waits for them, and re-layouts  21.6 us (15%)
  matrix products  4.08 us (3%)
  other arithmetic  3.4 us (2%)
    ppermute x15, starting transfers between devices, partner(): lax.ppermute(part, BOTH, [(i, i ^ mask) for i in range(lax.axis_size(BOTH...  22.3 us
    all_to_all x2, waiting for transfers between devices, exchange(): return lax.all_to_all(blocks, BOTH, 0, 0, tiled=True)  18.1 us
    all_to_all x2, starting transfers between devices, exchange(): return lax.all_to_all(blocks, BOTH, 0, 0, tiled=True)  16.8 us
    pallas_call x1, Pallas kernels, forward(): pl.pallas_call(functools.partial(forward_kernel, 1.0 / seqs, width), grid...  14.7 us
    ppermute x15, waiting for transfers between devices, partner(): lax.ppermute(part, BOTH, [(i, i ^ mask) for i in range(lax.axis_size(BOTH...  11.5 us
    pallas_call x1, Pallas kernels, left_grads(): pl.pallas_call(functools.partial(left_kernel, 1.0 / seqs), in_specs=[pl.B...  10.1 us
    pallas_call x1, Pallas kernels, outer_grads(): pl.pallas_call(functools.partial(outer_grad_kernel, width), grid=(cols //...  9.63 us
    unnamed x30, local copies, waits for them, and re-layouts  7.02 us
  transfers between devices with their start and end apart: 19, of which 12 were waited for; matrix products, arithmetic and copies ran while one was open for 6% of the time, Pallas kernels for 28%

profile of v10, /device:TPU:1, one launch (start us, length us, event | category | flops | bytes accessed | tf_op | source)
XLA Modules:
  0.0 143.9 jit_solution(7966506186719131168)
XLA Ops:
  0.6 1.5 %copy.45 = bf16[2,1024,256]{1,2,0:T(8,128)(2,1)S(1)} copy(bf16[2,1024,256]{2,1,0:T(8,128)(2,1)} %param.8) | data formatting | bytes 2097152 | tf_op args[0]
  5.8 2.4 %pack.1 = bf16[8,8,2,2,4096]{4,3,2,1,0:T(2,128)(2,1)} custom-call(bf16[8,2,2,2048]{3,2,1,0:T(2,128)(2,1)} %reshape.107.left_ref, bf16[8,2,2,2048]{3,2,1,0:T(2,128)(2,1)} %bitcast.114), custom_call_target="tpu_custom_call" | custom-call | bytes 2097152 | tf_op jit(solution)/shard_map/pack/pallas_call | solution.py:207
  8.3 12.0 %all-to-all-start = ((bf16[128,2,4096]{2,1,0:T(2,128)(2,1)}), bf16[128,2,4096]{2,1,0:T(2,128)(2,1)}, u32[]{:S(2)}, u32[]{:S(2)}) async-start(bf16[128,2,4096]{2,1,0:T(2,128)(2,1)} %bitcast.110), calls=%async_computation | async-start | bytes 4194304 | tf_op jit(solution)/shard_map/all_to_all | solution.py:271
  20.7 2.9 %copy.85 = bf16[128,64,128]{2,0,1:T(8,128)(2,1)S(1)} copy(bf16[128,64,128]{2,1,0:T(8,128)(2,1)} %param.13) | data formatting | bytes 4194304 | tf_op args[5]
  23.7 9.6 %outer_grads.1.grad_ref = bf16[2048,4096]{1,0:T(8,128)(2,1)} custom-call(bf16[1024,128]{1,0:T(8,128)(2,1)S(1)} %copy.55.weight_ref, bf16[64,128,128]{2,1,0:T(8,128)(2,1)S(1)} %bitcast.105), custom_call_target="tpu_custom_call" | custom-call | flops 2147483648 | bytes 18874368 | tf_op jit(solution)/shard_map/outer_grads/pallas_call | solution.py:153
  33.3 17.1 %all-to-all-done = bf16[128,2,4096]{2,1,0:T(2,128)(2,1)} async-done(((bf16[128,2,4096]{2,1,0:T(2,128)(2,1)}), bf16[128,2,4096]{2,1,0:T(2,128)(2,1)}, u32[]{:S(2)}, u32[]{:S(2)}) %all-to-all-start) | async-done | bytes 2097184 | tf_op jit(solution)/shard_map/all_to_all | solution.py:271
  50.4 2.7 %reshape.110.came_ref.own_ref.right_ref = bf16[256,4096]{1,0:T(8,128)(2,1)S(1)} reshape(bf16[128,2,4096]{2,1,0:T(2,128)(2,1)} %all-to-all-done) | data formatting | bytes 4194304 | tf_op jit(solution)/shard_map/reshape | solution.py:374
  54.5 10.1 %left_grads.1 = (bf16[256,4096]{1,0:T(8,128)(2,1)S(1)}, f32[256,2048]{1,0:T(8,128)S(1)}) custom-call(bf16[256,4096]{1,0:T(8,128)(2,1)} %copy-done.2, bf16[2048,4096]{1,0:T(8,128)(2,1)} %outer_grads.1.grad_ref), custom_call_target="tpu_custom_call" | custom-call | flops 6442450944 | bytes 22020096 | tf_op jit(solution)/shard_map/left_grads/pallas_call | solution.py:170
  64.7 1.2 collective-permute-start.1
  65.8 4.6 %right_grads.1 = bf16[256,2048]{1,0:T(8,128)(2,1)S(1)} custom-call(bf16[256,2048]{1,0:T(8,128)(2,1)S(1)} %collective-permute-done.other_ref, f32[256,2048]{1,0:T(8,128)S(1)} %get-tuple-element.27.partial_ref, bf16[2048,4096]{1,0:T(8,128)(2,1)} %outer_grads.1.grad_ref), custom_call_target="tpu_custom_call" | custom-call | flops 2147483648 | bytes 12582912 | tf_op jit(solution)/shard_map/right_grads/pallas_call | solution.py:192
  71.0 2.6 %reshape.111 = bf16[128,2,4096]{2,1,0:T(2,128)(2,1)} reshape(bf16[256,4096]{1,0:T(8,128)(2,1)S(1)} %pad_maximum_fusion) | data formatting | bytes 4194304 | tf_op jit(solution)/shard_map/reshape | solution.py:381
  73.6 4.8 %all-to-all-start.1 = ((bf16[128,2,4096]{2,1,0:T(2,128)(2,1)}), bf16[128,2,4096]{2,1,0:T(2,128)(2,1)}, u32[]{:S(2)}, u32[]{:S(2)}) async-start(bf16[128,2,4096]{2,1,0:T(2,128)(2,1)} %reshape.111), calls=%async_computation.1 | async-start | bytes 4194304 | tf_op jit(solution)/shard_map/all_to_all | solution.py:271
  78.5 14.7 %forward.1 = (bf16[64,128,128]{2,1,0:T(8,128)(2,1)S(1)}, f32[1024,128]{1,0:T(8,128)S(1)}) custom-call(s32[1]{0:T(128)} %bitcast.7.core_ref, bf16[256,4096]{1,0:T(8,128)(2,1)S(1)} %copy-done.3, bf16[256,2048]{1,0:T(8,128)(2,1)S(1)} %collective-permute-done.other_ref, bf16[256,4096]{1,0:T(8,128)(2,1)S(1)} %copy-done.3, bf16[128,1024]{1,0:T(8,128)(2,1)S(1)} %bitcast.107, ...), custom_call_target="tpu_custom_call" | custom-call | flops 8589934592 | bytes 8388608 | tf_op jit(solution)/shard_map/forward/pallas_call | solution.py:223
  93.3 1.3 copy-done.4
  95.4 1.2 collective-permute-start.2
  96.6 1.2 collective-permute-done.2
  99.4 2.4 %collective-permute-start.4 = (f32[16,8,128]{2,1,0:T(8,128)S(1)}, f32[16,8,128]{2,1,0:T(8,128)S(1)}, u32[]{:S(2)}, u32[]{:S(2)}) collective-permute-start(f32[16,8,128]{2,1,0:T(8,128)S(1)} %get-tuple-element.42), channel_id=1, source_target_pairs={{0,4},{1,5},{2,6},{3,7},{4,0},{5,1},{6,2},{7,3},{8,12},{9,13},{10,... | collective-permute-start | bytes 196616 | tf_op jit(solution)/shard_map/ppermute | solution.py:297
  103.3 2.9 %collective-permute-done.4 = f32[16,8,128]{2,1,0:T(8,128)S(1)} collective-permute-done((f32[16,8,128]{2,1,0:T(8,128)S(1)}, f32[16,8,128]{2,1,0:T(8,128)S(1)}, u32[]{:S(2)}, u32[]{:S(2)}) %collective-permute-start.4) | collective-permute-done | bytes 65568 | tf_op jit(solution)/shard_map/ppermute | solution.py:297
  106.2 1.4 collective-permute-done.5
  108.6 2.7 %reshape.112 = bf16[256,4096]{1,0:T(8,128)(2,1)S(1)} reshape(bf16[128,2,4096]{2,1,0:T(2,128)(2,1)} %all-to-all-done.1) | data formatting | bytes 4194304 | tf_op jit(solution)/shard_map/reshape | solution.py:383
  114.5 1.5 %collective-permute-start.6 = (f32[32,256]{1,0:T(8,128)S(1)}, f32[32,256]{1,0:T(8,128)S(1)}, u32[]{:S(2)}, u32[]{:S(2)}) collective-permute-start(f32[32,256]{1,0:T(8,128)S(1)} %get-tuple-element.62), channel_id=1, source_target_pairs={{0,1},{1,0},{2,3},{3,2},{4,5},{5,4},{6,7},{7,6},{8,9},{9,8},{10,11... | collective-permute-start | bytes 98312 | tf_op jit(solution)/shard_map/ppermute | solution.py:297
  116.8 2.7 %collective-permute-start.9 = (f32[32,256]{1,0:T(8,128)S(1)}, f32[32,256]{1,0:T(8,128)S(1)}, u32[]{:S(2)}, u32[]{:S(2)}) collective-permute-start(f32[32,256]{1,0:T(8,128)S(1)} %select_add_fusion), channel_id=1, source_target_pairs={{0,6},{1,7},{2,4},{3,5},{4,2},{5,3},{6,0},{7,1},{8,14},{9,15},{10,... | collective-permute-start | bytes 98312 | tf_op jit(solution)/shard_map/ppermute | solution.py:297
  119.5 1.7 %collective-permute-done.8 = f32[32,256]{1,0:T(8,128)S(1)} collective-permute-done((f32[32,256]{1,0:T(8,128)S(1)}, f32[32,256]{1,0:T(8,128)S(1)}, u32[]{:S(2)}, u32[]{:S(2)}) %collective-permute-start.8) | collective-permute-done | bytes 32800 | tf_op jit(solution)/shard_map/ppermute | solution.py:297
  121.2 1.2 collective-permute-done.7
  122.5 2.3 %collective-permute-start.11 = (f32[32,384]{1,0:T(8,128)S(1)}, f32[32,384]{1,0:T(8,128)S(1)}, u32[]{:S(2)}, u32[]{:S(2)}) collective-permute-start(f32[32,384]{1,0:T(8,128)S(1)} %get-tuple-element.57), channel_id=1, source_target_pairs={{0,16},{1,17},{2,18},{3,19},{4,20},{5,21},{6,22},{7,23},{8,24},{9,... | collective-permute-start | bytes 147464 | tf_op jit(solution)/shard_map/ppermute | solution.py:297
  124.8 1.6 %collective-permute-start.12 = (f32[32,384]{1,0:T(8,128)S(1)}, f32[32,384]{1,0:T(8,128)S(1)}, u32[]{:S(2)}, u32[]{:S(2)}) collective-permute-start(f32[32,384]{1,0:T(8,128)S(1)} %get-tuple-element.55), channel_id=1, source_target_pairs={{0,24},{1,25},{2,26},{3,27},{4,28},{5,29},{6,30},{7,31},{8,16},{9,... | collective-permute-start | bytes 147464 | tf_op jit(solution)/shard_map/ppermute | solution.py:297
  127.0 1.3 flip.1
  129.1 1.9 %collective-permute-start.13 = (f32[32,384]{1,0:T(8,128)S(1)}, f32[32,384]{1,0:T(8,128)S(1)}, u32[]{:S(2)}, u32[]{:S(2)}) collective-permute-start(f32[32,384]{1,0:T(8,128)S(1)} %get-tuple-element.53), channel_id=1, source_target_pairs={{0,32},{1,33},{2,34},{3,35},{4,36},{5,37},{6,38},{7,39},{8,40},{9,... | collective-permute-start | bytes 147464 | tf_op jit(solution)/shard_map/ppermute | solution.py:297
  130.9 2.5 %collective-permute-start.14 = (f32[32,384]{1,0:T(8,128)S(1)}, f32[32,384]{1,0:T(8,128)S(1)}, u32[]{:S(2)}, u32[]{:S(2)}) collective-permute-start(f32[32,384]{1,0:T(8,128)S(1)} %get-tuple-element.54), channel_id=1, source_target_pairs={{0,64},{1,65},{2,66},{3,67},{4,68},{5,69},{6,70},{7,71},{8,72},{9,... | collective-permute-start | bytes 147464 | tf_op jit(solution)/shard_map/ppermute | solution.py:297
  133.5 2.7 %copy.84 = bf16[64,128,128]{2,0,1:T(8,128)(2,1)} copy(bf16[64,128,128]{2,1,0:T(8,128)(2,1)S(1)} %copy-done.5) | data formatting | bytes 4194304 | tf_op jit(solution)/shard_map/optimization_barrier | solution.py:388
  136.2 1.5 %collective-permute-done.15 = f32[32,384]{1,0:T(8,128)S(1)} collective-permute-done((f32[32,384]{1,0:T(8,128)S(1)}, f32[32,384]{1,0:T(8,128)S(1)}, u32[]{:S(2)}, u32[]{:S(2)}) %collective-permute-start.15) | collective-permute-done | bytes 49184 | tf_op jit(solution)/shard_map/ppermute | solution.py:297
  137.6 4.7 %collective-permute-start.16 = (f32[32,256]{1,0:T(8,128)S(1)}, f32[32,256]{1,0:T(8,128)S(1)}, u32[]{:S(2)}, u32[]{:S(2)}) collective-permute-start(f32[32,256]{1,0:T(8,128)S(1)} %slice.49), channel_id=1, source_target_pairs={{0,1},{1,0},{2,3},{3,2},{4,5},{5,4},{6,7},{7,6},{8,9},{9,8},{10,11... | collective-permute-start | bytes 98312 | tf_op jit(solution)/shard_map/ppermute | solution.py:297
  (92 shorter events, 17.9 us)
Async XLA Ops:
  0.6 2.1 %copy-start = (bf16[256,32]{0,1:T(8,128)(2,1)S(1)}, bf16[256,32]{0,1:T(8,128)(2,1)}, u32[]{:S(2)}) copy-start(bf16[256,32]{0,1:T(8,128)(2,1)} %param.9) | copy-start | bytes 49156
  2.1 1.7 %copy-start.7 = (bf16[2,1024,256]{1,2,0:T(8,128)(2,1)}, bf16[2,1024,256]{1,2,0:T(8,128)(2,1)S(1)}, u32[]{:S(2)}) copy-start(bf16[2,1024,256]{1,2,0:T(8,128)(2,1)S(1)} %copy.45) | copy-start | bytes 3145732
  2.2 1.7 %copy-start.10 = (bf16[256,32]{0,1:T(8,128)(2,1)S(1)}, bf16[256,32]{0,1:T(8,128)(2,1)}, u32[]{:S(2)}) copy-start(bf16[256,32]{0,1:T(8,128)(2,1)} %param.10) | copy-start | bytes 49156
  8.3 12.0 %copy-start.9 = (bf16[1024,128]{1,0:T(8,128)(2,1)S(1)}, bf16[1024,128]{1,0:T(8,128)(2,1)}, u32[]{:S(2)}) copy-start(bf16[1024,128]{1,0:T(8,128)(2,1)} %param.11) | copy-start | bytes 786436
  8.3 42.1 %all-to-all-start = ((bf16[128,2,4096]{2,1,0:T(2,128)(2,1)}), bf16[128,2,4096]{2,1,0:T(2,128)(2,1)}, u32[]{:S(2)}, u32[]{:S(2)}) async-start(bf16[128,2,4096]{2,1,0:T(2,128)(2,1)} %bitcast.110), calls=%async_computation | async-start | bytes 4194304 | tf_op jit(solution)/shard_map/all_to_all | solution.py:271
  23.6 9.6 %copy-start.1 = (bf16[128,64,128]{2,0,1:T(8,128)(2,1)}, bf16[128,64,128]{2,0,1:T(8,128)(2,1)S(1)}, u32[]{:S(2)}) copy-start(bf16[128,64,128]{2,0,1:T(8,128)(2,1)S(1)} %copy.85) | copy-start | bytes 6291460
  53.2 1.3 copy-start.2
  53.2 11.3 %collective-permute-start = (bf16[256,2048]{1,0:T(8,128)(2,1)S(1)}, bf16[256,2048]{1,0:T(8,128)(2,1)S(1)}, u32[]{:S(2)}, u32[]{:S(2)}) collective-permute-start(bf16[256,2048]{1,0:T(8,128)(2,1)S(1)} %slice.46), channel_id=1, source_target_pairs={{0,1},{1,0},{2,3},{3,2},{4,5},{5,4},{6,7},{7,6},{8,9},{9,8},{10,11... | collective-permute-start | bytes 3145736 | tf_op jit(solution)/shard_map/ppermute | solution.py:275
  64.7 5.8 %collective-permute-start.1 = (bf16[256,2048]{1,0:T(8,128)(2,1)S(1)}, bf16[256,2048]{1,0:T(8,128)(2,1)S(1)}, u32[]{:S(2)}, u32[]{:S(2)}) collective-permute-start(bf16[256,2048]{1,0:T(8,128)(2,1)S(1)} %slice.37), channel_id=1, source_target_pairs={{0,1},{1,0},{2,3},{3,2},{4,5},{5,4},{6,7},{7,6},{8,9},{9,8},{10,11... | collective-permute-start | bytes 3145736 | tf_op jit(solution)/shard_map/ppermute | solution.py:275
  73.6 4.9 %copy-start.12 = (bf16[128]{0:T(256)(128)(2,1)S(1)}, bf16[128]{0:T(256)(128)(2,1)}, u32[]{:S(2)}) copy-start(bf16[128]{0:T(256)(128)(2,1)} %param.12) | copy-start | bytes 772
  73.6 4.9 %copy-start.3 = (bf16[256,4096]{1,0:T(8,128)(2,1)S(1)}, bf16[256,4096]{1,0:T(8,128)(2,1)}, u32[]{:S(2)}) copy-start(bf16[256,4096]{1,0:T(8,128)(2,1)} %copy-done.2) | copy-start | bytes 6291460
  73.6 35.0 %all-to-all-start.1 = ((bf16[128,2,4096]{2,1,0:T(2,128)(2,1)}), bf16[128,2,4096]{2,1,0:T(2,128)(2,1)}, u32[]{:S(2)}, u32[]{:S(2)}) async-start(bf16[128,2,4096]{2,1,0:T(2,128)(2,1)} %reshape.111), calls=%async_computation.1 | async-start | bytes 4194304 | tf_op jit(solution)/shard_map/all_to_all | solution.py:271
  93.3 1.3 copy-start.4
  94.6 0.8 copy-start.6
  95.4 2.3 %collective-permute-start.2 = (f32[64,8,128]{2,1,0:T(8,128)S(1)}, f32[64,8,128]{2,1,0:T(8,128)S(1)}, u32[]{:S(2)}, u32[]{:S(2)}) collective-permute-start(f32[64,8,128]{2,1,0:T(8,128)S(1)} %dynamic-slice_bitcast_fusion), channel_id=1, source_target_pairs={{0,1},{1,0},{2,3},{3,2},{4,5},{5,4},{6,7},{7,6},{8,9},{9,8},{10,11... | collective-permute-start | bytes 786440 | tf_op jit(solution)/shard_map/ppermute | solution.py:297
  98.8 4.5 %collective-permute-start.3 = (f32[16,8,128]{2,1,0:T(8,128)S(1)}, f32[16,8,128]{2,1,0:T(8,128)S(1)}, u32[]{:S(2)}, u32[]{:S(2)}) collective-permute-start(f32[16,8,128]{2,1,0:T(8,128)S(1)} %get-tuple-element.43), channel_id=1, source_target_pairs={{0,2},{1,3},{2,0},{3,1},{4,6},{5,7},{6,4},{7,5},{8,10},{9,11},{10,... | collective-permute-start | bytes 196616 | tf_op jit(solution)/shard_map/ppermute | solution.py:297
  99.4 6.9 %collective-permute-start.4 = (f32[16,8,128]{2,1,0:T(8,128)S(1)}, f32[16,8,128]{2,1,0:T(8,128)S(1)}, u32[]{:S(2)}, u32[]{:S(2)}) collective-permute-start(f32[16,8,128]{2,1,0:T(8,128)S(1)} %get-tuple-element.42), channel_id=1, source_target_pairs={{0,4},{1,5},{2,6},{3,7},{4,0},{5,1},{6,2},{7,3},{8,12},{9,13},{10,... | collective-permute-start | bytes 196616 | tf_op jit(solution)/shard_map/ppermute | solution.py:297
  101.8 5.8 %collective-permute-start.5 = (f32[16,8,128]{2,1,0:T(8,128)S(1)}, f32[16,8,128]{2,1,0:T(8,128)S(1)}, u32[]{:S(2)}, u32[]{:S(2)}) collective-permute-start(f32[16,8,128]{2,1,0:T(8,128)S(1)} %get-tuple-element.41), channel_id=1, source_target_pairs={{0,6},{1,7},{2,4},{3,5},{4,2},{5,3},{6,0},{7,1},{8,14},{9,15},{10,... | collective-permute-start | bytes 196616 | tf_op jit(solution)/shard_map/ppermute | solution.py:297
  107.6 3.7 %copy-start.11 = (bf16[32,256]{1,0:T(8,128)(2,1)S(1)}, bf16[32,256]{1,0:T(8,128)(2,1)}, u32[]{:S(2)}) copy-start(bf16[32,256]{1,0:T(8,128)(2,1)} %constant.144.clone) | copy-start | bytes 49156
  107.6 4.1 %copy-start.8 = (bf16[2,1024,256]{1,2,0:T(8,128)(2,1)S(1)}, bf16[2,1024,256]{1,2,0:T(8,128)(2,1)}, u32[]{:S(2)}) copy-start(bf16[2,1024,256]{1,2,0:T(8,128)(2,1)} %copy-done.7) | copy-start | bytes 3145732
  114.5 2.3 %collective-permute-start.6 = (f32[32,256]{1,0:T(8,128)S(1)}, f32[32,256]{1,0:T(8,128)S(1)}, u32[]{:S(2)}, u32[]{:S(2)}) collective-permute-start(f32[32,256]{1,0:T(8,128)S(1)} %get-tuple-element.62), channel_id=1, source_target_pairs={{0,1},{1,0},{2,3},{3,2},{4,5},{5,4},{6,7},{7,6},{8,9},{9,8},{10,11... | collective-permute-start | bytes 98312 | tf_op jit(solution)/shard_map/ppermute | solution.py:297
  116.8 4.4 %collective-permute-start.8 = (f32[32,256]{1,0:T(8,128)S(1)}, f32[32,256]{1,0:T(8,128)S(1)}, u32[]{:S(2)}, u32[]{:S(2)}) collective-permute-start(f32[32,256]{1,0:T(8,128)S(1)} %select_add_fusion), channel_id=1, source_target_pairs={{0,4},{1,5},{2,6},{3,7},{4,0},{5,1},{6,2},{7,3},{8,12},{9,13},{10,... | collective-permute-start | bytes 98312 | tf_op jit(solution)/shard_map/ppermute | solution.py:297
  116.8 4.4 %collective-permute-start.9 = (f32[32,256]{1,0:T(8,128)S(1)}, f32[32,256]{1,0:T(8,128)S(1)}, u32[]{:S(2)}, u32[]{:S(2)}) collective-permute-start(f32[32,256]{1,0:T(8,128)S(1)} %select_add_fusion), channel_id=1, source_target_pairs={{0,6},{1,7},{2,4},{3,5},{4,2},{5,3},{6,0},{7,1},{8,14},{9,15},{10,... | collective-permute-start | bytes 98312 | tf_op jit(solution)/shard_map/ppermute | solution.py:297
  119.5 2.9 %collective-permute-start.7 = (f32[32,256]{1,0:T(8,128)S(1)}, f32[32,256]{1,0:T(8,128)S(1)}, u32[]{:S(2)}, u32[]{:S(2)}) collective-permute-start(f32[32,256]{1,0:T(8,128)S(1)} %select_add_fusion), channel_id=1, source_target_pairs={{0,2},{1,3},{2,0},{3,1},{4,6},{5,7},{6,4},{7,5},{8,10},{9,11},{10,... | collective-permute-start | bytes 98312 | tf_op jit(solution)/shard_map/ppermute | solution.py:297
  122.5 5.8 %collective-permute-start.10 = (f32[32,384]{1,0:T(8,128)S(1)}, f32[32,384]{1,0:T(8,128)S(1)}, u32[]{:S(2)}, u32[]{:S(2)}) collective-permute-start(f32[32,384]{1,0:T(8,128)S(1)} %get-tuple-element.56), channel_id=1, source_target_pairs={{0,8},{1,9},{2,10},{3,11},{4,12},{5,13},{6,14},{7,15},{8,0},{9,1},... | collective-permute-start | bytes 147464 | tf_op jit(solution)/shard_map/ppermute | solution.py:297
  122.5 5.7 %collective-permute-start.11 = (f32[32,384]{1,0:T(8,128)S(1)}, f32[32,384]{1,0:T(8,128)S(1)}, u32[]{:S(2)}, u32[]{:S(2)}) collective-permute-start(f32[32,384]{1,0:T(8,128)S(1)} %get-tuple-element.57), channel_id=1, source_target_pairs={{0,16},{1,17},{2,18},{3,19},{4,20},{5,21},{6,22},{7,23},{8,24},{9,... | collective-permute-start | bytes 147464 | tf_op jit(solution)/shard_map/ppermute | solution.py:297
  124.8 4.2 %collective-permute-start.12 = (f32[32,384]{1,0:T(8,128)S(1)}, f32[32,384]{1,0:T(8,128)S(1)}, u32[]{:S(2)}, u32[]{:S(2)}) collective-permute-start(f32[32,384]{1,0:T(8,128)S(1)} %get-tuple-element.55), channel_id=1, source_target_pairs={{0,24},{1,25},{2,26},{3,27},{4,28},{5,29},{6,30},{7,31},{8,16},{9,... | collective-permute-start | bytes 147464 | tf_op jit(solution)/shard_map/ppermute | solution.py:297
  127.0 6.5 %copy-start.5 = (bf16[64,128,128]{2,1,0:T(8,128)(2,1)S(1)}, bf16[64,128,128]{2,1,0:T(8,128)(2,1)}, u32[]{:S(2)}) copy-start(bf16[64,128,128]{2,1,0:T(8,128)(2,1)} %copy-done.4) | copy-start | bytes 6291460
  129.1 7.1 %collective-permute-start.13 = (f32[32,384]{1,0:T(8,128)S(1)}, f32[32,384]{1,0:T(8,128)S(1)}, u32[]{:S(2)}, u32[]{:S(2)}) collective-permute-start(f32[32,384]{1,0:T(8,128)S(1)} %get-tuple-element.53), channel_id=1, source_target_pairs={{0,32},{1,33},{2,34},{3,35},{4,36},{5,37},{6,38},{7,39},{8,40},{9,... | collective-permute-start | bytes 147464 | tf_op jit(solution)/shard_map/ppermute | solution.py:297
  130.9 5.2 %collective-permute-start.14 = (f32[32,384]{1,0:T(8,128)S(1)}, f32[32,384]{1,0:T(8,128)S(1)}, u32[]{:S(2)}, u32[]{:S(2)}) collective-permute-start(f32[32,384]{1,0:T(8,128)S(1)} %get-tuple-element.54), channel_id=1, source_target_pairs={{0,64},{1,65},{2,66},{3,67},{4,68},{5,69},{6,70},{7,71},{8,72},{9,... | collective-permute-start | bytes 147464 | tf_op jit(solution)/shard_map/ppermute | solution.py:297
  133.5 4.2 %collective-permute-start.15 = (f32[32,384]{1,0:T(8,128)S(1)}, f32[32,384]{1,0:T(8,128)S(1)}, u32[]{:S(2)}, u32[]{:S(2)}) collective-permute-start(f32[32,384]{1,0:T(8,128)S(1)} %get-tuple-element.52), channel_id=1, source_target_pairs={{0,96},{1,97},{2,98},{3,99},{4,100},{5,101},{6,102},{7,103},{8,104... | collective-permute-start | bytes 147464 | tf_op jit(solution)/shard_map/ppermute | solution.py:297
  137.6 5.6 %collective-permute-start.16 = (f32[32,256]{1,0:T(8,128)S(1)}, f32[32,256]{1,0:T(8,128)S(1)}, u32[]{:S(2)}, u32[]{:S(2)}) collective-permute-start(f32[32,256]{1,0:T(8,128)S(1)} %slice.49), channel_id=1, source_target_pairs={{0,1},{1,0},{2,3},{3,2},{4,5},{5,4},{6,7},{7,6},{8,9},{9,8},{10,11... | collective-permute-start | bytes 98312 | tf_op jit(solution)/shard_map/ppermute | solution.py:297

commit v11 on v8

--- a/solution.py
+++ b/solution.py
@@ -10,7 +10,7 @@
 from jax.sharding import PartitionSpec as P
 
 BOTH = ("row", "col")
-TILE = 16
+TILE = 32
 GRAD_TILE = 8
 BLOCKS = 4
 CORES = 2

time: 144 us -> 144 us (level)
  transfers between devices with their start and end apart: 19 -> 19, of which waited for: 12 -> 12; matrix products, arithmetic and copies ran while one was open for 6% -> 6% of each run, Pallas kernels for 28% -> 27%
where the time goes in v11:
time: 144 us; the launch traced here: 143 us
  Pallas kernels  41.7 us (29%)
  starting transfers between devices  41.3 us (29%)
  waiting for transfers between devices  30 us (21%)
  local copies, waits for them, and re-layouts  21.6 us (15%)
  matrix products  4.08 us (3%)
  other arithmetic  3.4 us (2%)
    ppermute x15, starting transfers between devices, partner(): lax.ppermute(part, BOTH, [(i, i ^ mask) for i in range(lax.axis_size(BOTH...  22.3 us
    all_to_all x2, waiting for transfers between devices, exchange(): return lax.all_to_all(blocks, BOTH, 0, 0, tiled=True)  18.6 us
    all_to_all x2, starting transfers between devices, exchange(): return lax.all_to_all(blocks, BOTH, 0, 0, tiled=True)  16.8 us
    pallas_call x1, Pallas kernels, forward(): pl.pallas_call(functools.partial(forward_kernel, 1.0 / seqs, width), grid...  13.7 us
    ppermute x15, waiting for transfers between devices, partner(): lax.ppermute(part, BOTH, [(i, i ^ mask) for i in range(lax.axis_size(BOTH...  11.4 us
    pallas_call x1, Pallas kernels, left_grads(): pl.pallas_call(functools.partial(left_kernel, 1.0 / seqs), in_specs=[pl.B...  10 us
    pallas_call x1, Pallas kernels, outer_grads(): pl.pallas_call(functools.partial(outer_grad_kernel, width), grid=(cols //...  9.63 us
    unnamed x30, local copies, waits for them, and re-layouts  7.02 us
  transfers between devices with their start and end apart: 19, of which 12 were waited for; matrix products, arithmetic and copies ran while one was open for 6% of the time, Pallas kernels for 27%

profile of v11, /device:TPU:1, one launch (start us, length us, event | category | flops | bytes accessed | tf_op | source)
XLA Modules:
  0.0 143.3 jit_solution(7777901330500610485)
XLA Ops:
  0.6 1.5 %copy.45 = bf16[2,1024,256]{1,2,0:T(8,128)(2,1)S(1)} copy(bf16[2,1024,256]{2,1,0:T(8,128)(2,1)} %param.8) | data formatting | bytes 2097152 | tf_op args[0]
  5.8 2.4 %pack.1 = bf16[8,8,2,2,4096]{4,3,2,1,0:T(2,128)(2,1)} custom-call(bf16[8,2,2,2048]{3,2,1,0:T(2,128)(2,1)} %reshape.107.left_ref, bf16[8,2,2,2048]{3,2,1,0:T(2,128)(2,1)} %bitcast.114), custom_call_target="tpu_custom_call" | custom-call | bytes 2097152 | tf_op jit(solution)/shard_map/pack/pallas_call | solution.py:206
  8.3 12.0 %all-to-all-start = ((bf16[128,2,4096]{2,1,0:T(2,128)(2,1)}), bf16[128,2,4096]{2,1,0:T(2,128)(2,1)}, u32[]{:S(2)}, u32[]{:S(2)}) async-start(bf16[128,2,4096]{2,1,0:T(2,128)(2,1)} %bitcast.110), calls=%async_computation | async-start | bytes 4194304 | tf_op jit(solution)/shard_map/all_to_all | solution.py:270
  20.7 2.9 %copy.85 = bf16[128,64,128]{2,0,1:T(8,128)(2,1)S(1)} copy(bf16[128,64,128]{2,1,0:T(8,128)(2,1)} %param.13) | data formatting | bytes 4194304 | tf_op args[5]
  23.7 9.6 %outer_grads.1.grad_ref = bf16[2048,4096]{1,0:T(8,128)(2,1)} custom-call(bf16[1024,128]{1,0:T(8,128)(2,1)S(1)} %copy.55.weight_ref, bf16[64,128,128]{2,1,0:T(8,128)(2,1)S(1)} %bitcast.105), custom_call_target="tpu_custom_call" | custom-call | flops 2147483648 | bytes 18874368 | tf_op jit(solution)/shard_map/outer_grads/pallas_call | solution.py:152
  33.3 17.1 %all-to-all-done = bf16[128,2,4096]{2,1,0:T(2,128)(2,1)} async-done(((bf16[128,2,4096]{2,1,0:T(2,128)(2,1)}), bf16[128,2,4096]{2,1,0:T(2,128)(2,1)}, u32[]{:S(2)}, u32[]{:S(2)}) %all-to-all-start) | async-done | bytes 2097184 | tf_op jit(solution)/shard_map/all_to_all | solution.py:270
  50.4 2.7 %reshape.110.came_ref.own_ref.right_ref = bf16[256,4096]{1,0:T(8,128)(2,1)S(1)} reshape(bf16[128,2,4096]{2,1,0:T(2,128)(2,1)} %all-to-all-done) | data formatting | bytes 4194304 | tf_op jit(solution)/shard_map/reshape | solution.py:373
  54.5 10.0 %left_grads.1 = (bf16[256,4096]{1,0:T(8,128)(2,1)S(1)}, f32[256,2048]{1,0:T(8,128)S(1)}) custom-call(bf16[256,4096]{1,0:T(8,128)(2,1)} %copy-done.2, bf16[2048,4096]{1,0:T(8,128)(2,1)} %outer_grads.1.grad_ref), custom_call_target="tpu_custom_call" | custom-call | flops 6442450944 | bytes 22020096 | tf_op jit(solution)/shard_map/left_grads/pallas_call | solution.py:169
  64.6 1.2 collective-permute-start.1
  65.8 4.6 %right_grads.1 = bf16[256,2048]{1,0:T(8,128)(2,1)S(1)} custom-call(bf16[256,2048]{1,0:T(8,128)(2,1)S(1)} %collective-permute-done.other_ref, f32[256,2048]{1,0:T(8,128)S(1)} %get-tuple-element.27.partial_ref, bf16[2048,4096]{1,0:T(8,128)(2,1)} %outer_grads.1.grad_ref), custom_call_target="tpu_custom_call" | custom-call | flops 2147483648 | bytes 12582912 | tf_op jit(solution)/shard_map/right_grads/pallas_call | solution.py:191
  71.0 2.6 %reshape.111 = bf16[128,2,4096]{2,1,0:T(2,128)(2,1)} reshape(bf16[256,4096]{1,0:T(8,128)(2,1)S(1)} %pad_maximum_fusion) | data formatting | bytes 4194304 | tf_op jit(solution)/shard_map/reshape | solution.py:380
  73.6 4.8 %all-to-all-start.1 = ((bf16[128,2,4096]{2,1,0:T(2,128)(2,1)}), bf16[128,2,4096]{2,1,0:T(2,128)(2,1)}, u32[]{:S(2)}, u32[]{:S(2)}) async-start(bf16[128,2,4096]{2,1,0:T(2,128)(2,1)} %reshape.111), calls=%async_computation.1 | async-start | bytes 4194304 | tf_op jit(solution)/shard_map/all_to_all | solution.py:270
  78.5 13.7 %forward.1 = (bf16[64,128,128]{2,1,0:T(8,128)(2,1)S(1)}, f32[1024,128]{1,0:T(8,128)S(1)}) custom-call(s32[1]{0:T(128)} %bitcast.7.core_ref, bf16[256,4096]{1,0:T(8,128)(2,1)S(1)} %copy-done.3, bf16[256,2048]{1,0:T(8,128)(2,1)S(1)} %collective-permute-done.other_ref, bf16[256,4096]{1,0:T(8,128)(2,1)S(1)} %copy-done.3, bf16[128,1024]{1,0:T(8,128)(2,1)S(1)} %bitcast.107, ...), custom_call_target="tpu_custom_call" | custom-call | flops 8589934592 | bytes 8388608 | tf_op jit(solution)/shard_map/forward/pallas_call | solution.py:222
  92.3 1.3 copy-done.4
  94.4 1.2 collective-permute-start.2
  98.3 2.4 %collective-permute-start.4 = (f32[16,8,128]{2,1,0:T(8,128)S(1)}, f32[16,8,128]{2,1,0:T(8,128)S(1)}, u32[]{:S(2)}, u32[]{:S(2)}) collective-permute-start(f32[16,8,128]{2,1,0:T(8,128)S(1)} %get-tuple-element.42), channel_id=1, source_target_pairs={{0,4},{1,5},{2,6},{3,7},{4,0},{5,1},{6,2},{7,3},{8,12},{9,13},{10,... | collective-permute-start | bytes 196616 | tf_op jit(solution)/shard_map/ppermute | solution.py:296
  101.7 1.6 %collective-permute-done.3 = f32[16,8,128]{2,1,0:T(8,128)S(1)} collective-permute-done((f32[16,8,128]{2,1,0:T(8,128)S(1)}, f32[16,8,128]{2,1,0:T(8,128)S(1)}, u32[]{:S(2)}, u32[]{:S(2)}) %collective-permute-start.3) | collective-permute-done | bytes 65568 | tf_op jit(solution)/shard_map/ppermute | solution.py:296
  103.3 2.9 %collective-permute-done.4 = f32[16,8,128]{2,1,0:T(8,128)S(1)} collective-permute-done((f32[16,8,128]{2,1,0:T(8,128)S(1)}, f32[16,8,128]{2,1,0:T(8,128)S(1)}, u32[]{:S(2)}, u32[]{:S(2)}) %collective-permute-start.4) | collective-permute-done | bytes 65568 | tf_op jit(solution)/shard_map/ppermute | solution.py:296
  107.1 1.5 %all-to-all-done.1 = bf16[128,2,4096]{2,1,0:T(2,128)(2,1)} async-done(((bf16[128,2,4096]{2,1,0:T(2,128)(2,1)}), bf16[128,2,4096]{2,1,0:T(2,128)(2,1)}, u32[]{:S(2)}, u32[]{:S(2)}) %all-to-all-start.1) | async-done | bytes 2097184 | tf_op jit(solution)/shard_map/all_to_all | solution.py:270
  108.6 2.7 %reshape.112 = bf16[256,4096]{1,0:T(8,128)(2,1)S(1)} reshape(bf16[128,2,4096]{2,1,0:T(2,128)(2,1)} %all-to-all-done.1) | data formatting | bytes 4194304 | tf_op jit(solution)/shard_map/reshape | solution.py:382
  114.4 1.5 %collective-permute-start.6 = (f32[32,256]{1,0:T(8,128)S(1)}, f32[32,256]{1,0:T(8,128)S(1)}, u32[]{:S(2)}, u32[]{:S(2)}) collective-permute-start(f32[32,256]{1,0:T(8,128)S(1)} %get-tuple-element.62), channel_id=1, source_target_pairs={{0,1},{1,0},{2,3},{3,2},{4,5},{5,4},{6,7},{7,6},{8,9},{9,8},{10,11... | collective-permute-start | bytes 98312 | tf_op jit(solution)/shard_map/ppermute | solution.py:296
  116.8 2.7 %collective-permute-start.9 = (f32[32,256]{1,0:T(8,128)S(1)}, f32[32,256]{1,0:T(8,128)S(1)}, u32[]{:S(2)}, u32[]{:S(2)}) collective-permute-start(f32[32,256]{1,0:T(8,128)S(1)} %select_add_fusion), channel_id=1, source_target_pairs={{0,6},{1,7},{2,4},{3,5},{4,2},{5,3},{6,0},{7,1},{8,14},{9,15},{10,... | collective-permute-start | bytes 98312 | tf_op jit(solution)/shard_map/ppermute | solution.py:296
  119.5 1.7 %collective-permute-done.8 = f32[32,256]{1,0:T(8,128)S(1)} collective-permute-done((f32[32,256]{1,0:T(8,128)S(1)}, f32[32,256]{1,0:T(8,128)S(1)}, u32[]{:S(2)}, u32[]{:S(2)}) %collective-permute-start.8) | collective-permute-done | bytes 32800 | tf_op jit(solution)/shard_map/ppermute | solution.py:296
  121.2 1.2 collective-permute-done.7
  122.5 1.7 %collective-permute-start.11 = (f32[32,384]{1,0:T(8,128)S(1)}, f32[32,384]{1,0:T(8,128)S(1)}, u32[]{:S(2)}, u32[]{:S(2)}) collective-permute-start(f32[32,384]{1,0:T(8,128)S(1)} %get-tuple-element.57), channel_id=1, source_target_pairs={{0,16},{1,17},{2,18},{3,19},{4,20},{5,21},{6,22},{7,23},{8,24},{9,... | collective-permute-start | bytes 147464 | tf_op jit(solution)/shard_map/ppermute | solution.py:296
  124.2 2.1 %collective-permute-start.12 = (f32[32,384]{1,0:T(8,128)S(1)}, f32[32,384]{1,0:T(8,128)S(1)}, u32[]{:S(2)}, u32[]{:S(2)}) collective-permute-start(f32[32,384]{1,0:T(8,128)S(1)} %get-tuple-element.55), channel_id=1, source_target_pairs={{0,24},{1,25},{2,26},{3,27},{4,28},{5,29},{6,30},{7,31},{8,16},{9,... | collective-permute-start | bytes 147464 | tf_op jit(solution)/shard_map/ppermute | solution.py:296
  126.9 1.3 flip.1
  128.5 1.9 %collective-permute-start.13 = (f32[32,384]{1,0:T(8,128)S(1)}, f32[32,384]{1,0:T(8,128)S(1)}, u32[]{:S(2)}, u32[]{:S(2)}) collective-permute-start(f32[32,384]{1,0:T(8,128)S(1)} %get-tuple-element.53), channel_id=1, source_target_pairs={{0,32},{1,33},{2,34},{3,35},{4,36},{5,37},{6,38},{7,39},{8,40},{9,... | collective-permute-start | bytes 147464 | tf_op jit(solution)/shard_map/ppermute | solution.py:296
  130.3 2.5 %collective-permute-start.14 = (f32[32,384]{1,0:T(8,128)S(1)}, f32[32,384]{1,0:T(8,128)S(1)}, u32[]{:S(2)}, u32[]{:S(2)}) collective-permute-start(f32[32,384]{1,0:T(8,128)S(1)} %get-tuple-element.54), channel_id=1, source_target_pairs={{0,64},{1,65},{2,66},{3,67},{4,68},{5,69},{6,70},{7,71},{8,72},{9,... | collective-permute-start | bytes 147464 | tf_op jit(solution)/shard_map/ppermute | solution.py:296
  132.9 2.7 %copy.84 = bf16[64,128,128]{2,0,1:T(8,128)(2,1)} copy(bf16[64,128,128]{2,1,0:T(8,128)(2,1)S(1)} %copy-done.5) | data formatting | bytes 4194304 | tf_op jit(solution)/shard_map/optimization_barrier | solution.py:387
  135.5 1.5 %collective-permute-done.15 = f32[32,384]{1,0:T(8,128)S(1)} collective-permute-done((f32[32,384]{1,0:T(8,128)S(1)}, f32[32,384]{1,0:T(8,128)S(1)}, u32[]{:S(2)}, u32[]{:S(2)}) %collective-permute-start.15) | collective-permute-done | bytes 49184 | tf_op jit(solution)/shard_map/ppermute | solution.py:296
  137.0 4.7 %collective-permute-start.16 = (f32[32,256]{1,0:T(8,128)S(1)}, f32[32,256]{1,0:T(8,128)S(1)}, u32[]{:S(2)}, u32[]{:S(2)}) collective-permute-start(f32[32,256]{1,0:T(8,128)S(1)} %slice.49), channel_id=1, source_target_pairs={{0,1},{1,0},{2,3},{3,2},{4,5},{5,4},{6,7},{7,6},{8,9},{9,8},{10,11... | collective-permute-start | bytes 98312 | tf_op jit(solution)/shard_map/ppermute | solution.py:296
  (92 shorter events, 17.7 us)
Async XLA Ops:
  0.6 2.1 %copy-start = (bf16[256,32]{0,1:T(8,128)(2,1)S(1)}, bf16[256,32]{0,1:T(8,128)(2,1)}, u32[]{:S(2)}) copy-start(bf16[256,32]{0,1:T(8,128)(2,1)} %param.9) | copy-start | bytes 49156
  2.1 1.7 %copy-start.7 = (bf16[2,1024,256]{1,2,0:T(8,128)(2,1)}, bf16[2,1024,256]{1,2,0:T(8,128)(2,1)S(1)}, u32[]{:S(2)}) copy-start(bf16[2,1024,256]{1,2,0:T(8,128)(2,1)S(1)} %copy.45) | copy-start | bytes 3145732
  2.2 1.7 %copy-start.10 = (bf16[256,32]{0,1:T(8,128)(2,1)S(1)}, bf16[256,32]{0,1:T(8,128)(2,1)}, u32[]{:S(2)}) copy-start(bf16[256,32]{0,1:T(8,128)(2,1)} %param.10) | copy-start | bytes 49156
  8.3 12.0 %copy-start.9 = (bf16[1024,128]{1,0:T(8,128)(2,1)S(1)}, bf16[1024,128]{1,0:T(8,128)(2,1)}, u32[]{:S(2)}) copy-start(bf16[1024,128]{1,0:T(8,128)(2,1)} %param.11) | copy-start | bytes 786436
  8.3 42.1 %all-to-all-start = ((bf16[128,2,4096]{2,1,0:T(2,128)(2,1)}), bf16[128,2,4096]{2,1,0:T(2,128)(2,1)}, u32[]{:S(2)}, u32[]{:S(2)}) async-start(bf16[128,2,4096]{2,1,0:T(2,128)(2,1)} %bitcast.110), calls=%async_computation | async-start | bytes 4194304 | tf_op jit(solution)/shard_map/all_to_all | solution.py:270
  23.6 9.6 %copy-start.1 = (bf16[128,64,128]{2,0,1:T(8,128)(2,1)}, bf16[128,64,128]{2,0,1:T(8,128)(2,1)S(1)}, u32[]{:S(2)}) copy-start(bf16[128,64,128]{2,0,1:T(8,128)(2,1)S(1)} %copy.85) | copy-start | bytes 6291460
  53.2 1.3 copy-start.2
  53.2 11.3 %collective-permute-start = (bf16[256,2048]{1,0:T(8,128)(2,1)S(1)}, bf16[256,2048]{1,0:T(8,128)(2,1)S(1)}, u32[]{:S(2)}, u32[]{:S(2)}) collective-permute-start(bf16[256,2048]{1,0:T(8,128)(2,1)S(1)} %slice.46), channel_id=1, source_target_pairs={{0,1},{1,0},{2,3},{3,2},{4,5},{5,4},{6,7},{7,6},{8,9},{9,8},{10,11... | collective-permute-start | bytes 3145736 | tf_op jit(solution)/shard_map/ppermute | solution.py:274
  64.6 5.8 %collective-permute-start.1 = (bf16[256,2048]{1,0:T(8,128)(2,1)S(1)}, bf16[256,2048]{1,0:T(8,128)(2,1)S(1)}, u32[]{:S(2)}, u32[]{:S(2)}) collective-permute-start(bf16[256,2048]{1,0:T(8,128)(2,1)S(1)} %slice.37), channel_id=1, source_target_pairs={{0,1},{1,0},{2,3},{3,2},{4,5},{5,4},{6,7},{7,6},{8,9},{9,8},{10,11... | collective-permute-start | bytes 3145736 | tf_op jit(solution)/shard_map/ppermute | solution.py:274
  73.6 4.9 %copy-start.12 = (bf16[128]{0:T(256)(128)(2,1)S(1)}, bf16[128]{0:T(256)(128)(2,1)}, u32[]{:S(2)}) copy-start(bf16[128]{0:T(256)(128)(2,1)} %param.12) | copy-start | bytes 772
  73.6 4.9 %copy-start.3 = (bf16[256,4096]{1,0:T(8,128)(2,1)S(1)}, bf16[256,4096]{1,0:T(8,128)(2,1)}, u32[]{:S(2)}) copy-start(bf16[256,4096]{1,0:T(8,128)(2,1)} %copy-done.2) | copy-start | bytes 6291460
  73.6 35.0 %all-to-all-start.1 = ((bf16[128,2,4096]{2,1,0:T(2,128)(2,1)}), bf16[128,2,4096]{2,1,0:T(2,128)(2,1)}, u32[]{:S(2)}, u32[]{:S(2)}) async-start(bf16[128,2,4096]{2,1,0:T(2,128)(2,1)} %reshape.111), calls=%async_computation.1 | async-start | bytes 4194304 | tf_op jit(solution)/shard_map/all_to_all | solution.py:270
  92.3 1.3 copy-start.4
  93.6 0.8 copy-start.6
  94.4 2.3 %collective-permute-start.2 = (f32[64,8,128]{2,1,0:T(8,128)S(1)}, f32[64,8,128]{2,1,0:T(8,128)S(1)}, u32[]{:S(2)}, u32[]{:S(2)}) collective-permute-start(f32[64,8,128]{2,1,0:T(8,128)S(1)} %dynamic-slice_bitcast_fusion), channel_id=1, source_target_pairs={{0,1},{1,0},{2,3},{3,2},{4,5},{5,4},{6,7},{7,6},{8,9},{9,8},{10,11... | collective-permute-start | bytes 786440 | tf_op jit(solution)/shard_map/ppermute | solution.py:296
  97.8 5.5 %collective-permute-start.3 = (f32[16,8,128]{2,1,0:T(8,128)S(1)}, f32[16,8,128]{2,1,0:T(8,128)S(1)}, u32[]{:S(2)}, u32[]{:S(2)}) collective-permute-start(f32[16,8,128]{2,1,0:T(8,128)S(1)} %get-tuple-element.43), channel_id=1, source_target_pairs={{0,2},{1,3},{2,0},{3,1},{4,6},{5,7},{6,4},{7,5},{8,10},{9,11},{10,... | collective-permute-start | bytes 196616 | tf_op jit(solution)/shard_map/ppermute | solution.py:296
  98.3 7.9 %collective-permute-start.4 = (f32[16,8,128]{2,1,0:T(8,128)S(1)}, f32[16,8,128]{2,1,0:T(8,128)S(1)}, u32[]{:S(2)}, u32[]{:S(2)}) collective-permute-start(f32[16,8,128]{2,1,0:T(8,128)S(1)} %get-tuple-element.42), channel_id=1, source_target_pairs={{0,4},{1,5},{2,6},{3,7},{4,0},{5,1},{6,2},{7,3},{8,12},{9,13},{10,... | collective-permute-start | bytes 196616 | tf_op jit(solution)/shard_map/ppermute | solution.py:296
  100.8 6.3 %collective-permute-start.5 = (f32[16,8,128]{2,1,0:T(8,128)S(1)}, f32[16,8,128]{2,1,0:T(8,128)S(1)}, u32[]{:S(2)}, u32[]{:S(2)}) collective-permute-start(f32[16,8,128]{2,1,0:T(8,128)S(1)} %get-tuple-element.41), channel_id=1, source_target_pairs={{0,6},{1,7},{2,4},{3,5},{4,2},{5,3},{6,0},{7,1},{8,14},{9,15},{10,... | collective-permute-start | bytes 196616 | tf_op jit(solution)/shard_map/ppermute | solution.py:296
  107.1 4.3 %copy-start.11 = (bf16[32,256]{1,0:T(8,128)(2,1)S(1)}, bf16[32,256]{1,0:T(8,128)(2,1)}, u32[]{:S(2)}) copy-start(bf16[32,256]{1,0:T(8,128)(2,1)} %constant.144.clone) | copy-start | bytes 49156
  107.1 4.6 %copy-start.8 = (bf16[2,1024,256]{1,2,0:T(8,128)(2,1)S(1)}, bf16[2,1024,256]{1,2,0:T(8,128)(2,1)}, u32[]{:S(2)}) copy-start(bf16[2,1024,256]{1,2,0:T(8,128)(2,1)} %copy-done.7) | copy-start | bytes 3145732
  114.4 2.3 %collective-permute-start.6 = (f32[32,256]{1,0:T(8,128)S(1)}, f32[32,256]{1,0:T(8,128)S(1)}, u32[]{:S(2)}, u32[]{:S(2)}) collective-permute-start(f32[32,256]{1,0:T(8,128)S(1)} %get-tuple-element.62), channel_id=1, source_target_pairs={{0,1},{1,0},{2,3},{3,2},{4,5},{5,4},{6,7},{7,6},{8,9},{9,8},{10,11... | collective-permute-start | bytes 98312 | tf_op jit(solution)/shard_map/ppermute | solution.py:296
  116.8 4.4 %collective-permute-start.8 = (f32[32,256]{1,0:T(8,128)S(1)}, f32[32,256]{1,0:T(8,128)S(1)}, u32[]{:S(2)}, u32[]{:S(2)}) collective-permute-start(f32[32,256]{1,0:T(8,128)S(1)} %select_add_fusion), channel_id=1, source_target_pairs={{0,4},{1,5},{2,6},{3,7},{4,0},{5,1},{6,2},{7,3},{8,12},{9,13},{10,... | collective-permute-start | bytes 98312 | tf_op jit(solution)/shard_map/ppermute | solution.py:296
  116.8 4.4 %collective-permute-start.9 = (f32[32,256]{1,0:T(8,128)S(1)}, f32[32,256]{1,0:T(8,128)S(1)}, u32[]{:S(2)}, u32[]{:S(2)}) collective-permute-start(f32[32,256]{1,0:T(8,128)S(1)} %select_add_fusion), channel_id=1, source_target_pairs={{0,6},{1,7},{2,4},{3,5},{4,2},{5,3},{6,0},{7,1},{8,14},{9,15},{10,... | collective-permute-start | bytes 98312 | tf_op jit(solution)/shard_map/ppermute | solution.py:296
  119.5 2.9 %collective-permute-start.7 = (f32[32,256]{1,0:T(8,128)S(1)}, f32[32,256]{1,0:T(8,128)S(1)}, u32[]{:S(2)}, u32[]{:S(2)}) collective-permute-start(f32[32,256]{1,0:T(8,128)S(1)} %select_add_fusion), channel_id=1, source_target_pairs={{0,2},{1,3},{2,0},{3,1},{4,6},{5,7},{6,4},{7,5},{8,10},{9,11},{10,... | collective-permute-start | bytes 98312 | tf_op jit(solution)/shard_map/ppermute | solution.py:296
  122.4 5.8 %collective-permute-start.10 = (f32[32,384]{1,0:T(8,128)S(1)}, f32[32,384]{1,0:T(8,128)S(1)}, u32[]{:S(2)}, u32[]{:S(2)}) collective-permute-start(f32[32,384]{1,0:T(8,128)S(1)} %get-tuple-element.56), channel_id=1, source_target_pairs={{0,8},{1,9},{2,10},{3,11},{4,12},{5,13},{6,14},{7,15},{8,0},{9,1},... | collective-permute-start | bytes 147464 | tf_op jit(solution)/shard_map/ppermute | solution.py:296
  122.5 5.7 %collective-permute-start.11 = (f32[32,384]{1,0:T(8,128)S(1)}, f32[32,384]{1,0:T(8,128)S(1)}, u32[]{:S(2)}, u32[]{:S(2)}) collective-permute-start(f32[32,384]{1,0:T(8,128)S(1)} %get-tuple-element.57), channel_id=1, source_target_pairs={{0,16},{1,17},{2,18},{3,19},{4,20},{5,21},{6,22},{7,23},{8,24},{9,... | collective-permute-start | bytes 147464 | tf_op jit(solution)/shard_map/ppermute | solution.py:296
  124.2 4.2 %collective-permute-start.12 = (f32[32,384]{1,0:T(8,128)S(1)}, f32[32,384]{1,0:T(8,128)S(1)}, u32[]{:S(2)}, u32[]{:S(2)}) collective-permute-start(f32[32,384]{1,0:T(8,128)S(1)} %get-tuple-element.55), channel_id=1, source_target_pairs={{0,24},{1,25},{2,26},{3,27},{4,28},{5,29},{6,30},{7,31},{8,16},{9,... | collective-permute-start | bytes 147464 | tf_op jit(solution)/shard_map/ppermute | solution.py:296
  126.9 5.9 %copy-start.5 = (bf16[64,128,128]{2,1,0:T(8,128)(2,1)S(1)}, bf16[64,128,128]{2,1,0:T(8,128)(2,1)}, u32[]{:S(2)}) copy-start(bf16[64,128,128]{2,1,0:T(8,128)(2,1)} %copy-done.4) | copy-start | bytes 6291460
  128.5 7.1 %collective-permute-start.13 = (f32[32,384]{1,0:T(8,128)S(1)}, f32[32,384]{1,0:T(8,128)S(1)}, u32[]{:S(2)}, u32[]{:S(2)}) collective-permute-start(f32[32,384]{1,0:T(8,128)S(1)} %get-tuple-element.53), channel_id=1, source_target_pairs={{0,32},{1,33},{2,34},{3,35},{4,36},{5,37},{6,38},{7,39},{8,40},{9,... | collective-permute-start | bytes 147464 | tf_op jit(solution)/shard_map/ppermute | solution.py:296
  130.3 5.2 %collective-permute-start.14 = (f32[32,384]{1,0:T(8,128)S(1)}, f32[32,384]{1,0:T(8,128)S(1)}, u32[]{:S(2)}, u32[]{:S(2)}) collective-permute-start(f32[32,384]{1,0:T(8,128)S(1)} %get-tuple-element.54), channel_id=1, source_target_pairs={{0,64},{1,65},{2,66},{3,67},{4,68},{5,69},{6,70},{7,71},{8,72},{9,... | collective-permute-start | bytes 147464 | tf_op jit(solution)/shard_map/ppermute | solution.py:296
  132.9 4.2 %collective-permute-start.15 = (f32[32,384]{1,0:T(8,128)S(1)}, f32[32,384]{1,0:T(8,128)S(1)}, u32[]{:S(2)}, u32[]{:S(2)}) collective-permute-start(f32[32,384]{1,0:T(8,128)S(1)} %get-tuple-element.52), channel_id=1, source_target_pairs={{0,96},{1,97},{2,98},{3,99},{4,100},{5,101},{6,102},{7,103},{8,104... | collective-permute-start | bytes 147464 | tf_op jit(solution)/shard_map/ppermute | solution.py:296
  137.0 5.6 %collective-permute-start.16 = (f32[32,256]{1,0:T(8,128)S(1)}, f32[32,256]{1,0:T(8,128)S(1)}, u32[]{:S(2)}, u32[]{:S(2)}) collective-permute-start(f32[32,256]{1,0:T(8,128)S(1)} %slice.49), channel_id=1, source_target_pairs={{0,1},{1,0},{2,3},{3,2},{4,5},{5,4},{6,7},{7,6},{8,9},{9,8},{10,11... | collective-permute-start | bytes 98312 | tf_op jit(solution)/shard_map/ppermute | solution.py:296
